TPU v7x, 128 devices: a whole 4x4x4 slice. The times are simulated.
128 devices in a mesh: slab: 2 (over z_lo), tile: 64 (over z_hi, x, y, core).
Axes of the slice: x: 4, y: 4, z: 4 (z_hi: 2, z_lo: 2; z = z_hi * 2 + z_lo), core: 2. Of those that a mesh axis runs over, the one named last changes fastest.
Arguments:
- transmission: float32 [4, 2, 8192, 384], P('slab', None, 'tile'), may hold values from -4.2 to 4.2
- probe: float32 [2, 256, 256], replicated, may hold values from -6 to 6
- scan_offsets: int32 [128, 2], P('tile'), may hold values from 0 to 128, as said below
- amplitudes: float32 [128, 256, 256], P('tile'), may hold values from 0.2 to 2
Outputs:
- object_grad: float32 [4, 2, 8192, 384], P('slab', None, 'tile')
- probe_grad: float32 [2, 256, 256], replicated
Inputs may be any that keep to these rules, and one draw needn't show every extreme that they name: `scan_offsets`: column 0 lies within 0 to 128 and column 1 within 0 to 128; both ends of both columns occur.
All inputs are finite; a program needn't handle non-finite values.
Results may differ from a plain program's by a relative error of at most 0.0003.
Values sent between devices are 32-bit elements; how exact they have to be, the bound alone decides.
No kernel may reach another device: no remote copies, remote signals or barrier semaphores. Data moves between devices by JAX's collectives and lax.ppermute only.
A program may use at most 128 MiB of HBM per device.

v0:
```python
import jax
import jax.numpy as jnp
from jax import lax
from jax.sharding import PartitionSpec as P

HALO = 128


prop_strength = 12.0
highest = lax.Precision.HIGHEST


def padded(cells, sides, width):
    for axis, dim in sides:
        count = lax.axis_size(axis)
        head = lax.slice_in_dim(cells, 0, width, axis=dim)
        tail = lax.slice_in_dim(cells, cells.shape[dim] - width, cells.shape[dim], axis=dim)
        cells = jnp.concatenate(
            [
                lax.ppermute(tail, axis, [(i, (i + 1) % count) for i in range(count)]),
                cells,
                lax.ppermute(head, axis, [((i + 1) % count, i) for i in range(count)]),
            ],
            axis=dim,
        )
    return cells


def from_behind(array, axis, by):
    devices = lax.axis_size(axis)
    pairs = [(i, i + by) for i in range(devices) if 0 <= i + by < devices]
    return lax.ppermute(array, axis, pairs)


def passed_along(array, axis, by):
    devices = lax.axis_size(axis)
    return lax.ppermute(array, axis, [(i, (i + by) % devices) for i in range(devices)])


def make_tables(width):
    index = jnp.arange(width)
    angle = -2.0 * jnp.pi / width * (index[:, None] * index[None, :] % width).astype(jnp.float32)
    scale = 1.0 / jnp.sqrt(jnp.float32(width))
    freq = ((index + width // 2) % width - width // 2).astype(jnp.float32) / width
    phase = -prop_strength * (freq[:, None] ** 2 + freq[None, :] ** 2)
    return (jnp.cos(angle) * scale, jnp.sin(angle) * scale, jnp.cos(phase), jnp.sin(phase))


def left_mult(matrix, batch):
    return jnp.einsum("jk,pkl->pjl", matrix, batch, precision=highest)


def right_mult(batch, matrix):
    return jnp.einsum("pjk,kl->pjl", batch, matrix, precision=highest)


def transform(real_part, imag_part, table_real, table_imag):
    first_real = left_mult(table_real, real_part) - left_mult(table_imag, imag_part)
    first_imag = left_mult(table_real, imag_part) + left_mult(table_imag, real_part)
    out_real = right_mult(first_real, table_real) - right_mult(first_imag, table_imag)
    out_imag = right_mult(first_real, table_imag) + right_mult(first_imag, table_real)
    return (out_real, out_imag)


def propagate(real_part, imag_part, tables):
    table_real, table_imag, kernel_real, kernel_imag = tables
    spec_real, spec_imag = transform(real_part, imag_part, table_real, table_imag)
    next_real = spec_real * kernel_real - spec_imag * kernel_imag
    next_imag = spec_real * kernel_imag + spec_imag * kernel_real
    return transform(next_real, next_imag, table_real, -table_imag)


def local_forward(extended, start, offsets, tables):
    width = start.shape[-1]
    depth = extended.shape[0]

    def cut(row_start, col_start):
        zero = jnp.int32(0)
        return lax.dynamic_slice(
            extended, (zero, zero, row_start, col_start), (depth, 2, width, width)
        )

    windows = jax.vmap(cut)(offsets[:, 0], offsets[:, 1])
    real_part = start[:, 0]
    imag_part = start[:, 1]
    for slice_index in range(depth):
        piece_real = windows[:, slice_index, 0]
        piece_imag = windows[:, slice_index, 1]
        prod_real = real_part * piece_real - imag_part * piece_imag
        prod_imag = real_part * piece_imag + imag_part * piece_real
        real_part, imag_part = propagate(prod_real, prod_imag, tables)
    return jnp.stack([real_part, imag_part], axis=1)


def far_loss(waves, target, tables):
    far_real, far_imag = transform(waves[:, 0], waves[:, 1], tables[0], tables[1])
    model = jnp.sqrt(far_real * far_real + far_imag * far_imag + 1.0)
    return 0.5 * jnp.sum((model - target) ** 2)


def shards(transmission, probe, scan_offsets, amplitudes):
    width = probe.shape[-1]
    band = transmission.shape[2]
    count = scan_offsets.shape[0]
    tables = make_tables(width)
    extended = padded(transmission, (("tile", 2),), HALO)
    probes = jnp.broadcast_to(probe[None], (count, 2, width, width))
    sections = lax.axis_size("slab")
    place = lax.axis_index("slab")
    start = probes
    leaving = local_forward(extended, start, scan_offsets, tables)
    arrived = from_behind(leaving, "slab", 1)
    start = jnp.where(place == 0, probes, arrived)
    leaving, pull = jax.vjp(
        lambda ext, beginning: local_forward(ext, beginning, scan_offsets, tables), extended, start
    )
    _, far_pull = jax.vjp(lambda waves: far_loss(waves, amplitudes, tables), leaving)
    grad_far = far_pull(jnp.float32(1.0))[0]
    grad_leaving = grad_far
    grad_ext, grad_start = pull(grad_leaving)
    arrived = from_behind(grad_start, "slab", -1)
    grad_leaving = jnp.where(place == sections - 1, grad_far, arrived)
    grad_own, grad_start = pull(grad_leaving)
    half = count // 2
    kept = jnp.sum(grad_start[:half], axis=0)
    handed = from_behind(grad_start[half:], "slab", 1)
    received = jnp.sum(handed, axis=0)
    probe_term = jnp.where(place == 0, kept, jnp.where(place == 1, received, jnp.zeros_like(probe)))
    probe_grad = lax.psum(probe_term, ("slab", "tile"))
    core = grad_own[:, :, HALO : HALO + band]
    from_next = passed_along(grad_own[:, :, :HALO], "tile", -1)
    from_prev = passed_along(grad_own[:, :, HALO + band :], "tile", 1)
    core = core + from_next
    core = core + from_prev
    return (core, probe_grad)


def solution(mesh):
    placed = (P("slab", None, "tile", None), P(), P("tile", None), P("tile", None, None))
    return jax.shard_map(
        shards,
        mesh=mesh,
        in_specs=placed,
        out_specs=(P("slab", None, "tile", None), P()),
        check_vma=False,
    )
```

profile of v0, /device:TPU:1, one launch (start us, length us, event | category | flops | bytes accessed | tf_op | source)
XLA Modules:
  0.0 574.8 jit_solution(9080661059306504255)
XLA Ops:
  7.2 2.8 collective-permute-start
  13.6 5.6 collective-permute-done
  23.4 6.6 %while.2 = (s32[]{:T(128)}, f32[2,2,384,384]{3,2,1,0:T(8,128)S(1)}, s32[2,4]{1,0:T(2,128)S(1)}, f32[2,2,2,256,256]{4,3,0,2,1:T(8,128)}, s32[]{:T(128)}) while((s32[]{:T(128)}, f32[2,2,384,384]{3,2,1,0:T(8,128)S(1)}, s32[2,4]{1,0:T(2,128)S(1)}, f32[2,2,2,256,256]{4,3,0,2,1:T(8,128)}, s32[]{:T(128)}) %tuple.59), condition=%wide.while_cond, body=%wide.while_body.sunk | while | flops 2 | bytes 2098301 | solution.py:79
  24.0 2.6 bitcast_dynamic-update-slice_fusion.2
  27.2 2.6 bitcast_dynamic-update-slice_fusion.2
  30.0 3.2 fusion.315
  33.3 3.1 fusion.319
  36.4 1.9 fusion.55
  41.9 1.9 fusion.54
  43.8 2.3 convolution_add_fusion.52
  48.0 1.9 fusion.308
  49.9 1.9 fusion.312
  51.8 1.9 fusion.53
  55.5 2.0 fusion.310
  57.5 1.9 fusion.52
  61.2 1.9 fusion.65
  66.7 2.1 fusion.51
  78.1 2.3 fusion.294
  80.4 1.9 fusion.298
  82.3 1.9 fusion.49
  87.8 1.9 fusion.48
  91.6 2.0 fusion.46
  94.6 4.5 collective-permute-start.2
  99.1 16.6 %collective-permute-done.2 = f32[2,2,256,256]{3,2,0,1:T(8,128)} collective-permute-done((f32[2,2,256,256]{3,2,0,1:T(8,128)}, f32[2,2,256,256]{3,2,0,1:T(8,128)}, u32[]{:S(2)}, u32[]{:S(2)}) %collective-permute-start.2) | collective-permute-done | bytes 1048608 | tf_op jit(solution)/shard_map/ppermute | solution.py:32
  127.1 2.2 convolution_add_fusion.44
  129.3 1.9 convolution_subtract_fusion.8
  131.2 1.9 fusion.280
  133.1 1.9 fusion.284
  135.0 1.9 fusion.43
  138.7 2.0 fusion.282
  140.7 1.9 fusion.42
  144.4 2.7 fusion.67
  150.7 2.0 fusion.41
  162.0 1.9 fusion.266
  163.9 2.3 fusion.270
  166.2 1.9 fusion.39
  171.7 1.9 fusion.38
  175.4 2.0 convolution_subtract_fusion.2
  186.7 2.0 fusion.36
  192.5 1.9 fusion.177
  194.4 1.9 fusion.256
  196.2 1.9 fusion.35
  198.1 2.1 fusion.174
  201.9 1.9 fusion.34
  235.2 2.0 fusion.238
  258.6 2.2 fusion.77
  263.1 21.1 %collective-permute-done.3 = f32[2,2,256,256]{3,2,0,1:T(8,128)} collective-permute-done((f32[2,2,256,256]{3,2,0,1:T(8,128)}, f32[2,2,256,256]{3,2,0,1:T(8,128)}, u32[]{:S(2)}, u32[]{:S(2)}) %collective-permute-start.3) | collective-permute-done | bytes 1048608 | tf_op jit(solution)/shard_map/ppermute | solution.py:32
  308.7 1.9 fusion.8
  310.6 2.0 add_bitcast_fusion.3
  320.7 2.0 fusion.6
  337.6 3.0 fusion.83
  342.7 43.2 %while.3 = (s32[]{:T(128)}, f32[2,2,384,384]{3,2,1,0:T(8,128)S(1)}, s32[2,4]{1,0:T(2,128)S(1)}, f32[2,2,2,256,256]{4,3,0,2,1:T(8,128)}, s32[]{:T(128)}, /*index=5*/s32[4]{0:T(128)S(1)}, s32[]{:T(128)}) while((s32[]{:T(128)}, f32[2,2,384,384]{3,2,1,0:T(8,128)S(1)}, s32[2,4]{1,0:T(2,128)S(1)}, f32[2,2,2,256,256]{4,3,0,2,1:T(8,128)}, s32[]{:T(128)}, ...), condition=%wide.while_cond.1, body=%wide.while_body.1.sunk | while | flops 524317 | bytes 5243083 | solution.py:79
  343.4 3.2 and_reduce_fusion.2
  346.6 3.5 add_select_fusion.3
  350.1 11.9 %dynamic-update-slice.8 = f32[2,2,384,384]{3,2,1,0:T(8,128)S(1)} dynamic-update-slice(f32[2,2,384,384]{3,2,1,0:T(8,128)S(1)} %get-tuple-element.162, f32[2,2,256,256]{3,2,1,0:T(8,128)S(1)} %add_select_fusion.3, s32[]{:T(128)} %constant.21.clone.1..sunk, s32[]{:T(128)} %constant.21.clone.1..sunk, s32[]{:T(128)} %bitcast.718, s32[]{:T(128)} %bitcast.719) | dynamic-update-slice | bytes 2097156 | tf_op jit(solution)/shard_map/transpose(jvp(vmap()))/scatter-add
  362.7 3.2 and_reduce_fusion.2
  365.9 3.5 add_select_fusion.3
  369.5 16.4 %dynamic-update-slice.8 = f32[2,2,384,384]{3,2,1,0:T(8,128)S(1)} dynamic-update-slice(f32[2,2,384,384]{3,2,1,0:T(8,128)S(1)} %get-tuple-element.162, f32[2,2,256,256]{3,2,1,0:T(8,128)S(1)} %add_select_fusion.3, s32[]{:T(128)} %constant.21.clone.1..sunk, s32[]{:T(128)} %constant.21.clone.1..sunk, s32[]{:T(128)} %bitcast.718, s32[]{:T(128)} %bitcast.719) | dynamic-update-slice | bytes 2097156 | tf_op jit(solution)/shard_map/transpose(jvp(vmap()))/scatter-add
  387.2 7.4 %collective-permute-start.4 = (f32[2,2,128,384]{3,2,1,0:T(8,128)}, f32[2,2,128,384]{3,2,1,0:T(8,128)S(1)}, u32[]{:S(2)}, u32[]{:S(2)}) collective-permute-start(f32[2,2,128,384]{3,2,1,0:T(8,128)} %get-tuple-element.60), channel_id=1, source_target_pairs={{0,63},{1,0},{2,1},{3,2},{4,3},{5,4},{6,5},{7,6},{8,7},{9,8},{10,9... | collective-permute-start | bytes 2359304 | tf_op jit(solution)/shard_map/ppermute | solution.py:37
  394.6 5.8 %collective-permute-start.5 = (f32[2,2,128,384]{3,2,1,0:T(8,128)}, f32[2,2,128,384]{3,2,1,0:T(8,128)}, u32[]{:S(2)}, u32[]{:S(2)}) collective-permute-start(f32[2,2,128,384]{3,2,1,0:T(8,128)} %get-tuple-element.61), channel_id=1, source_target_pairs={{0,1},{1,2},{2,3},{3,4},{4,5},{5,6},{6,7},{7,8},{8,9},{9,10},{10,1... | collective-permute-start | bytes 2359304 | tf_op jit(solution)/shard_map/ppermute | solution.py:37
  401.7 17.1 %collective-permute-done.6 = f32[1,2,256,256]{3,2,0,1:T(8,128)S(1)} collective-permute-done((f32[1,2,256,256]{3,2,0,1:T(8,128)S(1)}, f32[1,2,256,256]{3,2,0,1:T(8,128)S(1)}, u32[]{:S(2)}, u32[]{:S(2)}) %collective-permute-start.6) | collective-permute-done | bytes 524320 | tf_op jit(solution)/shard_map/ppermute | solution.py:32
  419.8 2.1 add_add_fusion
  421.9 144.0 %all-reduce.12.cloned.1.call-done = f32[2,256,256]{2,1,0:T(8,128)} async-done(((f32[2,256,256]{2,1,0:T(8,128)}), f32[2,256,256]{2,1,0:T(8,128)}) %all-reduce.12.cloned.1.call-update) | async-done | bytes 524304 | tf_op jit(solution)/shard_map/psum | solution.py:129
  565.9 1.9 copy.327
  (162 shorter events, 194.5 us)
Async XLA Ops:
  7.2 558.7 %all-reduce.12.cloned.1.call-start = ((), (), s32[]{:S(2)}) async-start(), calls=%async_computation | async-start | bytes 1048576 | tf_op jit(solution)/shard_map/psum | solution.py:129
  7.2 12.0 %collective-permute-start = (f32[2,2,128,384]{3,2,1,0:T(8,128)}, f32[2,2,128,384]{3,2,1,0:T(8,128)S(1)}, u32[]{:S(2)}, u32[]{:S(2)}) collective-permute-start(f32[2,2,128,384]{3,2,1,0:T(8,128)} %param.4), channel_id=1, source_target_pairs={{0,1},{1,2},{2,3},{3,4},{4,5},{5,6},{6,7},{7,8},{8,9},{9,10},{10,1... | collective-permute-start | bytes 2359304 | tf_op jit(solution)/shard_map/ppermute | solution.py:20
  10.0 11.9 %collective-permute-start.1 = (f32[2,2,128,384]{3,2,1,0:T(8,128)}, f32[2,2,128,384]{3,2,1,0:T(8,128)}, u32[]{:S(2)}, u32[]{:S(2)}) collective-permute-start(f32[2,2,128,384]{3,2,1,0:T(8,128)} %param.4), channel_id=1, source_target_pairs={{1,0},{2,1},{3,2},{4,3},{5,4},{6,5},{7,6},{8,7},{9,8},{10,9},{11,1... | collective-permute-start | bytes 2359304 | tf_op jit(solution)/shard_map/ppermute | solution.py:22
  10.0 11.9 %copy-start.9 = (f32[2,2,128,384]{3,2,1,0:T(8,128)S(1)}, f32[2,2,128,384]{3,2,1,0:T(8,128)}, u32[]{:S(2)}) copy-start(f32[2,2,128,384]{3,2,1,0:T(8,128)} %param.4) | copy-start | bytes 2359300
  19.2 0.9 copy-start.10
  30.0 6.3 %copy-start = (f32[2,2,2,256,256]{4,3,0,2,1:T(8,128)S(1)}, f32[2,2,2,256,256]{4,3,0,2,1:T(8,128)}, u32[]{:S(2)}) copy-start(f32[2,2,2,256,256]{4,3,0,2,1:T(8,128)} %get-tuple-element.9) | copy-start | bytes 6291460
  91.6 24.2 %copy-start.8 = (f32[2,256,256]{2,1,0:T(8,128)S(1)}, f32[2,256,256]{2,1,0:T(8,128)}, u32[]{:S(2)}) copy-start(f32[2,256,256]{2,1,0:T(8,128)} %param.5) | copy-start | bytes 1572868
  94.6 21.2 %collective-permute-start.2 = (f32[2,2,256,256]{3,2,0,1:T(8,128)}, f32[2,2,256,256]{3,2,0,1:T(8,128)}, u32[]{:S(2)}, u32[]{:S(2)}) collective-permute-start(f32[2,2,256,256]{3,2,0,1:T(8,128)} %pad_maximum_fusion.1), channel_id=1, source_target_pairs={{0,64},{1,65},{2,66},{3,67},{4,68},{5,69},{6,70},{7,71},{8,72},{9,... | collective-permute-start | bytes 3145736 | tf_op jit(solution)/shard_map/ppermute | solution.py:32
  115.9 2.0 copy-start.1
  186.7 5.8 %copy-start.12 = (f32[2,256,256]{2,1,0:T(8,128)S(1)}, f32[2,256,256]{2,1,0:T(8,128)}, u32[]{:S(2)}) copy-start(f32[2,256,256]{2,1,0:T(8,128)} %param.7) | copy-start | bytes 1572868
  205.4 13.2 %copy-start.5 = (f32[2,1,256,256]{3,2,0,1:T(8,128)}, f32[2,1,256,256]{3,2,0,1:T(8,128)S(1)}, u32[]{:S(2)}) copy-start(f32[2,1,256,256]{3,2,0,1:T(8,128)S(1)} %fusion.32) | copy-start | bytes 1572868
  207.1 9.8 %copy-start.6 = (f32[2,1,256,256]{3,2,0,1:T(8,128)}, f32[2,1,256,256]{3,2,0,1:T(8,128)S(1)}, u32[]{:S(2)}) copy-start(f32[2,1,256,256]{3,2,0,1:T(8,128)S(1)} %fusion.33) | copy-start | bytes 1572868
  261.8 22.4 %collective-permute-start.3 = (f32[2,2,256,256]{3,2,0,1:T(8,128)}, f32[2,2,256,256]{3,2,0,1:T(8,128)}, u32[]{:S(2)}, u32[]{:S(2)}) collective-permute-start(f32[2,2,256,256]{3,2,0,1:T(8,128)} %pad_add_fusion.2), channel_id=1, source_target_pairs={{64,0},{65,1},{66,2},{67,3},{68,4},{69,5},{70,6},{71,7},{72,8},{73... | collective-permute-start | bytes 3145736 | tf_op jit(solution)/shard_map/ppermute | solution.py:32
  307.1 3.5 copy-start.7
  334.3 3.3 copy-start.2
  342.0 0.7 copy-start.11
  385.9 14.5 %copy-start.3 = (f32[2,1,256,256]{3,2,0,1:T(8,128)S(1)}, f32[2,1,256,256]{3,2,0,1:T(8,128)}, u32[]{:S(2)}) copy-start(f32[2,1,256,256]{3,2,0,1:T(8,128)} %get-tuple-element.46) | copy-start | bytes 1572868
  385.9 14.5 %copy-start.4 = (f32[2,1,256,256]{3,2,0,1:T(8,128)S(1)}, f32[2,1,256,256]{3,2,0,1:T(8,128)}, u32[]{:S(2)}) copy-start(f32[2,1,256,256]{3,2,0,1:T(8,128)} %get-tuple-element.47) | copy-start | bytes 1572868
  387.2 32.5 %collective-permute-start.4 = (f32[2,2,128,384]{3,2,1,0:T(8,128)}, f32[2,2,128,384]{3,2,1,0:T(8,128)S(1)}, u32[]{:S(2)}, u32[]{:S(2)}) collective-permute-start(f32[2,2,128,384]{3,2,1,0:T(8,128)} %get-tuple-element.60), channel_id=1, source_target_pairs={{0,63},{1,0},{2,1},{3,2},{4,3},{5,4},{6,5},{7,6},{8,7},{9,8},{10,9... | collective-permute-start | bytes 2359304 | tf_op jit(solution)/shard_map/ppermute | solution.py:37
  394.6 25.2 %collective-permute-start.5 = (f32[2,2,128,384]{3,2,1,0:T(8,128)}, f32[2,2,128,384]{3,2,1,0:T(8,128)}, u32[]{:S(2)}, u32[]{:S(2)}) collective-permute-start(f32[2,2,128,384]{3,2,1,0:T(8,128)} %get-tuple-element.61), channel_id=1, source_target_pairs={{0,1},{1,2},{2,3},{3,4},{4,5},{5,6},{6,7},{7,8},{8,9},{9,10},{10,1... | collective-permute-start | bytes 2359304 | tf_op jit(solution)/shard_map/ppermute | solution.py:37
  400.4 18.5 %collective-permute-start.6 = (f32[1,2,256,256]{3,2,0,1:T(8,128)S(1)}, f32[1,2,256,256]{3,2,0,1:T(8,128)S(1)}, u32[]{:S(2)}, u32[]{:S(2)}) collective-permute-start(f32[1,2,256,256]{3,2,0,1:T(8,128)S(1)} %pad_add_fusion.3), channel_id=1, source_target_pairs={{0,64},{1,65},{2,66},{3,67},{4,68},{5,69},{6,70},{7,71},{8,72},{9,... | collective-permute-start | bytes 1572872 | tf_op jit(solution)/shard_map/ppermute | solution.py:32
Sparse Core Ops, SparseCore 0:
  419.9 145.9 all-reduce.11
where the time goes:
time: 578 us; the launch traced here: 575 us
  matrix products  262 us (45%)
  waiting for transfers between devices  206 us (36%)
  local copies, waits for them, and re-layouts  41.8 us (7%)
  other arithmetic  26.1 us (5%)
  starting transfers between devices  23.1 us (4%)
  between operations  15.6 us (3%)
    psum x1, waiting for transfers between devices, shards(): probe_grad = lax.psum(probe_term, ('slab', 'tile'))  144 us
    dot_general x72, matrix products, left_mult(): return jnp.einsum('jk,pkl->pjl', matrix, batch, precision=highest)  134 us
    dot_general x72, matrix products, right_mult(): return jnp.einsum('pjk,kl->pjl', batch, matrix, precision=highest)  128 us
    ppermute x3, waiting for transfers between devices, from_behind(): return lax.ppermute(array, axis, pairs)  54.9 us
    scatter-add x6, local copies, waits for them, and re-layouts  29.7 us
    scatter-add x4, other arithmetic  13.5 us
    ppermute x2, starting transfers between devices, passed_along(): lax.ppermute(array, axis, [(i, (i + by) % devices) for i in range(devices)])  13.2 us
  transfers between devices with their start and end apart: 8, of which 6 were waited for; matrix products, arithmetic and copies ran while one was open for 1% of the time, Pallas kernels for 0%

commit v1 on v0

v1 whole, which is shorter than its diff:
```python
import jax
import jax.numpy as jnp
import numpy as np
from jax import lax
from jax.experimental import pallas as pl
from jax.experimental.pallas import tpu as pltpu
from jax.sharding import PartitionSpec as P

WIDTH = 256
HALO = 128
COLS = 384
ROWS = 392
PROP_STRENGTH = 12.0
BF16 = jnp.bfloat16
F32 = jnp.float32


def split_table(table):
    parts = []
    for part in (table.real, table.imag):
        part = part.astype(np.float32)
        high = part.astype(jnp.bfloat16)
        low = (part - high.astype(np.float32)).astype(jnp.bfloat16)
        parts += [high, low]
    return np.stack(parts)


def make_tables():
    index = np.arange(WIDTH)
    dft = np.exp(-2j * np.pi / WIDTH * (index[:, None] * index[None, :] % WIDTH)) / np.sqrt(WIDTH)
    freq = ((index + WIDTH // 2) % WIDTH - WIDTH // 2) / WIDTH
    phase = np.exp(-1j * PROP_STRENGTH * freq**2)
    prop = dft.conj() @ (phase[:, None] * dft)
    far = phase[:, None] * dft
    return np.stack([split_table(prop), split_table(far), split_table(far.T)])


def split(x):
    high = x.astype(BF16)
    low = (x - high.astype(F32)).astype(BF16)
    return high, low


def dot(a, b):
    return jnp.dot(a, b, preferred_element_type=F32)


def right_mult(x, table):
    (rh, rl), (ih, il) = split(x[0]), split(x[1])
    nh, nl = -ih, -il
    trh, trl, tih, til = (table[i] for i in range(4))
    re = dot(
        jnp.concatenate([rh, rl, rh, nh, nl, nh], axis=1),
        jnp.concatenate([trh, trh, trl, tih, tih, til], axis=0),
    )
    im = dot(
        jnp.concatenate([rh, rl, rh, ih, il, ih], axis=1),
        jnp.concatenate([tih, tih, til, trh, trh, trl], axis=0),
    )
    return re, im


def left_mult(table, x):
    (rh, rl), (ih, il) = split(x[0]), split(x[1])
    nh, nl = -ih, -il
    trh, trl, tih, til = (table[i] for i in range(4))
    left_re = jnp.concatenate([trh, trl, trh, tih, til, tih], axis=1)
    left_im = jnp.concatenate([tih, til, tih, trh, trl, trh], axis=1)
    re = dot(left_re, jnp.concatenate([rh, rh, rl, nh, nh, nl], axis=0))
    im = dot(left_im, jnp.concatenate([rh, rh, rl, ih, ih, il], axis=0))
    return re, im


def times(a, b):
    return a[0] * b[0] - a[1] * b[1], a[0] * b[1] + a[1] * b[0]


def kernel(
    place_ref,
    offsets_ref,
    tables_ref,
    probe_ref,
    amp_hbm,
    own_hbm,
    own_prev_hbm,
    own_next_hbm,
    oth_hbm,
    oth_prev_hbm,
    oth_next_hbm,
    probe_out,
    own_core_out,
    own_head_out,
    own_tail_out,
    oth_core_out,
    oth_head_out,
    oth_tail_out,
    ext,
    amp,
    windows,
    waves,
    grads,
    in_sem,
    amp_sem,
    out_sem,
):
    place = place_ref[0]
    row = offsets_ref[place, 0]
    col = offsets_ref[place, 1]
    fine = lax.rem(row, 8)
    base = pl.multiple_of(row - fine, 8)
    ins = ((own_prev_hbm, own_hbm, own_next_hbm), (oth_prev_hbm, oth_hbm, oth_next_hbm))
    outs = ((own_head_out, own_core_out, own_tail_out), (oth_head_out, oth_core_out, oth_tail_out))

    def in_copies(s, sources):
        return [
            pltpu.make_async_copy(
                sources[k].at[s % 2], ext.at[s, :, k * HALO : (k + 1) * HALO, :], in_sem.at[s, k]
            )
            for k in range(3)
        ]

    def out_copies(s, targets):
        return [
            pltpu.make_async_copy(
                grads.at[s, :, k * HALO : (k + 1) * HALO, :], targets[k].at[s % 2], out_sem.at[s, k]
            )
            for k in range(3)
        ]

    for s in range(4):
        mine = place == s // 2

        @pl.when(mine)
        def _():
            for copy in in_copies(s, ins[0]):
                copy.start()

        @pl.when(jnp.logical_not(mine))
        def _():
            for copy in in_copies(s, ins[1]):
                copy.start()

    amp_copy = pltpu.make_async_copy(amp_hbm.at[place], amp, amp_sem)
    amp_copy.start()

    prop, far, far_t = tables_ref.at[0], tables_ref.at[1], tables_ref.at[2]
    wave = (probe_ref[0], probe_ref[1])
    for s in range(4):
        for copy in in_copies(s, ins[0]):
            copy.wait()
        window = []
        for c in range(2):
            rows = ext[s, c, pl.ds(base, WIDTH + 8), :]
            rows = pltpu.roll(rows, lax.rem(WIDTH + 8 - fine, WIDTH + 8), 0)[:WIDTH]
            piece = pltpu.roll(rows, lax.rem(COLS - col, COLS), 1)[:, :WIDTH]
            window.append(piece)
            windows[s, c] = piece
            if s > 0:
                waves[s, c] = wave[c]
        prod = times(wave, window)
        if s < 3:
            wave = left_mult(prop, right_mult(prod, prop))
    field = left_mult(far, right_mult(prod, far_t))
    amp_copy.wait()
    model = jnp.sqrt(field[0] * field[0] + field[1] * field[1] + 1.0)
    ratio = (model - amp[...]) / model
    grad = (field[0] * ratio, -(field[1] * ratio))
    grad = left_mult(far_t, right_mult(grad, far))
    for s in range(3, -1, -1):
        window = (windows[s, 0], windows[s, 1])
        wave = (waves[s, 0], waves[s, 1]) if s > 0 else (probe_ref[0], probe_ref[1])
        object_grad = times(wave, grad)
        for c in range(2):
            value = object_grad[c] if c == 0 else -object_grad[c]
            wide = jnp.concatenate([value, jnp.zeros((WIDTH, COLS - WIDTH), F32)], axis=1)
            wide = pltpu.roll(wide, col, 1)
            wide = jnp.concatenate([wide, jnp.zeros((8, COLS), F32)], axis=0)
            grads[s, c, 0:HALO, :] = jnp.zeros((HALO, COLS), F32)
            grads[s, c, 2 * HALO : 3 * HALO, :] = jnp.zeros((HALO, COLS), F32)
            grads[s, c, pl.ds(base, WIDTH + 8), :] = pltpu.roll(wide, fine, 0)
        mine = place == s // 2

        @pl.when(mine)
        def _():
            for copy in out_copies(s, outs[0]):
                copy.start()

        @pl.when(jnp.logical_not(mine))
        def _():
            for copy in out_copies(s, outs[1]):
                copy.start()

        grad = times(window, grad)
        if s > 0:
            grad = left_mult(prop, right_mult(grad, prop))
    probe_out[0] = grad[0]
    probe_out[1] = -grad[1]
    for s in range(4):
        for copy in out_copies(s, outs[0]):
            copy.wait()


def position(place, offsets, tables, probe, amplitudes, own, oth):
    band = jax.ShapeDtypeStruct((2, 2, HALO, COLS), F32)
    vmem = pl.BlockSpec(memory_space=pltpu.VMEM)
    smem = pl.BlockSpec(memory_space=pltpu.SMEM)
    hbm = pl.BlockSpec(memory_space=pl.ANY)
    return pl.pallas_call(
        kernel,
        out_shape=(jax.ShapeDtypeStruct((2, WIDTH, WIDTH), F32),) + (band,) * 6,
        in_specs=[smem, smem, vmem, vmem] + [hbm] * 7,
        out_specs=(vmem,) + (hbm,) * 6,
        scratch_shapes=[
            pltpu.VMEM((4, 2, ROWS, COLS), F32),
            pltpu.VMEM((WIDTH, WIDTH), F32),
            pltpu.VMEM((4, 2, WIDTH, WIDTH), F32),
            pltpu.VMEM((4, 2, WIDTH, WIDTH), F32),
            pltpu.VMEM((4, 2, ROWS, COLS), F32),
            pltpu.SemaphoreType.DMA((4, 3)),
            pltpu.SemaphoreType.DMA,
            pltpu.SemaphoreType.DMA((4, 3)),
        ],
        compiler_params=pltpu.CompilerParams(vmem_limit_bytes=48 * 1024 * 1024),
        cost_estimate=pl.CostEstimate(flops=6_000_000_000, bytes_accessed=12_000_000, transcendentals=0),
        name="position",
    )(place, offsets, tables, probe, amplitudes, *own, *oth)


def along_tile(x, by):
    count = lax.axis_size("tile")
    return lax.ppermute(x, "tile", [(i, (i + by) % count) for i in range(count)])


def swap_slab(x):
    return lax.ppermute(x, "slab", [(0, 1), (1, 0)])


def shards(transmission, probe, scan_offsets, amplitudes):
    tables = jnp.asarray(make_tables())
    place = lax.axis_index("slab").astype(jnp.int32).reshape(1)
    own = transmission
    oth = swap_slab(own)
    own_prev, own_next = along_tile(own, 1), along_tile(own, -1)
    oth_prev, oth_next = along_tile(oth, 1), along_tile(oth, -1)
    probe_term, own_core, own_head, own_tail, oth_core, oth_head, oth_tail = position(
        place, scan_offsets, tables, probe, amplitudes, (own, own_prev, own_next), (oth, oth_prev, oth_next)
    )
    oth_sum = oth_core + along_tile(oth_head, -1) + along_tile(oth_tail, 1)
    own_sum = own_core + along_tile(own_head, -1) + along_tile(own_tail, 1)
    object_grad = own_sum + swap_slab(oth_sum)

    axes = ("slab", "tile")
    devices = lax.axis_size(axes)
    parts = probe_term.reshape(devices, 8, 128)
    mine = jnp.sum(lax.all_to_all(parts, axes, 0, 0, tiled=True), axis=0)
    spread = jnp.broadcast_to(mine[None], (devices, 8, 128))
    probe_grad = lax.all_to_all(spread, axes, 0, 0, tiled=True).reshape(probe.shape)
    return object_grad, probe_grad


def solution(mesh):
    placed = (P("slab", None, "tile", None), P(), P("tile", None), P("tile", None, None))
    return jax.shard_map(
        shards,
        mesh=mesh,
        in_specs=placed,
        out_specs=(P("slab", None, "tile", None), P()),
        check_vma=False,
    )
```

time: 578 us -> 133 us (0.23)
  matrix products: 262 us -> 0 us
  waiting for transfers between devices: 206 us -> 41.2 us
  local copies, waits for them, and re-layouts: 41.8 us -> 6.31 us
  blocking collectives: 0 us -> 29.8 us
  other arithmetic: 26.1 us -> 5.13 us
  Pallas kernels: 0 us -> 16.3 us
  between operations: 15.6 us -> 0.71 us
  starting transfers between devices: 23.1 us -> 32.7 us
    dot_general x144 -> x0, matrix products: 262 us -> none  [the longest x72 134 us: left_mult(): return jnp.einsum('jk,pkl->pjl', matrix, batch, precision=highest)]
    psum x1 -> x0, waiting for transfers between devices: 144 us -> none  [shards(): probe_grad = lax.psum(probe_term, ('slab', 'tile'))]
    all_to_all x0 -> x1, blocking collectives: none -> 29.8 us  [shards(): lax.all_to_all(spread, axes, 0, 0, tiled=True).reshape(probe.shape)]
    scatter-add x6 -> x0, local copies, waits for them, and re-layouts: 29.7 us -> none
    ppermute x7 -> x10, waiting for transfers between devices: 62.2 us -> 33.4 us  [the longest x2 23.7 us: swap_slab(): return lax.ppermute(x, 'slab', [(0, 1), (1, 0)])]
    pallas_call x0 -> x1, Pallas kernels: none -> 16.3 us  [position(): pl.pallas_call(kernel, out_shape=(jax.ShapeDtypeStruct((2, WIDTH, WIDTH),...]
    scatter-add x4 -> x0, other arithmetic: 13.5 us -> none
    all_to_all x0 -> x1, starting transfers between devices: none -> 9.78 us  [shards(): mine = jnp.sum(lax.all_to_all(parts, axes, 0, 0, tiled=True), axis=0)]
  transfers between devices with their start and end apart: 8 -> 11, of which waited for: 6 -> 3; matrix products, arithmetic and copies ran while one was open for 1% -> 3% of each run, Pallas kernels for 0% -> 0%
where the time goes in v1:
time: 133 us; the launch traced here: 132 us
  waiting for transfers between devices  41.2 us (31%)
  starting transfers between devices  32.7 us (25%)
  blocking collectives  29.8 us (22%)
  Pallas kernels  16.3 us (12%)
  local copies, waits for them, and re-layouts  6.31 us (5%)
  other arithmetic  5.13 us (4%)
    all_to_all x1, blocking collectives, shards(): lax.all_to_all(spread, axes, 0, 0, tiled=True).reshape(probe.shape)  29.8 us
    ppermute x2, waiting for transfers between devices, swap_slab(): return lax.ppermute(x, 'slab', [(0, 1), (1, 0)])  23.7 us
    ppermute x8, starting transfers between devices, along_tile(): lax.ppermute(x, 'tile', [(i, (i + by) % count) for i in range(count)])  18.8 us
    pallas_call x1, Pallas kernels, position(): pl.pallas_call(kernel, out_shape=(jax.ShapeDtypeStruct((2, WIDTH, WIDTH),...  16.3 us
    all_to_all x1, starting transfers between devices, shards(): mine = jnp.sum(lax.all_to_all(parts, axes, 0, 0, tiled=True), axis=0)  9.78 us
    ppermute x8, waiting for transfers between devices, along_tile(): lax.ppermute(x, 'tile', [(i, (i + by) % count) for i in range(count)])  9.66 us
    all_to_all x1, waiting for transfers between devices, shards(): mine = jnp.sum(lax.all_to_all(parts, axes, 0, 0, tiled=True), axis=0)  7.82 us
    unnamed x16, local copies, waits for them, and re-layouts  4.51 us
  transfers between devices with their start and end apart: 11, of which 3 were waited for; matrix products, arithmetic and copies ran while one was open for 3% of the time, Pallas kernels for 0%

profile of v1, /device:TPU:1, one launch (start us, length us, event | category | flops | bytes accessed | tf_op | source)
XLA Modules:
  0.0 132.1 jit_solution(2211588171526874659)
XLA Ops:
  0.6 2.5 %collective-permute-start.2 = (f32[2,2,128,384]{3,2,1,0:T(8,128)}, f32[2,2,128,384]{3,2,1,0:T(8,128)S(1)}, u32[]{:S(2)}, u32[]{:S(2)}) collective-permute-start(f32[2,2,128,384]{3,2,1,0:T(8,128)} %own_hbm.1), channel_id=1, source_target_pairs={{0,64},{64,0},{1,65},{65,1},{2,66},{66,2},{3,67},{67,3},{4,68},{68... | collective-permute-start | bytes 2359304 | tf_op jit(solution)/shard_map/ppermute | solution.py:235
  3.2 1.0 collective-permute-start.1
  4.1 1.2 collective-permute-start
  5.3 23.7 %collective-permute-done.2.oth_hbm = f32[2,2,128,384]{3,2,1,0:T(8,128)S(1)} collective-permute-done((f32[2,2,128,384]{3,2,1,0:T(8,128)}, f32[2,2,128,384]{3,2,1,0:T(8,128)S(1)}, u32[]{:S(2)}, u32[]{:S(2)}) %collective-permute-start.2) | collective-permute-done | bytes 786464 | tf_op jit(solution)/shard_map/ppermute | solution.py:235
  29.1 0.0 copy-start.4
  29.1 1.3 collective-permute-start.4
  30.3 0.5 collective-permute-start.3
  30.8 0.0 collective-permute-done.1.own_next_hbm
  30.8 0.0 copy-start.5
  30.8 0.0 collective-permute-done.own_prev_hbm
  30.8 0.0 copy-start.6
  30.8 9.6 %collective-permute-done.4.oth_next_hbm = f32[2,2,128,384]{3,2,1,0:T(8,128)S(1)} collective-permute-done((f32[2,2,128,384]{3,2,1,0:T(8,128)S(1)}, f32[2,2,128,384]{3,2,1,0:T(8,128)S(1)}, u32[]{:S(2)}, u32[]{:S(2)}) %collective-permute-start.4) | collective-permute-done | bytes 786464 | tf_op jit(solution)/shard_map/ppermute | solution.py:231
  40.5 0.0 copy-start.7
  40.5 0.0 collective-permute-done.3.oth_prev_hbm
  40.5 0.0 copy-done.4
  40.5 0.0 copy-done.5
  40.5 0.0 copy-done.6
  40.5 0.9 copy-done.7
  41.4 0.0 copy-start.1
  41.4 1.0 copy-done.1
  42.4 0.0 copy-start.2
  42.4 1.0 copy-done.2
  43.4 0.0 copy-start.3
  43.4 0.7 copy-done.3
  44.1 16.3 %position.1 = (f32[2,256,256]{2,1,0:T(8,128)S(1)}, f32[2,2,128,384]{3,2,1,0:T(8,128)S(1)}, f32[2,2,128,384]{3,2,1,0:T(8,128)S(1)}, f32[2,2,128,384]{3,2,1,0:T(8,...) custom-call(s32[1]{0:T(128)} %bitcast.place_ref, ...), custom_call_target="tpu_custom_call" | custom-call | flops 6000000000 | bytes 12000000 | tf_op jit(solution)/shard_map/position/pallas_call | solution.py:208
  60.4 0.0 copy-start
  60.4 0.9 copy-done
  61.3 13.1 %collective-permute-start.7 = (f32[2,2,128,384]{3,2,1,0:T(8,128)}, f32[2,2,128,384]{3,2,1,0:T(8,128)}, u32[]{:S(2)}, u32[]{:S(2)}) collective-permute-start(f32[2,2,128,384]{3,2,1,0:T(8,128)} %get-tuple-element.13), channel_id=1, source_target_pairs={{0,63},{1,0},{2,1},{3,2},{4,3},{5,4},{6,5},{7,6},{8,7},{9,8},{10,9... | collective-permute-start | bytes 2359304 | tf_op jit(solution)/shard_map/ppermute | solution.py:231
  74.5 0.0 collective-permute-start.8
  74.5 0.8 reshape.15
  75.3 9.8 %all-to-all-start = ((f32[128,8,128]{2,1,0:T(8,128)}), f32[128,8,128]{2,1,0:T(8,128)S(1)}, u32[]{:S(2)}, u32[]{:S(2)}) async-start(f32[128,8,128]{2,1,0:T(8,128)} %reshape.15), calls=%async_computation | async-start | bytes 1048576 | tf_op jit(solution)/shard_map/all_to_all | solution.py:255
  85.1 1.1 collective-permute-start.5
  86.2 0.7 collective-permute-start.6
  86.9 0.0 collective-permute-done.7
  86.9 0.0 collective-permute-done.8
  86.9 2.4 %add_add_fusion = f32[2,2,128,384]{3,2,1,0:T(8,128)} fusion(f32[2,2,128,384]{3,2,1,0:T(8,128)} %collective-permute-done.8, f32[2,2,128,384]{3,2,1,0:T(8,128)S(1)} %get-tuple-element.12, f32[2,2,128,384]{3,2,1,0:T(8,128)} %collective-permute-done.7), kind=kLoop, calls=%fused_computation | loop fusion | flops 393216 | bytes 3145728 | tf_op jit(solution)/shard_map/add | solution.py:248
  89.3 1.5 %collective-permute-start.9 = (f32[2,2,128,384]{3,2,1,0:T(8,128)}, f32[2,2,128,384]{3,2,1,0:T(8,128)}, u32[]{:S(2)}, u32[]{:S(2)}) collective-permute-start(f32[2,2,128,384]{3,2,1,0:T(8,128)} %add_add_fusion), channel_id=1, source_target_pairs={{0,64},{64,0},{1,65},{65,1},{2,66},{66,2},{3,67},{67,3},{4,68},{68... | collective-permute-start | bytes 2359304 | tf_op jit(solution)/shard_map/ppermute | solution.py:235
  90.8 7.8 %all-to-all-done = f32[128,8,128]{2,1,0:T(8,128)S(1)} async-done(((f32[128,8,128]{2,1,0:T(8,128)}), f32[128,8,128]{2,1,0:T(8,128)S(1)}, u32[]{:S(2)}, u32[]{:S(2)}) %all-to-all-start) | async-done | bytes 524320 | tf_op jit(solution)/shard_map/all_to_all | solution.py:255
  98.6 0.1 reduce_sum.9
  98.8 29.8 %all_to_all.10 = f32[128,8,128]{2,1,0:T(8,128)S(1)} all-to-all(f32[128,8,128]{2,1,0:T(8,128)S(1)} %broadcast_in_dim.2), channel_id=1, replica_groups=mesh['slab'=2,'tile'=64] {'slab','tile'}, dimensions={0} | all-to-all | bytes 1048576 | tf_op jit(solution)/shard_map/all_to_all | solution.py:257
  128.6 0.9 reshape.16
  129.5 0.0 collective-permute-done.5
  129.5 0.0 collective-permute-done.6
  129.5 0.0 collective-permute-done.9
  129.5 2.6 %add_add_fusion.1 = f32[2,2,128,384]{3,2,1,0:T(8,128)} fusion(f32[2,2,128,384]{3,2,1,0:T(8,128)} %collective-permute-done.9, f32[2,2,128,384]{3,2,1,0:T(8,128)} %collective-permute-done.6, f32[2,2,128,384]{3,2,1,0:T(8,128)S(1)} %get-tuple-element.9, f32[2,2,128,384]{3,2,1,0:T(8,128)} %collective-permute-done.5), kind=kLoop, calls=%fused_computation.1 | loop fusion | flops 589824 | bytes 3932160 | tf_op jit(solution)/shard_map/add | solution.py:250
  (1 shorter events, 0.0 us)
Async XLA Ops:
  0.6 28.4 %collective-permute-start.2 = (f32[2,2,128,384]{3,2,1,0:T(8,128)}, f32[2,2,128,384]{3,2,1,0:T(8,128)S(1)}, u32[]{:S(2)}, u32[]{:S(2)}) collective-permute-start(f32[2,2,128,384]{3,2,1,0:T(8,128)} %own_hbm.1), channel_id=1, source_target_pairs={{0,64},{64,0},{1,65},{65,1},{2,66},{66,2},{3,67},{67,3},{4,68},{68... | collective-permute-start | bytes 2359304 | tf_op jit(solution)/shard_map/ppermute | solution.py:235
  3.2 27.6 %collective-permute-start.1 = (f32[2,2,128,384]{3,2,1,0:T(8,128)}, f32[2,2,128,384]{3,2,1,0:T(8,128)S(1)}, u32[]{:S(2)}, u32[]{:S(2)}) collective-permute-start(f32[2,2,128,384]{3,2,1,0:T(8,128)} %own_hbm.1), channel_id=1, source_target_pairs={{0,63},{1,0},{2,1},{3,2},{4,3},{5,4},{6,5},{7,6},{8,7},{9,8},{10,9... | collective-permute-start | bytes 2359304 | tf_op jit(solution)/shard_map/ppermute | solution.py:231
  4.1 26.7 %collective-permute-start = (f32[2,2,128,384]{3,2,1,0:T(8,128)}, f32[2,2,128,384]{3,2,1,0:T(8,128)S(1)}, u32[]{:S(2)}, u32[]{:S(2)}) collective-permute-start(f32[2,2,128,384]{3,2,1,0:T(8,128)} %own_hbm.1), channel_id=1, source_target_pairs={{0,1},{1,2},{2,3},{3,4},{4,5},{5,6},{6,7},{7,8},{8,9},{9,10},{10,1... | collective-permute-start | bytes 2359304 | tf_op jit(solution)/shard_map/ppermute | solution.py:231
  29.1 11.4 %copy-start.4 = (f32[2,2,128,384]{3,2,1,0:T(8,128)}, f32[2,2,128,384]{3,2,1,0:T(8,128)S(1)}, u32[]{:S(2)}) copy-start(f32[2,2,128,384]{3,2,1,0:T(8,128)S(1)} %collective-permute-done.2.oth_hbm) | copy-start | bytes 2359300
  29.1 11.4 %collective-permute-start.4 = (f32[2,2,128,384]{3,2,1,0:T(8,128)S(1)}, f32[2,2,128,384]{3,2,1,0:T(8,128)S(1)}, u32[]{:S(2)}, u32[]{:S(2)}) collective-permute-start(f32[2,2,128,384]{3,2,1,0:T(8,128)S(1)} %collective-permute-done.2.oth_hbm), channel_id=1, source_target_pairs={{0,63},{1,0},{2,1},{3,2},{4,3},{5,4},{6,5},{7,6},{8,7},{9,8},{10,9... | collective-permute-start | bytes 2359304 | tf_op jit(solution)/shard_map/ppermute | solution.py:231
  30.3 10.2 %collective-permute-start.3 = (f32[2,2,128,384]{3,2,1,0:T(8,128)S(1)}, f32[2,2,128,384]{3,2,1,0:T(8,128)}, u32[]{:S(2)}, u32[]{:S(2)}) collective-permute-start(f32[2,2,128,384]{3,2,1,0:T(8,128)S(1)} %collective-permute-done.2.oth_hbm), channel_id=1, source_target_pairs={{0,1},{1,2},{2,3},{3,4},{4,5},{5,6},{6,7},{7,8},{8,9},{9,10},{10,1... | collective-permute-start | bytes 2359304 | tf_op jit(solution)/shard_map/ppermute | solution.py:231
  30.8 9.7 %copy-start.5 = (f32[2,2,128,384]{3,2,1,0:T(8,128)}, f32[2,2,128,384]{3,2,1,0:T(8,128)S(1)}, u32[]{:S(2)}) copy-start(f32[2,2,128,384]{3,2,1,0:T(8,128)S(1)} %collective-permute-done.1.own_next_hbm) | copy-start | bytes 2359300
  30.8 9.7 %copy-start.6 = (f32[2,2,128,384]{3,2,1,0:T(8,128)}, f32[2,2,128,384]{3,2,1,0:T(8,128)S(1)}, u32[]{:S(2)}) copy-start(f32[2,2,128,384]{3,2,1,0:T(8,128)S(1)} %collective-permute-done.own_prev_hbm) | copy-start | bytes 2359300
  40.5 0.9 copy-start.7
  41.4 1.0 copy-start.1
  42.4 1.0 copy-start.2
  43.4 0.7 copy-start.3
  60.4 0.9 copy-start
  61.3 25.6 %collective-permute-start.7 = (f32[2,2,128,384]{3,2,1,0:T(8,128)}, f32[2,2,128,384]{3,2,1,0:T(8,128)}, u32[]{:S(2)}, u32[]{:S(2)}) collective-permute-start(f32[2,2,128,384]{3,2,1,0:T(8,128)} %get-tuple-element.13), channel_id=1, source_target_pairs={{0,63},{1,0},{2,1},{3,2},{4,3},{5,4},{6,5},{7,6},{8,7},{9,8},{10,9... | collective-permute-start | bytes 2359304 | tf_op jit(solution)/shard_map/ppermute | solution.py:231
  74.5 12.4 %collective-permute-start.8 = (f32[2,2,128,384]{3,2,1,0:T(8,128)}, f32[2,2,128,384]{3,2,1,0:T(8,128)}, u32[]{:S(2)}, u32[]{:S(2)}) collective-permute-start(f32[2,2,128,384]{3,2,1,0:T(8,128)} %get-tuple-element.14), channel_id=1, source_target_pairs={{0,1},{1,2},{2,3},{3,4},{4,5},{5,6},{6,7},{7,8},{8,9},{9,10},{10,1... | collective-permute-start | bytes 2359304 | tf_op jit(solution)/shard_map/ppermute | solution.py:231
  75.3 23.3 %all-to-all-start = ((f32[128,8,128]{2,1,0:T(8,128)}), f32[128,8,128]{2,1,0:T(8,128)S(1)}, u32[]{:S(2)}, u32[]{:S(2)}) async-start(f32[128,8,128]{2,1,0:T(8,128)} %reshape.15), calls=%async_computation | async-start | bytes 1048576 | tf_op jit(solution)/shard_map/all_to_all | solution.py:255
  85.1 44.4 %collective-permute-start.5 = (f32[2,2,128,384]{3,2,1,0:T(8,128)}, f32[2,2,128,384]{3,2,1,0:T(8,128)}, u32[]{:S(2)}, u32[]{:S(2)}) collective-permute-start(f32[2,2,128,384]{3,2,1,0:T(8,128)} %copy-done), channel_id=1, source_target_pairs={{0,63},{1,0},{2,1},{3,2},{4,3},{5,4},{6,5},{7,6},{8,7},{9,8},{10,9... | collective-permute-start | bytes 2359304 | tf_op jit(solution)/shard_map/ppermute | solution.py:231
  86.2 43.3 %collective-permute-start.6 = (f32[2,2,128,384]{3,2,1,0:T(8,128)S(1)}, f32[2,2,128,384]{3,2,1,0:T(8,128)}, u32[]{:S(2)}, u32[]{:S(2)}) collective-permute-start(f32[2,2,128,384]{3,2,1,0:T(8,128)S(1)} %get-tuple-element.11), channel_id=1, source_target_pairs={{0,1},{1,2},{2,3},{3,4},{4,5},{5,6},{6,7},{7,8},{8,9},{9,10},{10,1... | collective-permute-start | bytes 2359304 | tf_op jit(solution)/shard_map/ppermute | solution.py:231
  89.3 40.2 %collective-permute-start.9 = (f32[2,2,128,384]{3,2,1,0:T(8,128)}, f32[2,2,128,384]{3,2,1,0:T(8,128)}, u32[]{:S(2)}, u32[]{:S(2)}) collective-permute-start(f32[2,2,128,384]{3,2,1,0:T(8,128)} %add_add_fusion), channel_id=1, source_target_pairs={{0,64},{64,0},{1,65},{65,1},{2,66},{66,2},{3,67},{67,3},{4,68},{68... | collective-permute-start | bytes 2359304 | tf_op jit(solution)/shard_map/ppermute | solution.py:235

commit v2 on v0

v2 whole, which is shorter than its diff:
```python
import jax
import jax.numpy as jnp
import numpy as np
from jax import lax
from jax.experimental import pallas as pl
from jax.experimental.pallas import tpu as pltpu
from jax.sharding import PartitionSpec as P

WIDTH = 256
HALF = 128
HALO = 128
COLS = 384
PROP_STRENGTH = 12.0
BF16 = jnp.bfloat16
F32 = jnp.float32
VMEM = pl.BlockSpec(memory_space=pltpu.VMEM)
SMEM = pl.BlockSpec(memory_space=pltpu.SMEM)


def high_low(table):
    table = table.astype(np.float32)
    high = table.astype(jnp.bfloat16)
    low = (table - high.astype(np.float32)).astype(jnp.bfloat16)
    return np.stack([high, low])


def on_right(m):
    return high_low(np.block([[m.real, m.imag], [-m.imag, m.real]]))


def on_left(m):
    return high_low(np.block([[m.real, -m.imag], [m.imag, m.real]]))


def make_tables():
    index = np.arange(WIDTH)
    dft = np.exp(-2j * np.pi / WIDTH * (index[:, None] * index[None, :] % WIDTH)) / np.sqrt(WIDTH)
    freq = ((index + WIDTH // 2) % WIDTH - WIDTH // 2) / WIDTH
    phase = np.exp(-1j * PROP_STRENGTH * freq**2)
    prop = dft.conj() @ (phase[:, None] * dft)
    far = phase[:, None] * dft
    p, q = prop[:HALF, :HALF], prop[:HALF, HALF:]
    props = ((p + q) / 2, (p - q) / 2)
    fars = (far[0::2, :HALF], far[1::2, :HALF])
    return np.stack(
        [
            np.stack([on_right(m) for m in props]),
            np.stack([on_left(m) for m in props]),
            np.stack([on_right(m.T) for m in fars]),
            np.stack([on_left(m) for m in fars]),
            np.stack([on_right(m) for m in fars]),
            np.stack([on_left(m.T) for m in fars]),
        ]
    )


PROP_RIGHT, PROP_LEFT, FAR_RIGHT, FAR_LEFT, BACK_RIGHT, BACK_LEFT = range(6)


def split(x):
    high = x.astype(BF16)
    low = (x - high.astype(F32)).astype(BF16)
    return high, low


def dot(a, b):
    return jnp.dot(a, b, preferred_element_type=F32)


def fold(x):
    x = jnp.concatenate([x[:HALF] + x[HALF:], x[:HALF] - x[HALF:]], axis=0)
    return jnp.concatenate([x[:, :HALF] + x[:, HALF:], x[:, :HALF] - x[:, HALF:]], axis=1)


def right_mult(x, tables, which):
    re, im = [], []
    for h in range(2):
        part = slice(h * HALF, (h + 1) * HALF)
        high, low = split(jnp.concatenate([x[0][:, part], x[1][:, part]], axis=1))
        th, tl = tables[which, h, 0], tables[which, h, 1]
        out = dot(jnp.concatenate([high, low, high], axis=1), jnp.concatenate([th, th, tl], axis=0))
        re.append(out[:, :HALF])
        im.append(out[:, HALF:])
    return jnp.concatenate(re, axis=1), jnp.concatenate(im, axis=1)


def left_mult(x, tables, which):
    re, im = [], []
    for h in range(2):
        part = slice(h * HALF, (h + 1) * HALF)
        high, low = split(jnp.concatenate([x[0][part], x[1][part]], axis=0))
        th, tl = tables[which, h, 0], tables[which, h, 1]
        out = dot(jnp.concatenate([th, th, tl], axis=1), jnp.concatenate([high, low, high], axis=0))
        re.append(out[:HALF])
        im.append(out[HALF:])
    return jnp.concatenate(re, axis=0), jnp.concatenate(im, axis=0)


def propagate(x, tables):
    y = right_mult((fold(x[0]), fold(x[1])), tables, PROP_RIGHT)
    y = left_mult(y, tables, PROP_LEFT)
    return fold(y[0]), fold(y[1])


def times(a, b):
    return a[0] * b[0] - a[1] * b[1], a[0] * b[1] + a[1] * b[0]


def pick_columns(x, col):
    lane = lax.broadcasted_iota(jnp.int32, x.shape[:-1] + (HALF,), len(x.shape) - 1)
    left = jnp.where(lane >= col, x[..., :HALF], x[..., 2 * HALF :])
    return jnp.concatenate([left, x[..., HALF : 2 * HALF]], axis=-1)


def pick_rows(prev, after, row):
    line = lax.broadcasted_iota(jnp.int32, prev.shape, len(prev.shape) - 2)
    return jnp.where(line >= row, prev, after)


def roll_probe_kernel(place_ref, offsets_ref, probe_ref, out_ref):
    row, col = offsets_ref[place_ref[0], 0], offsets_ref[place_ref[0], 1]
    for c in range(2):
        out_ref[c] = pltpu.roll(pltpu.roll(probe_ref[c], row, 0), col, 1)


def core_kernel(place_ref, offsets_ref, own_ref, out_ref):
    col = offsets_ref[1 - place_ref[0], 1]
    out_ref[...] = pick_columns(own_ref[...], col)


def halo_kernel(place_ref, offsets_ref, prev_ref, next_ref, out_ref):
    other = 1 - place_ref[0]
    row, col = offsets_ref[other, 0], offsets_ref[other, 1]
    out_ref[...] = pick_columns(pick_rows(prev_ref[...], next_ref[...], row), col)


def window_kernel(place_ref, offsets_ref, own_ref, prev_ref, next_ref, out_ref):
    row, col = offsets_ref[place_ref[0], 0], offsets_ref[place_ref[0], 1]
    out_ref[:, :, :HALO] = pick_columns(pick_rows(prev_ref[...], next_ref[...], row), col)
    out_ref[:, :, HALO:] = pick_columns(own_ref[...], col)


def position_kernel(
    place_ref,
    offsets_ref,
    tables_ref,
    probe_ref,
    amp_ref,
    own_ref,
    core_ref,
    halo_ref,
    probe_out,
    own_out,
    oth_out,
    waves,
):
    place = place_ref[0]
    row, col = offsets_ref[place, 0], offsets_ref[place, 1]

    def window_of(s):
        mine = place == s // 2
        out = []
        for c in range(2):
            other = jnp.concatenate([halo_ref[s % 2, c], core_ref[s % 2, c]], axis=0)
            out.append(jnp.where(mine, own_ref[s % 2, c], other))
        return out

    wave = (probe_ref[0], probe_ref[1])
    for s in range(4):
        if s > 0:
            waves[s - 1, 0], waves[s - 1, 1] = wave
        prod = times(wave, window_of(s))
        if s < 3:
            wave = propagate(prod, tables_ref)
    field = right_mult((fold(prod[0]), fold(prod[1])), tables_ref, FAR_RIGHT)
    field = left_mult(field, tables_ref, FAR_LEFT)
    model = jnp.sqrt(field[0] * field[0] + field[1] * field[1] + 1.0)
    ratio = (model - amp_ref[...]) / model
    grad = (field[0] * ratio, -(field[1] * ratio))
    grad = right_mult(grad, tables_ref, BACK_RIGHT)
    grad = left_mult(grad, tables_ref, BACK_LEFT)
    grad = (fold(grad[0]), fold(grad[1]))
    for s in range(3, -1, -1):
        wave = (waves[s - 1, 0], waves[s - 1, 1]) if s > 0 else (probe_ref[0], probe_ref[1])
        object_grad = times(wave, grad)
        mine = place == s // 2

        @pl.when(mine)
        def _():
            own_out[s % 2, 0] = object_grad[0]
            own_out[s % 2, 1] = -object_grad[1]

        @pl.when(jnp.logical_not(mine))
        def _():
            oth_out[s % 2, 0] = object_grad[0]
            oth_out[s % 2, 1] = -object_grad[1]

        grad = times(window_of(s), grad)
        if s > 0:
            grad = propagate(grad, tables_ref)
    for c in range(2):
        value = grad[c] if c == 0 else -grad[c]
        value = pltpu.roll(value, lax.rem(WIDTH - row, WIDTH), 0)
        value = pltpu.roll(value, lax.rem(WIDTH - col, WIDTH), 1)
        for h in range(2):
            probe_out[c, :, h] = value[:, h * HALF : (h + 1) * HALF].reshape(WIDTH // 8, 8, HALF)


def spread_kernel(place_ref, offsets_ref, own_ref, got_ref, core_out, prev_out, next_out):
    place = place_ref[0]
    core = prev = after = 0.0
    for ref, index in ((own_ref, place), (got_ref, 1 - place)):
        row, col = offsets_ref[index, 0], offsets_ref[index, 1]
        grad = ref[...]
        lane = lax.broadcasted_iota(jnp.int32, grad.shape[:-1] + (HALF,), 3)
        kept = lane >= col
        wide = jnp.concatenate(
            [
                jnp.where(kept, grad[..., :HALF], 0.0),
                grad[..., HALF:],
                jnp.where(kept, 0.0, grad[..., :HALF]),
            ],
            axis=-1,
        )
        core = core + wide[:, :, HALO:]
        halo = wide[:, :, :HALO]
        line = lax.broadcasted_iota(jnp.int32, halo.shape, 2)
        prev = prev + jnp.where(line >= row, halo, 0.0)
        after = after + jnp.where(line >= row, 0.0, halo)
    core_out[...] = core
    prev_out[...] = prev
    next_out[...] = after


def call(kernel, shapes, smem, vmem, name, scratch=(), flops=0, nbytes=2_000_000):
    single = isinstance(shapes[0], int)
    shapes = (shapes,) if single else shapes
    out = pl.pallas_call(
        kernel,
        out_shape=tuple(jax.ShapeDtypeStruct(shape, F32) for shape in shapes),
        in_specs=[SMEM] * len(smem) + [VMEM] * len(vmem),
        out_specs=(VMEM,) * len(shapes),
        scratch_shapes=scratch,
        compiler_params=pltpu.CompilerParams(vmem_limit_bytes=40 * 1024 * 1024),
        cost_estimate=pl.CostEstimate(flops=flops, bytes_accessed=nbytes, transcendentals=0),
        name=name,
    )(*smem, *vmem)
    return out[0] if single else out


def along_tile(x, by):
    count = lax.axis_size("tile")
    return lax.ppermute(x, "tile", [(i, (i + by) % count) for i in range(count)])


def swap_slab(x):
    return lax.ppermute(x, "slab", [(0, 1), (1, 0)])


def shards(transmission, probe, scan_offsets, amplitudes):
    tables = jnp.asarray(make_tables())
    index = lax.axis_index("slab").astype(jnp.int32)
    where = (index.reshape(1), scan_offsets)
    own = transmission
    part, whole, band = (2, 2, HALO, WIDTH), (2, 2, WIDTH, WIDTH), (2, 2, HALO, COLS)

    core = swap_slab(call(core_kernel, part, where, (own,), "core"))
    prev, after = along_tile(own, 1), along_tile(own, -1)
    rolled = call(roll_probe_kernel, (2, WIDTH, WIDTH), where, (probe,), "roll")
    amp = lax.dynamic_index_in_dim(amplitudes, index, 0, keepdims=False)
    amp = amp.reshape(HALF, 2, HALF, 2).transpose(1, 0, 3, 2).reshape(WIDTH, WIDTH)
    halo = swap_slab(call(halo_kernel, part, where, (prev, after), "halo"))
    windows = call(window_kernel, whole, where, (own, prev, after), "window")

    tiles = (2, WIDTH // 8, 2, 8, HALF)
    probe_term, own_grad, oth_grad = call(
        position_kernel,
        (tiles, whole, whole),
        where,
        (tables, rolled, amp, windows, core, halo),
        "position",
        scratch=[pltpu.VMEM((3, 2, WIDTH, WIDTH), F32)],
        flops=3_300_000_000,
        nbytes=10_000_000,
    )
    got = swap_slab(oth_grad)
    axes = ("slab", "tile")
    devices = lax.axis_size(axes)
    parts = probe_term.reshape(devices, 8, HALF)
    mine = jnp.sum(lax.all_to_all(parts, axes, 0, 0, tiled=True), axis=0)
    spread = jnp.broadcast_to(mine[None], (devices, 8, HALF))
    probe_grad = lax.all_to_all(spread, axes, 0, 0, tiled=True).reshape(tiles)
    probe_grad = probe_grad.transpose(0, 1, 3, 2, 4).reshape(probe.shape)

    own_sum, to_prev, to_next = call(spread_kernel, (band,) * 3, where, (own_grad, got), "spread")
    object_grad = own_sum + along_tile(to_prev, -1) + along_tile(to_next, 1)
    return object_grad, probe_grad


def solution(mesh):
    placed = (P("slab", None, "tile", None), P(), P("tile", None), P("tile", None, None))
    return jax.shard_map(
        shards,
        mesh=mesh,
        in_specs=placed,
        out_specs=(P("slab", None, "tile", None), P()),
        check_vma=False,
    )
```

time: 578 us -> 127 us (0.22)
  matrix products: 262 us -> 0 us
  waiting for transfers between devices: 206 us -> 18.7 us
  blocking collectives: 0 us -> 25.2 us
  other arithmetic: 26.1 us -> 3.3 us
  between operations: 15.6 us -> 0.74 us
  Pallas kernels: 0 us -> 14.6 us
    dot_general x144 -> x0, matrix products: 262 us -> none  [the longest x72 134 us: left_mult(): return jnp.einsum('jk,pkl->pjl', matrix, batch, precision=highest)]
    psum x1 -> x0, waiting for transfers between devices: 144 us -> none  [shards(): probe_grad = lax.psum(probe_term, ('slab', 'tile'))]
    ppermute x7, waiting for transfers between devices: 62.2 us -> 18.7 us  [the longest x3 10.9 us: swap_slab(): return lax.ppermute(x, 'slab', [(0, 1), (1, 0)])]
    scatter-add x6 -> x0, local copies, waits for them, and re-layouts: 29.7 us -> none
    all_to_all x0 -> x1, blocking collectives: none -> 25.2 us  [shards(): probe_grad = lax.all_to_all(spread, axes, 0, 0, tiled=True).reshape(tiles)]
    reshape x0 -> x1, local copies, waits for them, and re-layouts: none -> 18.9 us  [shards(): amp.reshape(HALF, 2, HALF, 2).transpose(1, 0, 3, 2).reshape(WIDTH, WIDTH)]
    pallas_call x0 -> x6, Pallas kernels: none -> 14.6 us  [call(): pl.pallas_call(kernel, out_shape=tuple((jax.ShapeDtypeStruct(shape, F32)...]
    all_to_all x0 -> x1, starting transfers between devices: none -> 14.3 us  [shards(): mine = jnp.sum(lax.all_to_all(parts, axes, 0, 0, tiled=True), axis=0)]
  transfers between devices with their start and end apart: 8 -> 8, of which waited for: 6 -> 3; matrix products, arithmetic and copies ran while one was open for 1% -> 25% of each run, Pallas kernels for 0% -> 4%
where the time goes in v2:
time: 127 us
  local copies, waits for them, and re-layouts  37.8 us (30%)
  starting transfers between devices  26.4 us (21%)
  blocking collectives  25.2 us (20%)
  waiting for transfers between devices  18.7 us (15%)
  Pallas kernels  14.6 us (11%)
  other arithmetic  3.3 us (3%)
    all_to_all x1, blocking collectives, shards(): probe_grad = lax.all_to_all(spread, axes, 0, 0, tiled=True).reshape(tiles)  25.2 us
    reshape x1, local copies, waits for them, and re-layouts, shards(): amp.reshape(HALF, 2, HALF, 2).transpose(1, 0, 3, 2).reshape(WIDTH, WIDTH)  18.9 us
    pallas_call x6, Pallas kernels, call(): pl.pallas_call(kernel, out_shape=tuple((jax.ShapeDtypeStruct(shape, F32)...  14.6 us
    all_to_all x1, starting transfers between devices, shards(): mine = jnp.sum(lax.all_to_all(parts, axes, 0, 0, tiled=True), axis=0)  14.3 us
    ppermute x3, waiting for transfers between devices, swap_slab(): return lax.ppermute(x, 'slab', [(0, 1), (1, 0)])  10.9 us
    transpose x1, local copies, waits for them, and re-layouts, shards(): amp.reshape(HALF, 2, HALF, 2).transpose(1, 0, 3, 2).reshape(WIDTH, WIDTH)  9.79 us
    ppermute x4, starting transfers between devices, along_tile(): lax.ppermute(x, 'tile', [(i, (i + by) % count) for i in range(count)])  8.73 us
    unnamed x20, local copies, waits for them, and re-layouts  8.37 us
  transfers between devices with their start and end apart: 8, of which 3 were waited for; matrix products, arithmetic and copies ran while one was open for 25% of the time, Pallas kernels for 4%

profile of v2, /device:TPU:1, one launch (start us, length us, event | category | flops | bytes accessed | tf_op | source)
XLA Modules:
  0.0 126.8 jit_solution(9018576431032753337)
XLA Ops:
  0.6 0.0 copy-start
  0.6 2.8 %collective-permute-start = (f32[2,2,128,384]{3,2,1,0:T(8,128)}, f32[2,2,128,384]{3,2,1,0:T(8,128)S(1)}, u32[]{:S(2)}, u32[]{:S(2)}) collective-permute-start(f32[2,2,128,384]{3,2,1,0:T(8,128)} %own_ref.3), channel_id=1, source_target_pairs={{0,1},{1,2},{2,3},{3,4},{4,5},{5,6},{6,7},{7,8},{8,9},{9,10},{10,1... | collective-permute-start | bytes 2359304 | tf_op jit(solution)/shard_map/ppermute | solution.py:253
  3.4 0.0 collective-permute-start.1
  3.4 0.0 copy-start.1
  3.4 1.2 copy-done.1
  4.6 0.0 copy-start.6
  4.6 0.7 copy-done.6
  5.2 0.6 core.1
  5.8 1.7 %collective-permute-start.2 = (f32[2,2,128,256]{3,2,1,0:T(8,128)S(1)}, f32[2,2,128,256]{3,2,1,0:T(8,128)}, u32[]{:S(2)}, u32[]{:S(2)}) collective-permute-start(f32[2,2,128,256]{3,2,1,0:T(8,128)S(1)} %core.1), channel_id=1, source_target_pairs={{0,64},{64,0},{1,65},{65,1},{2,66},{66,2},{3,67},{67,3},{4,68},{68... | collective-permute-start | bytes 1572872 | tf_op jit(solution)/shard_map/ppermute | solution.py:257
  7.6 5.1 %collective-permute-done.prev_ref = f32[2,2,128,384]{3,2,1,0:T(8,128)S(1)} collective-permute-done((f32[2,2,128,384]{3,2,1,0:T(8,128)}, f32[2,2,128,384]{3,2,1,0:T(8,128)S(1)}, u32[]{:S(2)}, u32[]{:S(2)}) %collective-permute-start) | collective-permute-done | bytes 786464 | tf_op jit(solution)/shard_map/ppermute | solution.py:253
  12.7 2.7 %collective-permute-done.1.next_ref = f32[2,2,128,384]{3,2,1,0:T(8,128)S(1)} collective-permute-done((f32[2,2,128,384]{3,2,1,0:T(8,128)}, f32[2,2,128,384]{3,2,1,0:T(8,128)S(1)}, u32[]{:S(2)}, u32[]{:S(2)}) %collective-permute-start.1) | collective-permute-done | bytes 786464 | tf_op jit(solution)/shard_map/ppermute | solution.py:253
  15.3 1.4 %halo.1 = f32[2,2,128,256]{3,2,1,0:T(8,128)} custom-call(s32[1]{0:T(128)} %bitcast.place_ref, s32[2,2]{1,0:T(2,128)S(1)} %copy-done.6, f32[2,2,128,384]{3,2,1,0:T(8,128)S(1)} %collective-permute-done.prev_ref, f32[2,2,128,384]{3,2,1,0:T(8,128)S(1)} %collective-permute-done.1.next_ref), custom_call_target="tpu_custom_call" | custom-call | bytes 2000000 | tf_op jit(solution)/shard_map/halo/pallas_call | solution.py:238
  16.7 1.6 %collective-permute-start.3 = (f32[2,2,128,256]{3,2,1,0:T(8,128)}, f32[2,2,128,256]{3,2,1,0:T(8,128)}, u32[]{:S(2)}, u32[]{:S(2)}) collective-permute-start(f32[2,2,128,256]{3,2,1,0:T(8,128)} %halo.1), channel_id=1, source_target_pairs={{0,64},{64,0},{1,65},{65,1},{2,66},{66,2},{3,67},{67,3},{4,68},{68... | collective-permute-start | bytes 1572872 | tf_op jit(solution)/shard_map/ppermute | solution.py:257
  18.4 0.0 copy-start.3
  18.4 1.0 copy-done.3
  19.4 0.8 roll.1.probe_ref
  20.2 0.0 copy-start.4
  20.2 0.8 copy-done.4
  21.0 0.0 copy-done
  21.0 0.7 constant_dynamic-slice_fusion
  21.7 0.0 copy-start.2
  21.7 0.0 copy-start.7
  21.7 18.9 %reshape.25 = f32[128,2,128,2]{3,2,1,0:T(8,128)} reshape(f32[1,256,256]{2,1,0:T(8,128)} %constant_dynamic-slice_fusion) | data formatting | bytes 524288 | tf_op jit(solution)/shard_map/reshape | solution.py:271
  40.6 9.8 %copy.7 = f32[2,128,2,128]{3,2,1,0:T(2,128)} copy(f32[2,128,2,128]{2,3,0,1:T(8,128)} %bitcast.14) | data formatting | bytes 524288 | tf_op jit(solution)/shard_map/transpose | solution.py:271
  50.4 1.0 copy.10
  51.4 0.0 copy-done.2
  51.4 0.0 copy-done.7
  51.4 0.7 window.1.own_ref
  52.1 0.0 collective-permute-done.2.core_ref
  52.1 0.0 collective-permute-done.3.halo_ref
  52.1 0.0 copy-start.5
  52.1 1.0 copy-done.5
  53.2 0.0 copy-start.8
  53.2 1.9 %copy-done.8 = bf16[6,2,2,256,256]{4,3,2,1,0:T(8,128)(2,1)S(1)} copy-done((bf16[6,2,2,256,256]{4,3,2,1,0:T(8,128)(2,1)S(1)}, bf16[6,2,2,256,256]{4,3,2,1,0:T(8,128)(2,1)}, u32[]{:S(2)}) %copy-start.8) | copy-done | bytes 3145752
  55.0 9.3 %position.1 = (f32[2,32,2,8,128]{4,3,2,1,0:T(8,128)}, f32[2,2,256,256]{3,2,1,0:T(8,128)S(1)}, f32[2,2,256,256]{3,2,1,0:T(8,128)}) custom-call(s32[1]{0:T(128)} %bitcast.place_ref, s32[2,2]{1,0:T(2,128)S(1)} %copy-done.7, bf16[6,2,2,256,256]{4,3,2,1,0:T(8,128)(2,1)S(1)} %copy-done.8, f32[2,256,256]{2,1,0:T(8,128)S(1)} %copy-done.5, f32[256,256]{1,0:T(8,128)S(1)} %bitcast.13, ...), custom_call_target="tpu_custom_call" | custom-call | flops 3300000000 | bytes 10000000 | tf_op jit(solution)/shard_map/position/pallas_call | solution.py:238
  64.3 0.0 collective-permute-start.4
  64.3 14.3 %all-to-all-start = ((f32[128,8,128]{2,1,0:T(8,128)}), f32[128,8,128]{2,1,0:T(8,128)}, u32[]{:S(2)}, u32[]{:S(2)}) async-start(f32[128,8,128]{2,1,0:T(8,128)} %bitcast.2), calls=%async_computation | async-start | bytes 1048576 | tf_op jit(solution)/shard_map/all_to_all | solution.py:290
  78.7 10.9 %collective-permute-done.4.got_ref = f32[2,2,256,256]{3,2,1,0:T(8,128)S(1)} collective-permute-done((f32[2,2,256,256]{3,2,1,0:T(8,128)}, f32[2,2,256,256]{3,2,1,0:T(8,128)S(1)}, u32[]{:S(2)}, u32[]{:S(2)}) %collective-permute-start.4) | collective-permute-done | bytes 1048608 | tf_op jit(solution)/shard_map/ppermute | solution.py:257
  89.6 1.8 %spread.1 = (f32[2,2,128,384]{3,2,1,0:T(8,128)S(1)}, f32[2,2,128,384]{3,2,1,0:T(8,128)}, f32[2,2,128,384]{3,2,1,0:T(8,128)}) custom-call(s32[1]{0:T(128)} %bitcast.place_ref, s32[2,2]{1,0:T(2,128)S(1)} %copy-done.7, f32[2,2,256,256]{3,2,1,0:T(8,128)S(1)} %get-tuple-element.8.own_ref, f32[2,2,256,256]{3,2,1,0:T(8,128)S(1)} %collective-permute-done.4.got_ref), custom_call_target="tpu_custom_call" | custom-call | bytes 2000000 | tf_op jit(solution)/shard_map/spread/pallas_call | solution.py:238
  91.4 5.4 %collective-permute-start.6 = (f32[2,2,128,384]{3,2,1,0:T(8,128)}, f32[2,2,128,384]{3,2,1,0:T(8,128)S(1)}, u32[]{:S(2)}, u32[]{:S(2)}) collective-permute-start(f32[2,2,128,384]{3,2,1,0:T(8,128)} %get-tuple-element.12), channel_id=1, source_target_pairs={{0,1},{1,2},{2,3},{3,4},{4,5},{5,6},{6,7},{7,8},{8,9},{9,10},{10,1... | collective-permute-start | bytes 2359304 | tf_op jit(solution)/shard_map/ppermute | solution.py:253
  96.8 0.6 collective-permute-start.5
  97.4 0.0 all-to-all-done
  97.4 1.2 reduce_sum.9
  98.6 25.2 %all_to_all.10 = f32[128,8,128]{2,1,0:T(8,128)S(1)} all-to-all(f32[128,8,128]{2,1,0:T(8,128)S(1)} %broadcast_in_dim.2), channel_id=1, replica_groups=mesh['slab'=2,'tile'=64] {'slab','tile'}, dimensions={0} | all-to-all | bytes 1048576 | tf_op jit(solution)/shard_map/all_to_all | solution.py:292
  123.8 0.0 collective-permute-done.6
  123.8 0.0 collective-permute-done.5
  123.9 2.1 %add_add_fusion = f32[2,2,128,384]{3,2,1,0:T(8,128)} fusion(f32[2,2,128,384]{3,2,1,0:T(8,128)S(1)} %collective-permute-done.6, f32[2,2,128,384]{3,2,1,0:T(8,128)S(1)} %get-tuple-element.10, f32[2,2,128,384]{3,2,1,0:T(8,128)} %collective-permute-done.5), kind=kLoop, calls=%fused_computation | loop fusion | flops 393216 | bytes 3145728 | tf_op jit(solution)/shard_map/add | solution.py:296
  126.0 0.8 copy.12
  (1 shorter events, 0.0 us)
Async XLA Ops:
  0.6 20.4 %copy-start = (f32[2,256,256]{2,1,0:T(8,128)S(1)}, f32[2,256,256]{2,1,0:T(8,128)}, u32[]{:S(2)}) copy-start(f32[2,256,256]{2,1,0:T(8,128)} %param.8) | copy-start | bytes 1572868
  0.6 12.0 %collective-permute-start = (f32[2,2,128,384]{3,2,1,0:T(8,128)}, f32[2,2,128,384]{3,2,1,0:T(8,128)S(1)}, u32[]{:S(2)}, u32[]{:S(2)}) collective-permute-start(f32[2,2,128,384]{3,2,1,0:T(8,128)} %own_ref.3), channel_id=1, source_target_pairs={{0,1},{1,2},{2,3},{3,4},{4,5},{5,6},{6,7},{7,8},{8,9},{9,10},{10,1... | collective-permute-start | bytes 2359304 | tf_op jit(solution)/shard_map/ppermute | solution.py:253
  3.4 11.9 %collective-permute-start.1 = (f32[2,2,128,384]{3,2,1,0:T(8,128)}, f32[2,2,128,384]{3,2,1,0:T(8,128)S(1)}, u32[]{:S(2)}, u32[]{:S(2)}) collective-permute-start(f32[2,2,128,384]{3,2,1,0:T(8,128)} %own_ref.3), channel_id=1, source_target_pairs={{0,63},{1,0},{2,1},{3,2},{4,3},{5,4},{6,5},{7,6},{8,7},{9,8},{10,9... | collective-permute-start | bytes 2359304 | tf_op jit(solution)/shard_map/ppermute | solution.py:253
  3.4 1.2 copy-start.1
  4.6 0.7 copy-start.6
  5.8 46.2 %collective-permute-start.2 = (f32[2,2,128,256]{3,2,1,0:T(8,128)S(1)}, f32[2,2,128,256]{3,2,1,0:T(8,128)}, u32[]{:S(2)}, u32[]{:S(2)}) collective-permute-start(f32[2,2,128,256]{3,2,1,0:T(8,128)S(1)} %core.1), channel_id=1, source_target_pairs={{0,64},{64,0},{1,65},{65,1},{2,66},{66,2},{3,67},{67,3},{4,68},{68... | collective-permute-start | bytes 1572872 | tf_op jit(solution)/shard_map/ppermute | solution.py:257
  16.7 35.4 %collective-permute-start.3 = (f32[2,2,128,256]{3,2,1,0:T(8,128)}, f32[2,2,128,256]{3,2,1,0:T(8,128)}, u32[]{:S(2)}, u32[]{:S(2)}) collective-permute-start(f32[2,2,128,256]{3,2,1,0:T(8,128)} %halo.1), channel_id=1, source_target_pairs={{0,64},{64,0},{1,65},{65,1},{2,66},{66,2},{3,67},{67,3},{4,68},{68... | collective-permute-start | bytes 1572872 | tf_op jit(solution)/shard_map/ppermute | solution.py:257
  18.4 1.0 copy-start.3
  20.2 0.8 copy-start.4
  21.7 29.7 %copy-start.2 = (f32[2,2,128,384]{3,2,1,0:T(8,128)S(1)}, f32[2,2,128,384]{3,2,1,0:T(8,128)}, u32[]{:S(2)}) copy-start(f32[2,2,128,384]{3,2,1,0:T(8,128)} %own_ref.3) | copy-start | bytes 2359300
  21.7 29.7 %copy-start.7 = (s32[2,2]{1,0:T(2,128)S(1)}, s32[2,2]{1,0:T(2,128)}, u32[]{:S(2)}) copy-start(s32[2,2]{1,0:T(2,128)} %offsets_ref.11) | copy-start | bytes 52
  52.1 1.0 copy-start.5
  53.2 1.9 %copy-start.8 = (bf16[6,2,2,256,256]{4,3,2,1,0:T(8,128)(2,1)S(1)}, bf16[6,2,2,256,256]{4,3,2,1,0:T(8,128)(2,1)}, u32[]{:S(2)}) copy-start(bf16[6,2,2,256,256]{4,3,2,1,0:T(8,128)(2,1)} %constant.16.clone.tables_ref) | copy-start | bytes 9437188
  64.3 25.3 %collective-permute-start.4 = (f32[2,2,256,256]{3,2,1,0:T(8,128)}, f32[2,2,256,256]{3,2,1,0:T(8,128)S(1)}, u32[]{:S(2)}, u32[]{:S(2)}) collective-permute-start(f32[2,2,256,256]{3,2,1,0:T(8,128)} %get-tuple-element.9), channel_id=1, source_target_pairs={{0,64},{64,0},{1,65},{65,1},{2,66},{66,2},{3,67},{67,3},{4,68},{68... | collective-permute-start | bytes 3145736 | tf_op jit(solution)/shard_map/ppermute | solution.py:257
  64.3 33.1 %all-to-all-start = ((f32[128,8,128]{2,1,0:T(8,128)}), f32[128,8,128]{2,1,0:T(8,128)}, u32[]{:S(2)}, u32[]{:S(2)}) async-start(f32[128,8,128]{2,1,0:T(8,128)} %bitcast.2), calls=%async_computation | async-start | bytes 1048576 | tf_op jit(solution)/shard_map/all_to_all | solution.py:290
  91.4 32.4 %collective-permute-start.6 = (f32[2,2,128,384]{3,2,1,0:T(8,128)}, f32[2,2,128,384]{3,2,1,0:T(8,128)S(1)}, u32[]{:S(2)}, u32[]{:S(2)}) collective-permute-start(f32[2,2,128,384]{3,2,1,0:T(8,128)} %get-tuple-element.12), channel_id=1, source_target_pairs={{0,1},{1,2},{2,3},{3,4},{4,5},{5,6},{6,7},{7,8},{8,9},{9,10},{10,1... | collective-permute-start | bytes 2359304 | tf_op jit(solution)/shard_map/ppermute | solution.py:253
  96.8 27.0 %collective-permute-start.5 = (f32[2,2,128,384]{3,2,1,0:T(8,128)}, f32[2,2,128,384]{3,2,1,0:T(8,128)}, u32[]{:S(2)}, u32[]{:S(2)}) collective-permute-start(f32[2,2,128,384]{3,2,1,0:T(8,128)} %get-tuple-element.11), channel_id=1, source_target_pairs={{0,63},{1,0},{2,1},{3,2},{4,3},{5,4},{6,5},{7,6},{8,7},{9,8},{10,9... | collective-permute-start | bytes 2359304 | tf_op jit(solution)/shard_map/ppermute | solution.py:253

commit v3 on v2

--- a/solution.py
+++ b/solution.py
@@ -1,3 +1,5 @@
+import functools
+
 import jax
 import jax.numpy as jnp
 import numpy as np
@@ -112,9 +114,9 @@
     return jnp.concatenate([left, x[..., HALF : 2 * HALF]], axis=-1)
 
 
-def pick_rows(prev, after, row):
-    line = lax.broadcasted_iota(jnp.int32, prev.shape, len(prev.shape) - 2)
-    return jnp.where(line >= row, prev, after)
+def pick_rows(across, beside, row, odd):
+    line = lax.broadcasted_iota(jnp.int32, across.shape, len(across.shape) - 2)
+    return jnp.where(jnp.where(line >= row, 1, 0) == odd, beside, across)
 
 
 def roll_probe_kernel(place_ref, offsets_ref, probe_ref, out_ref):
@@ -123,20 +125,37 @@
         out_ref[c] = pltpu.roll(pltpu.roll(probe_ref[c], row, 0), col, 1)
 
 
-def core_kernel(place_ref, offsets_ref, own_ref, out_ref):
+def core_kernel(place_ref, offsets_ref, own_ref, out_ref, copy_ref):
     col = offsets_ref[1 - place_ref[0], 1]
-    out_ref[...] = pick_columns(own_ref[...], col)
-
-
-def halo_kernel(place_ref, offsets_ref, prev_ref, next_ref, out_ref):
+    own = own_ref[...]
+    out_ref[...] = pick_columns(own, col)
+    copy_ref[...] = own
+
+
+def amp_kernel(place_ref, offsets_ref, amp_ref, out_ref):
+    x = amp_ref[place_ref[0]]
+    line = lax.broadcasted_iota(jnp.int32, (WIDTH, WIDTH), 0)
+    lane = lax.broadcasted_iota(jnp.int32, (WIDTH, WIDTH), 1)
+    rows = jnp.where(lane == 2 * (line % HALF) + line // HALF, 1.0, 0.0).astype(BF16)
+    cols = jnp.where(line == 2 * (lane % HALF) + lane // HALF, 1.0, 0.0).astype(BF16)
+
+    def parts(value):
+        high, rest = split(value)
+        return high, rest, (value - high.astype(F32) - rest.astype(F32)).astype(BF16)
+
+    x = sum(dot(rows, part) for part in parts(x))
+    out_ref[...] = sum(dot(part, cols) for part in parts(x))
+
+
+def halo_kernel(place_ref, offsets_ref, across_ref, beside_ref, out_ref):
     other = 1 - place_ref[0]
     row, col = offsets_ref[other, 0], offsets_ref[other, 1]
-    out_ref[...] = pick_columns(pick_rows(prev_ref[...], next_ref[...], row), col)
-
-
-def window_kernel(place_ref, offsets_ref, own_ref, prev_ref, next_ref, out_ref):
+    out_ref[...] = pick_columns(pick_rows(across_ref[...], beside_ref[...], row, place_ref[1]), col)
+
+
+def window_kernel(place_ref, offsets_ref, own_ref, across_ref, beside_ref, out_ref):
     row, col = offsets_ref[place_ref[0], 0], offsets_ref[place_ref[0], 1]
-    out_ref[:, :, :HALO] = pick_columns(pick_rows(prev_ref[...], next_ref[...], row), col)
+    out_ref[:, :, :HALO] = pick_columns(pick_rows(across_ref[...], beside_ref[...], row, place_ref[1]), col)
     out_ref[:, :, HALO:] = pick_columns(own_ref[...], col)
 
 
@@ -150,19 +169,22 @@
     core_ref,
     halo_ref,
     probe_out,
-    own_out,
-    oth_out,
+    core_out,
+    halo_out,
     waves,
 ):
     place = place_ref[0]
     row, col = offsets_ref[place, 0], offsets_ref[place, 1]
+    line = lax.broadcasted_iota(jnp.int32, (HALO, WIDTH), 0)
+    turned = jnp.where(jnp.where(line >= row, 1, 0) == place_ref[1], 0, place_ref[2])
 
     def window_of(s):
-        mine = place == s // 2
+        mine = jnp.where(place == s // 2, 1, 0)
         out = []
         for c in range(2):
-            other = jnp.concatenate([halo_ref[s % 2, c], core_ref[s % 2, c]], axis=0)
-            out.append(jnp.where(mine, own_ref[s % 2, c], other))
+            halo = jnp.where(turned == mine, halo_ref[s % 2, c], own_ref[s % 2, c, :HALO])
+            core = jnp.where(mine == 1, own_ref[s % 2, c, HALO:], core_ref[s % 2, c])
+            out.append(jnp.concatenate([halo, core], axis=0))
         return out
 
     wave = (probe_ref[0], probe_ref[1])
@@ -183,21 +205,17 @@
     for s in range(3, -1, -1):
         wave = (waves[s - 1, 0], waves[s - 1, 1]) if s > 0 else (probe_ref[0], probe_ref[1])
         object_grad = times(wave, grad)
-        mine = place == s // 2
-
-        @pl.when(mine)
-        def _():
-            own_out[s % 2, 0] = object_grad[0]
-            own_out[s % 2, 1] = -object_grad[1]
-
-        @pl.when(jnp.logical_not(mine))
-        def _():
-            oth_out[s % 2, 0] = object_grad[0]
-            oth_out[s % 2, 1] = -object_grad[1]
-
+        slot = jnp.where(place == s // 2, s % 2, 2 + s % 2)
+        for c in range(2):
+            value = object_grad[c] if c == 0 else -object_grad[c]
+            core_out[slot, c] = value[HALO:]
+            start = pl.multiple_of((slot * 2 + c) * HALO, HALO)
+            halo_out[pl.ds(start, HALO)] = value[:HALO]
         grad = times(window_of(s), grad)
         if s > 0:
             grad = propagate(grad, tables_ref)
+    meta = lax.broadcasted_iota(jnp.int32, (8, WIDTH), 0)
+    halo_out[8 * HALO :] = jnp.where(meta == 0, row, col).astype(F32)
     for c in range(2):
         value = grad[c] if c == 0 else -grad[c]
         value = pltpu.roll(value, lax.rem(WIDTH - row, WIDTH), 0)
@@ -206,30 +224,31 @@
             probe_out[c, :, h] = value[:, h * HALF : (h + 1) * HALF].reshape(WIDTH // 8, 8, HALF)
 
 
-def spread_kernel(place_ref, offsets_ref, own_ref, got_ref, core_out, prev_out, next_out):
-    place = place_ref[0]
-    core = prev = after = 0.0
-    for ref, index in ((own_ref, place), (got_ref, 1 - place)):
-        row, col = offsets_ref[index, 0], offsets_ref[index, 1]
-        grad = ref[...]
-        lane = lax.broadcasted_iota(jnp.int32, grad.shape[:-1] + (HALF,), 3)
-        kept = lane >= col
-        wide = jnp.concatenate(
-            [
-                jnp.where(kept, grad[..., :HALF], 0.0),
-                grad[..., HALF:],
-                jnp.where(kept, 0.0, grad[..., :HALF]),
-            ],
-            axis=-1,
-        )
-        core = core + wide[:, :, HALO:]
-        halo = wide[:, :, :HALO]
-        line = lax.broadcasted_iota(jnp.int32, halo.shape, 2)
-        prev = prev + jnp.where(line >= row, halo, 0.0)
-        after = after + jnp.where(line >= row, 0.0, halo)
-    core_out[...] = core
-    prev_out[...] = prev
-    next_out[...] = after
+def widen(x, kept):
+    left, right = x[..., :HALF], x[..., HALF:]
+    return jnp.concatenate([jnp.where(kept, left, 0.0), right, jnp.where(kept, 0.0, left)], axis=-1)
+
+
+def sum_kernel(place_ref, offsets_ref, core_ref, across_ref, beside_ref, out_ref, *, first):
+    col = offsets_ref[place_ref[0], 1]
+    lane = lax.broadcasted_iota(jnp.int32, (HALO, HALF), 1)
+    line = lax.broadcasted_iota(jnp.int32, (HALO, WIDTH), 0).astype(F32)
+    column = lax.broadcasted_iota(jnp.int32, (HALO, HALF), 1).astype(F32)
+    sides = []
+    odd = place_ref[1]
+    for ref, after, turned in ((across_ref, odd, place_ref[2]), (beside_ref, 1 - odd, 0)):
+        base = pl.multiple_of(((first + 2 * turned) % 4) * 2 * HALO, HALO)
+        row = ref[8 * HALO : 8 * HALO + 1]
+        kept = column >= ref[8 * HALO + 1 : 8 * HALO + 2, :HALF]
+        mask = jnp.where(line >= row, 1, 0) == after
+        sides.append((ref, base, mask, kept))
+    for j in range(2):
+        for c in range(2):
+            total = widen(core_ref[first + j, c], lane >= col)
+            for ref, base, mask, kept in sides:
+                part = jnp.where(mask, ref[pl.ds(base + (j * 2 + c) * HALO, HALO)], 0.0)
+                total = total + widen(part, kept)
+            out_ref[j, c] = total
 
 
 def call(kernel, shapes, smem, vmem, name, scratch=(), flops=0, nbytes=2_000_000):
@@ -248,9 +267,15 @@
     return out[0] if single else out
 
 
-def along_tile(x, by):
-    count = lax.axis_size("tile")
-    return lax.ppermute(x, "tile", [(i, (i + by) % count) for i in range(count)])
+def swap_tile(x, beside):
+    slabs, tiles = lax.axis_size("slab"), lax.axis_size("tile")
+    pairs = []
+    for slab in range(slabs):
+        for tile in range(tiles):
+            to = (tile + (1 if tile % 2 != beside else -1)) % tiles
+            turned = tile // (tiles // 2) != to // (tiles // 2)
+            pairs.append((slab * tiles + tile, (slab ^ turned) * tiles + to))
+    return lax.ppermute(x, ("slab", "tile"), pairs)
 
 
 def swap_slab(x):
@@ -260,22 +285,26 @@
 def shards(transmission, probe, scan_offsets, amplitudes):
     tables = jnp.asarray(make_tables())
     index = lax.axis_index("slab").astype(jnp.int32)
-    where = (index.reshape(1), scan_offsets)
+    half = lax.axis_size("tile") // 2
+    within = lax.axis_index("tile").astype(jnp.int32) % half
+    turned = (within == 0) | (within == half - 1)
+    flags = jnp.stack([index, within % 2, jnp.int32(turned)])
+    where = (flags, scan_offsets)
     own = transmission
     part, whole, band = (2, 2, HALO, WIDTH), (2, 2, WIDTH, WIDTH), (2, 2, HALO, COLS)
 
-    core = swap_slab(call(core_kernel, part, where, (own,), "core"))
-    prev, after = along_tile(own, 1), along_tile(own, -1)
+    core, own = call(core_kernel, (part, band), where, (own,), "core")
+    core = swap_slab(core)
+    beside, across = swap_tile(own, 1), swap_tile(own, 0)
     rolled = call(roll_probe_kernel, (2, WIDTH, WIDTH), where, (probe,), "roll")
-    amp = lax.dynamic_index_in_dim(amplitudes, index, 0, keepdims=False)
-    amp = amp.reshape(HALF, 2, HALF, 2).transpose(1, 0, 3, 2).reshape(WIDTH, WIDTH)
-    halo = swap_slab(call(halo_kernel, part, where, (prev, after), "halo"))
-    windows = call(window_kernel, whole, where, (own, prev, after), "window")
+    amp = call(amp_kernel, (WIDTH, WIDTH), where, (amplitudes,), "amp")
+    halo = swap_slab(call(halo_kernel, part, where, (across, beside), "halo"))
+    windows = call(window_kernel, whole, where, (own, across, beside), "window")
 
     tiles = (2, WIDTH // 8, 2, 8, HALF)
-    probe_term, own_grad, oth_grad = call(
+    probe_term, cores, halos = call(
         position_kernel,
-        (tiles, whole, whole),
+        (tiles, (4, 2, HALO, WIDTH), (8 * HALO + 8, WIDTH)),
         where,
         (tables, rolled, amp, windows, core, halo),
         "position",
@@ -283,7 +312,10 @@
         flops=3_300_000_000,
         nbytes=10_000_000,
     )
-    got = swap_slab(oth_grad)
+    sides = (cores, swap_tile(halos, 0), swap_tile(halos, 1))
+    oth_sum = call(functools.partial(sum_kernel, first=2), band, where, sides, "sum_other")
+    got = swap_slab(oth_sum)
+    own_sum = call(functools.partial(sum_kernel, first=0), band, where, sides, "sum_own")
     axes = ("slab", "tile")
     devices = lax.axis_size(axes)
     parts = probe_term.reshape(devices, 8, HALF)
@@ -292,8 +324,7 @@
     probe_grad = lax.all_to_all(spread, axes, 0, 0, tiled=True).reshape(tiles)
     probe_grad = probe_grad.transpose(0, 1, 3, 2, 4).reshape(probe.shape)
 
-    own_sum, to_prev, to_next = call(spread_kernel, (band,) * 3, where, (own_grad, got), "spread")
-    object_grad = own_sum + along_tile(to_prev, -1) + along_tile(to_next, 1)
+    object_grad = own_sum + got
     return object_grad, probe_grad
 
 

time: 127 us -> 97.4 us (0.77)
  local copies, waits for them, and re-layouts: 37.8 us -> 4.14 us
  waiting for transfers between devices: 18.7 us -> 27.1 us
  starting transfers between devices: 26.4 us -> 23.3 us
    reshape x1 -> x0, local copies, waits for them, and re-layouts: 18.9 us -> none  [shards(): amp.reshape(HALF, 2, HALF, 2).transpose(1, 0, 3, 2).reshape(WIDTH, WIDTH)]
    transpose x1 -> x0, local copies, waits for them, and re-layouts: 9.79 us -> none  [shards(): amp.reshape(HALF, 2, HALF, 2).transpose(1, 0, 3, 2).reshape(WIDTH, WIDTH)]
    ppermute x4, waiting for transfers between devices: 7.76 us -> 16.1 us  [swap_tile(): return lax.ppermute(x, ('slab', 'tile'), pairs)]
    all_to_all x1, waiting for transfers between devices: 0.01 us -> 5.12 us  [shards(): mine = jnp.sum(lax.all_to_all(parts, axes, 0, 0, tiled=True), axis=0)]
    ppermute x3, waiting for transfers between devices: 10.9 us -> 5.87 us  [swap_slab(): return lax.ppermute(x, 'slab', [(0, 1), (1, 0)])]
    unnamed x20 -> x17, local copies, waits for them, and re-layouts: 8.37 us -> 4.1 us
    all_to_all x1, starting transfers between devices: 14.3 us -> 11.1 us  [shards(): mine = jnp.sum(lax.all_to_all(parts, axes, 0, 0, tiled=True), axis=0)]
    all_to_all x1, blocking collectives: 25.2 us -> 24 us  [shards(): probe_grad = lax.all_to_all(spread, axes, 0, 0, tiled=True).reshape(tiles)]
  transfers between devices with their start and end apart: 8 -> 8, of which waited for: 3 -> 4; matrix products, arithmetic and copies ran while one was open for 25% -> 1% of each run, Pallas kernels for 4% -> 6%
where the time goes in v3:
time: 97.4 us; the launch traced here: 97.1 us
  waiting for transfers between devices  27.1 us (28%)
  blocking collectives  24 us (25%)
  starting transfers between devices  23.3 us (24%)
  Pallas kernels  14.5 us (15%)
  local copies, waits for them, and re-layouts  4.14 us (4%)
  other arithmetic  3.35 us (3%)
    all_to_all x1, blocking collectives, shards(): probe_grad = lax.all_to_all(spread, axes, 0, 0, tiled=True).reshape(tiles)  24 us
    ppermute x4, waiting for transfers between devices, swap_tile(): return lax.ppermute(x, ('slab', 'tile'), pairs)  16.1 us
    pallas_call x8, Pallas kernels, call(): pl.pallas_call(kernel, out_shape=tuple((jax.ShapeDtypeStruct(shape, F32)...  14.5 us
    all_to_all x1, starting transfers between devices, shards(): mine = jnp.sum(lax.all_to_all(parts, axes, 0, 0, tiled=True), axis=0)  11.1 us
    ppermute x4, starting transfers between devices, swap_tile(): return lax.ppermute(x, ('slab', 'tile'), pairs)  8.77 us
    ppermute x3, waiting for transfers between devices, swap_slab(): return lax.ppermute(x, 'slab', [(0, 1), (1, 0)])  5.87 us
    all_to_all x1, waiting for transfers between devices, shards(): mine = jnp.sum(lax.all_to_all(parts, axes, 0, 0, tiled=True), axis=0)  5.12 us
    unnamed x17, local copies, waits for them, and re-layouts  4.1 us
  transfers between devices with their start and end apart: 8, of which 4 were waited for; matrix products, arithmetic and copies ran while one was open for 1% of the time, Pallas kernels for 6%

profile of v3, /device:TPU:1, one launch (start us, length us, event | category | flops | bytes accessed | tf_op | source)
XLA Modules:
  0.0 97.1 jit_solution(2195843728895800987)
XLA Ops:
  0.7 0.1 pad_add_fusion.place_ref
  0.7 0.0 copy-start
  0.7 1.1 %copy-done = f32[2,2,128,384]{3,2,1,0:T(8,128)S(1)} copy-done((f32[2,2,128,384]{3,2,1,0:T(8,128)S(1)}, f32[2,2,128,384]{3,2,1,0:T(8,128)}, u32[]{:S(2)}) %copy-start) | copy-done | bytes 786456
  1.9 0.0 copy-start.4
  1.9 0.7 copy-done.4
  2.6 0.6 core.1
  3.2 0.0 copy-start.1
  3.2 1.5 %collective-permute-start.1 = (f32[2,2,128,384]{3,2,1,0:T(8,128)S(1)}, f32[2,2,128,384]{3,2,1,0:T(8,128)S(1)}, u32[]{:S(2)}, u32[]{:S(2)}) collective-permute-start(f32[2,2,128,384]{3,2,1,0:T(8,128)S(1)} %get-tuple-element.7.own_ref), channel_id=1, source_target_pairs={{0,1},{1,0},{2,3},{3,2},{4,5},{5,4},{6,7},{7,6},{8,9},{9,8},{10,11... | collective-permute-start | bytes 2359304 | tf_op jit(solution)/shard_map/ppermute | solution.py:278
  4.7 1.4 %collective-permute-start = (f32[2,2,128,384]{3,2,1,0:T(8,128)S(1)}, f32[2,2,128,384]{3,2,1,0:T(8,128)S(1)}, u32[]{:S(2)}, u32[]{:S(2)}) collective-permute-start(f32[2,2,128,384]{3,2,1,0:T(8,128)S(1)} %get-tuple-element.7.own_ref), channel_id=1, source_target_pairs={{0,127},{1,2},{2,1},{3,4},{4,3},{5,6},{6,5},{7,8},{8,7},{9,10},{10... | collective-permute-start | bytes 2359304 | tf_op jit(solution)/shard_map/ppermute | solution.py:278
  6.1 0.0 copy-start.2
  6.1 1.6 %collective-permute-start.2 = (f32[2,2,128,256]{3,2,1,0:T(8,128)S(1)}, f32[2,2,128,256]{3,2,1,0:T(8,128)S(1)}, u32[]{:S(2)}, u32[]{:S(2)}) collective-permute-start(f32[2,2,128,256]{3,2,1,0:T(8,128)S(1)} %get-tuple-element.8), channel_id=1, source_target_pairs={{0,64},{64,0},{1,65},{65,1},{2,66},{66,2},{3,67},{67,3},{4,68},{68... | collective-permute-start | bytes 1572872 | tf_op jit(solution)/shard_map/ppermute | solution.py:282
  7.7 0.0 collective-permute-done.1.beside_ref
  7.7 8.7 %collective-permute-done.across_ref = f32[2,2,128,384]{3,2,1,0:T(8,128)S(1)} collective-permute-done((f32[2,2,128,384]{3,2,1,0:T(8,128)S(1)}, f32[2,2,128,384]{3,2,1,0:T(8,128)S(1)}, u32[]{:S(2)}, u32[]{:S(2)}) %collective-permute-start) | collective-permute-done | bytes 786464 | tf_op jit(solution)/shard_map/ppermute | solution.py:278
  16.4 0.0 copy-start.5
  16.4 0.7 copy-done.5
  17.1 0.6 halo.1
  17.7 1.8 %collective-permute-start.3 = (f32[2,2,128,256]{3,2,1,0:T(8,128)S(1)}, f32[2,2,128,256]{3,2,1,0:T(8,128)S(1)}, u32[]{:S(2)}, u32[]{:S(2)}) collective-permute-start(f32[2,2,128,256]{3,2,1,0:T(8,128)S(1)} %halo.1), channel_id=1, source_target_pairs={{0,64},{64,0},{1,65},{65,1},{2,66},{66,2},{3,67},{67,3},{4,68},{68... | collective-permute-start | bytes 1572872 | tf_op jit(solution)/shard_map/ppermute | solution.py:282
  19.5 0.0 copy-done.1
  19.5 1.2 %amp.1.amp_ref = f32[256,256]{1,0:T(8,128)S(1)} custom-call(s32[3]{0:T(128)S(1)} %pad_add_fusion.place_ref, s32[2,2]{1,0:T(2,128)S(1)} %copy-done.5, f32[2,256,256]{2,1,0:T(8,128)S(1)} %copy-done.1), custom_call_target="tpu_custom_call" | custom-call | bytes 2000000 | tf_op jit(solution)/shard_map/amp/pallas_call | solution.py:257
  20.7 0.0 copy-done.2
  20.7 0.8 roll.1.probe_ref
  21.5 0.0 copy-start.6
  21.5 0.0 copy-start.7
  21.5 0.7 window.1.own_ref
  22.2 0.0 collective-permute-done.2.core_ref
  22.2 5.9 %collective-permute-done.3.halo_ref = f32[2,2,128,256]{3,2,1,0:T(8,128)S(1)} collective-permute-done((f32[2,2,128,256]{3,2,1,0:T(8,128)S(1)}, f32[2,2,128,256]{3,2,1,0:T(8,128)S(1)}, u32[]{:S(2)}, u32[]{:S(2)}) %collective-permute-start.3) | collective-permute-done | bytes 524320 | tf_op jit(solution)/shard_map/ppermute | solution.py:282
  28.1 0.0 copy-done.6
  28.1 0.0 copy-done.7
  28.1 8.2 %position.1 = (f32[2,32,2,8,128]{4,3,2,1,0:T(8,128)S(1)}, f32[4,2,128,256]{3,2,1,0:T(8,128)S(1)}, f32[1032,256]{1,0:T(8,128)}) custom-call(s32[3]{0:T(128)S(1)} %pad_add_fusion.place_ref, s32[2,2]{1,0:T(2,128)S(1)} %copy-done.6, bf16[6,2,2,256,256]{4,3,2,1,0:T(8,128)(2,1)S(1)} %copy-done.7, f32[2,256,256]{2,1,0:T(8,128)S(1)} %roll.1.probe_ref, ...), custom_call_target="tpu_custom_call" | custom-call | flops 3300000000 | bytes 10000000 | tf_op jit(solution)/shard_map/position/pallas_call | solution.py:257
  36.3 0.0 copy-start.3
  36.3 0.8 copy-done.3
  37.1 5.9 %collective-permute-start.5 = (f32[1032,256]{1,0:T(8,128)}, f32[1032,256]{1,0:T(8,128)S(1)}, u32[]{:S(2)}, u32[]{:S(2)}) collective-permute-start(f32[1032,256]{1,0:T(8,128)} %get-tuple-element.10), channel_id=1, source_target_pairs={{0,1},{1,0},{2,3},{3,2},{4,5},{5,4},{6,7},{7,6},{8,9},{9,8},{10,11... | collective-permute-start | bytes 3170312 | tf_op jit(solution)/shard_map/ppermute | solution.py:278
  43.0 0.0 collective-permute-start.4
  43.0 11.1 %all-to-all-start = ((f32[128,8,128]{2,1,0:T(8,128)}), f32[128,8,128]{2,1,0:T(8,128)}, u32[]{:S(2)}, u32[]{:S(2)}) async-start(f32[128,8,128]{2,1,0:T(8,128)} %bitcast.9), calls=%async_computation | async-start | bytes 1048576 | tf_op jit(solution)/shard_map/all_to_all | solution.py:322
  54.1 0.0 collective-permute-done.5.beside_ref
  54.1 7.4 %collective-permute-done.4.across_ref = f32[1032,256]{1,0:T(8,128)S(1)} collective-permute-done((f32[1032,256]{1,0:T(8,128)}, f32[1032,256]{1,0:T(8,128)S(1)}, u32[]{:S(2)}, u32[]{:S(2)}) %collective-permute-start.4) | collective-permute-done | bytes 1056800 | tf_op jit(solution)/shard_map/ppermute | solution.py:278
  61.5 1.6 %sum_other.1 = f32[2,2,128,384]{3,2,1,0:T(8,128)} custom-call(s32[3]{0:T(128)S(1)} %pad_add_fusion.place_ref, s32[2,2]{1,0:T(2,128)S(1)} %copy-done.6, f32[4,2,128,256]{3,2,1,0:T(8,128)S(1)} %get-tuple-element.9.core_ref, f32[1032,256]{1,0:T(8,128)S(1)} %collective-permute-done.4.across_ref, f32[1032,256]{1,0:T(8,128)S(1)} %collective-permute-done.5.beside_ref), custom_call_target="tpu_custom_call" | custom-call | bytes 2000000 | tf_op jit(solution)/shard_map/sum_other/pallas_call | solution.py:257
  63.2 0.0 collective-permute-start.6
  63.2 5.1 %all-to-all-done = f32[128,8,128]{2,1,0:T(8,128)} async-done(((f32[128,8,128]{2,1,0:T(8,128)}), f32[128,8,128]{2,1,0:T(8,128)}, u32[]{:S(2)}, u32[]{:S(2)}) %all-to-all-start) | async-done | bytes 524320 | tf_op jit(solution)/shard_map/all_to_all | solution.py:322
  68.3 1.2 %reduce_sum.9 = f32[8,128]{1,0:T(8,128)S(1)} reduce(f32[128,8,128]{2,1,0:T(8,128)} %all-to-all-done, f32[]{:T(128)} %constant.37.clone.1), dimensions={0}, to_apply=%region_0.1 | reduce | flops 130048 | bytes 528388 | tf_op jit(solution)/shard_map/reduce_sum | solution.py:322
  69.5 24.0 %all_to_all.10 = f32[128,8,128]{2,1,0:T(8,128)S(1)} all-to-all(f32[128,8,128]{2,1,0:T(8,128)S(1)} %broadcast_in_dim.2), channel_id=1, replica_groups=mesh['slab'=2,'tile'=64] {'slab','tile'}, dimensions={0} | all-to-all | bytes 1048576 | tf_op jit(solution)/shard_map/all_to_all | solution.py:324
  93.5 0.7 sum_own.1
  94.2 0.0 collective-permute-done.6
  94.2 2.1 %add.12 = f32[2,2,128,384]{3,2,1,0:T(8,128)} add(f32[2,2,128,384]{3,2,1,0:T(8,128)S(1)} %sum_own.1, f32[2,2,128,384]{3,2,1,0:T(8,128)} %collective-permute-done.6) | non-fusion elementwise | flops 196608 | bytes 2359296 | tf_op jit(solution)/shard_map/add | solution.py:327
  96.3 0.8 copy.8
  (1 shorter events, 0.0 us)
Async XLA Ops:
  0.7 1.1 %copy-start = (f32[2,2,128,384]{3,2,1,0:T(8,128)S(1)}, f32[2,2,128,384]{3,2,1,0:T(8,128)}, u32[]{:S(2)}) copy-start(f32[2,2,128,384]{3,2,1,0:T(8,128)} %own_ref.1) | copy-start | bytes 2359300
  1.9 0.7 copy-start.4
  3.2 16.3 %copy-start.1 = (f32[2,256,256]{2,1,0:T(8,128)S(1)}, f32[2,256,256]{2,1,0:T(8,128)}, u32[]{:S(2)}) copy-start(f32[2,256,256]{2,1,0:T(8,128)} %amp_ref.1) | copy-start | bytes 1572868
  3.2 4.5 %collective-permute-start.1 = (f32[2,2,128,384]{3,2,1,0:T(8,128)S(1)}, f32[2,2,128,384]{3,2,1,0:T(8,128)S(1)}, u32[]{:S(2)}, u32[]{:S(2)}) collective-permute-start(f32[2,2,128,384]{3,2,1,0:T(8,128)S(1)} %get-tuple-element.7.own_ref), channel_id=1, source_target_pairs={{0,1},{1,0},{2,3},{3,2},{4,5},{5,4},{6,7},{7,6},{8,9},{9,8},{10,11... | collective-permute-start | bytes 2359304 | tf_op jit(solution)/shard_map/ppermute | solution.py:278
  4.7 11.7 %collective-permute-start = (f32[2,2,128,384]{3,2,1,0:T(8,128)S(1)}, f32[2,2,128,384]{3,2,1,0:T(8,128)S(1)}, u32[]{:S(2)}, u32[]{:S(2)}) collective-permute-start(f32[2,2,128,384]{3,2,1,0:T(8,128)S(1)} %get-tuple-element.7.own_ref), channel_id=1, source_target_pairs={{0,127},{1,2},{2,1},{3,4},{4,3},{5,6},{6,5},{7,8},{8,7},{9,10},{10... | collective-permute-start | bytes 2359304 | tf_op jit(solution)/shard_map/ppermute | solution.py:278
  6.1 14.7 %copy-start.2 = (f32[2,256,256]{2,1,0:T(8,128)S(1)}, f32[2,256,256]{2,1,0:T(8,128)}, u32[]{:S(2)}) copy-start(f32[2,256,256]{2,1,0:T(8,128)} %probe_ref.1) | copy-start | bytes 1572868
  6.1 16.2 %collective-permute-start.2 = (f32[2,2,128,256]{3,2,1,0:T(8,128)S(1)}, f32[2,2,128,256]{3,2,1,0:T(8,128)S(1)}, u32[]{:S(2)}, u32[]{:S(2)}) collective-permute-start(f32[2,2,128,256]{3,2,1,0:T(8,128)S(1)} %get-tuple-element.8), channel_id=1, source_target_pairs={{0,64},{64,0},{1,65},{65,1},{2,66},{66,2},{3,67},{67,3},{4,68},{68... | collective-permute-start | bytes 1572872 | tf_op jit(solution)/shard_map/ppermute | solution.py:282
  16.4 0.7 copy-start.5
  17.7 10.4 %collective-permute-start.3 = (f32[2,2,128,256]{3,2,1,0:T(8,128)S(1)}, f32[2,2,128,256]{3,2,1,0:T(8,128)S(1)}, u32[]{:S(2)}, u32[]{:S(2)}) collective-permute-start(f32[2,2,128,256]{3,2,1,0:T(8,128)S(1)} %halo.1), channel_id=1, source_target_pairs={{0,64},{64,0},{1,65},{65,1},{2,66},{66,2},{3,67},{67,3},{4,68},{68... | collective-permute-start | bytes 1572872 | tf_op jit(solution)/shard_map/ppermute | solution.py:282
  21.5 6.6 %copy-start.6 = (s32[2,2]{1,0:T(2,128)S(1)}, s32[2,2]{1,0:T(2,128)}, u32[]{:S(2)}) copy-start(s32[2,2]{1,0:T(2,128)} %offsets_ref.15) | copy-start | bytes 52
  21.5 6.6 %copy-start.7 = (bf16[6,2,2,256,256]{4,3,2,1,0:T(8,128)(2,1)S(1)}, bf16[6,2,2,256,256]{4,3,2,1,0:T(8,128)(2,1)}, u32[]{:S(2)}) copy-start(bf16[6,2,2,256,256]{4,3,2,1,0:T(8,128)(2,1)} %constant.38.clone.tables_ref) | copy-start | bytes 9437188
  36.3 0.8 copy-start.3
  37.1 17.0 %collective-permute-start.5 = (f32[1032,256]{1,0:T(8,128)}, f32[1032,256]{1,0:T(8,128)S(1)}, u32[]{:S(2)}, u32[]{:S(2)}) collective-permute-start(f32[1032,256]{1,0:T(8,128)} %get-tuple-element.10), channel_id=1, source_target_pairs={{0,1},{1,0},{2,3},{3,2},{4,5},{5,4},{6,7},{7,6},{8,9},{9,8},{10,11... | collective-permute-start | bytes 3170312 | tf_op jit(solution)/shard_map/ppermute | solution.py:278
  43.0 18.5 %collective-permute-start.4 = (f32[1032,256]{1,0:T(8,128)}, f32[1032,256]{1,0:T(8,128)S(1)}, u32[]{:S(2)}, u32[]{:S(2)}) collective-permute-start(f32[1032,256]{1,0:T(8,128)} %get-tuple-element.10), channel_id=1, source_target_pairs={{0,127},{1,2},{2,1},{3,4},{4,3},{5,6},{6,5},{7,8},{8,7},{9,10},{10... | collective-permute-start | bytes 3170312 | tf_op jit(solution)/shard_map/ppermute | solution.py:278
  43.0 25.2 %all-to-all-start = ((f32[128,8,128]{2,1,0:T(8,128)}), f32[128,8,128]{2,1,0:T(8,128)}, u32[]{:S(2)}, u32[]{:S(2)}) async-start(f32[128,8,128]{2,1,0:T(8,128)} %bitcast.9), calls=%async_computation | async-start | bytes 1048576 | tf_op jit(solution)/shard_map/all_to_all | solution.py:322
  63.2 31.0 %collective-permute-start.6 = (f32[2,2,128,384]{3,2,1,0:T(8,128)}, f32[2,2,128,384]{3,2,1,0:T(8,128)}, u32[]{:S(2)}, u32[]{:S(2)}) collective-permute-start(f32[2,2,128,384]{3,2,1,0:T(8,128)} %sum_other.1), channel_id=1, source_target_pairs={{0,64},{64,0},{1,65},{65,1},{2,66},{66,2},{3,67},{67,3},{4,68},{68... | collective-permute-start | bytes 2359304 | tf_op jit(solution)/shard_map/ppermute | solution.py:282

commit v4 on v3

--- a/solution.py
+++ b/solution.py
@@ -17,6 +17,7 @@
 F32 = jnp.float32
 VMEM = pl.BlockSpec(memory_space=pltpu.VMEM)
 SMEM = pl.BlockSpec(memory_space=pltpu.SMEM)
+HBM = pl.BlockSpec(memory_space=pltpu.HBM)
 
 
 def high_low(table):
@@ -125,11 +126,9 @@
         out_ref[c] = pltpu.roll(pltpu.roll(probe_ref[c], row, 0), col, 1)
 
 
-def core_kernel(place_ref, offsets_ref, own_ref, out_ref, copy_ref):
+def core_kernel(place_ref, offsets_ref, own_ref, out_ref):
     col = offsets_ref[1 - place_ref[0], 1]
-    own = own_ref[...]
-    out_ref[...] = pick_columns(own, col)
-    copy_ref[...] = own
+    out_ref[...] = pick_columns(own_ref[...], col)
 
 
 def amp_kernel(place_ref, offsets_ref, amp_ref, out_ref):
@@ -168,10 +167,13 @@
     own_ref,
     core_ref,
     halo_ref,
-    probe_out,
+    keep_out,
+    send_out,
     core_out,
     halo_out,
     waves,
+    halos,
+    sems,
 ):
     place = place_ref[0]
     row, col = offsets_ref[place, 0], offsets_ref[place, 1]
@@ -202,6 +204,7 @@
     grad = right_mult(grad, tables_ref, BACK_RIGHT)
     grad = left_mult(grad, tables_ref, BACK_LEFT)
     grad = (fold(grad[0]), fold(grad[1]))
+    copies = []
     for s in range(3, -1, -1):
         wave = (waves[s - 1, 0], waves[s - 1, 1]) if s > 0 else (probe_ref[0], probe_ref[1])
         object_grad = times(wave, grad)
@@ -209,19 +212,30 @@
         for c in range(2):
             value = object_grad[c] if c == 0 else -object_grad[c]
             core_out[slot, c] = value[HALO:]
-            start = pl.multiple_of((slot * 2 + c) * HALO, HALO)
-            halo_out[pl.ds(start, HALO)] = value[:HALO]
+            halos[slot, pl.ds(c * HALO, HALO)] = value[:HALO]
+        start = pl.multiple_of(slot * 2 * HALO, HALO)
+        copy = pltpu.make_async_copy(halos.at[slot], halo_out.at[pl.ds(start, 2 * HALO)], sems.at[s])
+        copy.start()
+        copies.append(copy)
         grad = times(window_of(s), grad)
         if s > 0:
             grad = propagate(grad, tables_ref)
     meta = lax.broadcasted_iota(jnp.int32, (8, WIDTH), 0)
-    halo_out[8 * HALO :] = jnp.where(meta == 0, row, col).astype(F32)
+    halos[4, :8] = jnp.where(meta == 0, row, col).astype(F32)
+    copy = pltpu.make_async_copy(halos.at[4, :8], halo_out.at[8 * HALO :], sems.at[4])
+    copy.start()
+    copies.append(copy)
+    odd = place_ref[1]
+    value = [grad[0], -grad[1]]
     for c in range(2):
-        value = grad[c] if c == 0 else -grad[c]
-        value = pltpu.roll(value, lax.rem(WIDTH - row, WIDTH), 0)
-        value = pltpu.roll(value, lax.rem(WIDTH - col, WIDTH), 1)
+        value[c] = pltpu.roll(value[c], lax.rem(WIDTH - row, WIDTH), 0)
+        value[c] = pltpu.roll(value[c], lax.rem(WIDTH - col, WIDTH), 1)
+    for ref, which in ((keep_out, odd), (send_out, 1 - odd)):
+        part = jnp.where(which == 0, value[0], value[1])
         for h in range(2):
-            probe_out[c, :, h] = value[:, h * HALF : (h + 1) * HALF].reshape(WIDTH // 8, 8, HALF)
+            ref[:, h] = part[:, h * HALF : (h + 1) * HALF].reshape(WIDTH // 8, 8, HALF)
+    for copy in copies:
+        copy.wait()
 
 
 def widen(x, kept):
@@ -229,7 +243,7 @@
     return jnp.concatenate([jnp.where(kept, left, 0.0), right, jnp.where(kept, 0.0, left)], axis=-1)
 
 
-def sum_kernel(place_ref, offsets_ref, core_ref, across_ref, beside_ref, out_ref, *, first):
+def add_halos(place_ref, offsets_ref, core_ref, across_ref, beside_ref, out_ref, first, extra=None):
     col = offsets_ref[place_ref[0], 1]
     lane = lax.broadcasted_iota(jnp.int32, (HALO, HALF), 1)
     line = lax.broadcasted_iota(jnp.int32, (HALO, WIDTH), 0).astype(F32)
@@ -248,17 +262,50 @@
             for ref, base, mask, kept in sides:
                 part = jnp.where(mask, ref[pl.ds(base + (j * 2 + c) * HALO, HALO)], 0.0)
                 total = total + widen(part, kept)
-            out_ref[j, c] = total
-
-
-def call(kernel, shapes, smem, vmem, name, scratch=(), flops=0, nbytes=2_000_000):
+            out_ref[j, c] = total if extra is None else total + extra[j, c]
+
+
+def add_kernel(keep_ref, got_ref, out_ref):
+    out_ref[...] = keep_ref[...] + got_ref[...]
+
+
+def sum_kernel(
+    place_ref, offsets_ref, core_ref, across_ref, beside_ref, parts_ref, sum_out, spread_out
+):
+    add_halos(place_ref, offsets_ref, core_ref, across_ref, beside_ref, sum_out, 2)
+    total = jnp.sum(parts_ref[...], axis=0, keepdims=True)
+    spread_out[...] = jnp.broadcast_to(total, spread_out.shape)
+
+
+def finish_kernel(
+    place_ref,
+    offsets_ref,
+    core_ref,
+    across_ref,
+    beside_ref,
+    swapped_ref,
+    keep_ref,
+    got_ref,
+    object_out,
+    probe_out,
+):
+    add_halos(
+        place_ref, offsets_ref, core_ref, across_ref, beside_ref, object_out, 0, swapped_ref
+    )
+    odd = place_ref[1]
+    for ref, which in ((keep_ref, odd), (got_ref, 1 - odd)):
+        for h in range(2):
+            probe_out[which, :, h * HALF : (h + 1) * HALF] = ref[:, h].reshape(WIDTH, HALF)
+
+
+def call(kernel, shapes, smem, vmem, name, scratch=(), flops=0, nbytes=2_000_000, outs=None):
     single = isinstance(shapes[0], int)
     shapes = (shapes,) if single else shapes
     out = pl.pallas_call(
         kernel,
         out_shape=tuple(jax.ShapeDtypeStruct(shape, F32) for shape in shapes),
         in_specs=[SMEM] * len(smem) + [VMEM] * len(vmem),
-        out_specs=(VMEM,) * len(shapes),
+        out_specs=outs or (VMEM,) * len(shapes),
         scratch_shapes=scratch,
         compiler_params=pltpu.CompilerParams(vmem_limit_bytes=40 * 1024 * 1024),
         cost_estimate=pl.CostEstimate(flops=flops, bytes_accessed=nbytes, transcendentals=0),
@@ -276,6 +323,18 @@
             turned = tile // (tiles // 2) != to // (tiles // 2)
             pairs.append((slab * tiles + tile, (slab ^ turned) * tiles + to))
     return lax.ppermute(x, ("slab", "tile"), pairs)
+
+
+def swap_core(x):
+    count = lax.axis_size("tile")
+    return lax.ppermute(x, "tile", [(i, i ^ 1) for i in range(count)])
+
+
+def among_chips(x):
+    axes = ("slab", "tile")
+    devices = lax.axis_size(axes)
+    groups = [list(range(core, devices, 2)) for core in range(2)]
+    return lax.all_to_all(x, axes, 0, 0, tiled=True, axis_index_groups=groups)
 
 
 def swap_slab(x):
@@ -293,38 +352,43 @@
     own = transmission
     part, whole, band = (2, 2, HALO, WIDTH), (2, 2, WIDTH, WIDTH), (2, 2, HALO, COLS)
 
-    core, own = call(core_kernel, (part, band), where, (own,), "core")
-    core = swap_slab(core)
+    core = swap_slab(call(core_kernel, part, where, (own,), "core"))
     beside, across = swap_tile(own, 1), swap_tile(own, 0)
     rolled = call(roll_probe_kernel, (2, WIDTH, WIDTH), where, (probe,), "roll")
     amp = call(amp_kernel, (WIDTH, WIDTH), where, (amplitudes,), "amp")
     halo = swap_slab(call(halo_kernel, part, where, (across, beside), "halo"))
     windows = call(window_kernel, whole, where, (own, across, beside), "window")
 
-    tiles = (2, WIDTH // 8, 2, 8, HALF)
-    probe_term, cores, halos = call(
+    tiles = (WIDTH // 8, 2, 8, HALF)
+    keep, send, cores, halos = call(
         position_kernel,
-        (tiles, (4, 2, HALO, WIDTH), (8 * HALO + 8, WIDTH)),
+        (tiles, tiles, (4, 2, HALO, WIDTH), (8 * HALO + 8, WIDTH)),
         where,
         (tables, rolled, amp, windows, core, halo),
         "position",
-        scratch=[pltpu.VMEM((3, 2, WIDTH, WIDTH), F32)],
+        scratch=[
+            pltpu.VMEM((3, 2, WIDTH, WIDTH), F32),
+            pltpu.VMEM((5, 2 * HALO, WIDTH), F32),
+            pltpu.SemaphoreType.DMA((5,)),
+        ],
         flops=3_300_000_000,
         nbytes=10_000_000,
+        outs=(VMEM, VMEM, VMEM, HBM),
     )
     sides = (cores, swap_tile(halos, 0), swap_tile(halos, 1))
-    oth_sum = call(functools.partial(sum_kernel, first=2), band, where, sides, "sum_other")
+    parts = (WIDTH // 4, 8, HALF)
+    kept = call(add_kernel, tiles, (), (keep, swap_core(send)), "add").reshape(parts)
+    kept = among_chips(kept)
+    oth_sum, spread = call(sum_kernel, (band, parts), where, sides + (kept,), "sum")
     got = swap_slab(oth_sum)
-    own_sum = call(functools.partial(sum_kernel, first=0), band, where, sides, "sum_own")
-    axes = ("slab", "tile")
-    devices = lax.axis_size(axes)
-    parts = probe_term.reshape(devices, 8, HALF)
-    mine = jnp.sum(lax.all_to_all(parts, axes, 0, 0, tiled=True), axis=0)
-    spread = jnp.broadcast_to(mine[None], (devices, 8, HALF))
-    probe_grad = lax.all_to_all(spread, axes, 0, 0, tiled=True).reshape(tiles)
-    probe_grad = probe_grad.transpose(0, 1, 3, 2, 4).reshape(probe.shape)
-
-    object_grad = own_sum + got
+    kept = among_chips(spread)
+    object_grad, probe_grad = call(
+        finish_kernel,
+        (band, probe.shape),
+        where,
+        sides + (got, kept.reshape(tiles), swap_core(kept).reshape(tiles)),
+        "finish",
+    )
     return object_grad, probe_grad
 
 

time: 97.4 us -> 91.7 us (0.941)
  blocking collectives: 24 us -> 37.6 us
  waiting for transfers between devices: 27.1 us -> 18.4 us
  starting transfers between devices: 23.3 us -> 18.5 us
  other arithmetic: 3.35 us -> 0.08 us
  local copies, waits for them, and re-layouts: 4.14 us -> 1.84 us
    all_to_all x1 -> x2, blocking collectives: 24 us -> 37.6 us  [among_chips(): return lax.all_to_all(x, axes, 0, 0, tiled=True, axis_index_groups=groups)]
    all_to_all x1 -> x0, starting transfers between devices: 11.1 us -> none  [shards(): mine = jnp.sum(lax.all_to_all(parts, axes, 0, 0, tiled=True), axis=0)]
    ppermute x4, waiting for transfers between devices: 16.1 us -> 6.33 us  [swap_tile(): return lax.ppermute(x, ('slab', 'tile'), pairs)]
    ppermute x0 -> x2, starting transfers between devices: none -> 6.56 us  [swap_core(): return lax.ppermute(x, 'tile', [(i, i ^ 1) for i in range(count)])]
    all_to_all x1 -> x0, waiting for transfers between devices: 5.12 us -> none  [shards(): mine = jnp.sum(lax.all_to_all(parts, axes, 0, 0, tiled=True), axis=0)]
    ppermute x3, waiting for transfers between devices: 5.87 us -> 9.78 us  [swap_slab(): return lax.ppermute(x, 'slab', [(0, 1), (1, 0)])]
    ppermute x0 -> x2, waiting for transfers between devices: none -> 2.32 us  [swap_core(): return lax.ppermute(x, 'tile', [(i, i ^ 1) for i in range(count)])]
    unnamed x17 -> x14, local copies, waits for them, and re-layouts: 4.1 us -> 1.84 us
  transfers between devices with their start and end apart: 8 -> 9, of which waited for: 4 -> 4; matrix products, arithmetic and copies ran while one was open for 1% -> 0% of each run, Pallas kernels for 6% -> 4%
where the time goes in v4:
time: 91.7 us; the launch traced here: 91.5 us
  blocking collectives  37.6 us (41%)
  starting transfers between devices  18.5 us (20%)
  waiting for transfers between devices  18.4 us (20%)
  Pallas kernels  14.2 us (15%)
  local copies, waits for them, and re-layouts  1.84 us (2%)
    all_to_all x2, blocking collectives, among_chips(): return lax.all_to_all(x, axes, 0, 0, tiled=True, axis_index_groups=groups)  37.6 us
    pallas_call x9, Pallas kernels, call(): pl.pallas_call(kernel, out_shape=tuple((jax.ShapeDtypeStruct(shape, F32)...  14.2 us
    ppermute x3, waiting for transfers between devices, swap_slab(): return lax.ppermute(x, 'slab', [(0, 1), (1, 0)])  9.78 us
    ppermute x4, starting transfers between devices, swap_tile(): return lax.ppermute(x, ('slab', 'tile'), pairs)  8 us
    ppermute x2, starting transfers between devices, swap_core(): return lax.ppermute(x, 'tile', [(i, i ^ 1) for i in range(count)])  6.56 us
    ppermute x4, waiting for transfers between devices, swap_tile(): return lax.ppermute(x, ('slab', 'tile'), pairs)  6.33 us
    ppermute x3, starting transfers between devices, swap_slab(): return lax.ppermute(x, 'slab', [(0, 1), (1, 0)])  3.97 us
    ppermute x2, waiting for transfers between devices, swap_core(): return lax.ppermute(x, 'tile', [(i, i ^ 1) for i in range(count)])  2.32 us
  transfers between devices with their start and end apart: 9, of which 4 were waited for; matrix products, arithmetic and copies ran while one was open for 0% of the time, Pallas kernels for 4%

profile of v4, /device:TPU:1, one launch (start us, length us, event | category | flops | bytes accessed | tf_op | source)
XLA Modules:
  0.0 91.5 jit_solution(14740025593925004416)
XLA Ops:
  0.6 1.5 %collective-permute-start.1 = (f32[2,2,128,384]{3,2,1,0:T(8,128)}, f32[2,2,128,384]{3,2,1,0:T(8,128)S(1)}, u32[]{:S(2)}, u32[]{:S(2)}) collective-permute-start(f32[2,2,128,384]{3,2,1,0:T(8,128)} %own_ref.3), channel_id=1, source_target_pairs={{0,1},{1,0},{2,3},{3,2},{4,5},{5,4},{6,7},{7,6},{8,9},{9,8},{10,11... | collective-permute-start | bytes 2359304 | tf_op jit(solution)/shard_map/ppermute | solution.py:325
  2.1 1.4 %collective-permute-start = (f32[2,2,128,384]{3,2,1,0:T(8,128)}, f32[2,2,128,384]{3,2,1,0:T(8,128)S(1)}, u32[]{:S(2)}, u32[]{:S(2)}) collective-permute-start(f32[2,2,128,384]{3,2,1,0:T(8,128)} %own_ref.3), channel_id=1, source_target_pairs={{0,127},{1,2},{2,1},{3,4},{4,3},{5,6},{6,5},{7,8},{8,7},{9,10},{10... | collective-permute-start | bytes 2359304 | tf_op jit(solution)/shard_map/ppermute | solution.py:325
  3.5 0.1 pad_add_fusion.place_ref
  3.6 0.0 copy-start
  3.6 1.1 %copy-done = f32[2,2,128,384]{3,2,1,0:T(8,128)S(1)} copy-done((f32[2,2,128,384]{3,2,1,0:T(8,128)S(1)}, f32[2,2,128,384]{3,2,1,0:T(8,128)}, u32[]{:S(2)}) %copy-start) | copy-done | bytes 786456
  4.7 0.0 copy-start.4
  4.7 0.7 copy-done.4
  5.4 0.6 core.1
  6.0 0.0 copy-start.2
  6.0 0.0 copy-start.3
  6.0 1.7 %collective-permute-start.2 = (f32[2,2,128,256]{3,2,1,0:T(8,128)S(1)}, f32[2,2,128,256]{3,2,1,0:T(8,128)S(1)}, u32[]{:S(2)}, u32[]{:S(2)}) collective-permute-start(f32[2,2,128,256]{3,2,1,0:T(8,128)S(1)} %core.1), channel_id=1, source_target_pairs={{0,64},{64,0},{1,65},{65,1},{2,66},{66,2},{3,67},{67,3},{4,68},{68... | collective-permute-start | bytes 1572872 | tf_op jit(solution)/shard_map/ppermute | solution.py:341
  7.7 0.0 collective-permute-done.1.beside_ref
  7.7 6.3 %collective-permute-done.across_ref = f32[2,2,128,384]{3,2,1,0:T(8,128)S(1)} collective-permute-done((f32[2,2,128,384]{3,2,1,0:T(8,128)}, f32[2,2,128,384]{3,2,1,0:T(8,128)S(1)}, u32[]{:S(2)}, u32[]{:S(2)}) %collective-permute-start) | collective-permute-done | bytes 786464 | tf_op jit(solution)/shard_map/ppermute | solution.py:325
  14.1 0.6 halo.1
  14.7 0.0 copy-start.1
  14.7 1.8 %collective-permute-start.3 = (f32[2,2,128,256]{3,2,1,0:T(8,128)S(1)}, f32[2,2,128,256]{3,2,1,0:T(8,128)S(1)}, u32[]{:S(2)}, u32[]{:S(2)}) collective-permute-start(f32[2,2,128,256]{3,2,1,0:T(8,128)S(1)} %halo.1), channel_id=1, source_target_pairs={{0,64},{64,0},{1,65},{65,1},{2,66},{66,2},{3,67},{67,3},{4,68},{68... | collective-permute-start | bytes 1572872 | tf_op jit(solution)/shard_map/ppermute | solution.py:341
  16.5 0.0 copy-done.2
  16.5 1.2 %amp.1.amp_ref = f32[256,256]{1,0:T(8,128)S(1)} custom-call(s32[3]{0:T(128)S(1)} %pad_add_fusion.place_ref, s32[2,2]{1,0:T(2,128)S(1)} %copy-done.4, f32[2,256,256]{2,1,0:T(8,128)S(1)} %copy-done.2), custom_call_target="tpu_custom_call" | custom-call | bytes 2000000 | tf_op jit(solution)/shard_map/amp/pallas_call | solution.py:304
  17.7 0.0 copy-done.3
  17.7 0.8 roll.1.probe_ref
  18.5 0.0 copy-done.1
  18.5 0.0 copy-start.6
  18.5 0.7 window.1.own_ref
  19.2 0.0 collective-permute-done.2.core_ref
  19.2 9.8 %collective-permute-done.3.halo_ref = f32[2,2,128,256]{3,2,1,0:T(8,128)S(1)} collective-permute-done((f32[2,2,128,256]{3,2,1,0:T(8,128)S(1)}, f32[2,2,128,256]{3,2,1,0:T(8,128)S(1)}, u32[]{:S(2)}, u32[]{:S(2)}) %collective-permute-start.3) | collective-permute-done | bytes 524320 | tf_op jit(solution)/shard_map/ppermute | solution.py:341
  29.0 0.0 copy-done.6
  29.0 7.7 %position.1 = (f32[32,2,8,128]{3,2,1,0:T(8,128)S(1)}, f32[32,2,8,128]{3,2,1,0:T(8,128)S(1)}, f32[4,2,128,256]{3,2,1,0:T(8,128)S(1)}, f32[1032,256]{1,0:T(8,128)S(1)}) custom-call(s32[3]{0:T(128)S(1)} %pad_add_fusion.place_ref, s32[2,2]{1,0:T(2,128)S(1)} %copy-done.4, bf16[6,2,2,256,256]{4,3,2,1,0:T(8,128)(2,1)S(1)} %copy-done.6, ...), custom_call_target="tpu_custom_call" | custom-call | flops 3300000000 | bytes 10000000 | tf_op jit(solution)/shard_map/position/pallas_call | solution.py:304
  36.7 0.0 copy-start.5
  36.7 5.1 %collective-permute-start.5 = (f32[1032,256]{1,0:T(8,128)S(1)}, f32[1032,256]{1,0:T(8,128)S(1)}, u32[]{:S(2)}, u32[]{:S(2)}) collective-permute-start(f32[1032,256]{1,0:T(8,128)S(1)} %get-tuple-element.9), channel_id=1, source_target_pairs={{0,1},{1,0},{2,3},{3,2},{4,5},{5,4},{6,7},{7,6},{8,9},{9,8},{10,11... | collective-permute-start | bytes 3170312 | tf_op jit(solution)/shard_map/ppermute | solution.py:325
  41.9 0.0 collective-permute-start.4
  41.9 4.6 %collective-permute-start.6 = (f32[32,2,8,128]{3,2,1,0:T(8,128)S(1)}, f32[32,2,8,128]{3,2,1,0:T(8,128)S(1)}, u32[]{:S(2)}, u32[]{:S(2)}) collective-permute-start(f32[32,2,8,128]{3,2,1,0:T(8,128)S(1)} %get-tuple-element.11), channel_id=1, source_target_pairs={{0,1},{1,0},{2,3},{3,2},{4,5},{5,4},{6,7},{7,6},{8,9},{9,8},{10,11... | collective-permute-start | bytes 786440 | tf_op jit(solution)/shard_map/ppermute | solution.py:330
  46.4 1.2 %collective-permute-done.6.got_ref = f32[32,2,8,128]{3,2,1,0:T(8,128)S(1)} collective-permute-done((f32[32,2,8,128]{3,2,1,0:T(8,128)S(1)}, f32[32,2,8,128]{3,2,1,0:T(8,128)S(1)}, u32[]{:S(2)}, u32[]{:S(2)}) %collective-permute-start.6) | collective-permute-done | bytes 262176 | tf_op jit(solution)/shard_map/ppermute | solution.py:330
  47.6 16.2 %all_to_all.10.parts_ref = f32[64,8,128]{2,1,0:T(8,128)S(1)} all-to-all(f32[64,8,128]{2,1,0:T(8,128)S(1)} %bitcast.6), channel_id=1, replica_groups={{0,2,4,6,8,10,12,14,16,18,20,22,24,26,28,30,32,34,36,38,40,42,44,46,48,..., dimensions={0} | all-to-all | bytes 524288 | tf_op jit(solution)/shard_map/all_to_all | solution.py:337
  63.8 0.0 collective-permute-done.5.beside_ref
  63.8 0.0 collective-permute-done.4.across_ref
  63.8 0.0 copy-done.5
  63.8 0.8 sum.1
  64.6 0.5 collective-permute-start.7
  65.1 21.5 %all_to_all.11 = f32[64,8,128]{2,1,0:T(8,128)S(1)} all-to-all(f32[64,8,128]{2,1,0:T(8,128)S(1)} %get-tuple-element.13), channel_id=1, replica_groups={{0,2,4,6,8,10,12,14,16,18,20,22,24,26,28,30,32,34,36,38,40,42,44,46,48,..., dimensions={0} | all-to-all | bytes 524288 | tf_op jit(solution)/shard_map/all_to_all | solution.py:337
  86.5 2.0 %collective-permute-start.8 = (f32[64,8,128]{2,1,0:T(8,128)S(1)}, f32[64,8,128]{2,1,0:T(8,128)S(1)}, u32[]{:S(2)}, u32[]{:S(2)}) collective-permute-start(f32[64,8,128]{2,1,0:T(8,128)S(1)} %all_to_all.11), channel_id=1, source_target_pairs={{0,1},{1,0},{2,3},{3,2},{4,5},{5,4},{6,7},{7,6},{8,9},{9,8},{10,11... | collective-permute-start | bytes 786440 | tf_op jit(solution)/shard_map/ppermute | solution.py:330
  88.5 1.2 %collective-permute-done.8 = f32[64,8,128]{2,1,0:T(8,128)S(1)} collective-permute-done((f32[64,8,128]{2,1,0:T(8,128)S(1)}, f32[64,8,128]{2,1,0:T(8,128)S(1)}, u32[]{:S(2)}, u32[]{:S(2)}) %collective-permute-start.8) | collective-permute-done | bytes 262176 | tf_op jit(solution)/shard_map/ppermute | solution.py:330
  89.7 0.0 collective-permute-done.7.swapped_ref
  89.7 1.8 %finish.1 = (f32[2,2,128,384]{3,2,1,0:T(8,128)}, f32[2,256,256]{2,1,0:T(8,128)}) custom-call(s32[3]{0:T(128)S(1)} %pad_add_fusion.place_ref, s32[2,2]{1,0:T(2,128)S(1)} %copy-done.5, f32[4,2,128,256]{3,2,1,0:T(8,128)S(1)} %get-tuple-element.8.core_ref, f32[1032,256]{1,0:T(8,128)S(1)} %collective-permute-done.4.across_ref, ...), custom_call_target="tpu_custom_call" | custom-call | bytes 2000000 | tf_op jit(solution)/shard_map/finish/pallas_call | solution.py:304
  (1 shorter events, 0.0 us)
Async XLA Ops:
  0.6 7.1 %collective-permute-start.1 = (f32[2,2,128,384]{3,2,1,0:T(8,128)}, f32[2,2,128,384]{3,2,1,0:T(8,128)S(1)}, u32[]{:S(2)}, u32[]{:S(2)}) collective-permute-start(f32[2,2,128,384]{3,2,1,0:T(8,128)} %own_ref.3), channel_id=1, source_target_pairs={{0,1},{1,0},{2,3},{3,2},{4,5},{5,4},{6,7},{7,6},{8,9},{9,8},{10,11... | collective-permute-start | bytes 2359304 | tf_op jit(solution)/shard_map/ppermute | solution.py:325
  2.1 11.9 %collective-permute-start = (f32[2,2,128,384]{3,2,1,0:T(8,128)}, f32[2,2,128,384]{3,2,1,0:T(8,128)S(1)}, u32[]{:S(2)}, u32[]{:S(2)}) collective-permute-start(f32[2,2,128,384]{3,2,1,0:T(8,128)} %own_ref.3), channel_id=1, source_target_pairs={{0,127},{1,2},{2,1},{3,4},{4,3},{5,6},{6,5},{7,8},{8,7},{9,10},{10... | collective-permute-start | bytes 2359304 | tf_op jit(solution)/shard_map/ppermute | solution.py:325
  3.6 1.1 %copy-start = (f32[2,2,128,384]{3,2,1,0:T(8,128)S(1)}, f32[2,2,128,384]{3,2,1,0:T(8,128)}, u32[]{:S(2)}) copy-start(f32[2,2,128,384]{3,2,1,0:T(8,128)} %own_ref.3) | copy-start | bytes 2359300
  4.7 0.7 copy-start.4
  6.0 10.5 %copy-start.2 = (f32[2,256,256]{2,1,0:T(8,128)S(1)}, f32[2,256,256]{2,1,0:T(8,128)}, u32[]{:S(2)}) copy-start(f32[2,256,256]{2,1,0:T(8,128)} %amp_ref.1) | copy-start | bytes 1572868
  6.0 11.7 %copy-start.3 = (f32[2,256,256]{2,1,0:T(8,128)S(1)}, f32[2,256,256]{2,1,0:T(8,128)}, u32[]{:S(2)}) copy-start(f32[2,256,256]{2,1,0:T(8,128)} %probe_ref.1) | copy-start | bytes 1572868
  6.0 13.2 %collective-permute-start.2 = (f32[2,2,128,256]{3,2,1,0:T(8,128)S(1)}, f32[2,2,128,256]{3,2,1,0:T(8,128)S(1)}, u32[]{:S(2)}, u32[]{:S(2)}) collective-permute-start(f32[2,2,128,256]{3,2,1,0:T(8,128)S(1)} %core.1), channel_id=1, source_target_pairs={{0,64},{64,0},{1,65},{65,1},{2,66},{66,2},{3,67},{67,3},{4,68},{68... | collective-permute-start | bytes 1572872 | tf_op jit(solution)/shard_map/ppermute | solution.py:341
  14.7 3.8 %copy-start.1 = (f32[2,2,128,384]{3,2,1,0:T(8,128)S(1)}, f32[2,2,128,384]{3,2,1,0:T(8,128)}, u32[]{:S(2)}) copy-start(f32[2,2,128,384]{3,2,1,0:T(8,128)} %own_ref.3) | copy-start | bytes 2359300
  14.7 14.3 %collective-permute-start.3 = (f32[2,2,128,256]{3,2,1,0:T(8,128)S(1)}, f32[2,2,128,256]{3,2,1,0:T(8,128)S(1)}, u32[]{:S(2)}, u32[]{:S(2)}) collective-permute-start(f32[2,2,128,256]{3,2,1,0:T(8,128)S(1)} %halo.1), channel_id=1, source_target_pairs={{0,64},{64,0},{1,65},{65,1},{2,66},{66,2},{3,67},{67,3},{4,68},{68... | collective-permute-start | bytes 1572872 | tf_op jit(solution)/shard_map/ppermute | solution.py:341
  18.5 10.5 %copy-start.6 = (bf16[6,2,2,256,256]{4,3,2,1,0:T(8,128)(2,1)S(1)}, bf16[6,2,2,256,256]{4,3,2,1,0:T(8,128)(2,1)}, u32[]{:S(2)}) copy-start(bf16[6,2,2,256,256]{4,3,2,1,0:T(8,128)(2,1)} %constant.36.clone.tables_ref) | copy-start | bytes 9437188
  36.7 27.1 %copy-start.5 = (s32[2,2]{1,0:T(2,128)S(1)}, s32[2,2]{1,0:T(2,128)}, u32[]{:S(2)}) copy-start(s32[2,2]{1,0:T(2,128)} %offsets_ref.15) | copy-start | bytes 52
  36.7 27.1 %collective-permute-start.5 = (f32[1032,256]{1,0:T(8,128)S(1)}, f32[1032,256]{1,0:T(8,128)S(1)}, u32[]{:S(2)}, u32[]{:S(2)}) collective-permute-start(f32[1032,256]{1,0:T(8,128)S(1)} %get-tuple-element.9), channel_id=1, source_target_pairs={{0,1},{1,0},{2,3},{3,2},{4,5},{5,4},{6,7},{7,6},{8,9},{9,8},{10,11... | collective-permute-start | bytes 3170312 | tf_op jit(solution)/shard_map/ppermute | solution.py:325
  41.9 21.9 %collective-permute-start.4 = (f32[1032,256]{1,0:T(8,128)S(1)}, f32[1032,256]{1,0:T(8,128)S(1)}, u32[]{:S(2)}, u32[]{:S(2)}) collective-permute-start(f32[1032,256]{1,0:T(8,128)S(1)} %get-tuple-element.9), channel_id=1, source_target_pairs={{0,127},{1,2},{2,1},{3,4},{4,3},{5,6},{6,5},{7,8},{8,7},{9,10},{10... | collective-permute-start | bytes 3170312 | tf_op jit(solution)/shard_map/ppermute | solution.py:325
  41.9 5.7 %collective-permute-start.6 = (f32[32,2,8,128]{3,2,1,0:T(8,128)S(1)}, f32[32,2,8,128]{3,2,1,0:T(8,128)S(1)}, u32[]{:S(2)}, u32[]{:S(2)}) collective-permute-start(f32[32,2,8,128]{3,2,1,0:T(8,128)S(1)} %get-tuple-element.11), channel_id=1, source_target_pairs={{0,1},{1,0},{2,3},{3,2},{4,5},{5,4},{6,7},{7,6},{8,9},{9,8},{10,11... | collective-permute-start | bytes 786440 | tf_op jit(solution)/shard_map/ppermute | solution.py:330
  64.6 25.0 %collective-permute-start.7 = (f32[2,2,128,384]{3,2,1,0:T(8,128)S(1)}, f32[2,2,128,384]{3,2,1,0:T(8,128)S(1)}, u32[]{:S(2)}, u32[]{:S(2)}) collective-permute-start(f32[2,2,128,384]{3,2,1,0:T(8,128)S(1)} %get-tuple-element.12), channel_id=1, source_target_pairs={{0,64},{64,0},{1,65},{65,1},{2,66},{66,2},{3,67},{67,3},{4,68},{68... | collective-permute-start | bytes 2359304 | tf_op jit(solution)/shard_map/ppermute | solution.py:341
  86.5 3.1 %collective-permute-start.8 = (f32[64,8,128]{2,1,0:T(8,128)S(1)}, f32[64,8,128]{2,1,0:T(8,128)S(1)}, u32[]{:S(2)}, u32[]{:S(2)}) collective-permute-start(f32[64,8,128]{2,1,0:T(8,128)S(1)} %all_to_all.11), channel_id=1, source_target_pairs={{0,1},{1,0},{2,3},{3,2},{4,5},{5,4},{6,7},{7,6},{8,9},{9,8},{10,11... | collective-permute-start | bytes 786440 | tf_op jit(solution)/shard_map/ppermute | solution.py:330

commit v5 on v4

--- a/solution.py
+++ b/solution.py
@@ -109,15 +109,31 @@
     return a[0] * b[0] - a[1] * b[1], a[0] * b[1] + a[1] * b[0]
 
 
-def pick_columns(x, col):
-    lane = lax.broadcasted_iota(jnp.int32, x.shape[:-1] + (HALF,), len(x.shape) - 1)
-    left = jnp.where(lane >= col, x[..., :HALF], x[..., 2 * HALF :])
-    return jnp.concatenate([left, x[..., HALF : 2 * HALF]], axis=-1)
-
-
-def pick_rows(across, beside, row, odd):
-    line = lax.broadcasted_iota(jnp.int32, across.shape, len(across.shape) - 2)
-    return jnp.where(jnp.where(line >= row, 1, 0) == odd, beside, across)
+def here():
+    half = lax.axis_size("tile") // 2
+    within = lax.axis_index("tile") % half
+    turned = jnp.where((within == 0) | (within == half - 1), 1, 0)
+    return lax.axis_index("slab"), within % 2, turned
+
+
+def masks(info_ref, which):
+    row = jnp.broadcast_to(info_ref[2 * which : 2 * which + 1], (HALO, HALF))
+    col = jnp.broadcast_to(info_ref[2 * which + 1 : 2 * which + 2], (HALO, HALF))
+    line = lax.broadcasted_iota(jnp.int32, (HALO, HALF), 0)
+    lane = lax.broadcasted_iota(jnp.int32, (HALO, HALF), 1)
+    return jnp.where(line >= row, 1, 0) == here()[1], lane >= col
+
+
+def columns_of(x, kept):
+    return jnp.where(kept, x(0), x(2)), x(1)
+
+
+def halo_of(across_ref, beside_ref, at, from_beside, kept):
+    def column(i):
+        cols = slice(i * HALF, (i + 1) * HALF)
+        return jnp.where(from_beside, beside_ref[at + (slice(None), cols)], across_ref[at + (slice(None), cols)])
+
+    return columns_of(column, kept)
 
 
 def roll_probe_kernel(place_ref, offsets_ref, probe_ref, out_ref):
@@ -126,9 +142,24 @@
         out_ref[c] = pltpu.roll(pltpu.roll(probe_ref[c], row, 0), col, 1)
 
 
-def core_kernel(place_ref, offsets_ref, own_ref, out_ref):
-    col = offsets_ref[1 - place_ref[0], 1]
-    out_ref[...] = pick_columns(own_ref[...], col)
+def core_kernel(offsets_ref, own_ref, out_ref, offsets, cols, sems, out_sems):
+    load = pltpu.make_async_copy(offsets_ref, offsets, sems.at[4])
+    load.start()
+    loads = [pltpu.make_async_copy(own_ref.at[i // 2, i % 2], cols.at[i], sems.at[i]) for i in range(4)]
+    for copy in loads:
+        copy.start()
+    load.wait()
+    lane = lax.broadcasted_iota(jnp.int32, (HALO, HALF), 1)
+    kept = lane >= offsets[1 - lax.axis_index("slab"), 1]
+    stores = []
+    for i in range(4):
+        loads[i].wait()
+        cols[i, :, :HALF] = jnp.where(kept, cols[i, :, :HALF], cols[i, :, 2 * HALF :])
+        store = pltpu.make_async_copy(cols.at[i, :, :WIDTH], out_ref.at[i // 2, i % 2], out_sems.at[i])
+        store.start()
+        stores.append(store)
+    for copy in stores:
+        copy.wait()
 
 
 def amp_kernel(place_ref, offsets_ref, amp_ref, out_ref):
@@ -146,20 +177,29 @@
     out_ref[...] = sum(dot(part, cols) for part in parts(x))
 
 
-def halo_kernel(place_ref, offsets_ref, across_ref, beside_ref, out_ref):
-    other = 1 - place_ref[0]
-    row, col = offsets_ref[other, 0], offsets_ref[other, 1]
-    out_ref[...] = pick_columns(pick_rows(across_ref[...], beside_ref[...], row, place_ref[1]), col)
-
-
-def window_kernel(place_ref, offsets_ref, own_ref, across_ref, beside_ref, out_ref):
-    row, col = offsets_ref[place_ref[0], 0], offsets_ref[place_ref[0], 1]
-    out_ref[:, :, :HALO] = pick_columns(pick_rows(across_ref[...], beside_ref[...], row, place_ref[1]), col)
-    out_ref[:, :, HALO:] = pick_columns(own_ref[...], col)
+def halo_kernel(info_ref, across_ref, beside_ref, out_ref):
+    from_beside, kept = masks(info_ref, 1)
+    for j in range(2):
+        for c in range(2):
+            left, right = halo_of(across_ref, beside_ref, (j, c), from_beside, kept)
+            out_ref[j, c, :, :HALF] = left
+            out_ref[j, c, :, HALF:] = right
+
+
+def window_kernel(info_ref, own_ref, across_ref, beside_ref, out_ref):
+    from_beside, kept = masks(info_ref, 0)
+    for j in range(2):
+        for c in range(2):
+            left, right = halo_of(across_ref, beside_ref, (j, c), from_beside, kept)
+            out_ref[j, c, :HALO, :HALF] = left
+            out_ref[j, c, :HALO, HALF:] = right
+            left, right = columns_of(lambda i: own_ref[j, c, :, i * HALF : (i + 1) * HALF], kept)
+            out_ref[j, c, HALO:, :HALF] = left
+            out_ref[j, c, HALO:, HALF:] = right
 
 
 def position_kernel(
-    place_ref,
+    info_ref,
     offsets_ref,
     tables_ref,
     probe_ref,
@@ -173,12 +213,14 @@
     halo_out,
     waves,
     halos,
+    offsets,
     sems,
 ):
-    place = place_ref[0]
-    row, col = offsets_ref[place, 0], offsets_ref[place, 1]
-    line = lax.broadcasted_iota(jnp.int32, (HALO, WIDTH), 0)
-    turned = jnp.where(jnp.where(line >= row, 1, 0) == place_ref[1], 0, place_ref[2])
+    place, odd, turned = here()
+    load = pltpu.make_async_copy(offsets_ref, offsets, sems.at[5])
+    load.start()
+    from_beside = masks(info_ref, 0)[0]
+    turned = jnp.where(jnp.concatenate([from_beside, from_beside], axis=1), 0, turned)
 
     def window_of(s):
         mine = jnp.where(place == s // 2, 1, 0)
@@ -220,12 +262,13 @@
         grad = times(window_of(s), grad)
         if s > 0:
             grad = propagate(grad, tables_ref)
-    meta = lax.broadcasted_iota(jnp.int32, (8, WIDTH), 0)
-    halos[4, :8] = jnp.where(meta == 0, row, col).astype(F32)
+    meta = info_ref[...].astype(F32)
+    halos[4, :8] = jnp.concatenate([meta, meta], axis=1)
     copy = pltpu.make_async_copy(halos.at[4, :8], halo_out.at[8 * HALO :], sems.at[4])
     copy.start()
     copies.append(copy)
-    odd = place_ref[1]
+    load.wait()
+    row, col = offsets[place, 0], offsets[place, 1]
     value = [grad[0], -grad[1]]
     for c in range(2):
         value[c] = pltpu.roll(value[c], lax.rem(WIDTH - row, WIDTH), 0)
@@ -243,22 +286,21 @@
     return jnp.concatenate([jnp.where(kept, left, 0.0), right, jnp.where(kept, 0.0, left)], axis=-1)
 
 
-def add_halos(place_ref, offsets_ref, core_ref, across_ref, beside_ref, out_ref, first, extra=None):
-    col = offsets_ref[place_ref[0], 1]
-    lane = lax.broadcasted_iota(jnp.int32, (HALO, HALF), 1)
+def add_halos(info_ref, core_ref, across_ref, beside_ref, out_ref, first, extra=None):
+    _, odd, turned = here()
+    own_kept = masks(info_ref, 0)[1]
     line = lax.broadcasted_iota(jnp.int32, (HALO, WIDTH), 0).astype(F32)
     column = lax.broadcasted_iota(jnp.int32, (HALO, HALF), 1).astype(F32)
     sides = []
-    odd = place_ref[1]
-    for ref, after, turned in ((across_ref, odd, place_ref[2]), (beside_ref, 1 - odd, 0)):
-        base = pl.multiple_of(((first + 2 * turned) % 4) * 2 * HALO, HALO)
+    for ref, after, shift in ((across_ref, odd, turned), (beside_ref, 1 - odd, 0)):
+        base = pl.multiple_of(((first + 2 * shift) % 4) * 2 * HALO, HALO)
         row = ref[8 * HALO : 8 * HALO + 1]
         kept = column >= ref[8 * HALO + 1 : 8 * HALO + 2, :HALF]
         mask = jnp.where(line >= row, 1, 0) == after
         sides.append((ref, base, mask, kept))
     for j in range(2):
         for c in range(2):
-            total = widen(core_ref[first + j, c], lane >= col)
+            total = widen(core_ref[first + j, c], own_kept)
             for ref, base, mask, kept in sides:
                 part = jnp.where(mask, ref[pl.ds(base + (j * 2 + c) * HALO, HALO)], 0.0)
                 total = total + widen(part, kept)
@@ -269,17 +311,21 @@
     out_ref[...] = keep_ref[...] + got_ref[...]
 
 
-def sum_kernel(
-    place_ref, offsets_ref, core_ref, across_ref, beside_ref, parts_ref, sum_out, spread_out
-):
-    add_halos(place_ref, offsets_ref, core_ref, across_ref, beside_ref, sum_out, 2)
-    total = jnp.sum(parts_ref[...], axis=0, keepdims=True)
-    spread_out[...] = jnp.broadcast_to(total, spread_out.shape)
+def reduce_kernel(parts_ref, out_ref):
+    out_ref[...] = jnp.sum(parts_ref[...], axis=0)
+
+
+def total_kernel(first_ref, second_ref, third_ref, fourth_ref, out_ref):
+    total = (first_ref[...] + second_ref[...]) + (third_ref[...] + fourth_ref[...])
+    out_ref[...] = jnp.broadcast_to(total[None], out_ref.shape)
+
+
+def sum_kernel(info_ref, core_ref, across_ref, beside_ref, after_ref, out_ref):
+    add_halos(info_ref, core_ref, across_ref, beside_ref, out_ref, 2)
 
 
 def finish_kernel(
-    place_ref,
-    offsets_ref,
+    info_ref,
     core_ref,
     across_ref,
     beside_ref,
@@ -289,25 +335,23 @@
     object_out,
     probe_out,
 ):
-    add_halos(
-        place_ref, offsets_ref, core_ref, across_ref, beside_ref, object_out, 0, swapped_ref
-    )
-    odd = place_ref[1]
+    add_halos(info_ref, core_ref, across_ref, beside_ref, object_out, 0, swapped_ref)
+    odd = here()[1]
     for ref, which in ((keep_ref, odd), (got_ref, 1 - odd)):
         for h in range(2):
             probe_out[which, :, h * HALF : (h + 1) * HALF] = ref[:, h].reshape(WIDTH, HALF)
 
 
-def call(kernel, shapes, smem, vmem, name, scratch=(), flops=0, nbytes=2_000_000, outs=None):
+def call(kernel, shapes, smem, vmem, name, scratch=(), flops=0, nbytes=2_000_000, ins=None, outs=None, vmem_limit=40):
     single = isinstance(shapes[0], int)
     shapes = (shapes,) if single else shapes
     out = pl.pallas_call(
         kernel,
         out_shape=tuple(jax.ShapeDtypeStruct(shape, F32) for shape in shapes),
-        in_specs=[SMEM] * len(smem) + [VMEM] * len(vmem),
+        in_specs=[SMEM] * len(smem) + list(ins or [VMEM] * len(vmem)),
         out_specs=outs or (VMEM,) * len(shapes),
         scratch_shapes=scratch,
-        compiler_params=pltpu.CompilerParams(vmem_limit_bytes=40 * 1024 * 1024),
+        compiler_params=pltpu.CompilerParams(vmem_limit_bytes=vmem_limit * 1024 * 1024),
         cost_estimate=pl.CostEstimate(flops=flops, bytes_accessed=nbytes, transcendentals=0),
         name=name,
     )(*smem, *vmem)
@@ -330,11 +374,24 @@
     return lax.ppermute(x, "tile", [(i, i ^ 1) for i in range(count)])
 
 
-def among_chips(x):
-    axes = ("slab", "tile")
-    devices = lax.axis_size(axes)
-    groups = [list(range(core, devices, 2)) for core in range(2)]
-    return lax.all_to_all(x, axes, 0, 0, tiled=True, axis_index_groups=groups)
+def among_columns(x):
+    slabs, tiles = lax.axis_size("slab"), lax.axis_size("tile")
+    half = tiles // 2
+    planes = [slab * tiles + far * half for slab in range(slabs) for far in range(2)]
+    groups = [[plane + i for i in range(core, half, 2)] for plane in planes for core in range(2)]
+    return lax.all_to_all(x, ("slab", "tile"), 0, 0, tiled=True, axis_index_groups=groups)
+
+
+def along_z(x, by):
+    slabs, tiles = lax.axis_size("slab"), lax.axis_size("tile")
+    half = tiles // 2
+    pairs = []
+    for z in range(2 * slabs):
+        to = (z + by) % (2 * slabs)
+        for i in range(half):
+            source = z % slabs * tiles + z // slabs * half + i
+            pairs.append((source, to % slabs * tiles + to // slabs * half + i))
+    return lax.ppermute(x, ("slab", "tile"), pairs)
 
 
 def swap_slab(x):
@@ -344,48 +401,65 @@
 def shards(transmission, probe, scan_offsets, amplitudes):
     tables = jnp.asarray(make_tables())
     index = lax.axis_index("slab").astype(jnp.int32)
-    half = lax.axis_size("tile") // 2
-    within = lax.axis_index("tile").astype(jnp.int32) % half
-    turned = (within == 0) | (within == half - 1)
-    flags = jnp.stack([index, within % 2, jnp.int32(turned)])
-    where = (flags, scan_offsets)
+    where = (index.reshape(1), scan_offsets)
+    info = jnp.where(index == 0, scan_offsets, scan_offsets[::-1]).reshape(4, 1)
+    info = jnp.broadcast_to(jnp.concatenate([info, info]), (8, HALF))
     own = transmission
     part, whole, band = (2, 2, HALO, WIDTH), (2, 2, WIDTH, WIDTH), (2, 2, HALO, COLS)
 
-    core = swap_slab(call(core_kernel, part, where, (own,), "core"))
+    core = call(
+        core_kernel,
+        part,
+        (),
+        (scan_offsets, own),
+        "core",
+        scratch=[
+            pltpu.SMEM((2, 2), jnp.int32),
+            pltpu.VMEM((4, HALO, COLS), F32),
+            pltpu.SemaphoreType.DMA((5,)),
+            pltpu.SemaphoreType.DMA((4,)),
+        ],
+        ins=(HBM, HBM),
+        outs=(HBM,),
+        vmem_limit=60,
+    )
+    core = swap_slab(core)
     beside, across = swap_tile(own, 1), swap_tile(own, 0)
     rolled = call(roll_probe_kernel, (2, WIDTH, WIDTH), where, (probe,), "roll")
     amp = call(amp_kernel, (WIDTH, WIDTH), where, (amplitudes,), "amp")
-    halo = swap_slab(call(halo_kernel, part, where, (across, beside), "halo"))
-    windows = call(window_kernel, whole, where, (own, across, beside), "window")
+    halo = swap_slab(call(halo_kernel, part, (), (info, across, beside), "halo"))
+    windows = call(window_kernel, whole, (), (info, own, across, beside), "window")
 
     tiles = (WIDTH // 8, 2, 8, HALF)
     keep, send, cores, halos = call(
         position_kernel,
         (tiles, tiles, (4, 2, HALO, WIDTH), (8 * HALO + 8, WIDTH)),
-        where,
-        (tables, rolled, amp, windows, core, halo),
+        (),
+        (info, scan_offsets, tables, rolled, amp, windows, core, halo),
         "position",
         scratch=[
             pltpu.VMEM((3, 2, WIDTH, WIDTH), F32),
             pltpu.VMEM((5, 2 * HALO, WIDTH), F32),
-            pltpu.SemaphoreType.DMA((5,)),
+            pltpu.SMEM((2, 2), jnp.int32),
+            pltpu.SemaphoreType.DMA((6,)),
         ],
+        ins=(VMEM, HBM) + (VMEM,) * 6,
         flops=3_300_000_000,
         nbytes=10_000_000,
         outs=(VMEM, VMEM, VMEM, HBM),
     )
-    sides = (cores, swap_tile(halos, 0), swap_tile(halos, 1))
-    parts = (WIDTH // 4, 8, HALF)
+    sides = (info, cores, swap_tile(halos, 0), swap_tile(halos, 1))
+    parts = (WIDTH // 16, 4, 8, HALF)
     kept = call(add_kernel, tiles, (), (keep, swap_core(send)), "add").reshape(parts)
-    kept = among_chips(kept)
-    oth_sum, spread = call(sum_kernel, (band, parts), where, sides + (kept,), "sum")
-    got = swap_slab(oth_sum)
-    kept = among_chips(spread)
+    kept = call(reduce_kernel, parts[1:], (), (among_columns(kept),), "reduce")
+    planes = (kept, along_z(kept, 1), along_z(kept, 3), along_z(kept, 2))
+    kept = call(total_kernel, parts, (), planes, "total")
+    got = swap_slab(call(sum_kernel, band, (), sides + (kept,), "sum"))
+    kept = among_columns(kept)
     object_grad, probe_grad = call(
         finish_kernel,
         (band, probe.shape),
-        where,
+        (),
         sides + (got, kept.reshape(tiles), swap_core(kept).reshape(tiles)),
         "finish",
     )

time: 91.7 us -> 88.3 us (0.963)
  blocking collectives: 37.6 us -> 26.3 us
  starting transfers between devices: 18.5 us -> 25.3 us
  waiting for transfers between devices: 18.4 us -> 22.2 us
  local copies, waits for them, and re-layouts: 1.84 us -> 0.2 us
  Pallas kernels: 14.2 us -> 13 us
    all_to_all x2, blocking collectives: 37.6 us -> 26.3 us  [among_columns(): lax.all_to_all(x, ('slab', 'tile'), 0, 0, tiled=True, axis_index_groups=g...]
    ppermute x2, starting transfers between devices: 6.56 us -> 10.6 us  [swap_core(): return lax.ppermute(x, 'tile', [(i, i ^ 1) for i in range(count)])]
    ppermute x0 -> x3, starting transfers between devices: none -> 2.86 us  [along_z(): return lax.ppermute(x, ('slab', 'tile'), pairs)]
    ppermute x0 -> x3, waiting for transfers between devices: none -> 2.85 us  [along_z(): return lax.ppermute(x, ('slab', 'tile'), pairs)]
    unnamed x14 -> x10, local copies, waits for them, and re-layouts: 1.84 us -> 0.02 us
    pallas_call x9 -> x11, Pallas kernels: 14.2 us -> 13 us  [call(): pl.pallas_call(kernel, out_shape=tuple((jax.ShapeDtypeStruct(shape, F32)...]
  transfers between devices with their start and end apart: 9 -> 12, of which waited for: 4 -> 6; matrix products, arithmetic and copies ran while one was open for 0% -> 0% of each run, Pallas kernels for 4% -> 5%
where the time goes in v5:
time: 88.3 us; the launch traced here: 87.8 us
  blocking collectives  26.3 us (30%)
  starting transfers between devices  25.3 us (29%)
  waiting for transfers between devices  22.2 us (25%)
  Pallas kernels  13 us (15%)
    all_to_all x2, blocking collectives, among_columns(): lax.all_to_all(x, ('slab', 'tile'), 0, 0, tiled=True, axis_index_groups=g...  26.3 us
    pallas_call x11, Pallas kernels, call(): pl.pallas_call(kernel, out_shape=tuple((jax.ShapeDtypeStruct(shape, F32)...  13 us
    ppermute x2, starting transfers between devices, swap_core(): return lax.ppermute(x, 'tile', [(i, i ^ 1) for i in range(count)])  10.6 us
    ppermute x3, waiting for transfers between devices, swap_slab(): return lax.ppermute(x, 'slab', [(0, 1), (1, 0)])  10.3 us
    ppermute x4, starting transfers between devices, swap_tile(): return lax.ppermute(x, ('slab', 'tile'), pairs)  8.13 us
    ppermute x4, waiting for transfers between devices, swap_tile(): return lax.ppermute(x, ('slab', 'tile'), pairs)  6.69 us
    ppermute x3, starting transfers between devices, swap_slab(): return lax.ppermute(x, 'slab', [(0, 1), (1, 0)])  3.63 us
    ppermute x3, starting transfers between devices, along_z(): return lax.ppermute(x, ('slab', 'tile'), pairs)  2.86 us
  transfers between devices with their start and end apart: 12, of which 6 were waited for; matrix products, arithmetic and copies ran while one was open for 0% of the time, Pallas kernels for 5%

profile of v5, /device:TPU:1, one launch (start us, length us, event | category | flops | bytes accessed | tf_op | source)
XLA Modules:
  0.0 87.8 jit_solution(4366683934152445823)
XLA Ops:
  0.6 0.0 copy-start.3
  0.6 1.5 %collective-permute-start.1 = (f32[2,2,128,384]{3,2,1,0:T(8,128)}, f32[2,2,128,384]{3,2,1,0:T(8,128)S(1)}, u32[]{:S(2)}, u32[]{:S(2)}) collective-permute-start(f32[2,2,128,384]{3,2,1,0:T(8,128)} %own_ref.3), channel_id=1, source_target_pairs={{0,1},{1,0},{2,3},{3,2},{4,5},{5,4},{6,7},{7,6},{8,9},{9,8},{10,11... | collective-permute-start | bytes 2359304 | tf_op jit(solution)/shard_map/ppermute | solution.py:369
  2.1 1.4 %collective-permute-start = (f32[2,2,128,384]{3,2,1,0:T(8,128)}, f32[2,2,128,384]{3,2,1,0:T(8,128)S(1)}, u32[]{:S(2)}, u32[]{:S(2)}) collective-permute-start(f32[2,2,128,384]{3,2,1,0:T(8,128)} %own_ref.3), channel_id=1, source_target_pairs={{0,127},{1,2},{2,1},{3,4},{4,3},{5,6},{6,5},{7,8},{8,7},{9,10},{10... | collective-permute-start | bytes 2359304 | tf_op jit(solution)/shard_map/ppermute | solution.py:369
  3.5 1.9 %core.1 = f32[2,2,128,256]{3,2,1,0:T(8,128)} custom-call(s32[2,2]{1,0:T(2,128)} %offsets_ref.7, f32[2,2,128,384]{3,2,1,0:T(8,128)} %own_ref.3), custom_call_target="tpu_custom_call" | custom-call | bytes 2000000 | tf_op jit(solution)/shard_map/core/pallas_call | solution.py:348
  5.5 1.7 %collective-permute-start.2 = (f32[2,2,128,256]{3,2,1,0:T(8,128)}, f32[2,2,128,256]{3,2,1,0:T(8,128)S(1)}, u32[]{:S(2)}, u32[]{:S(2)}) collective-permute-start(f32[2,2,128,256]{3,2,1,0:T(8,128)} %core.1), channel_id=1, source_target_pairs={{0,64},{64,0},{1,65},{65,1},{2,66},{66,2},{3,67},{67,3},{4,68},{68... | collective-permute-start | bytes 1572872 | tf_op jit(solution)/shard_map/ppermute | solution.py:398
  7.2 0.0 copy-done.3
  7.2 0.0 copy-start.1
  7.2 0.1 reshape.19
  7.3 0.1 add_bitcast_fusion
  7.4 0.0 collective-permute-done.1.beside_ref
  7.4 6.7 %collective-permute-done.across_ref = f32[2,2,128,384]{3,2,1,0:T(8,128)S(1)} collective-permute-done((f32[2,2,128,384]{3,2,1,0:T(8,128)}, f32[2,2,128,384]{3,2,1,0:T(8,128)S(1)}, u32[]{:S(2)}, u32[]{:S(2)}) %collective-permute-start) | collective-permute-done | bytes 786464 | tf_op jit(solution)/shard_map/ppermute | solution.py:369
  14.1 0.1 broadcast_in_dim.8.info_ref
  14.1 0.0 copy-start.2
  14.1 0.1 halo.1
  14.2 0.0 copy-start
  14.2 1.8 %collective-permute-start.3 = (f32[2,2,128,256]{3,2,1,0:T(8,128)S(1)}, f32[2,2,128,256]{3,2,1,0:T(8,128)S(1)}, u32[]{:S(2)}, u32[]{:S(2)}) collective-permute-start(f32[2,2,128,256]{3,2,1,0:T(8,128)S(1)} %halo.1), channel_id=1, source_target_pairs={{0,64},{64,0},{1,65},{65,1},{2,66},{66,2},{3,67},{67,3},{4,68},{68... | collective-permute-start | bytes 1572872 | tf_op jit(solution)/shard_map/ppermute | solution.py:398
  16.0 0.0 copy-done.1
  16.0 1.2 %amp.1.amp_ref = f32[256,256]{1,0:T(8,128)S(1)} custom-call(s32[1]{0:T(128)} %bitcast.1.place_ref, s32[2,2]{1,0:T(2,128)S(1)} %copy-done.3, f32[2,256,256]{2,1,0:T(8,128)S(1)} %copy-done.1), custom_call_target="tpu_custom_call" | custom-call | bytes 2000000 | tf_op jit(solution)/shard_map/amp/pallas_call | solution.py:348
  17.2 0.0 copy-done.2
  17.2 0.8 roll.1.probe_ref
  18.0 0.0 copy-done
  18.0 0.0 copy-start.4
  18.0 0.1 window.1.own_ref
  18.2 0.0 collective-permute-done.2.core_ref
  18.2 10.3 %collective-permute-done.3.halo_ref = f32[2,2,128,256]{3,2,1,0:T(8,128)S(1)} collective-permute-done((f32[2,2,128,256]{3,2,1,0:T(8,128)S(1)}, f32[2,2,128,256]{3,2,1,0:T(8,128)S(1)}, u32[]{:S(2)}, u32[]{:S(2)}) %collective-permute-start.3) | collective-permute-done | bytes 524320 | tf_op jit(solution)/shard_map/ppermute | solution.py:398
  28.5 0.0 copy-done.4
  28.5 7.3 %position.1 = (f32[32,2,8,128]{3,2,1,0:T(8,128)S(1)}, f32[32,2,8,128]{3,2,1,0:T(8,128)S(1)}, f32[4,2,128,256]{3,2,1,0:T(8,128)S(1)}, f32[1032,256]{1,0:T(8,128)S(1)}) custom-call(s32[8,128]{1,0:T(8,128)S(1)} %broadcast_in_dim.8.info_ref, s32[2,2]{1,0:T(2,128)S(1)} %copy-done.3, bf16[6,2,2,256,256]{4,3,2,1,0:T(8,128)(2,1)S(1)} %copy-done.4, ...), custom_call_target="tpu_custom_call" | custom-call | flops 3300000000 | bytes 10000000 | tf_op jit(solution)/shard_map/position/pallas_call | solution.py:348
  35.8 5.3 %collective-permute-start.5 = (f32[1032,256]{1,0:T(8,128)S(1)}, f32[1032,256]{1,0:T(8,128)S(1)}, u32[]{:S(2)}, u32[]{:S(2)}) collective-permute-start(f32[1032,256]{1,0:T(8,128)S(1)} %get-tuple-element.7), channel_id=1, source_target_pairs={{0,1},{1,0},{2,3},{3,2},{4,5},{5,4},{6,7},{7,6},{8,9},{9,8},{10,11... | collective-permute-start | bytes 3170312 | tf_op jit(solution)/shard_map/ppermute | solution.py:369
  41.1 0.0 collective-permute-start.4
  41.1 4.6 %collective-permute-start.6 = (f32[32,2,8,128]{3,2,1,0:T(8,128)S(1)}, f32[32,2,8,128]{3,2,1,0:T(8,128)S(1)}, u32[]{:S(2)}, u32[]{:S(2)}) collective-permute-start(f32[32,2,8,128]{3,2,1,0:T(8,128)S(1)} %get-tuple-element.9), channel_id=1, source_target_pairs={{0,1},{1,0},{2,3},{3,2},{4,5},{5,4},{6,7},{7,6},{8,9},{9,8},{10,11... | collective-permute-start | bytes 786440 | tf_op jit(solution)/shard_map/ppermute | solution.py:374
  45.7 1.2 %collective-permute-done.6.got_ref = f32[32,2,8,128]{3,2,1,0:T(8,128)S(1)} collective-permute-done((f32[32,2,8,128]{3,2,1,0:T(8,128)S(1)}, f32[32,2,8,128]{3,2,1,0:T(8,128)S(1)}, u32[]{:S(2)}, u32[]{:S(2)}) %collective-permute-start.6) | collective-permute-done | bytes 262176 | tf_op jit(solution)/shard_map/ppermute | solution.py:374
  46.9 15.4 %all_to_all.10.parts_ref = f32[16,4,8,128]{3,2,1,0:T(8,128)S(1)} all-to-all(f32[16,4,8,128]{3,2,1,0:T(8,128)S(1)} %bitcast.7), channel_id=1, replica_groups={{0,2,4,6,8,10,12,14,16,18,20,22,24,26,28,30},{1,3,5,7,9,11,13,15,17,19,..., dimensions={0} | all-to-all | bytes 524288 | tf_op jit(solution)/shard_map/all_to_all | solution.py:382
  62.3 1.4 %collective-permute-start.9 = (f32[4,8,128]{2,1,0:T(8,128)S(1)}, f32[4,8,128]{2,1,0:T(8,128)S(1)}, u32[]{:S(2)}, u32[]{:S(2)}) collective-permute-start(f32[4,8,128]{2,1,0:T(8,128)S(1)} %reduce.1.first_ref), channel_id=1, source_target_pairs={{0,32},{1,33},{2,34},{3,35},{4,36},{5,37},{6,38},{7,39},{8,40},{9,... | collective-permute-start | bytes 49160 | tf_op jit(solution)/shard_map/ppermute | solution.py:394
  63.7 0.5 collective-permute-start.8
  64.2 0.9 %collective-permute-start.7 = (f32[4,8,128]{2,1,0:T(8,128)S(1)}, f32[4,8,128]{2,1,0:T(8,128)S(1)}, u32[]{:S(2)}, u32[]{:S(2)}) collective-permute-start(f32[4,8,128]{2,1,0:T(8,128)S(1)} %reduce.1.first_ref), channel_id=1, source_target_pairs={{0,64},{1,65},{2,66},{3,67},{4,68},{5,69},{6,70},{7,71},{8,72},{9,... | collective-permute-start | bytes 49160 | tf_op jit(solution)/shard_map/ppermute | solution.py:394
  65.1 1.3 %collective-permute-done.9.fourth_ref = f32[4,8,128]{2,1,0:T(8,128)S(1)} collective-permute-done((f32[4,8,128]{2,1,0:T(8,128)S(1)}, f32[4,8,128]{2,1,0:T(8,128)S(1)}, u32[]{:S(2)}, u32[]{:S(2)}) %collective-permute-start.9) | collective-permute-done | bytes 16416 | tf_op jit(solution)/shard_map/ppermute | solution.py:394
  66.5 0.0 collective-permute-done.8.third_ref
  66.5 1.5 %collective-permute-done.7.second_ref = f32[4,8,128]{2,1,0:T(8,128)S(1)} collective-permute-done((f32[4,8,128]{2,1,0:T(8,128)S(1)}, f32[4,8,128]{2,1,0:T(8,128)S(1)}, u32[]{:S(2)}, u32[]{:S(2)}) %collective-permute-start.7) | collective-permute-done | bytes 16416 | tf_op jit(solution)/shard_map/ppermute | solution.py:394
  68.0 0.0 collective-permute-done.5.beside_ref
  68.0 0.0 collective-permute-done.4.across_ref
  68.0 0.2 sum.1
  68.3 0.1 collective-permute-start.10
  68.4 10.9 %all_to_all.11 = f32[16,4,8,128]{3,2,1,0:T(8,128)S(1)} all-to-all(f32[16,4,8,128]{3,2,1,0:T(8,128)S(1)} %total.1.after_ref), channel_id=1, replica_groups={{0,2,4,6,8,10,12,14,16,18,20,22,24,26,28,30},{1,3,5,7,9,11,13,15,17,19,..., dimensions={0} | all-to-all | bytes 524288 | tf_op jit(solution)/shard_map/all_to_all | solution.py:382
  79.3 6.1 %collective-permute-start.11 = (f32[16,4,8,128]{3,2,1,0:T(8,128)S(1)}, f32[16,4,8,128]{3,2,1,0:T(8,128)S(1)}, u32[]{:S(2)}, u32[]{:S(2)}) collective-permute-start(f32[16,4,8,128]{3,2,1,0:T(8,128)S(1)} %all_to_all.11), channel_id=1, source_target_pairs={{0,1},{1,0},{2,3},{3,2},{4,5},{5,4},{6,7},{7,6},{8,9},{9,8},{10,11... | collective-permute-start | bytes 786440 | tf_op jit(solution)/shard_map/ppermute | solution.py:374
  85.4 1.2 %collective-permute-done.11 = f32[16,4,8,128]{3,2,1,0:T(8,128)S(1)} collective-permute-done((f32[16,4,8,128]{3,2,1,0:T(8,128)S(1)}, f32[16,4,8,128]{3,2,1,0:T(8,128)S(1)}, u32[]{:S(2)}, u32[]{:S(2)}) %collective-permute-start.11) | collective-permute-done | bytes 262176 | tf_op jit(solution)/shard_map/ppermute | solution.py:374
  86.6 0.0 collective-permute-done.10.swapped_ref
  86.6 1.3 %finish.1 = (f32[2,2,128,384]{3,2,1,0:T(8,128)}, f32[2,256,256]{2,1,0:T(8,128)}) custom-call(s32[8,128]{1,0:T(8,128)S(1)} %broadcast_in_dim.8.info_ref, f32[4,2,128,256]{3,2,1,0:T(8,128)S(1)} %get-tuple-element.6.core_ref, f32[1032,256]{1,0:T(8,128)S(1)} %collective-permute-done.4.across_ref, f32[1032,256]{1,0:T(8,128)S(1)} %collective-permute-done.5.beside_ref, ...), custom_call_target="tpu_custom_call" | custom-call | bytes 2000000 | tf_op jit(solution)/shard_map/finish/pallas_call | solution.py:348
  (5 shorter events, 0.1 us)
Async XLA Ops:
  0.6 6.5 %copy-start.3 = (s32[2,2]{1,0:T(2,128)S(1)}, s32[2,2]{1,0:T(2,128)}, u32[]{:S(2)}) copy-start(s32[2,2]{1,0:T(2,128)} %offsets_ref.7) | copy-start | bytes 52
  0.6 6.7 %collective-permute-start.1 = (f32[2,2,128,384]{3,2,1,0:T(8,128)}, f32[2,2,128,384]{3,2,1,0:T(8,128)S(1)}, u32[]{:S(2)}, u32[]{:S(2)}) collective-permute-start(f32[2,2,128,384]{3,2,1,0:T(8,128)} %own_ref.3), channel_id=1, source_target_pairs={{0,1},{1,0},{2,3},{3,2},{4,5},{5,4},{6,7},{7,6},{8,9},{9,8},{10,11... | collective-permute-start | bytes 2359304 | tf_op jit(solution)/shard_map/ppermute | solution.py:369
  2.1 11.9 %collective-permute-start = (f32[2,2,128,384]{3,2,1,0:T(8,128)}, f32[2,2,128,384]{3,2,1,0:T(8,128)S(1)}, u32[]{:S(2)}, u32[]{:S(2)}) collective-permute-start(f32[2,2,128,384]{3,2,1,0:T(8,128)} %own_ref.3), channel_id=1, source_target_pairs={{0,127},{1,2},{2,1},{3,4},{4,3},{5,6},{6,5},{7,8},{8,7},{9,10},{10... | collective-permute-start | bytes 2359304 | tf_op jit(solution)/shard_map/ppermute | solution.py:369
  5.5 12.7 %collective-permute-start.2 = (f32[2,2,128,256]{3,2,1,0:T(8,128)}, f32[2,2,128,256]{3,2,1,0:T(8,128)S(1)}, u32[]{:S(2)}, u32[]{:S(2)}) collective-permute-start(f32[2,2,128,256]{3,2,1,0:T(8,128)} %core.1), channel_id=1, source_target_pairs={{0,64},{64,0},{1,65},{65,1},{2,66},{66,2},{3,67},{67,3},{4,68},{68... | collective-permute-start | bytes 1572872 | tf_op jit(solution)/shard_map/ppermute | solution.py:398
  7.2 8.8 %copy-start.1 = (f32[2,256,256]{2,1,0:T(8,128)S(1)}, f32[2,256,256]{2,1,0:T(8,128)}, u32[]{:S(2)}) copy-start(f32[2,256,256]{2,1,0:T(8,128)} %amp_ref.1) | copy-start | bytes 1572868
  14.1 3.1 %copy-start.2 = (f32[2,256,256]{2,1,0:T(8,128)S(1)}, f32[2,256,256]{2,1,0:T(8,128)}, u32[]{:S(2)}) copy-start(f32[2,256,256]{2,1,0:T(8,128)} %probe_ref.1) | copy-start | bytes 1572868
  14.2 3.8 %copy-start = (f32[2,2,128,384]{3,2,1,0:T(8,128)S(1)}, f32[2,2,128,384]{3,2,1,0:T(8,128)}, u32[]{:S(2)}) copy-start(f32[2,2,128,384]{3,2,1,0:T(8,128)} %own_ref.3) | copy-start | bytes 2359300
  14.2 14.3 %collective-permute-start.3 = (f32[2,2,128,256]{3,2,1,0:T(8,128)S(1)}, f32[2,2,128,256]{3,2,1,0:T(8,128)S(1)}, u32[]{:S(2)}, u32[]{:S(2)}) collective-permute-start(f32[2,2,128,256]{3,2,1,0:T(8,128)S(1)} %halo.1), channel_id=1, source_target_pairs={{0,64},{64,0},{1,65},{65,1},{2,66},{66,2},{3,67},{67,3},{4,68},{68... | collective-permute-start | bytes 1572872 | tf_op jit(solution)/shard_map/ppermute | solution.py:398
  18.0 10.5 %copy-start.4 = (bf16[6,2,2,256,256]{4,3,2,1,0:T(8,128)(2,1)S(1)}, bf16[6,2,2,256,256]{4,3,2,1,0:T(8,128)(2,1)}, u32[]{:S(2)}) copy-start(bf16[6,2,2,256,256]{4,3,2,1,0:T(8,128)(2,1)} %constant.10.clone.tables_ref) | copy-start | bytes 9437188
  35.8 32.2 %collective-permute-start.5 = (f32[1032,256]{1,0:T(8,128)S(1)}, f32[1032,256]{1,0:T(8,128)S(1)}, u32[]{:S(2)}, u32[]{:S(2)}) collective-permute-start(f32[1032,256]{1,0:T(8,128)S(1)} %get-tuple-element.7), channel_id=1, source_target_pairs={{0,1},{1,0},{2,3},{3,2},{4,5},{5,4},{6,7},{7,6},{8,9},{9,8},{10,11... | collective-permute-start | bytes 3170312 | tf_op jit(solution)/shard_map/ppermute | solution.py:369
  41.1 26.9 %collective-permute-start.4 = (f32[1032,256]{1,0:T(8,128)S(1)}, f32[1032,256]{1,0:T(8,128)S(1)}, u32[]{:S(2)}, u32[]{:S(2)}) collective-permute-start(f32[1032,256]{1,0:T(8,128)S(1)} %get-tuple-element.7), channel_id=1, source_target_pairs={{0,127},{1,2},{2,1},{3,4},{4,3},{5,6},{6,5},{7,8},{8,7},{9,10},{10... | collective-permute-start | bytes 3170312 | tf_op jit(solution)/shard_map/ppermute | solution.py:369
  41.1 5.7 %collective-permute-start.6 = (f32[32,2,8,128]{3,2,1,0:T(8,128)S(1)}, f32[32,2,8,128]{3,2,1,0:T(8,128)S(1)}, u32[]{:S(2)}, u32[]{:S(2)}) collective-permute-start(f32[32,2,8,128]{3,2,1,0:T(8,128)S(1)} %get-tuple-element.9), channel_id=1, source_target_pairs={{0,1},{1,0},{2,3},{3,2},{4,5},{5,4},{6,7},{7,6},{8,9},{9,8},{10,11... | collective-permute-start | bytes 786440 | tf_op jit(solution)/shard_map/ppermute | solution.py:374
  62.3 4.2 %collective-permute-start.9 = (f32[4,8,128]{2,1,0:T(8,128)S(1)}, f32[4,8,128]{2,1,0:T(8,128)S(1)}, u32[]{:S(2)}, u32[]{:S(2)}) collective-permute-start(f32[4,8,128]{2,1,0:T(8,128)S(1)} %reduce.1.first_ref), channel_id=1, source_target_pairs={{0,32},{1,33},{2,34},{3,35},{4,36},{5,37},{6,38},{7,39},{8,40},{9,... | collective-permute-start | bytes 49160 | tf_op jit(solution)/shard_map/ppermute | solution.py:394
  63.7 2.8 %collective-permute-start.8 = (f32[4,8,128]{2,1,0:T(8,128)S(1)}, f32[4,8,128]{2,1,0:T(8,128)S(1)}, u32[]{:S(2)}, u32[]{:S(2)}) collective-permute-start(f32[4,8,128]{2,1,0:T(8,128)S(1)} %reduce.1.first_ref), channel_id=1, source_target_pairs={{0,96},{1,97},{2,98},{3,99},{4,100},{5,101},{6,102},{7,103},{8,104... | collective-permute-start | bytes 49160 | tf_op jit(solution)/shard_map/ppermute | solution.py:394
  64.2 3.8 %collective-permute-start.7 = (f32[4,8,128]{2,1,0:T(8,128)S(1)}, f32[4,8,128]{2,1,0:T(8,128)S(1)}, u32[]{:S(2)}, u32[]{:S(2)}) collective-permute-start(f32[4,8,128]{2,1,0:T(8,128)S(1)} %reduce.1.first_ref), channel_id=1, source_target_pairs={{0,64},{1,65},{2,66},{3,67},{4,68},{5,69},{6,70},{7,71},{8,72},{9,... | collective-permute-start | bytes 49160 | tf_op jit(solution)/shard_map/ppermute | solution.py:394
  68.3 18.3 %collective-permute-start.10 = (f32[2,2,128,384]{3,2,1,0:T(8,128)S(1)}, f32[2,2,128,384]{3,2,1,0:T(8,128)S(1)}, u32[]{:S(2)}, u32[]{:S(2)}) collective-permute-start(f32[2,2,128,384]{3,2,1,0:T(8,128)S(1)} %sum.1), channel_id=1, source_target_pairs={{0,64},{64,0},{1,65},{65,1},{2,66},{66,2},{3,67},{67,3},{4,68},{68... | collective-permute-start | bytes 2359304 | tf_op jit(solution)/shard_map/ppermute | solution.py:398
  79.3 7.2 %collective-permute-start.11 = (f32[16,4,8,128]{3,2,1,0:T(8,128)S(1)}, f32[16,4,8,128]{3,2,1,0:T(8,128)S(1)}, u32[]{:S(2)}, u32[]{:S(2)}) collective-permute-start(f32[16,4,8,128]{3,2,1,0:T(8,128)S(1)} %all_to_all.11), channel_id=1, source_target_pairs={{0,1},{1,0},{2,3},{3,2},{4,5},{5,4},{6,7},{7,6},{8,9},{9,8},{10,11... | collective-permute-start | bytes 786440 | tf_op jit(solution)/shard_map/ppermute | solution.py:374

commit v6 on v5

--- a/solution.py
+++ b/solution.py
@@ -210,16 +210,19 @@
     keep_out,
     send_out,
     core_out,
-    halo_out,
+    beside_out,
+    early_out,
+    late_out,
     waves,
     halos,
     offsets,
     sems,
 ):
     place, odd, turned = here()
-    load = pltpu.make_async_copy(offsets_ref, offsets, sems.at[5])
+    load = pltpu.make_async_copy(offsets_ref, offsets, sems.at[0, 5])
     load.start()
     from_beside = masks(info_ref, 0)[0]
+    across_turned = turned
     turned = jnp.where(jnp.concatenate([from_beside, from_beside], axis=1), 0, turned)
 
     def window_of(s):
@@ -256,17 +259,28 @@
             core_out[slot, c] = value[HALO:]
             halos[slot, pl.ds(c * HALO, HALO)] = value[:HALO]
         start = pl.multiple_of(slot * 2 * HALO, HALO)
-        copy = pltpu.make_async_copy(halos.at[slot], halo_out.at[pl.ds(start, 2 * HALO)], sems.at[s])
+        copy = pltpu.make_async_copy(halos.at[slot], beside_out.at[pl.ds(start, 2 * HALO)], sems.at[0, s])
         copy.start()
+        copies.append(copy)
+        start = pl.multiple_of(s % 2 * 2 * HALO, HALO)
+        early = jnp.where(slot // 2 == 1, 1, 0) != across_turned
+        for which, ref in enumerate((late_out, early_out)):
+            copy = pltpu.make_async_copy(halos.at[slot], ref.at[pl.ds(start, 2 * HALO)], sems.at[1, s])
+
+            @pl.when(early == (which == 1))
+            def _():
+                copy.start()
+
         copies.append(copy)
         grad = times(window_of(s), grad)
         if s > 0:
             grad = propagate(grad, tables_ref)
     meta = info_ref[...].astype(F32)
     halos[4, :8] = jnp.concatenate([meta, meta], axis=1)
-    copy = pltpu.make_async_copy(halos.at[4, :8], halo_out.at[8 * HALO :], sems.at[4])
-    copy.start()
-    copies.append(copy)
+    for i, (ref, start) in enumerate(((beside_out, 8 * HALO), (early_out, 4 * HALO))):
+        copy = pltpu.make_async_copy(halos.at[4, :8], ref.at[pl.ds(start, 8)], sems.at[i, 4])
+        copy.start()
+        copies.append(copy)
     load.wait()
     row, col = offsets[place, 0], offsets[place, 1]
     value = [grad[0], -grad[1]]
@@ -286,24 +300,25 @@
     return jnp.concatenate([jnp.where(kept, left, 0.0), right, jnp.where(kept, 0.0, left)], axis=-1)
 
 
-def add_halos(info_ref, core_ref, across_ref, beside_ref, out_ref, first, extra=None):
-    _, odd, turned = here()
+def add_halos(info_ref, core_ref, across_ref, early_ref, beside_ref, out_ref, first, extra=None):
+    odd = here()[1]
     own_kept = masks(info_ref, 0)[1]
     line = lax.broadcasted_iota(jnp.int32, (HALO, WIDTH), 0).astype(F32)
     column = lax.broadcasted_iota(jnp.int32, (HALO, HALF), 1).astype(F32)
     sides = []
-    for ref, after, shift in ((across_ref, odd, turned), (beside_ref, 1 - odd, 0)):
-        base = pl.multiple_of(((first + 2 * shift) % 4) * 2 * HALO, HALO)
-        row = ref[8 * HALO : 8 * HALO + 1]
-        kept = column >= ref[8 * HALO + 1 : 8 * HALO + 2, :HALF]
-        mask = jnp.where(line >= row, 1, 0) == after
+    for ref, base, meta, after in (
+        (across_ref, 0, early_ref[4 * HALO :], odd),
+        (beside_ref, first * 2 * HALO, beside_ref[8 * HALO :], 1 - odd),
+    ):
+        kept = column >= meta[1:2, :HALF]
+        mask = jnp.where(line >= meta[0:1], 1, 0) == after
         sides.append((ref, base, mask, kept))
     for j in range(2):
         for c in range(2):
             total = widen(core_ref[first + j, c], own_kept)
             for ref, base, mask, kept in sides:
-                part = jnp.where(mask, ref[pl.ds(base + (j * 2 + c) * HALO, HALO)], 0.0)
-                total = total + widen(part, kept)
+                start = base + (j * 2 + c) * HALO
+                total = total + widen(jnp.where(mask, ref[start : start + HALO], 0.0), kept)
             out_ref[j, c] = total if extra is None else total + extra[j, c]
 
 
@@ -320,22 +335,23 @@
     out_ref[...] = jnp.broadcast_to(total[None], out_ref.shape)
 
 
-def sum_kernel(info_ref, core_ref, across_ref, beside_ref, after_ref, out_ref):
-    add_halos(info_ref, core_ref, across_ref, beside_ref, out_ref, 2)
+def sum_kernel(info_ref, core_ref, early_ref, beside_ref, after_ref, out_ref):
+    add_halos(info_ref, core_ref, early_ref, early_ref, beside_ref, out_ref, 2)
 
 
 def finish_kernel(
     info_ref,
     core_ref,
-    across_ref,
+    early_ref,
     beside_ref,
+    late_ref,
     swapped_ref,
     keep_ref,
     got_ref,
     object_out,
     probe_out,
 ):
-    add_halos(info_ref, core_ref, across_ref, beside_ref, object_out, 0, swapped_ref)
+    add_halos(info_ref, core_ref, late_ref, early_ref, beside_ref, object_out, 0, swapped_ref)
     odd = here()[1]
     for ref, which in ((keep_ref, odd), (got_ref, 1 - odd)):
         for h in range(2):
@@ -431,9 +447,9 @@
     windows = call(window_kernel, whole, (), (info, own, across, beside), "window")
 
     tiles = (WIDTH // 8, 2, 8, HALF)
-    keep, send, cores, halos = call(
+    keep, send, cores, beside, early, late = call(
         position_kernel,
-        (tiles, tiles, (4, 2, HALO, WIDTH), (8 * HALO + 8, WIDTH)),
+        (tiles, tiles, (4, 2, HALO, WIDTH), (8 * HALO + 8, WIDTH), (4 * HALO + 8, WIDTH), (4 * HALO, WIDTH)),
         (),
         (info, scan_offsets, tables, rolled, amp, windows, core, halo),
         "position",
@@ -441,17 +457,19 @@
             pltpu.VMEM((3, 2, WIDTH, WIDTH), F32),
             pltpu.VMEM((5, 2 * HALO, WIDTH), F32),
             pltpu.SMEM((2, 2), jnp.int32),
-            pltpu.SemaphoreType.DMA((6,)),
+            pltpu.SemaphoreType.DMA((2, 6)),
         ],
         ins=(VMEM, HBM) + (VMEM,) * 6,
         flops=3_300_000_000,
         nbytes=10_000_000,
-        outs=(VMEM, VMEM, VMEM, HBM),
+        outs=(VMEM, VMEM, VMEM, HBM, HBM, HBM),
     )
-    sides = (info, cores, swap_tile(halos, 0), swap_tile(halos, 1))
+    sides = (info, cores, swap_tile(early, 0), swap_tile(beside, 1))
     parts = (WIDTH // 16, 4, 8, HALF)
     kept = call(add_kernel, tiles, (), (keep, swap_core(send)), "add").reshape(parts)
     kept = call(reduce_kernel, parts[1:], (), (among_columns(kept),), "reduce")
+    late, kept = lax.optimization_barrier((late, kept))
+    late = swap_tile(late, 0)
     planes = (kept, along_z(kept, 1), along_z(kept, 3), along_z(kept, 2))
     kept = call(total_kernel, parts, (), planes, "total")
     got = swap_slab(call(sum_kernel, band, (), sides + (kept,), "sum"))
@@ -460,7 +478,7 @@
         finish_kernel,
         (band, probe.shape),
         (),
-        sides + (got, kept.reshape(tiles), swap_core(kept).reshape(tiles)),
+        sides + (late, got, kept.reshape(tiles), swap_core(kept).reshape(tiles)),
         "finish",
     )
     return object_grad, probe_grad

time: 88.3 us -> 85.7 us (0.971)
  starting transfers between devices: 25.3 us -> 23.3 us
    ppermute x2, starting transfers between devices: 10.6 us -> 4.86 us  [swap_core(): return lax.ppermute(x, 'tile', [(i, i ^ 1) for i in range(count)])]
    ppermute x4 -> x5, starting transfers between devices: 8.13 us -> 11.8 us  [swap_tile(): return lax.ppermute(x, ('slab', 'tile'), pairs)]
    ppermute x4 -> x5, waiting for transfers between devices: 6.69 us -> 6.69 us  [swap_tile(): return lax.ppermute(x, ('slab', 'tile'), pairs)]
  transfers between devices with their start and end apart: 12 -> 13, of which waited for: 6 -> 6; matrix products, arithmetic and copies ran while one was open for 0% -> 0% of each run, Pallas kernels for 5% -> 5%
where the time goes in v6:
time: 85.7 us; the launch traced here: 85.5 us
  blocking collectives  26 us (30%)
  starting transfers between devices  23.3 us (27%)
  waiting for transfers between devices  22.2 us (26%)
  Pallas kernels  13 us (15%)
    all_to_all x2, blocking collectives, among_columns(): lax.all_to_all(x, ('slab', 'tile'), 0, 0, tiled=True, axis_index_groups=g...  26 us
    pallas_call x11, Pallas kernels, call(): pl.pallas_call(kernel, out_shape=tuple((jax.ShapeDtypeStruct(shape, F32)...  13 us
    ppermute x5, starting transfers between devices, swap_tile(): return lax.ppermute(x, ('slab', 'tile'), pairs)  11.8 us
    ppermute x3, waiting for transfers between devices, swap_slab(): return lax.ppermute(x, 'slab', [(0, 1), (1, 0)])  10.3 us
    ppermute x5, waiting for transfers between devices, swap_tile(): return lax.ppermute(x, ('slab', 'tile'), pairs)  6.69 us
    ppermute x2, starting transfers between devices, swap_core(): return lax.ppermute(x, 'tile', [(i, i ^ 1) for i in range(count)])  4.86 us
    ppermute x3, starting transfers between devices, swap_slab(): return lax.ppermute(x, 'slab', [(0, 1), (1, 0)])  3.72 us
    ppermute x3, starting transfers between devices, along_z(): return lax.ppermute(x, ('slab', 'tile'), pairs)  2.9 us
  transfers between devices with their start and end apart: 13, of which 6 were waited for; matrix products, arithmetic and copies ran while one was open for 0% of the time, Pallas kernels for 5%

profile of v6, /device:TPU:1, one launch (start us, length us, event | category | flops | bytes accessed | tf_op | source)
XLA Modules:
  0.0 85.5 jit_solution(13089964527418570091)
XLA Ops:
  0.6 0.0 copy-start.3
  0.6 1.5 %collective-permute-start.1 = (f32[2,2,128,384]{3,2,1,0:T(8,128)}, f32[2,2,128,384]{3,2,1,0:T(8,128)S(1)}, u32[]{:S(2)}, u32[]{:S(2)}) collective-permute-start(f32[2,2,128,384]{3,2,1,0:T(8,128)} %own_ref.3), channel_id=1, source_target_pairs={{0,1},{1,0},{2,3},{3,2},{4,5},{5,4},{6,7},{7,6},{8,9},{9,8},{10,11... | collective-permute-start | bytes 2359304 | tf_op jit(solution)/shard_map/ppermute | solution.py:385
  2.1 1.4 %collective-permute-start = (f32[2,2,128,384]{3,2,1,0:T(8,128)}, f32[2,2,128,384]{3,2,1,0:T(8,128)S(1)}, u32[]{:S(2)}, u32[]{:S(2)}) collective-permute-start(f32[2,2,128,384]{3,2,1,0:T(8,128)} %own_ref.3), channel_id=1, source_target_pairs={{0,127},{1,2},{2,1},{3,4},{4,3},{5,6},{6,5},{7,8},{8,7},{9,10},{10... | collective-permute-start | bytes 2359304 | tf_op jit(solution)/shard_map/ppermute | solution.py:385
  3.5 1.9 %core.1 = f32[2,2,128,256]{3,2,1,0:T(8,128)} custom-call(s32[2,2]{1,0:T(2,128)} %offsets_ref.7, f32[2,2,128,384]{3,2,1,0:T(8,128)} %own_ref.3), custom_call_target="tpu_custom_call" | custom-call | bytes 2000000 | tf_op jit(solution)/shard_map/core/pallas_call | solution.py:364
  5.5 1.7 %collective-permute-start.2 = (f32[2,2,128,256]{3,2,1,0:T(8,128)}, f32[2,2,128,256]{3,2,1,0:T(8,128)S(1)}, u32[]{:S(2)}, u32[]{:S(2)}) collective-permute-start(f32[2,2,128,256]{3,2,1,0:T(8,128)} %core.1), channel_id=1, source_target_pairs={{0,64},{64,0},{1,65},{65,1},{2,66},{66,2},{3,67},{67,3},{4,68},{68... | collective-permute-start | bytes 1572872 | tf_op jit(solution)/shard_map/ppermute | solution.py:414
  7.2 0.0 copy-done.3
  7.2 0.0 copy-start.1
  7.2 0.1 reshape.19
  7.3 0.1 add_bitcast_fusion
  7.4 0.0 collective-permute-done.1.beside_ref
  7.4 6.7 %collective-permute-done.across_ref = f32[2,2,128,384]{3,2,1,0:T(8,128)S(1)} collective-permute-done((f32[2,2,128,384]{3,2,1,0:T(8,128)}, f32[2,2,128,384]{3,2,1,0:T(8,128)S(1)}, u32[]{:S(2)}, u32[]{:S(2)}) %collective-permute-start) | collective-permute-done | bytes 786464 | tf_op jit(solution)/shard_map/ppermute | solution.py:385
  14.1 0.1 broadcast_in_dim.8.info_ref
  14.1 0.0 copy-start.2
  14.1 0.1 halo.1
  14.2 0.0 copy-start
  14.2 1.8 %collective-permute-start.3 = (f32[2,2,128,256]{3,2,1,0:T(8,128)S(1)}, f32[2,2,128,256]{3,2,1,0:T(8,128)S(1)}, u32[]{:S(2)}, u32[]{:S(2)}) collective-permute-start(f32[2,2,128,256]{3,2,1,0:T(8,128)S(1)} %halo.1), channel_id=1, source_target_pairs={{0,64},{64,0},{1,65},{65,1},{2,66},{66,2},{3,67},{67,3},{4,68},{68... | collective-permute-start | bytes 1572872 | tf_op jit(solution)/shard_map/ppermute | solution.py:414
  16.0 0.0 copy-done.1
  16.0 1.2 %amp.1.amp_ref = f32[256,256]{1,0:T(8,128)S(1)} custom-call(s32[1]{0:T(128)} %bitcast.1.place_ref, s32[2,2]{1,0:T(2,128)S(1)} %copy-done.3, f32[2,256,256]{2,1,0:T(8,128)S(1)} %copy-done.1), custom_call_target="tpu_custom_call" | custom-call | bytes 2000000 | tf_op jit(solution)/shard_map/amp/pallas_call | solution.py:364
  17.2 0.0 copy-done.2
  17.2 0.8 roll.1.probe_ref
  18.0 0.0 copy-done
  18.0 0.0 copy-start.4
  18.0 0.1 window.1.own_ref
  18.2 0.0 collective-permute-done.2.core_ref
  18.2 10.3 %collective-permute-done.3.halo_ref = f32[2,2,128,256]{3,2,1,0:T(8,128)S(1)} collective-permute-done((f32[2,2,128,256]{3,2,1,0:T(8,128)S(1)}, f32[2,2,128,256]{3,2,1,0:T(8,128)S(1)}, u32[]{:S(2)}, u32[]{:S(2)}) %collective-permute-start.3) | collective-permute-done | bytes 524320 | tf_op jit(solution)/shard_map/ppermute | solution.py:414
  28.5 0.0 copy-done.4
  28.5 7.4 %position.1 = (f32[32,2,8,128]{3,2,1,0:T(8,128)S(1)}, f32[32,2,8,128]{3,2,1,0:T(8,128)S(1)}, f32[4,2,128,256]{3,2,1,0:T(8,128)S(1)}, f32[1032,256]{1,0:T(8,128)S...) custom-call(s32[8,128]{1,0:T(8,128)S(1)} %broadcast_in_dim.8.info_ref, s32[2,2]{1,0:T(2,128)S(1)} %copy-done.3, ...), custom_call_target="tpu_custom_call" | custom-call | flops 3300000000 | bytes 10000000 | tf_op jit(solution)/shard_map/position/pallas_call | solution.py:364
  35.9 5.3 %collective-permute-start.5 = (f32[1032,256]{1,0:T(8,128)S(1)}, f32[1032,256]{1,0:T(8,128)S(1)}, u32[]{:S(2)}, u32[]{:S(2)}) collective-permute-start(f32[1032,256]{1,0:T(8,128)S(1)} %get-tuple-element.12), channel_id=1, source_target_pairs={{0,1},{1,0},{2,3},{3,2},{4,5},{5,4},{6,7},{7,6},{8,9},{9,8},{10,11... | collective-permute-start | bytes 3170312 | tf_op jit(solution)/shard_map/ppermute | solution.py:385
  41.2 0.0 collective-permute-start.4
  41.2 4.6 %collective-permute-start.6 = (f32[32,2,8,128]{3,2,1,0:T(8,128)S(1)}, f32[32,2,8,128]{3,2,1,0:T(8,128)S(1)}, u32[]{:S(2)}, u32[]{:S(2)}) collective-permute-start(f32[32,2,8,128]{3,2,1,0:T(8,128)S(1)} %get-tuple-element.15), channel_id=1, source_target_pairs={{0,1},{1,0},{2,3},{3,2},{4,5},{5,4},{6,7},{7,6},{8,9},{9,8},{10,11... | collective-permute-start | bytes 786440 | tf_op jit(solution)/shard_map/ppermute | solution.py:390
  45.8 1.2 %collective-permute-done.6.got_ref = f32[32,2,8,128]{3,2,1,0:T(8,128)S(1)} collective-permute-done((f32[32,2,8,128]{3,2,1,0:T(8,128)S(1)}, f32[32,2,8,128]{3,2,1,0:T(8,128)S(1)}, u32[]{:S(2)}, u32[]{:S(2)}) %collective-permute-start.6) | collective-permute-done | bytes 262176 | tf_op jit(solution)/shard_map/ppermute | solution.py:390
  46.9 10.6 %all_to_all.10.parts_ref = f32[16,4,8,128]{3,2,1,0:T(8,128)S(1)} all-to-all(f32[16,4,8,128]{3,2,1,0:T(8,128)S(1)} %bitcast.7), channel_id=1, replica_groups={{0,2,4,6,8,10,12,14,16,18,20,22,24,26,28,30},{1,3,5,7,9,11,13,15,17,19,..., dimensions={0} | all-to-all | bytes 524288 | tf_op jit(solution)/shard_map/all_to_all | solution.py:398
  57.6 1.4 %collective-permute-start.10 = (f32[4,8,128]{2,1,0:T(8,128)S(1)}, f32[4,8,128]{2,1,0:T(8,128)S(1)}, u32[]{:S(2)}, u32[]{:S(2)}) collective-permute-start(f32[4,8,128]{2,1,0:T(8,128)S(1)} %reduce.1.first_ref), channel_id=1, source_target_pairs={{0,32},{1,33},{2,34},{3,35},{4,36},{5,37},{6,38},{7,39},{8,40},{9,... | collective-permute-start | bytes 49160 | tf_op jit(solution)/shard_map/ppermute | solution.py:410
  59.0 0.4 collective-permute-start.9
  59.5 1.0 %collective-permute-start.8 = (f32[4,8,128]{2,1,0:T(8,128)S(1)}, f32[4,8,128]{2,1,0:T(8,128)S(1)}, u32[]{:S(2)}, u32[]{:S(2)}) collective-permute-start(f32[4,8,128]{2,1,0:T(8,128)S(1)} %reduce.1.first_ref), channel_id=1, source_target_pairs={{0,64},{1,65},{2,66},{3,67},{4,68},{5,69},{6,70},{7,71},{8,72},{9,... | collective-permute-start | bytes 49160 | tf_op jit(solution)/shard_map/ppermute | solution.py:410
  60.5 1.3 %collective-permute-done.10.fourth_ref = f32[4,8,128]{2,1,0:T(8,128)S(1)} collective-permute-done((f32[4,8,128]{2,1,0:T(8,128)S(1)}, f32[4,8,128]{2,1,0:T(8,128)S(1)}, u32[]{:S(2)}, u32[]{:S(2)}) %collective-permute-start.10) | collective-permute-done | bytes 16416 | tf_op jit(solution)/shard_map/ppermute | solution.py:410
  61.8 0.0 collective-permute-done.9.third_ref
  61.8 1.5 %collective-permute-done.8.second_ref = f32[4,8,128]{2,1,0:T(8,128)S(1)} collective-permute-done((f32[4,8,128]{2,1,0:T(8,128)S(1)}, f32[4,8,128]{2,1,0:T(8,128)S(1)}, u32[]{:S(2)}, u32[]{:S(2)}) %collective-permute-start.8) | collective-permute-done | bytes 16416 | tf_op jit(solution)/shard_map/ppermute | solution.py:410
  63.3 0.0 collective-permute-done.4.early_ref
  63.3 0.0 collective-permute-done.5.beside_ref
  63.3 0.2 sum.1
  63.5 0.2 collective-permute-start.11
  63.7 3.7 %collective-permute-start.7 = (f32[512,256]{1,0:T(8,128)S(1)}, f32[512,256]{1,0:T(8,128)S(1)}, u32[]{:S(2)}, u32[]{:S(2)}) collective-permute-start(f32[512,256]{1,0:T(8,128)S(1)} %get-tuple-element.16), channel_id=1, source_target_pairs={{0,127},{1,2},{2,1},{3,4},{4,3},{5,6},{6,5},{7,8},{8,7},{9,10},{10... | collective-permute-start | bytes 1572872 | tf_op jit(solution)/shard_map/ppermute | solution.py:385
  67.4 15.3 %all_to_all.11 = f32[16,4,8,128]{3,2,1,0:T(8,128)S(1)} all-to-all(f32[16,4,8,128]{3,2,1,0:T(8,128)S(1)} %total.1.after_ref), channel_id=1, replica_groups={{0,2,4,6,8,10,12,14,16,18,20,22,24,26,28,30},{1,3,5,7,9,11,13,15,17,19,..., dimensions={0} | all-to-all | bytes 524288 | tf_op jit(solution)/shard_map/all_to_all | solution.py:398
  82.7 0.3 collective-permute-start.12
  83.0 1.2 %collective-permute-done.12 = f32[16,4,8,128]{3,2,1,0:T(8,128)S(1)} collective-permute-done((f32[16,4,8,128]{3,2,1,0:T(8,128)S(1)}, f32[16,4,8,128]{3,2,1,0:T(8,128)S(1)}, u32[]{:S(2)}, u32[]{:S(2)}) %collective-permute-start.12) | collective-permute-done | bytes 262176 | tf_op jit(solution)/shard_map/ppermute | solution.py:390
  84.3 0.0 collective-permute-done.7.late_ref
  84.3 0.0 collective-permute-done.11.swapped_ref
  84.3 1.3 %finish.1 = (f32[2,2,128,384]{3,2,1,0:T(8,128)}, f32[2,256,256]{2,1,0:T(8,128)}) custom-call(s32[8,128]{1,0:T(8,128)S(1)} %broadcast_in_dim.8.info_ref, f32[4,2,128,256]{3,2,1,0:T(8,128)S(1)} %get-tuple-element.10.core_ref, f32[520,256]{1,0:T(8,128)S(1)} %collective-permute-done.4.early_ref, f32[1032,256]{1,0:T(8,128)S(1)} %collective-permute-done.5.beside_ref, ...), custom_call_target="tpu_custom_call" | custom-call | bytes 2000000 | tf_op jit(solution)/shard_map/finish/pallas_call | solution.py:364
  (5 shorter events, 0.1 us)
Async XLA Ops:
  0.6 6.5 %copy-start.3 = (s32[2,2]{1,0:T(2,128)S(1)}, s32[2,2]{1,0:T(2,128)}, u32[]{:S(2)}) copy-start(s32[2,2]{1,0:T(2,128)} %offsets_ref.7) | copy-start | bytes 52
  0.6 6.7 %collective-permute-start.1 = (f32[2,2,128,384]{3,2,1,0:T(8,128)}, f32[2,2,128,384]{3,2,1,0:T(8,128)S(1)}, u32[]{:S(2)}, u32[]{:S(2)}) collective-permute-start(f32[2,2,128,384]{3,2,1,0:T(8,128)} %own_ref.3), channel_id=1, source_target_pairs={{0,1},{1,0},{2,3},{3,2},{4,5},{5,4},{6,7},{7,6},{8,9},{9,8},{10,11... | collective-permute-start | bytes 2359304 | tf_op jit(solution)/shard_map/ppermute | solution.py:385
  2.1 11.9 %collective-permute-start = (f32[2,2,128,384]{3,2,1,0:T(8,128)}, f32[2,2,128,384]{3,2,1,0:T(8,128)S(1)}, u32[]{:S(2)}, u32[]{:S(2)}) collective-permute-start(f32[2,2,128,384]{3,2,1,0:T(8,128)} %own_ref.3), channel_id=1, source_target_pairs={{0,127},{1,2},{2,1},{3,4},{4,3},{5,6},{6,5},{7,8},{8,7},{9,10},{10... | collective-permute-start | bytes 2359304 | tf_op jit(solution)/shard_map/ppermute | solution.py:385
  5.5 12.7 %collective-permute-start.2 = (f32[2,2,128,256]{3,2,1,0:T(8,128)}, f32[2,2,128,256]{3,2,1,0:T(8,128)S(1)}, u32[]{:S(2)}, u32[]{:S(2)}) collective-permute-start(f32[2,2,128,256]{3,2,1,0:T(8,128)} %core.1), channel_id=1, source_target_pairs={{0,64},{64,0},{1,65},{65,1},{2,66},{66,2},{3,67},{67,3},{4,68},{68... | collective-permute-start | bytes 1572872 | tf_op jit(solution)/shard_map/ppermute | solution.py:414
  7.2 8.8 %copy-start.1 = (f32[2,256,256]{2,1,0:T(8,128)S(1)}, f32[2,256,256]{2,1,0:T(8,128)}, u32[]{:S(2)}) copy-start(f32[2,256,256]{2,1,0:T(8,128)} %amp_ref.1) | copy-start | bytes 1572868
  14.1 3.1 %copy-start.2 = (f32[2,256,256]{2,1,0:T(8,128)S(1)}, f32[2,256,256]{2,1,0:T(8,128)}, u32[]{:S(2)}) copy-start(f32[2,256,256]{2,1,0:T(8,128)} %probe_ref.1) | copy-start | bytes 1572868
  14.2 3.8 %copy-start = (f32[2,2,128,384]{3,2,1,0:T(8,128)S(1)}, f32[2,2,128,384]{3,2,1,0:T(8,128)}, u32[]{:S(2)}) copy-start(f32[2,2,128,384]{3,2,1,0:T(8,128)} %own_ref.3) | copy-start | bytes 2359300
  14.2 14.3 %collective-permute-start.3 = (f32[2,2,128,256]{3,2,1,0:T(8,128)S(1)}, f32[2,2,128,256]{3,2,1,0:T(8,128)S(1)}, u32[]{:S(2)}, u32[]{:S(2)}) collective-permute-start(f32[2,2,128,256]{3,2,1,0:T(8,128)S(1)} %halo.1), channel_id=1, source_target_pairs={{0,64},{64,0},{1,65},{65,1},{2,66},{66,2},{3,67},{67,3},{4,68},{68... | collective-permute-start | bytes 1572872 | tf_op jit(solution)/shard_map/ppermute | solution.py:414
  18.0 10.5 %copy-start.4 = (bf16[6,2,2,256,256]{4,3,2,1,0:T(8,128)(2,1)S(1)}, bf16[6,2,2,256,256]{4,3,2,1,0:T(8,128)(2,1)}, u32[]{:S(2)}) copy-start(bf16[6,2,2,256,256]{4,3,2,1,0:T(8,128)(2,1)} %constant.10.clone.tables_ref) | copy-start | bytes 9437188
  35.9 27.4 %collective-permute-start.5 = (f32[1032,256]{1,0:T(8,128)S(1)}, f32[1032,256]{1,0:T(8,128)S(1)}, u32[]{:S(2)}, u32[]{:S(2)}) collective-permute-start(f32[1032,256]{1,0:T(8,128)S(1)} %get-tuple-element.12), channel_id=1, source_target_pairs={{0,1},{1,0},{2,3},{3,2},{4,5},{5,4},{6,7},{7,6},{8,9},{9,8},{10,11... | collective-permute-start | bytes 3170312 | tf_op jit(solution)/shard_map/ppermute | solution.py:385
  41.2 22.1 %collective-permute-start.4 = (f32[520,256]{1,0:T(8,128)S(1)}, f32[520,256]{1,0:T(8,128)S(1)}, u32[]{:S(2)}, u32[]{:S(2)}) collective-permute-start(f32[520,256]{1,0:T(8,128)S(1)} %get-tuple-element.11), channel_id=1, source_target_pairs={{0,127},{1,2},{2,1},{3,4},{4,3},{5,6},{6,5},{7,8},{8,7},{9,10},{10... | collective-permute-start | bytes 1597448 | tf_op jit(solution)/shard_map/ppermute | solution.py:385
  41.2 5.7 %collective-permute-start.6 = (f32[32,2,8,128]{3,2,1,0:T(8,128)S(1)}, f32[32,2,8,128]{3,2,1,0:T(8,128)S(1)}, u32[]{:S(2)}, u32[]{:S(2)}) collective-permute-start(f32[32,2,8,128]{3,2,1,0:T(8,128)S(1)} %get-tuple-element.15), channel_id=1, source_target_pairs={{0,1},{1,0},{2,3},{3,2},{4,5},{5,4},{6,7},{7,6},{8,9},{9,8},{10,11... | collective-permute-start | bytes 786440 | tf_op jit(solution)/shard_map/ppermute | solution.py:390
  57.6 4.2 %collective-permute-start.10 = (f32[4,8,128]{2,1,0:T(8,128)S(1)}, f32[4,8,128]{2,1,0:T(8,128)S(1)}, u32[]{:S(2)}, u32[]{:S(2)}) collective-permute-start(f32[4,8,128]{2,1,0:T(8,128)S(1)} %reduce.1.first_ref), channel_id=1, source_target_pairs={{0,32},{1,33},{2,34},{3,35},{4,36},{5,37},{6,38},{7,39},{8,40},{9,... | collective-permute-start | bytes 49160 | tf_op jit(solution)/shard_map/ppermute | solution.py:410
  59.0 2.7 %collective-permute-start.9 = (f32[4,8,128]{2,1,0:T(8,128)S(1)}, f32[4,8,128]{2,1,0:T(8,128)S(1)}, u32[]{:S(2)}, u32[]{:S(2)}) collective-permute-start(f32[4,8,128]{2,1,0:T(8,128)S(1)} %reduce.1.first_ref), channel_id=1, source_target_pairs={{0,96},{1,97},{2,98},{3,99},{4,100},{5,101},{6,102},{7,103},{8,104... | collective-permute-start | bytes 49160 | tf_op jit(solution)/shard_map/ppermute | solution.py:410
  59.5 3.8 %collective-permute-start.8 = (f32[4,8,128]{2,1,0:T(8,128)S(1)}, f32[4,8,128]{2,1,0:T(8,128)S(1)}, u32[]{:S(2)}, u32[]{:S(2)}) collective-permute-start(f32[4,8,128]{2,1,0:T(8,128)S(1)} %reduce.1.first_ref), channel_id=1, source_target_pairs={{0,64},{1,65},{2,66},{3,67},{4,68},{5,69},{6,70},{7,71},{8,72},{9,... | collective-permute-start | bytes 49160 | tf_op jit(solution)/shard_map/ppermute | solution.py:410
  63.5 20.7 %collective-permute-start.11 = (f32[2,2,128,384]{3,2,1,0:T(8,128)S(1)}, f32[2,2,128,384]{3,2,1,0:T(8,128)S(1)}, u32[]{:S(2)}, u32[]{:S(2)}) collective-permute-start(f32[2,2,128,384]{3,2,1,0:T(8,128)S(1)} %sum.1), channel_id=1, source_target_pairs={{0,64},{64,0},{1,65},{65,1},{2,66},{66,2},{3,67},{67,3},{4,68},{68... | collective-permute-start | bytes 2359304 | tf_op jit(solution)/shard_map/ppermute | solution.py:414
  63.7 20.5 %collective-permute-start.7 = (f32[512,256]{1,0:T(8,128)S(1)}, f32[512,256]{1,0:T(8,128)S(1)}, u32[]{:S(2)}, u32[]{:S(2)}) collective-permute-start(f32[512,256]{1,0:T(8,128)S(1)} %get-tuple-element.16), channel_id=1, source_target_pairs={{0,127},{1,2},{2,1},{3,4},{4,3},{5,6},{6,5},{7,8},{8,7},{9,10},{10... | collective-permute-start | bytes 1572872 | tf_op jit(solution)/shard_map/ppermute | solution.py:385
  82.7 1.5 %collective-permute-start.12 = (f32[16,4,8,128]{3,2,1,0:T(8,128)S(1)}, f32[16,4,8,128]{3,2,1,0:T(8,128)S(1)}, u32[]{:S(2)}, u32[]{:S(2)}) collective-permute-start(f32[16,4,8,128]{3,2,1,0:T(8,128)S(1)} %all_to_all.11), channel_id=1, source_target_pairs={{0,1},{1,0},{2,3},{3,2},{4,5},{5,4},{6,7},{7,6},{8,9},{9,8},{10,11... | collective-permute-start | bytes 786440 | tf_op jit(solution)/shard_map/ppermute | solution.py:390

commit v7 on v6

--- a/solution.py
+++ b/solution.py
@@ -142,24 +142,32 @@
         out_ref[c] = pltpu.roll(pltpu.roll(probe_ref[c], row, 0), col, 1)
 
 
-def core_kernel(offsets_ref, own_ref, out_ref, offsets, cols, sems, out_sems):
-    load = pltpu.make_async_copy(offsets_ref, offsets, sems.at[4])
+def core_kernel(offsets_ref, own_ref, out_ref, offsets, left, right, sems):
+    load = pltpu.make_async_copy(offsets_ref, offsets, sems.at[0, 4])
     load.start()
-    loads = [pltpu.make_async_copy(own_ref.at[i // 2, i % 2], cols.at[i], sems.at[i]) for i in range(4)]
-    for copy in loads:
-        copy.start()
+    loads = []
+    for i in range(4):
+        at = (i // 2, i % 2, slice(None))
+        loads.append(
+            [
+                pltpu.make_async_copy(own_ref.at[at + (slice(0, HALF),)], left.at[i], sems.at[0, i]),
+                pltpu.make_async_copy(own_ref.at[at + (slice(WIDTH, COLS),)], right.at[i], sems.at[1, i]),
+                pltpu.make_async_copy(
+                    own_ref.at[at + (slice(HALF, WIDTH),)], out_ref.at[at + (slice(HALF, WIDTH),)], sems.at[2, i]
+                ),
+            ]
+        )
+        for copy in loads[i]:
+            copy.start()
     load.wait()
     lane = lax.broadcasted_iota(jnp.int32, (HALO, HALF), 1)
     kept = lane >= offsets[1 - lax.axis_index("slab"), 1]
-    stores = []
     for i in range(4):
-        loads[i].wait()
-        cols[i, :, :HALF] = jnp.where(kept, cols[i, :, :HALF], cols[i, :, 2 * HALF :])
-        store = pltpu.make_async_copy(cols.at[i, :, :WIDTH], out_ref.at[i // 2, i % 2], out_sems.at[i])
-        store.start()
-        stores.append(store)
-    for copy in stores:
-        copy.wait()
+        loads[i][0].wait()
+        loads[i][1].wait()
+        out_ref[i // 2, i % 2, :, :HALF] = jnp.where(kept, left[i], right[i])
+    for i in range(4):
+        loads[i][2].wait()
 
 
 def amp_kernel(place_ref, offsets_ref, amp_ref, out_ref):
@@ -330,8 +338,8 @@
     out_ref[...] = jnp.sum(parts_ref[...], axis=0)
 
 
-def total_kernel(first_ref, second_ref, third_ref, fourth_ref, out_ref):
-    total = (first_ref[...] + second_ref[...]) + (third_ref[...] + fourth_ref[...])
+def total_kernel(first_ref, second_ref, out_ref):
+    total = first_ref[...] + second_ref[...]
     out_ref[...] = jnp.broadcast_to(total[None], out_ref.shape)
 
 
@@ -398,15 +406,14 @@
     return lax.all_to_all(x, ("slab", "tile"), 0, 0, tiled=True, axis_index_groups=groups)
 
 
-def along_z(x, by):
+def swap_far(x):
     slabs, tiles = lax.axis_size("slab"), lax.axis_size("tile")
     half = tiles // 2
-    pairs = []
-    for z in range(2 * slabs):
-        to = (z + by) % (2 * slabs)
-        for i in range(half):
-            source = z % slabs * tiles + z // slabs * half + i
-            pairs.append((source, to % slabs * tiles + to // slabs * half + i))
+    pairs = [
+        (slab * tiles + tile, (slabs - 1 - slab) * tiles + (tile + half) % tiles)
+        for slab in range(slabs)
+        for tile in range(tiles)
+    ]
     return lax.ppermute(x, ("slab", "tile"), pairs)
 
 
@@ -423,21 +430,20 @@
     own = transmission
     part, whole, band = (2, 2, HALO, WIDTH), (2, 2, WIDTH, WIDTH), (2, 2, HALO, COLS)
 
+    own_hbm, offsets_hbm = (pltpu.with_memory_space_constraint(x, pltpu.HBM) for x in (own, scan_offsets))
     core = call(
         core_kernel,
         part,
         (),
-        (scan_offsets, own),
+        (offsets_hbm, own_hbm),
         "core",
         scratch=[
             pltpu.SMEM((2, 2), jnp.int32),
-            pltpu.VMEM((4, HALO, COLS), F32),
-            pltpu.SemaphoreType.DMA((5,)),
-            pltpu.SemaphoreType.DMA((4,)),
+            pltpu.VMEM((4, HALO, HALF), F32),
+            pltpu.VMEM((4, HALO, HALF), F32),
+            pltpu.SemaphoreType.DMA((3, 5)),
         ],
         ins=(HBM, HBM),
-        outs=(HBM,),
-        vmem_limit=60,
     )
     core = swap_slab(core)
     beside, across = swap_tile(own, 1), swap_tile(own, 0)
@@ -470,9 +476,9 @@
     kept = call(reduce_kernel, parts[1:], (), (among_columns(kept),), "reduce")
     late, kept = lax.optimization_barrier((late, kept))
     late = swap_tile(late, 0)
-    planes = (kept, along_z(kept, 1), along_z(kept, 3), along_z(kept, 2))
-    kept = call(total_kernel, parts, (), planes, "total")
+    kept = call(add_kernel, parts[1:], (), (kept, swap_slab(kept)), "add_slabs")
     got = swap_slab(call(sum_kernel, band, (), sides + (kept,), "sum"))
+    kept = call(total_kernel, parts, (), (kept, swap_far(kept)), "total")
     kept = among_columns(kept)
     object_grad, probe_grad = call(
         finish_kernel,

time: 85.7 us -> 83.3 us (0.972)
  blocking collectives: 26 us -> 24.7 us
  starting transfers between devices: 23.3 us -> 22.2 us
    ppermute x3 -> x1, waiting for transfers between devices: 2.76 us -> 0.01 us  [swap_far(): return lax.ppermute(x, ('slab', 'tile'), pairs)]
    ppermute x3 -> x4, waiting for transfers between devices: 10.3 us -> 13 us  [swap_slab(): return lax.ppermute(x, 'slab', [(0, 1), (1, 0)])]
    all_to_all x2, blocking collectives: 26 us -> 24.7 us  [among_columns(): lax.all_to_all(x, ('slab', 'tile'), 0, 0, tiled=True, axis_index_groups=g...]
    ppermute x3 -> x1, starting transfers between devices: 2.9 us -> 1.64 us  [swap_far(): return lax.ppermute(x, ('slab', 'tile'), pairs)]
    ppermute x2, starting transfers between devices: 4.86 us -> 6.01 us  [swap_core(): return lax.ppermute(x, 'tile', [(i, i ^ 1) for i in range(count)])]
    ppermute x5, starting transfers between devices: 11.8 us -> 10.8 us  [swap_tile(): return lax.ppermute(x, ('slab', 'tile'), pairs)]
    pallas_call x11 -> x12, Pallas kernels: 13 us -> 12.5 us  [call(): pl.pallas_call(kernel, out_shape=tuple((jax.ShapeDtypeStruct(shape, F32)...]
    ppermute x3 -> x4, starting transfers between devices: 3.72 us -> 3.69 us  [swap_slab(): return lax.ppermute(x, 'slab', [(0, 1), (1, 0)])]
  transfers between devices with their start and end apart: 13 -> 12, of which waited for: 6 -> 5; matrix products, arithmetic and copies ran while one was open for 0% -> 0% of each run, Pallas kernels for 5% -> 4%
where the time goes in v7:
time: 83.3 us; the launch traced here: 83.1 us
  blocking collectives  24.7 us (30%)
  waiting for transfers between devices  22.7 us (27%)
  starting transfers between devices  22.2 us (27%)
  Pallas kernels  12.5 us (15%)
    all_to_all x2, blocking collectives, among_columns(): lax.all_to_all(x, ('slab', 'tile'), 0, 0, tiled=True, axis_index_groups=g...  24.7 us
    ppermute x4, waiting for transfers between devices, swap_slab(): return lax.ppermute(x, 'slab', [(0, 1), (1, 0)])  13 us
    pallas_call x12, Pallas kernels, call(): pl.pallas_call(kernel, out_shape=tuple((jax.ShapeDtypeStruct(shape, F32)...  12.5 us
    ppermute x5, starting transfers between devices, swap_tile(): return lax.ppermute(x, ('slab', 'tile'), pairs)  10.8 us
    ppermute x5, waiting for transfers between devices, swap_tile(): return lax.ppermute(x, ('slab', 'tile'), pairs)  7.35 us
    ppermute x2, starting transfers between devices, swap_core(): return lax.ppermute(x, 'tile', [(i, i ^ 1) for i in range(count)])  6.01 us
    ppermute x4, starting transfers between devices, swap_slab(): return lax.ppermute(x, 'slab', [(0, 1), (1, 0)])  3.69 us
    ppermute x2, waiting for transfers between devices, swap_core(): return lax.ppermute(x, 'tile', [(i, i ^ 1) for i in range(count)])  2.32 us
  transfers between devices with their start and end apart: 12, of which 5 were waited for; matrix products, arithmetic and copies ran while one was open for 0% of the time, Pallas kernels for 4%

profile of v7, /device:TPU:1, one launch (start us, length us, event | category | flops | bytes accessed | tf_op | source)
XLA Modules:
  0.0 83.1 jit_solution(7495992301720922594)
XLA Ops:
  0.6 0.0 copy-start.3
  0.6 1.5 %collective-permute-start.1 = (f32[2,2,128,384]{3,2,1,0:T(8,128)}, f32[2,2,128,384]{3,2,1,0:T(8,128)S(1)}, u32[]{:S(2)}, u32[]{:S(2)}) collective-permute-start(f32[2,2,128,384]{3,2,1,0:T(8,128)} %own_ref.3), channel_id=1, source_target_pairs={{0,1},{1,0},{2,3},{3,2},{4,5},{5,4},{6,7},{7,6},{8,9},{9,8},{10,11... | collective-permute-start | bytes 2359304 | tf_op jit(solution)/shard_map/ppermute | solution.py:393
  2.1 1.4 %collective-permute-start = (f32[2,2,128,384]{3,2,1,0:T(8,128)}, f32[2,2,128,384]{3,2,1,0:T(8,128)S(1)}, u32[]{:S(2)}, u32[]{:S(2)}) collective-permute-start(f32[2,2,128,384]{3,2,1,0:T(8,128)} %own_ref.3), channel_id=1, source_target_pairs={{0,127},{1,2},{2,1},{3,4},{4,3},{5,6},{6,5},{7,8},{8,7},{9,10},{10... | collective-permute-start | bytes 2359304 | tf_op jit(solution)/shard_map/ppermute | solution.py:393
  3.5 1.3 %core.1 = f32[2,2,128,256]{3,2,1,0:T(8,128)S(1)} custom-call(s32[2,2]{1,0:T(2,128)} %offsets_ref.7, f32[2,2,128,384]{3,2,1,0:T(8,128)} %own_ref.3), custom_call_target="tpu_custom_call" | custom-call | bytes 2000000 | tf_op jit(solution)/shard_map/core/pallas_call | solution.py:372
  4.8 1.7 %collective-permute-start.2 = (f32[2,2,128,256]{3,2,1,0:T(8,128)S(1)}, f32[2,2,128,256]{3,2,1,0:T(8,128)S(1)}, u32[]{:S(2)}, u32[]{:S(2)}) collective-permute-start(f32[2,2,128,256]{3,2,1,0:T(8,128)S(1)} %core.1), channel_id=1, source_target_pairs={{0,64},{64,0},{1,65},{65,1},{2,66},{66,2},{3,67},{67,3},{4,68},{68... | collective-permute-start | bytes 1572872 | tf_op jit(solution)/shard_map/ppermute | solution.py:421
  6.5 0.0 copy-done.3
  6.5 0.0 copy-start.1
  6.6 0.1 reshape.19
  6.6 0.1 add_bitcast_fusion
  6.7 0.0 collective-permute-done.1.beside_ref
  6.7 7.3 %collective-permute-done.across_ref = f32[2,2,128,384]{3,2,1,0:T(8,128)S(1)} collective-permute-done((f32[2,2,128,384]{3,2,1,0:T(8,128)}, f32[2,2,128,384]{3,2,1,0:T(8,128)S(1)}, u32[]{:S(2)}, u32[]{:S(2)}) %collective-permute-start) | collective-permute-done | bytes 786464 | tf_op jit(solution)/shard_map/ppermute | solution.py:393
  14.1 0.1 broadcast_in_dim.8.info_ref
  14.1 0.0 copy-start.2
  14.1 0.1 halo.1
  14.2 0.0 copy-start
  14.2 1.8 %collective-permute-start.3 = (f32[2,2,128,256]{3,2,1,0:T(8,128)S(1)}, f32[2,2,128,256]{3,2,1,0:T(8,128)S(1)}, u32[]{:S(2)}, u32[]{:S(2)}) collective-permute-start(f32[2,2,128,256]{3,2,1,0:T(8,128)S(1)} %halo.1), channel_id=1, source_target_pairs={{0,64},{64,0},{1,65},{65,1},{2,66},{66,2},{3,67},{67,3},{4,68},{68... | collective-permute-start | bytes 1572872 | tf_op jit(solution)/shard_map/ppermute | solution.py:421
  16.0 0.0 copy-done.1
  16.0 1.2 %amp.1.amp_ref = f32[256,256]{1,0:T(8,128)S(1)} custom-call(s32[1]{0:T(128)} %bitcast.1.place_ref, s32[2,2]{1,0:T(2,128)S(1)} %copy-done.3, f32[2,256,256]{2,1,0:T(8,128)S(1)} %copy-done.1), custom_call_target="tpu_custom_call" | custom-call | bytes 2000000 | tf_op jit(solution)/shard_map/amp/pallas_call | solution.py:372
  17.2 0.0 copy-done.2
  17.2 0.8 roll.1.probe_ref
  18.0 0.0 copy-done
  18.0 0.0 copy-start.4
  18.0 0.1 window.1.own_ref
  18.2 0.0 collective-permute-done.2.core_ref
  18.2 10.4 %collective-permute-done.3.halo_ref = f32[2,2,128,256]{3,2,1,0:T(8,128)S(1)} collective-permute-done((f32[2,2,128,256]{3,2,1,0:T(8,128)S(1)}, f32[2,2,128,256]{3,2,1,0:T(8,128)S(1)}, u32[]{:S(2)}, u32[]{:S(2)}) %collective-permute-start.3) | collective-permute-done | bytes 524320 | tf_op jit(solution)/shard_map/ppermute | solution.py:421
  28.6 0.0 copy-done.4
  28.6 7.5 %position.1 = (f32[32,2,8,128]{3,2,1,0:T(8,128)S(1)}, f32[32,2,8,128]{3,2,1,0:T(8,128)S(1)}, f32[4,2,128,256]{3,2,1,0:T(8,128)S(1)}, f32[1032,256]{1,0:T(8,128)S...) custom-call(s32[8,128]{1,0:T(8,128)S(1)} %broadcast_in_dim.8.info_ref, s32[2,2]{1,0:T(2,128)S(1)} %copy-done.3, ...), custom_call_target="tpu_custom_call" | custom-call | flops 3300000000 | bytes 10000000 | tf_op jit(solution)/shard_map/position/pallas_call | solution.py:372
  36.1 4.3 %collective-permute-start.5 = (f32[1032,256]{1,0:T(8,128)S(1)}, f32[1032,256]{1,0:T(8,128)S(1)}, u32[]{:S(2)}, u32[]{:S(2)}) collective-permute-start(f32[1032,256]{1,0:T(8,128)S(1)} %get-tuple-element.12), channel_id=1, source_target_pairs={{0,1},{1,0},{2,3},{3,2},{4,5},{5,4},{6,7},{7,6},{8,9},{9,8},{10,11... | collective-permute-start | bytes 3170312 | tf_op jit(solution)/shard_map/ppermute | solution.py:393
  40.4 0.0 collective-permute-start.4
  40.4 4.6 %collective-permute-start.6 = (f32[32,2,8,128]{3,2,1,0:T(8,128)S(1)}, f32[32,2,8,128]{3,2,1,0:T(8,128)S(1)}, u32[]{:S(2)}, u32[]{:S(2)}) collective-permute-start(f32[32,2,8,128]{3,2,1,0:T(8,128)S(1)} %get-tuple-element.15), channel_id=1, source_target_pairs={{0,1},{1,0},{2,3},{3,2},{4,5},{5,4},{6,7},{7,6},{8,9},{9,8},{10,11... | collective-permute-start | bytes 786440 | tf_op jit(solution)/shard_map/ppermute | solution.py:398
  45.0 1.2 %collective-permute-done.6.got_ref = f32[32,2,8,128]{3,2,1,0:T(8,128)S(1)} collective-permute-done((f32[32,2,8,128]{3,2,1,0:T(8,128)S(1)}, f32[32,2,8,128]{3,2,1,0:T(8,128)S(1)}, u32[]{:S(2)}, u32[]{:S(2)}) %collective-permute-start.6) | collective-permute-done | bytes 262176 | tf_op jit(solution)/shard_map/ppermute | solution.py:398
  46.2 10.6 %all_to_all.10.parts_ref = f32[16,4,8,128]{3,2,1,0:T(8,128)S(1)} all-to-all(f32[16,4,8,128]{3,2,1,0:T(8,128)S(1)} %bitcast.7), channel_id=1, replica_groups={{0,2,4,6,8,10,12,14,16,18,20,22,24,26,28,30},{1,3,5,7,9,11,13,15,17,19,..., dimensions={0} | all-to-all | bytes 524288 | tf_op jit(solution)/shard_map/all_to_all | solution.py:406
  56.8 0.1 collective-permute-start.8
  56.9 2.6 %collective-permute-done.8.got_ref = f32[4,8,128]{2,1,0:T(8,128)S(1)} collective-permute-done((f32[4,8,128]{2,1,0:T(8,128)S(1)}, f32[4,8,128]{2,1,0:T(8,128)S(1)}, u32[]{:S(2)}, u32[]{:S(2)}) %collective-permute-start.8) | collective-permute-done | bytes 16416 | tf_op jit(solution)/shard_map/ppermute | solution.py:421
  59.5 0.0 collective-permute-done.4.early_ref
  59.5 0.0 collective-permute-done.5.beside_ref
  59.5 0.2 sum.1
  59.7 0.1 collective-permute-start.9
  59.8 1.6 %collective-permute-start.10 = (f32[4,8,128]{2,1,0:T(8,128)S(1)}, f32[4,8,128]{2,1,0:T(8,128)S(1)}, u32[]{:S(2)}, u32[]{:S(2)}) collective-permute-start(f32[4,8,128]{2,1,0:T(8,128)S(1)} %add_slabs.1.after_ref.first_ref), channel_id=1, source_target_pairs={{0,96},{1,97},{2,98},{3,99},{4,100},{5,101},{6,102},{7,103},{8,104... | collective-permute-start | bytes 49160 | tf_op jit(solution)/shard_map/ppermute | solution.py:417
  61.5 3.7 %collective-permute-start.7 = (f32[512,256]{1,0:T(8,128)S(1)}, f32[512,256]{1,0:T(8,128)S(1)}, u32[]{:S(2)}, u32[]{:S(2)}) collective-permute-start(f32[512,256]{1,0:T(8,128)S(1)} %get-tuple-element.16), channel_id=1, source_target_pairs={{0,127},{1,2},{2,1},{3,4},{4,3},{5,6},{6,5},{7,8},{8,7},{9,10},{10... | collective-permute-start | bytes 1572872 | tf_op jit(solution)/shard_map/ppermute | solution.py:393
  65.1 0.0 collective-permute-done.10.second_ref
  65.2 14.1 %all_to_all.11 = f32[16,4,8,128]{3,2,1,0:T(8,128)S(1)} all-to-all(f32[16,4,8,128]{3,2,1,0:T(8,128)S(1)} %total.1), channel_id=1, replica_groups={{0,2,4,6,8,10,12,14,16,18,20,22,24,26,28,30},{1,3,5,7,9,11,13,15,17,19,..., dimensions={0} | all-to-all | bytes 524288 | tf_op jit(solution)/shard_map/all_to_all | solution.py:406
  79.2 1.4 %collective-permute-start.11 = (f32[16,4,8,128]{3,2,1,0:T(8,128)S(1)}, f32[16,4,8,128]{3,2,1,0:T(8,128)S(1)}, u32[]{:S(2)}, u32[]{:S(2)}) collective-permute-start(f32[16,4,8,128]{3,2,1,0:T(8,128)S(1)} %all_to_all.11), channel_id=1, source_target_pairs={{0,1},{1,0},{2,3},{3,2},{4,5},{5,4},{6,7},{7,6},{8,9},{9,8},{10,11... | collective-permute-start | bytes 786440 | tf_op jit(solution)/shard_map/ppermute | solution.py:398
  80.6 0.0 collective-permute-done.7.late_ref
  80.6 1.2 %collective-permute-done.11 = f32[16,4,8,128]{3,2,1,0:T(8,128)S(1)} collective-permute-done((f32[16,4,8,128]{3,2,1,0:T(8,128)S(1)}, f32[16,4,8,128]{3,2,1,0:T(8,128)S(1)}, u32[]{:S(2)}, u32[]{:S(2)}) %collective-permute-start.11) | collective-permute-done | bytes 262176 | tf_op jit(solution)/shard_map/ppermute | solution.py:398
  81.8 0.0 collective-permute-done.9.swapped_ref
  81.8 1.3 %finish.1 = (f32[2,2,128,384]{3,2,1,0:T(8,128)}, f32[2,256,256]{2,1,0:T(8,128)}) custom-call(s32[8,128]{1,0:T(8,128)S(1)} %broadcast_in_dim.8.info_ref, f32[4,2,128,256]{3,2,1,0:T(8,128)S(1)} %get-tuple-element.10.core_ref, f32[520,256]{1,0:T(8,128)S(1)} %collective-permute-done.4.early_ref, f32[1032,256]{1,0:T(8,128)S(1)} %collective-permute-done.5.beside_ref, ...), custom_call_target="tpu_custom_call" | custom-call | bytes 2000000 | tf_op jit(solution)/shard_map/finish/pallas_call | solution.py:372
  (6 shorter events, 0.1 us)
Async XLA Ops:
  0.6 5.9 %copy-start.3 = (s32[2,2]{1,0:T(2,128)S(1)}, s32[2,2]{1,0:T(2,128)}, u32[]{:S(2)}) copy-start(s32[2,2]{1,0:T(2,128)} %offsets_ref.7) | copy-start | bytes 52
  0.6 6.1 %collective-permute-start.1 = (f32[2,2,128,384]{3,2,1,0:T(8,128)}, f32[2,2,128,384]{3,2,1,0:T(8,128)S(1)}, u32[]{:S(2)}, u32[]{:S(2)}) collective-permute-start(f32[2,2,128,384]{3,2,1,0:T(8,128)} %own_ref.3), channel_id=1, source_target_pairs={{0,1},{1,0},{2,3},{3,2},{4,5},{5,4},{6,7},{7,6},{8,9},{9,8},{10,11... | collective-permute-start | bytes 2359304 | tf_op jit(solution)/shard_map/ppermute | solution.py:393
  2.1 11.9 %collective-permute-start = (f32[2,2,128,384]{3,2,1,0:T(8,128)}, f32[2,2,128,384]{3,2,1,0:T(8,128)S(1)}, u32[]{:S(2)}, u32[]{:S(2)}) collective-permute-start(f32[2,2,128,384]{3,2,1,0:T(8,128)} %own_ref.3), channel_id=1, source_target_pairs={{0,127},{1,2},{2,1},{3,4},{4,3},{5,6},{6,5},{7,8},{8,7},{9,10},{10... | collective-permute-start | bytes 2359304 | tf_op jit(solution)/shard_map/ppermute | solution.py:393
  4.8 13.4 %collective-permute-start.2 = (f32[2,2,128,256]{3,2,1,0:T(8,128)S(1)}, f32[2,2,128,256]{3,2,1,0:T(8,128)S(1)}, u32[]{:S(2)}, u32[]{:S(2)}) collective-permute-start(f32[2,2,128,256]{3,2,1,0:T(8,128)S(1)} %core.1), channel_id=1, source_target_pairs={{0,64},{64,0},{1,65},{65,1},{2,66},{66,2},{3,67},{67,3},{4,68},{68... | collective-permute-start | bytes 1572872 | tf_op jit(solution)/shard_map/ppermute | solution.py:421
  6.5 9.5 %copy-start.1 = (f32[2,256,256]{2,1,0:T(8,128)S(1)}, f32[2,256,256]{2,1,0:T(8,128)}, u32[]{:S(2)}) copy-start(f32[2,256,256]{2,1,0:T(8,128)} %amp_ref.1) | copy-start | bytes 1572868
  14.1 3.1 %copy-start.2 = (f32[2,256,256]{2,1,0:T(8,128)S(1)}, f32[2,256,256]{2,1,0:T(8,128)}, u32[]{:S(2)}) copy-start(f32[2,256,256]{2,1,0:T(8,128)} %probe_ref.1) | copy-start | bytes 1572868
  14.2 3.8 %copy-start = (f32[2,2,128,384]{3,2,1,0:T(8,128)S(1)}, f32[2,2,128,384]{3,2,1,0:T(8,128)}, u32[]{:S(2)}) copy-start(f32[2,2,128,384]{3,2,1,0:T(8,128)} %own_ref.3) | copy-start | bytes 2359300
  14.2 14.3 %collective-permute-start.3 = (f32[2,2,128,256]{3,2,1,0:T(8,128)S(1)}, f32[2,2,128,256]{3,2,1,0:T(8,128)S(1)}, u32[]{:S(2)}, u32[]{:S(2)}) collective-permute-start(f32[2,2,128,256]{3,2,1,0:T(8,128)S(1)} %halo.1), channel_id=1, source_target_pairs={{0,64},{64,0},{1,65},{65,1},{2,66},{66,2},{3,67},{67,3},{4,68},{68... | collective-permute-start | bytes 1572872 | tf_op jit(solution)/shard_map/ppermute | solution.py:421
  18.0 10.6 %copy-start.4 = (bf16[6,2,2,256,256]{4,3,2,1,0:T(8,128)(2,1)S(1)}, bf16[6,2,2,256,256]{4,3,2,1,0:T(8,128)(2,1)}, u32[]{:S(2)}) copy-start(bf16[6,2,2,256,256]{4,3,2,1,0:T(8,128)(2,1)} %constant.10.clone.tables_ref) | copy-start | bytes 9437188
  36.1 23.4 %collective-permute-start.5 = (f32[1032,256]{1,0:T(8,128)S(1)}, f32[1032,256]{1,0:T(8,128)S(1)}, u32[]{:S(2)}, u32[]{:S(2)}) collective-permute-start(f32[1032,256]{1,0:T(8,128)S(1)} %get-tuple-element.12), channel_id=1, source_target_pairs={{0,1},{1,0},{2,3},{3,2},{4,5},{5,4},{6,7},{7,6},{8,9},{9,8},{10,11... | collective-permute-start | bytes 3170312 | tf_op jit(solution)/shard_map/ppermute | solution.py:393
  40.4 19.1 %collective-permute-start.4 = (f32[520,256]{1,0:T(8,128)S(1)}, f32[520,256]{1,0:T(8,128)S(1)}, u32[]{:S(2)}, u32[]{:S(2)}) collective-permute-start(f32[520,256]{1,0:T(8,128)S(1)} %get-tuple-element.11), channel_id=1, source_target_pairs={{0,127},{1,2},{2,1},{3,4},{4,3},{5,6},{6,5},{7,8},{8,7},{9,10},{10... | collective-permute-start | bytes 1597448 | tf_op jit(solution)/shard_map/ppermute | solution.py:393
  40.4 5.7 %collective-permute-start.6 = (f32[32,2,8,128]{3,2,1,0:T(8,128)S(1)}, f32[32,2,8,128]{3,2,1,0:T(8,128)S(1)}, u32[]{:S(2)}, u32[]{:S(2)}) collective-permute-start(f32[32,2,8,128]{3,2,1,0:T(8,128)S(1)} %get-tuple-element.15), channel_id=1, source_target_pairs={{0,1},{1,0},{2,3},{3,2},{4,5},{5,4},{6,7},{7,6},{8,9},{9,8},{10,11... | collective-permute-start | bytes 786440 | tf_op jit(solution)/shard_map/ppermute | solution.py:398
  56.8 2.7 %collective-permute-start.8 = (f32[4,8,128]{2,1,0:T(8,128)S(1)}, f32[4,8,128]{2,1,0:T(8,128)S(1)}, u32[]{:S(2)}, u32[]{:S(2)}) collective-permute-start(f32[4,8,128]{2,1,0:T(8,128)S(1)} %reduce.1.keep_ref), channel_id=1, source_target_pairs={{0,64},{64,0},{1,65},{65,1},{2,66},{66,2},{3,67},{67,3},{4,68},{68... | collective-permute-start | bytes 49160 | tf_op jit(solution)/shard_map/ppermute | solution.py:421
  59.7 22.1 %collective-permute-start.9 = (f32[2,2,128,384]{3,2,1,0:T(8,128)S(1)}, f32[2,2,128,384]{3,2,1,0:T(8,128)S(1)}, u32[]{:S(2)}, u32[]{:S(2)}) collective-permute-start(f32[2,2,128,384]{3,2,1,0:T(8,128)S(1)} %sum.1), channel_id=1, source_target_pairs={{0,64},{64,0},{1,65},{65,1},{2,66},{66,2},{3,67},{67,3},{4,68},{68... | collective-permute-start | bytes 2359304 | tf_op jit(solution)/shard_map/ppermute | solution.py:421
  59.8 5.3 %collective-permute-start.10 = (f32[4,8,128]{2,1,0:T(8,128)S(1)}, f32[4,8,128]{2,1,0:T(8,128)S(1)}, u32[]{:S(2)}, u32[]{:S(2)}) collective-permute-start(f32[4,8,128]{2,1,0:T(8,128)S(1)} %add_slabs.1.after_ref.first_ref), channel_id=1, source_target_pairs={{0,96},{1,97},{2,98},{3,99},{4,100},{5,101},{6,102},{7,103},{8,104... | collective-permute-start | bytes 49160 | tf_op jit(solution)/shard_map/ppermute | solution.py:417
  61.5 19.2 %collective-permute-start.7 = (f32[512,256]{1,0:T(8,128)S(1)}, f32[512,256]{1,0:T(8,128)S(1)}, u32[]{:S(2)}, u32[]{:S(2)}) collective-permute-start(f32[512,256]{1,0:T(8,128)S(1)} %get-tuple-element.16), channel_id=1, source_target_pairs={{0,127},{1,2},{2,1},{3,4},{4,3},{5,6},{6,5},{7,8},{8,7},{9,10},{10... | collective-permute-start | bytes 1572872 | tf_op jit(solution)/shard_map/ppermute | solution.py:393
  79.2 2.6 %collective-permute-start.11 = (f32[16,4,8,128]{3,2,1,0:T(8,128)S(1)}, f32[16,4,8,128]{3,2,1,0:T(8,128)S(1)}, u32[]{:S(2)}, u32[]{:S(2)}) collective-permute-start(f32[16,4,8,128]{3,2,1,0:T(8,128)S(1)} %all_to_all.11), channel_id=1, source_target_pairs={{0,1},{1,0},{2,3},{3,2},{4,5},{5,4},{6,7},{7,6},{8,9},{9,8},{10,11... | collective-permute-start | bytes 786440 | tf_op jit(solution)/shard_map/ppermute | solution.py:398

commit v8 on v7

--- a/solution.py
+++ b/solution.py
@@ -222,6 +222,7 @@
     early_out,
     late_out,
     waves,
+    windows,
     halos,
     offsets,
     sems,
@@ -246,7 +247,9 @@
     for s in range(4):
         if s > 0:
             waves[s - 1, 0], waves[s - 1, 1] = wave
-        prod = times(wave, window_of(s))
+        window = window_of(s)
+        windows[s, 0], windows[s, 1] = window
+        prod = times(wave, window)
         if s < 3:
             wave = propagate(prod, tables_ref)
     field = right_mult((fold(prod[0]), fold(prod[1])), tables_ref, FAR_RIGHT)
@@ -280,7 +283,7 @@
                 copy.start()
 
         copies.append(copy)
-        grad = times(window_of(s), grad)
+        grad = times((windows[s, 0], windows[s, 1]), grad)
         if s > 0:
             grad = propagate(grad, tables_ref)
     meta = info_ref[...].astype(F32)
@@ -461,6 +464,7 @@
         "position",
         scratch=[
             pltpu.VMEM((3, 2, WIDTH, WIDTH), F32),
+            pltpu.VMEM((4, 2, WIDTH, WIDTH), F32),
             pltpu.VMEM((5, 2 * HALO, WIDTH), F32),
             pltpu.SMEM((2, 2), jnp.int32),
             pltpu.SemaphoreType.DMA((2, 6)),

time: 83.3 us -> 83.1 us (level)
  no operation moved by 1% of the time
where the time goes in v8:
time: 83.1 us; the launch traced here: 82.9 us
  blocking collectives  24.7 us (30%)
  waiting for transfers between devices  22.7 us (27%)
  starting transfers between devices  22.1 us (27%)
  Pallas kernels  12.3 us (15%)
    all_to_all x2, blocking collectives, among_columns(): lax.all_to_all(x, ('slab', 'tile'), 0, 0, tiled=True, axis_index_groups=g...  24.7 us
    ppermute x4, waiting for transfers between devices, swap_slab(): return lax.ppermute(x, 'slab', [(0, 1), (1, 0)])  13 us
    pallas_call x12, Pallas kernels, call(): pl.pallas_call(kernel, out_shape=tuple((jax.ShapeDtypeStruct(shape, F32)...  12.3 us
    ppermute x5, starting transfers between devices, swap_tile(): return lax.ppermute(x, ('slab', 'tile'), pairs)  10.8 us
    ppermute x5, waiting for transfers between devices, swap_tile(): return lax.ppermute(x, ('slab', 'tile'), pairs)  7.35 us
    ppermute x2, starting transfers between devices, swap_core(): return lax.ppermute(x, 'tile', [(i, i ^ 1) for i in range(count)])  5.98 us
    ppermute x4, starting transfers between devices, swap_slab(): return lax.ppermute(x, 'slab', [(0, 1), (1, 0)])  3.69 us
    ppermute x2, waiting for transfers between devices, swap_core(): return lax.ppermute(x, 'tile', [(i, i ^ 1) for i in range(count)])  2.32 us
  transfers between devices with their start and end apart: 12, of which 5 were waited for; matrix products, arithmetic and copies ran while one was open for 0% of the time, Pallas kernels for 4%

profile of v8, /device:TPU:1, one launch (start us, length us, event | category | flops | bytes accessed | tf_op | source)
XLA Modules:
  0.0 82.9 jit_solution(4387367253211627914)
XLA Ops:
  0.6 0.0 copy-start.3
  0.6 1.5 %collective-permute-start.1 = (f32[2,2,128,384]{3,2,1,0:T(8,128)}, f32[2,2,128,384]{3,2,1,0:T(8,128)S(1)}, u32[]{:S(2)}, u32[]{:S(2)}) collective-permute-start(f32[2,2,128,384]{3,2,1,0:T(8,128)} %own_ref.3), channel_id=1, source_target_pairs={{0,1},{1,0},{2,3},{3,2},{4,5},{5,4},{6,7},{7,6},{8,9},{9,8},{10,11... | collective-permute-start | bytes 2359304 | tf_op jit(solution)/shard_map/ppermute | solution.py:396
  2.1 1.4 %collective-permute-start = (f32[2,2,128,384]{3,2,1,0:T(8,128)}, f32[2,2,128,384]{3,2,1,0:T(8,128)S(1)}, u32[]{:S(2)}, u32[]{:S(2)}) collective-permute-start(f32[2,2,128,384]{3,2,1,0:T(8,128)} %own_ref.3), channel_id=1, source_target_pairs={{0,127},{1,2},{2,1},{3,4},{4,3},{5,6},{6,5},{7,8},{8,7},{9,10},{10... | collective-permute-start | bytes 2359304 | tf_op jit(solution)/shard_map/ppermute | solution.py:396
  3.5 1.3 %core.1 = f32[2,2,128,256]{3,2,1,0:T(8,128)S(1)} custom-call(s32[2,2]{1,0:T(2,128)} %offsets_ref.7, f32[2,2,128,384]{3,2,1,0:T(8,128)} %own_ref.3), custom_call_target="tpu_custom_call" | custom-call | bytes 2000000 | tf_op jit(solution)/shard_map/core/pallas_call | solution.py:375
  4.8 1.7 %collective-permute-start.2 = (f32[2,2,128,256]{3,2,1,0:T(8,128)S(1)}, f32[2,2,128,256]{3,2,1,0:T(8,128)S(1)}, u32[]{:S(2)}, u32[]{:S(2)}) collective-permute-start(f32[2,2,128,256]{3,2,1,0:T(8,128)S(1)} %core.1), channel_id=1, source_target_pairs={{0,64},{64,0},{1,65},{65,1},{2,66},{66,2},{3,67},{67,3},{4,68},{68... | collective-permute-start | bytes 1572872 | tf_op jit(solution)/shard_map/ppermute | solution.py:424
  6.5 0.0 copy-done.3
  6.5 0.0 copy-start.1
  6.6 0.1 reshape.19
  6.6 0.1 add_bitcast_fusion
  6.7 0.0 collective-permute-done.1.beside_ref
  6.7 7.3 %collective-permute-done.across_ref = f32[2,2,128,384]{3,2,1,0:T(8,128)S(1)} collective-permute-done((f32[2,2,128,384]{3,2,1,0:T(8,128)}, f32[2,2,128,384]{3,2,1,0:T(8,128)S(1)}, u32[]{:S(2)}, u32[]{:S(2)}) %collective-permute-start) | collective-permute-done | bytes 786464 | tf_op jit(solution)/shard_map/ppermute | solution.py:396
  14.1 0.1 broadcast_in_dim.8.info_ref
  14.1 0.0 copy-start.2
  14.1 0.1 halo.1
  14.2 0.0 copy-start
  14.2 1.8 %collective-permute-start.3 = (f32[2,2,128,256]{3,2,1,0:T(8,128)S(1)}, f32[2,2,128,256]{3,2,1,0:T(8,128)S(1)}, u32[]{:S(2)}, u32[]{:S(2)}) collective-permute-start(f32[2,2,128,256]{3,2,1,0:T(8,128)S(1)} %halo.1), channel_id=1, source_target_pairs={{0,64},{64,0},{1,65},{65,1},{2,66},{66,2},{3,67},{67,3},{4,68},{68... | collective-permute-start | bytes 1572872 | tf_op jit(solution)/shard_map/ppermute | solution.py:424
  16.0 0.0 copy-done.1
  16.0 1.2 %amp.1.amp_ref = f32[256,256]{1,0:T(8,128)S(1)} custom-call(s32[1]{0:T(128)} %bitcast.1.place_ref, s32[2,2]{1,0:T(2,128)S(1)} %copy-done.3, f32[2,256,256]{2,1,0:T(8,128)S(1)} %copy-done.1), custom_call_target="tpu_custom_call" | custom-call | bytes 2000000 | tf_op jit(solution)/shard_map/amp/pallas_call | solution.py:375
  17.2 0.0 copy-done.2
  17.2 0.8 roll.1.probe_ref
  18.0 0.0 copy-done
  18.0 0.0 copy-start.4
  18.0 0.1 window.1.own_ref
  18.2 0.0 collective-permute-done.2.core_ref
  18.2 10.4 %collective-permute-done.3.halo_ref = f32[2,2,128,256]{3,2,1,0:T(8,128)S(1)} collective-permute-done((f32[2,2,128,256]{3,2,1,0:T(8,128)S(1)}, f32[2,2,128,256]{3,2,1,0:T(8,128)S(1)}, u32[]{:S(2)}, u32[]{:S(2)}) %collective-permute-start.3) | collective-permute-done | bytes 524320 | tf_op jit(solution)/shard_map/ppermute | solution.py:424
  28.6 0.0 copy-done.4
  28.6 7.3 %position.1 = (f32[32,2,8,128]{3,2,1,0:T(8,128)S(1)}, f32[32,2,8,128]{3,2,1,0:T(8,128)S(1)}, f32[4,2,128,256]{3,2,1,0:T(8,128)S(1)}, f32[1032,256]{1,0:T(8,128)S...) custom-call(s32[8,128]{1,0:T(8,128)S(1)} %broadcast_in_dim.8.info_ref, s32[2,2]{1,0:T(2,128)S(1)} %copy-done.3, ...), custom_call_target="tpu_custom_call" | custom-call | flops 3300000000 | bytes 10000000 | tf_op jit(solution)/shard_map/position/pallas_call | solution.py:375
  35.9 4.3 %collective-permute-start.5 = (f32[1032,256]{1,0:T(8,128)S(1)}, f32[1032,256]{1,0:T(8,128)S(1)}, u32[]{:S(2)}, u32[]{:S(2)}) collective-permute-start(f32[1032,256]{1,0:T(8,128)S(1)} %get-tuple-element.12), channel_id=1, source_target_pairs={{0,1},{1,0},{2,3},{3,2},{4,5},{5,4},{6,7},{7,6},{8,9},{9,8},{10,11... | collective-permute-start | bytes 3170312 | tf_op jit(solution)/shard_map/ppermute | solution.py:396
  40.2 0.0 collective-permute-start.4
  40.2 4.6 %collective-permute-start.6 = (f32[32,2,8,128]{3,2,1,0:T(8,128)S(1)}, f32[32,2,8,128]{3,2,1,0:T(8,128)S(1)}, u32[]{:S(2)}, u32[]{:S(2)}) collective-permute-start(f32[32,2,8,128]{3,2,1,0:T(8,128)S(1)} %get-tuple-element.15), channel_id=1, source_target_pairs={{0,1},{1,0},{2,3},{3,2},{4,5},{5,4},{6,7},{7,6},{8,9},{9,8},{10,11... | collective-permute-start | bytes 786440 | tf_op jit(solution)/shard_map/ppermute | solution.py:401
  44.8 1.2 %collective-permute-done.6.got_ref = f32[32,2,8,128]{3,2,1,0:T(8,128)S(1)} collective-permute-done((f32[32,2,8,128]{3,2,1,0:T(8,128)S(1)}, f32[32,2,8,128]{3,2,1,0:T(8,128)S(1)}, u32[]{:S(2)}, u32[]{:S(2)}) %collective-permute-start.6) | collective-permute-done | bytes 262176 | tf_op jit(solution)/shard_map/ppermute | solution.py:401
  46.0 10.6 %all_to_all.10.parts_ref = f32[16,4,8,128]{3,2,1,0:T(8,128)S(1)} all-to-all(f32[16,4,8,128]{3,2,1,0:T(8,128)S(1)} %bitcast.7), channel_id=1, replica_groups={{0,2,4,6,8,10,12,14,16,18,20,22,24,26,28,30},{1,3,5,7,9,11,13,15,17,19,..., dimensions={0} | all-to-all | bytes 524288 | tf_op jit(solution)/shard_map/all_to_all | solution.py:409
  56.6 0.1 collective-permute-start.8
  56.7 2.6 %collective-permute-done.8.got_ref = f32[4,8,128]{2,1,0:T(8,128)S(1)} collective-permute-done((f32[4,8,128]{2,1,0:T(8,128)S(1)}, f32[4,8,128]{2,1,0:T(8,128)S(1)}, u32[]{:S(2)}, u32[]{:S(2)}) %collective-permute-start.8) | collective-permute-done | bytes 16416 | tf_op jit(solution)/shard_map/ppermute | solution.py:424
  59.3 0.0 collective-permute-done.4.early_ref
  59.3 0.0 collective-permute-done.5.beside_ref
  59.3 0.2 sum.1
  59.5 0.1 collective-permute-start.9
  59.6 1.6 %collective-permute-start.10 = (f32[4,8,128]{2,1,0:T(8,128)S(1)}, f32[4,8,128]{2,1,0:T(8,128)S(1)}, u32[]{:S(2)}, u32[]{:S(2)}) collective-permute-start(f32[4,8,128]{2,1,0:T(8,128)S(1)} %add_slabs.1.after_ref.first_ref), channel_id=1, source_target_pairs={{0,96},{1,97},{2,98},{3,99},{4,100},{5,101},{6,102},{7,103},{8,104... | collective-permute-start | bytes 49160 | tf_op jit(solution)/shard_map/ppermute | solution.py:420
  61.3 3.7 %collective-permute-start.7 = (f32[512,256]{1,0:T(8,128)S(1)}, f32[512,256]{1,0:T(8,128)S(1)}, u32[]{:S(2)}, u32[]{:S(2)}) collective-permute-start(f32[512,256]{1,0:T(8,128)S(1)} %get-tuple-element.16), channel_id=1, source_target_pairs={{0,127},{1,2},{2,1},{3,4},{4,3},{5,6},{6,5},{7,8},{8,7},{9,10},{10... | collective-permute-start | bytes 1572872 | tf_op jit(solution)/shard_map/ppermute | solution.py:396
  64.9 0.0 collective-permute-done.10.second_ref
  65.0 14.1 %all_to_all.11 = f32[16,4,8,128]{3,2,1,0:T(8,128)S(1)} all-to-all(f32[16,4,8,128]{3,2,1,0:T(8,128)S(1)} %total.1), channel_id=1, replica_groups={{0,2,4,6,8,10,12,14,16,18,20,22,24,26,28,30},{1,3,5,7,9,11,13,15,17,19,..., dimensions={0} | all-to-all | bytes 524288 | tf_op jit(solution)/shard_map/all_to_all | solution.py:409
  79.1 1.4 %collective-permute-start.11 = (f32[16,4,8,128]{3,2,1,0:T(8,128)S(1)}, f32[16,4,8,128]{3,2,1,0:T(8,128)S(1)}, u32[]{:S(2)}, u32[]{:S(2)}) collective-permute-start(f32[16,4,8,128]{3,2,1,0:T(8,128)S(1)} %all_to_all.11), channel_id=1, source_target_pairs={{0,1},{1,0},{2,3},{3,2},{4,5},{5,4},{6,7},{7,6},{8,9},{9,8},{10,11... | collective-permute-start | bytes 786440 | tf_op jit(solution)/shard_map/ppermute | solution.py:401
  80.5 0.0 collective-permute-done.7.late_ref
  80.5 1.2 %collective-permute-done.11 = f32[16,4,8,128]{3,2,1,0:T(8,128)S(1)} collective-permute-done((f32[16,4,8,128]{3,2,1,0:T(8,128)S(1)}, f32[16,4,8,128]{3,2,1,0:T(8,128)S(1)}, u32[]{:S(2)}, u32[]{:S(2)}) %collective-permute-start.11) | collective-permute-done | bytes 262176 | tf_op jit(solution)/shard_map/ppermute | solution.py:401
  81.6 0.0 collective-permute-done.9.swapped_ref
  81.6 1.3 %finish.1 = (f32[2,2,128,384]{3,2,1,0:T(8,128)}, f32[2,256,256]{2,1,0:T(8,128)}) custom-call(s32[8,128]{1,0:T(8,128)S(1)} %broadcast_in_dim.8.info_ref, f32[4,2,128,256]{3,2,1,0:T(8,128)S(1)} %get-tuple-element.10.core_ref, f32[520,256]{1,0:T(8,128)S(1)} %collective-permute-done.4.early_ref, f32[1032,256]{1,0:T(8,128)S(1)} %collective-permute-done.5.beside_ref, ...), custom_call_target="tpu_custom_call" | custom-call | bytes 2000000 | tf_op jit(solution)/shard_map/finish/pallas_call | solution.py:375
  (6 shorter events, 0.1 us)
Async XLA Ops:
  0.6 5.9 %copy-start.3 = (s32[2,2]{1,0:T(2,128)S(1)}, s32[2,2]{1,0:T(2,128)}, u32[]{:S(2)}) copy-start(s32[2,2]{1,0:T(2,128)} %offsets_ref.7) | copy-start | bytes 52
  0.6 6.1 %collective-permute-start.1 = (f32[2,2,128,384]{3,2,1,0:T(8,128)}, f32[2,2,128,384]{3,2,1,0:T(8,128)S(1)}, u32[]{:S(2)}, u32[]{:S(2)}) collective-permute-start(f32[2,2,128,384]{3,2,1,0:T(8,128)} %own_ref.3), channel_id=1, source_target_pairs={{0,1},{1,0},{2,3},{3,2},{4,5},{5,4},{6,7},{7,6},{8,9},{9,8},{10,11... | collective-permute-start | bytes 2359304 | tf_op jit(solution)/shard_map/ppermute | solution.py:396
  2.1 11.9 %collective-permute-start = (f32[2,2,128,384]{3,2,1,0:T(8,128)}, f32[2,2,128,384]{3,2,1,0:T(8,128)S(1)}, u32[]{:S(2)}, u32[]{:S(2)}) collective-permute-start(f32[2,2,128,384]{3,2,1,0:T(8,128)} %own_ref.3), channel_id=1, source_target_pairs={{0,127},{1,2},{2,1},{3,4},{4,3},{5,6},{6,5},{7,8},{8,7},{9,10},{10... | collective-permute-start | bytes 2359304 | tf_op jit(solution)/shard_map/ppermute | solution.py:396
  4.8 13.4 %collective-permute-start.2 = (f32[2,2,128,256]{3,2,1,0:T(8,128)S(1)}, f32[2,2,128,256]{3,2,1,0:T(8,128)S(1)}, u32[]{:S(2)}, u32[]{:S(2)}) collective-permute-start(f32[2,2,128,256]{3,2,1,0:T(8,128)S(1)} %core.1), channel_id=1, source_target_pairs={{0,64},{64,0},{1,65},{65,1},{2,66},{66,2},{3,67},{67,3},{4,68},{68... | collective-permute-start | bytes 1572872 | tf_op jit(solution)/shard_map/ppermute | solution.py:424
  6.5 9.5 %copy-start.1 = (f32[2,256,256]{2,1,0:T(8,128)S(1)}, f32[2,256,256]{2,1,0:T(8,128)}, u32[]{:S(2)}) copy-start(f32[2,256,256]{2,1,0:T(8,128)} %amp_ref.1) | copy-start | bytes 1572868
  14.1 3.1 %copy-start.2 = (f32[2,256,256]{2,1,0:T(8,128)S(1)}, f32[2,256,256]{2,1,0:T(8,128)}, u32[]{:S(2)}) copy-start(f32[2,256,256]{2,1,0:T(8,128)} %probe_ref.1) | copy-start | bytes 1572868
  14.2 3.8 %copy-start = (f32[2,2,128,384]{3,2,1,0:T(8,128)S(1)}, f32[2,2,128,384]{3,2,1,0:T(8,128)}, u32[]{:S(2)}) copy-start(f32[2,2,128,384]{3,2,1,0:T(8,128)} %own_ref.3) | copy-start | bytes 2359300
  14.2 14.3 %collective-permute-start.3 = (f32[2,2,128,256]{3,2,1,0:T(8,128)S(1)}, f32[2,2,128,256]{3,2,1,0:T(8,128)S(1)}, u32[]{:S(2)}, u32[]{:S(2)}) collective-permute-start(f32[2,2,128,256]{3,2,1,0:T(8,128)S(1)} %halo.1), channel_id=1, source_target_pairs={{0,64},{64,0},{1,65},{65,1},{2,66},{66,2},{3,67},{67,3},{4,68},{68... | collective-permute-start | bytes 1572872 | tf_op jit(solution)/shard_map/ppermute | solution.py:424
  18.0 10.6 %copy-start.4 = (bf16[6,2,2,256,256]{4,3,2,1,0:T(8,128)(2,1)S(1)}, bf16[6,2,2,256,256]{4,3,2,1,0:T(8,128)(2,1)}, u32[]{:S(2)}) copy-start(bf16[6,2,2,256,256]{4,3,2,1,0:T(8,128)(2,1)} %constant.10.clone.tables_ref) | copy-start | bytes 9437188
  35.9 23.4 %collective-permute-start.5 = (f32[1032,256]{1,0:T(8,128)S(1)}, f32[1032,256]{1,0:T(8,128)S(1)}, u32[]{:S(2)}, u32[]{:S(2)}) collective-permute-start(f32[1032,256]{1,0:T(8,128)S(1)} %get-tuple-element.12), channel_id=1, source_target_pairs={{0,1},{1,0},{2,3},{3,2},{4,5},{5,4},{6,7},{7,6},{8,9},{9,8},{10,11... | collective-permute-start | bytes 3170312 | tf_op jit(solution)/shard_map/ppermute | solution.py:396
  40.2 19.1 %collective-permute-start.4 = (f32[520,256]{1,0:T(8,128)S(1)}, f32[520,256]{1,0:T(8,128)S(1)}, u32[]{:S(2)}, u32[]{:S(2)}) collective-permute-start(f32[520,256]{1,0:T(8,128)S(1)} %get-tuple-element.11), channel_id=1, source_target_pairs={{0,127},{1,2},{2,1},{3,4},{4,3},{5,6},{6,5},{7,8},{8,7},{9,10},{10... | collective-permute-start | bytes 1597448 | tf_op jit(solution)/shard_map/ppermute | solution.py:396
  40.2 5.7 %collective-permute-start.6 = (f32[32,2,8,128]{3,2,1,0:T(8,128)S(1)}, f32[32,2,8,128]{3,2,1,0:T(8,128)S(1)}, u32[]{:S(2)}, u32[]{:S(2)}) collective-permute-start(f32[32,2,8,128]{3,2,1,0:T(8,128)S(1)} %get-tuple-element.15), channel_id=1, source_target_pairs={{0,1},{1,0},{2,3},{3,2},{4,5},{5,4},{6,7},{7,6},{8,9},{9,8},{10,11... | collective-permute-start | bytes 786440 | tf_op jit(solution)/shard_map/ppermute | solution.py:401
  56.6 2.7 %collective-permute-start.8 = (f32[4,8,128]{2,1,0:T(8,128)S(1)}, f32[4,8,128]{2,1,0:T(8,128)S(1)}, u32[]{:S(2)}, u32[]{:S(2)}) collective-permute-start(f32[4,8,128]{2,1,0:T(8,128)S(1)} %reduce.1.keep_ref), channel_id=1, source_target_pairs={{0,64},{64,0},{1,65},{65,1},{2,66},{66,2},{3,67},{67,3},{4,68},{68... | collective-permute-start | bytes 49160 | tf_op jit(solution)/shard_map/ppermute | solution.py:424
  59.5 22.1 %collective-permute-start.9 = (f32[2,2,128,384]{3,2,1,0:T(8,128)S(1)}, f32[2,2,128,384]{3,2,1,0:T(8,128)S(1)}, u32[]{:S(2)}, u32[]{:S(2)}) collective-permute-start(f32[2,2,128,384]{3,2,1,0:T(8,128)S(1)} %sum.1), channel_id=1, source_target_pairs={{0,64},{64,0},{1,65},{65,1},{2,66},{66,2},{3,67},{67,3},{4,68},{68... | collective-permute-start | bytes 2359304 | tf_op jit(solution)/shard_map/ppermute | solution.py:424
  59.6 5.3 %collective-permute-start.10 = (f32[4,8,128]{2,1,0:T(8,128)S(1)}, f32[4,8,128]{2,1,0:T(8,128)S(1)}, u32[]{:S(2)}, u32[]{:S(2)}) collective-permute-start(f32[4,8,128]{2,1,0:T(8,128)S(1)} %add_slabs.1.after_ref.first_ref), channel_id=1, source_target_pairs={{0,96},{1,97},{2,98},{3,99},{4,100},{5,101},{6,102},{7,103},{8,104... | collective-permute-start | bytes 49160 | tf_op jit(solution)/shard_map/ppermute | solution.py:420
  61.3 19.2 %collective-permute-start.7 = (f32[512,256]{1,0:T(8,128)S(1)}, f32[512,256]{1,0:T(8,128)S(1)}, u32[]{:S(2)}, u32[]{:S(2)}) collective-permute-start(f32[512,256]{1,0:T(8,128)S(1)} %get-tuple-element.16), channel_id=1, source_target_pairs={{0,127},{1,2},{2,1},{3,4},{4,3},{5,6},{6,5},{7,8},{8,7},{9,10},{10... | collective-permute-start | bytes 1572872 | tf_op jit(solution)/shard_map/ppermute | solution.py:396
  79.1 2.6 %collective-permute-start.11 = (f32[16,4,8,128]{3,2,1,0:T(8,128)S(1)}, f32[16,4,8,128]{3,2,1,0:T(8,128)S(1)}, u32[]{:S(2)}, u32[]{:S(2)}) collective-permute-start(f32[16,4,8,128]{3,2,1,0:T(8,128)S(1)} %all_to_all.11), channel_id=1, source_target_pairs={{0,1},{1,0},{2,3},{3,2},{4,5},{5,4},{6,7},{7,6},{8,9},{9,8},{10,11... | collective-permute-start | bytes 786440 | tf_op jit(solution)/shard_map/ppermute | solution.py:401

commit v9 on v8

--- a/solution.py
+++ b/solution.py
@@ -350,23 +350,16 @@
     add_halos(info_ref, core_ref, early_ref, early_ref, beside_ref, out_ref, 2)
 
 
-def finish_kernel(
-    info_ref,
-    core_ref,
-    early_ref,
-    beside_ref,
-    late_ref,
-    swapped_ref,
-    keep_ref,
-    got_ref,
-    object_out,
-    probe_out,
-):
-    add_halos(info_ref, core_ref, late_ref, early_ref, beside_ref, object_out, 0, swapped_ref)
+def object_kernel(info_ref, core_ref, early_ref, beside_ref, late_ref, swapped_ref, after_ref, out_ref, token_ref):
+    token_ref[...] = jnp.zeros(token_ref.shape, F32)
+    add_halos(info_ref, core_ref, late_ref, early_ref, beside_ref, out_ref, 0, swapped_ref)
+
+
+def probe_kernel(after_ref, keep_ref, got_ref, out_ref):
     odd = here()[1]
     for ref, which in ((keep_ref, odd), (got_ref, 1 - odd)):
         for h in range(2):
-            probe_out[which, :, h * HALF : (h + 1) * HALF] = ref[:, h].reshape(WIDTH, HALF)
+            out_ref[which, :, h * HALF : (h + 1) * HALF] = ref[:, h].reshape(WIDTH, HALF)
 
 
 def call(kernel, shapes, smem, vmem, name, scratch=(), flops=0, nbytes=2_000_000, ins=None, outs=None, vmem_limit=40):
@@ -484,12 +477,14 @@
     got = swap_slab(call(sum_kernel, band, (), sides + (kept,), "sum"))
     kept = call(total_kernel, parts, (), (kept, swap_far(kept)), "total")
     kept = among_columns(kept)
-    object_grad, probe_grad = call(
-        finish_kernel,
-        (band, probe.shape),
+    other = swap_core(kept)
+    object_grad, token = call(object_kernel, (band, (8, HALF)), (), sides + (late, got, kept), "object")
+    probe_grad = call(
+        probe_kernel,
+        probe.shape,
         (),
-        sides + (late, got, kept.reshape(tiles), swap_core(kept).reshape(tiles)),
-        "finish",
+        (token, kept.reshape(tiles), other.reshape(tiles)),
+        "probe",
     )
     return object_grad, probe_grad
 

time: 83.1 us -> 82.7 us (level)
  waiting for transfers between devices: 22.7 us -> 21.5 us
    ppermute x2, waiting for transfers between devices: 2.32 us -> 1.18 us  [swap_core(): return lax.ppermute(x, 'tile', [(i, i ^ 1) for i in range(count)])]
    pallas_call x12 -> x13, Pallas kernels: 12.3 us -> 13 us  [call(): pl.pallas_call(kernel, out_shape=tuple((jax.ShapeDtypeStruct(shape, F32)...]
  transfers between devices with their start and end apart: 12 -> 12, of which waited for: 5 -> 4; matrix products, arithmetic and copies ran while one was open for 0% -> 0% of each run, Pallas kernels for 4% -> 6%
where the time goes in v9:
time: 82.7 us; the launch traced here: 82.5 us
  blocking collectives  24.7 us (30%)
  starting transfers between devices  22.1 us (27%)
  waiting for transfers between devices  21.5 us (26%)
  Pallas kernels  13 us (16%)
    all_to_all x2, blocking collectives, among_columns(): lax.all_to_all(x, ('slab', 'tile'), 0, 0, tiled=True, axis_index_groups=g...  24.7 us
    pallas_call x13, Pallas kernels, call(): pl.pallas_call(kernel, out_shape=tuple((jax.ShapeDtypeStruct(shape, F32)...  13 us
    ppermute x4, waiting for transfers between devices, swap_slab(): return lax.ppermute(x, 'slab', [(0, 1), (1, 0)])  13 us
    ppermute x5, starting transfers between devices, swap_tile(): return lax.ppermute(x, ('slab', 'tile'), pairs)  10.8 us
    ppermute x5, waiting for transfers between devices, swap_tile(): return lax.ppermute(x, ('slab', 'tile'), pairs)  7.35 us
    ppermute x2, starting transfers between devices, swap_core(): return lax.ppermute(x, 'tile', [(i, i ^ 1) for i in range(count)])  5.98 us
    ppermute x4, starting transfers between devices, swap_slab(): return lax.ppermute(x, 'slab', [(0, 1), (1, 0)])  3.69 us
  transfers between devices with their start and end apart: 12, of which 4 were waited for; matrix products, arithmetic and copies ran while one was open for 0% of the time, Pallas kernels for 6%

profile of v9, /device:TPU:1, one launch (start us, length us, event | category | flops | bytes accessed | tf_op | source)
XLA Modules:
  0.0 82.5 jit_solution(12964475146044370195)
XLA Ops:
  0.6 0.0 copy-start.3
  0.6 1.5 %collective-permute-start.1 = (f32[2,2,128,384]{3,2,1,0:T(8,128)}, f32[2,2,128,384]{3,2,1,0:T(8,128)S(1)}, u32[]{:S(2)}, u32[]{:S(2)}) collective-permute-start(f32[2,2,128,384]{3,2,1,0:T(8,128)} %own_ref.3), channel_id=1, source_target_pairs={{0,1},{1,0},{2,3},{3,2},{4,5},{5,4},{6,7},{7,6},{8,9},{9,8},{10,11... | collective-permute-start | bytes 2359304 | tf_op jit(solution)/shard_map/ppermute | solution.py:389
  2.1 1.4 %collective-permute-start = (f32[2,2,128,384]{3,2,1,0:T(8,128)}, f32[2,2,128,384]{3,2,1,0:T(8,128)S(1)}, u32[]{:S(2)}, u32[]{:S(2)}) collective-permute-start(f32[2,2,128,384]{3,2,1,0:T(8,128)} %own_ref.3), channel_id=1, source_target_pairs={{0,127},{1,2},{2,1},{3,4},{4,3},{5,6},{6,5},{7,8},{8,7},{9,10},{10... | collective-permute-start | bytes 2359304 | tf_op jit(solution)/shard_map/ppermute | solution.py:389
  3.5 1.3 %core.1 = f32[2,2,128,256]{3,2,1,0:T(8,128)S(1)} custom-call(s32[2,2]{1,0:T(2,128)} %offsets_ref.7, f32[2,2,128,384]{3,2,1,0:T(8,128)} %own_ref.3), custom_call_target="tpu_custom_call" | custom-call | bytes 2000000 | tf_op jit(solution)/shard_map/core/pallas_call | solution.py:368
  4.8 1.7 %collective-permute-start.2 = (f32[2,2,128,256]{3,2,1,0:T(8,128)S(1)}, f32[2,2,128,256]{3,2,1,0:T(8,128)S(1)}, u32[]{:S(2)}, u32[]{:S(2)}) collective-permute-start(f32[2,2,128,256]{3,2,1,0:T(8,128)S(1)} %core.1), channel_id=1, source_target_pairs={{0,64},{64,0},{1,65},{65,1},{2,66},{66,2},{3,67},{67,3},{4,68},{68... | collective-permute-start | bytes 1572872 | tf_op jit(solution)/shard_map/ppermute | solution.py:417
  6.5 0.0 copy-done.3
  6.5 0.0 copy-start.1
  6.6 0.1 reshape.19
  6.6 0.1 add_bitcast_fusion
  6.7 0.0 collective-permute-done.1.beside_ref
  6.7 7.3 %collective-permute-done.across_ref = f32[2,2,128,384]{3,2,1,0:T(8,128)S(1)} collective-permute-done((f32[2,2,128,384]{3,2,1,0:T(8,128)}, f32[2,2,128,384]{3,2,1,0:T(8,128)S(1)}, u32[]{:S(2)}, u32[]{:S(2)}) %collective-permute-start) | collective-permute-done | bytes 786464 | tf_op jit(solution)/shard_map/ppermute | solution.py:389
  14.1 0.1 broadcast_in_dim.8.info_ref
  14.1 0.0 copy-start.2
  14.1 0.1 halo.1
  14.2 0.0 copy-start
  14.2 1.8 %collective-permute-start.3 = (f32[2,2,128,256]{3,2,1,0:T(8,128)S(1)}, f32[2,2,128,256]{3,2,1,0:T(8,128)S(1)}, u32[]{:S(2)}, u32[]{:S(2)}) collective-permute-start(f32[2,2,128,256]{3,2,1,0:T(8,128)S(1)} %halo.1), channel_id=1, source_target_pairs={{0,64},{64,0},{1,65},{65,1},{2,66},{66,2},{3,67},{67,3},{4,68},{68... | collective-permute-start | bytes 1572872 | tf_op jit(solution)/shard_map/ppermute | solution.py:417
  16.0 0.0 copy-done.1
  16.0 1.2 %amp.1.amp_ref = f32[256,256]{1,0:T(8,128)S(1)} custom-call(s32[1]{0:T(128)} %bitcast.1.place_ref, s32[2,2]{1,0:T(2,128)S(1)} %copy-done.3, f32[2,256,256]{2,1,0:T(8,128)S(1)} %copy-done.1), custom_call_target="tpu_custom_call" | custom-call | bytes 2000000 | tf_op jit(solution)/shard_map/amp/pallas_call | solution.py:368
  17.2 0.0 copy-done.2
  17.2 0.8 roll.1.probe_ref
  18.0 0.0 copy-done
  18.0 0.0 copy-start.4
  18.0 0.1 window.1.own_ref
  18.2 0.0 collective-permute-done.2.core_ref
  18.2 10.4 %collective-permute-done.3.halo_ref = f32[2,2,128,256]{3,2,1,0:T(8,128)S(1)} collective-permute-done((f32[2,2,128,256]{3,2,1,0:T(8,128)S(1)}, f32[2,2,128,256]{3,2,1,0:T(8,128)S(1)}, u32[]{:S(2)}, u32[]{:S(2)}) %collective-permute-start.3) | collective-permute-done | bytes 524320 | tf_op jit(solution)/shard_map/ppermute | solution.py:417
  28.6 0.0 copy-done.4
  28.6 7.3 %position.1 = (f32[32,2,8,128]{3,2,1,0:T(8,128)S(1)}, f32[32,2,8,128]{3,2,1,0:T(8,128)S(1)}, f32[4,2,128,256]{3,2,1,0:T(8,128)S(1)}, f32[1032,256]{1,0:T(8,128)S...) custom-call(s32[8,128]{1,0:T(8,128)S(1)} %broadcast_in_dim.8.info_ref, s32[2,2]{1,0:T(2,128)S(1)} %copy-done.3, ...), custom_call_target="tpu_custom_call" | custom-call | flops 3300000000 | bytes 10000000 | tf_op jit(solution)/shard_map/position/pallas_call | solution.py:368
  35.9 4.3 %collective-permute-start.5 = (f32[1032,256]{1,0:T(8,128)S(1)}, f32[1032,256]{1,0:T(8,128)S(1)}, u32[]{:S(2)}, u32[]{:S(2)}) collective-permute-start(f32[1032,256]{1,0:T(8,128)S(1)} %get-tuple-element.14), channel_id=1, source_target_pairs={{0,1},{1,0},{2,3},{3,2},{4,5},{5,4},{6,7},{7,6},{8,9},{9,8},{10,11... | collective-permute-start | bytes 3170312 | tf_op jit(solution)/shard_map/ppermute | solution.py:389
  40.2 0.0 collective-permute-start.4
  40.2 4.6 %collective-permute-start.6 = (f32[32,2,8,128]{3,2,1,0:T(8,128)S(1)}, f32[32,2,8,128]{3,2,1,0:T(8,128)S(1)}, u32[]{:S(2)}, u32[]{:S(2)}) collective-permute-start(f32[32,2,8,128]{3,2,1,0:T(8,128)S(1)} %get-tuple-element.17), channel_id=1, source_target_pairs={{0,1},{1,0},{2,3},{3,2},{4,5},{5,4},{6,7},{7,6},{8,9},{9,8},{10,11... | collective-permute-start | bytes 786440 | tf_op jit(solution)/shard_map/ppermute | solution.py:394
  44.8 1.2 %collective-permute-done.6.got_ref = f32[32,2,8,128]{3,2,1,0:T(8,128)S(1)} collective-permute-done((f32[32,2,8,128]{3,2,1,0:T(8,128)S(1)}, f32[32,2,8,128]{3,2,1,0:T(8,128)S(1)}, u32[]{:S(2)}, u32[]{:S(2)}) %collective-permute-start.6) | collective-permute-done | bytes 262176 | tf_op jit(solution)/shard_map/ppermute | solution.py:394
  46.0 10.6 %all_to_all.10.parts_ref = f32[16,4,8,128]{3,2,1,0:T(8,128)S(1)} all-to-all(f32[16,4,8,128]{3,2,1,0:T(8,128)S(1)} %bitcast.7), channel_id=1, replica_groups={{0,2,4,6,8,10,12,14,16,18,20,22,24,26,28,30},{1,3,5,7,9,11,13,15,17,19,..., dimensions={0} | all-to-all | bytes 524288 | tf_op jit(solution)/shard_map/all_to_all | solution.py:402
  56.6 0.1 collective-permute-start.8
  56.7 2.6 %collective-permute-done.8.got_ref = f32[4,8,128]{2,1,0:T(8,128)S(1)} collective-permute-done((f32[4,8,128]{2,1,0:T(8,128)S(1)}, f32[4,8,128]{2,1,0:T(8,128)S(1)}, u32[]{:S(2)}, u32[]{:S(2)}) %collective-permute-start.8) | collective-permute-done | bytes 16416 | tf_op jit(solution)/shard_map/ppermute | solution.py:417
  59.3 0.0 collective-permute-done.4.early_ref
  59.3 0.0 collective-permute-done.5.beside_ref
  59.3 0.2 sum.1
  59.5 0.1 collective-permute-start.9
  59.6 1.6 %collective-permute-start.10 = (f32[4,8,128]{2,1,0:T(8,128)S(1)}, f32[4,8,128]{2,1,0:T(8,128)S(1)}, u32[]{:S(2)}, u32[]{:S(2)}) collective-permute-start(f32[4,8,128]{2,1,0:T(8,128)S(1)} %add_slabs.1.after_ref.first_ref), channel_id=1, source_target_pairs={{0,96},{1,97},{2,98},{3,99},{4,100},{5,101},{6,102},{7,103},{8,104... | collective-permute-start | bytes 49160 | tf_op jit(solution)/shard_map/ppermute | solution.py:413
  61.3 3.7 %collective-permute-start.7 = (f32[512,256]{1,0:T(8,128)S(1)}, f32[512,256]{1,0:T(8,128)S(1)}, u32[]{:S(2)}, u32[]{:S(2)}) collective-permute-start(f32[512,256]{1,0:T(8,128)S(1)} %get-tuple-element.18), channel_id=1, source_target_pairs={{0,127},{1,2},{2,1},{3,4},{4,3},{5,6},{6,5},{7,8},{8,7},{9,10},{10... | collective-permute-start | bytes 1572872 | tf_op jit(solution)/shard_map/ppermute | solution.py:389
  64.9 0.0 collective-permute-done.10.second_ref
  65.0 14.1 %all_to_all.11.after_ref = f32[16,4,8,128]{3,2,1,0:T(8,128)S(1)} all-to-all(f32[16,4,8,128]{3,2,1,0:T(8,128)S(1)} %total.1), channel_id=1, replica_groups={{0,2,4,6,8,10,12,14,16,18,20,22,24,26,28,30},{1,3,5,7,9,11,13,15,17,19,..., dimensions={0} | all-to-all | bytes 524288 | tf_op jit(solution)/shard_map/all_to_all | solution.py:402
  79.1 1.4 %collective-permute-start.11 = (f32[16,4,8,128]{3,2,1,0:T(8,128)S(1)}, f32[16,4,8,128]{3,2,1,0:T(8,128)S(1)}, u32[]{:S(2)}, u32[]{:S(2)}) collective-permute-start(f32[16,4,8,128]{3,2,1,0:T(8,128)S(1)} %all_to_all.11.after_ref), channel_id=1, source_target_pairs={{0,1},{1,0},{2,3},{3,2},{4,5},{5,4},{6,7},{7,6},{8,9},{9,8},{10,11... | collective-permute-start | bytes 786440 | tf_op jit(solution)/shard_map/ppermute | solution.py:394
  80.5 0.0 collective-permute-done.7.late_ref
  80.5 0.0 collective-permute-done.9.swapped_ref
  80.5 1.1 %object.1 = (f32[2,2,128,384]{3,2,1,0:T(8,128)}, f32[8,128]{1,0:T(8,128)S(1)}) custom-call(s32[8,128]{1,0:T(8,128)S(1)} %broadcast_in_dim.8.info_ref, f32[4,2,128,256]{3,2,1,0:T(8,128)S(1)} %get-tuple-element.12.core_ref, f32[520,256]{1,0:T(8,128)S(1)} %collective-permute-done.4.early_ref, f32[1032,256]{1,0:T(8,128)S(1)} %collective-permute-done.5.beside_ref, ...), custom_call_target="tpu_custom_call" | custom-call | bytes 2000000 | tf_op jit(solution)/shard_map/object/pallas_call | solution.py:368
  81.6 0.0 collective-permute-done.11
  81.6 0.9 %probe.1 = f32[2,256,256]{2,1,0:T(8,128)} custom-call(f32[8,128]{1,0:T(8,128)S(1)} %get-tuple-element.21.after_ref, f32[32,2,8,128]{3,2,1,0:T(8,128)S(1)} %bitcast.6, f32[32,2,8,128]{3,2,1,0:T(8,128)S(1)} %bitcast.8), custom_call_target="tpu_custom_call" | custom-call | bytes 2000000 | tf_op jit(solution)/shard_map/probe/pallas_call | solution.py:368
  (6 shorter events, 0.1 us)
Async XLA Ops:
  0.6 5.9 %copy-start.3 = (s32[2,2]{1,0:T(2,128)S(1)}, s32[2,2]{1,0:T(2,128)}, u32[]{:S(2)}) copy-start(s32[2,2]{1,0:T(2,128)} %offsets_ref.7) | copy-start | bytes 52
  0.6 6.1 %collective-permute-start.1 = (f32[2,2,128,384]{3,2,1,0:T(8,128)}, f32[2,2,128,384]{3,2,1,0:T(8,128)S(1)}, u32[]{:S(2)}, u32[]{:S(2)}) collective-permute-start(f32[2,2,128,384]{3,2,1,0:T(8,128)} %own_ref.3), channel_id=1, source_target_pairs={{0,1},{1,0},{2,3},{3,2},{4,5},{5,4},{6,7},{7,6},{8,9},{9,8},{10,11... | collective-permute-start | bytes 2359304 | tf_op jit(solution)/shard_map/ppermute | solution.py:389
  2.1 11.9 %collective-permute-start = (f32[2,2,128,384]{3,2,1,0:T(8,128)}, f32[2,2,128,384]{3,2,1,0:T(8,128)S(1)}, u32[]{:S(2)}, u32[]{:S(2)}) collective-permute-start(f32[2,2,128,384]{3,2,1,0:T(8,128)} %own_ref.3), channel_id=1, source_target_pairs={{0,127},{1,2},{2,1},{3,4},{4,3},{5,6},{6,5},{7,8},{8,7},{9,10},{10... | collective-permute-start | bytes 2359304 | tf_op jit(solution)/shard_map/ppermute | solution.py:389
  4.8 13.4 %collective-permute-start.2 = (f32[2,2,128,256]{3,2,1,0:T(8,128)S(1)}, f32[2,2,128,256]{3,2,1,0:T(8,128)S(1)}, u32[]{:S(2)}, u32[]{:S(2)}) collective-permute-start(f32[2,2,128,256]{3,2,1,0:T(8,128)S(1)} %core.1), channel_id=1, source_target_pairs={{0,64},{64,0},{1,65},{65,1},{2,66},{66,2},{3,67},{67,3},{4,68},{68... | collective-permute-start | bytes 1572872 | tf_op jit(solution)/shard_map/ppermute | solution.py:417
  6.5 9.5 %copy-start.1 = (f32[2,256,256]{2,1,0:T(8,128)S(1)}, f32[2,256,256]{2,1,0:T(8,128)}, u32[]{:S(2)}) copy-start(f32[2,256,256]{2,1,0:T(8,128)} %amp_ref.1) | copy-start | bytes 1572868
  14.1 3.1 %copy-start.2 = (f32[2,256,256]{2,1,0:T(8,128)S(1)}, f32[2,256,256]{2,1,0:T(8,128)}, u32[]{:S(2)}) copy-start(f32[2,256,256]{2,1,0:T(8,128)} %probe_ref.1) | copy-start | bytes 1572868
  14.2 3.8 %copy-start = (f32[2,2,128,384]{3,2,1,0:T(8,128)S(1)}, f32[2,2,128,384]{3,2,1,0:T(8,128)}, u32[]{:S(2)}) copy-start(f32[2,2,128,384]{3,2,1,0:T(8,128)} %own_ref.3) | copy-start | bytes 2359300
  14.2 14.3 %collective-permute-start.3 = (f32[2,2,128,256]{3,2,1,0:T(8,128)S(1)}, f32[2,2,128,256]{3,2,1,0:T(8,128)S(1)}, u32[]{:S(2)}, u32[]{:S(2)}) collective-permute-start(f32[2,2,128,256]{3,2,1,0:T(8,128)S(1)} %halo.1), channel_id=1, source_target_pairs={{0,64},{64,0},{1,65},{65,1},{2,66},{66,2},{3,67},{67,3},{4,68},{68... | collective-permute-start | bytes 1572872 | tf_op jit(solution)/shard_map/ppermute | solution.py:417
  18.0 10.6 %copy-start.4 = (bf16[6,2,2,256,256]{4,3,2,1,0:T(8,128)(2,1)S(1)}, bf16[6,2,2,256,256]{4,3,2,1,0:T(8,128)(2,1)}, u32[]{:S(2)}) copy-start(bf16[6,2,2,256,256]{4,3,2,1,0:T(8,128)(2,1)} %constant.10.clone.tables_ref) | copy-start | bytes 9437188
  35.9 23.4 %collective-permute-start.5 = (f32[1032,256]{1,0:T(8,128)S(1)}, f32[1032,256]{1,0:T(8,128)S(1)}, u32[]{:S(2)}, u32[]{:S(2)}) collective-permute-start(f32[1032,256]{1,0:T(8,128)S(1)} %get-tuple-element.14), channel_id=1, source_target_pairs={{0,1},{1,0},{2,3},{3,2},{4,5},{5,4},{6,7},{7,6},{8,9},{9,8},{10,11... | collective-permute-start | bytes 3170312 | tf_op jit(solution)/shard_map/ppermute | solution.py:389
  40.2 19.1 %collective-permute-start.4 = (f32[520,256]{1,0:T(8,128)S(1)}, f32[520,256]{1,0:T(8,128)S(1)}, u32[]{:S(2)}, u32[]{:S(2)}) collective-permute-start(f32[520,256]{1,0:T(8,128)S(1)} %get-tuple-element.13), channel_id=1, source_target_pairs={{0,127},{1,2},{2,1},{3,4},{4,3},{5,6},{6,5},{7,8},{8,7},{9,10},{10... | collective-permute-start | bytes 1597448 | tf_op jit(solution)/shard_map/ppermute | solution.py:389
  40.2 5.7 %collective-permute-start.6 = (f32[32,2,8,128]{3,2,1,0:T(8,128)S(1)}, f32[32,2,8,128]{3,2,1,0:T(8,128)S(1)}, u32[]{:S(2)}, u32[]{:S(2)}) collective-permute-start(f32[32,2,8,128]{3,2,1,0:T(8,128)S(1)} %get-tuple-element.17), channel_id=1, source_target_pairs={{0,1},{1,0},{2,3},{3,2},{4,5},{5,4},{6,7},{7,6},{8,9},{9,8},{10,11... | collective-permute-start | bytes 786440 | tf_op jit(solution)/shard_map/ppermute | solution.py:394
  56.6 2.7 %collective-permute-start.8 = (f32[4,8,128]{2,1,0:T(8,128)S(1)}, f32[4,8,128]{2,1,0:T(8,128)S(1)}, u32[]{:S(2)}, u32[]{:S(2)}) collective-permute-start(f32[4,8,128]{2,1,0:T(8,128)S(1)} %reduce.1.keep_ref), channel_id=1, source_target_pairs={{0,64},{64,0},{1,65},{65,1},{2,66},{66,2},{3,67},{67,3},{4,68},{68... | collective-permute-start | bytes 49160 | tf_op jit(solution)/shard_map/ppermute | solution.py:417
  59.5 20.9 %collective-permute-start.9 = (f32[2,2,128,384]{3,2,1,0:T(8,128)S(1)}, f32[2,2,128,384]{3,2,1,0:T(8,128)S(1)}, u32[]{:S(2)}, u32[]{:S(2)}) collective-permute-start(f32[2,2,128,384]{3,2,1,0:T(8,128)S(1)} %sum.1), channel_id=1, source_target_pairs={{0,64},{64,0},{1,65},{65,1},{2,66},{66,2},{3,67},{67,3},{4,68},{68... | collective-permute-start | bytes 2359304 | tf_op jit(solution)/shard_map/ppermute | solution.py:417
  59.6 5.3 %collective-permute-start.10 = (f32[4,8,128]{2,1,0:T(8,128)S(1)}, f32[4,8,128]{2,1,0:T(8,128)S(1)}, u32[]{:S(2)}, u32[]{:S(2)}) collective-permute-start(f32[4,8,128]{2,1,0:T(8,128)S(1)} %add_slabs.1.after_ref.first_ref), channel_id=1, source_target_pairs={{0,96},{1,97},{2,98},{3,99},{4,100},{5,101},{6,102},{7,103},{8,104... | collective-permute-start | bytes 49160 | tf_op jit(solution)/shard_map/ppermute | solution.py:413
  61.3 19.2 %collective-permute-start.7 = (f32[512,256]{1,0:T(8,128)S(1)}, f32[512,256]{1,0:T(8,128)S(1)}, u32[]{:S(2)}, u32[]{:S(2)}) collective-permute-start(f32[512,256]{1,0:T(8,128)S(1)} %get-tuple-element.18), channel_id=1, source_target_pairs={{0,127},{1,2},{2,1},{3,4},{4,3},{5,6},{6,5},{7,8},{8,7},{9,10},{10... | collective-permute-start | bytes 1572872 | tf_op jit(solution)/shard_map/ppermute | solution.py:389
  79.1 2.6 %collective-permute-start.11 = (f32[16,4,8,128]{3,2,1,0:T(8,128)S(1)}, f32[16,4,8,128]{3,2,1,0:T(8,128)S(1)}, u32[]{:S(2)}, u32[]{:S(2)}) collective-permute-start(f32[16,4,8,128]{3,2,1,0:T(8,128)S(1)} %all_to_all.11.after_ref), channel_id=1, source_target_pairs={{0,1},{1,0},{2,3},{3,2},{4,5},{5,4},{6,7},{7,6},{8,9},{9,8},{10,11... | collective-permute-start | bytes 786440 | tf_op jit(solution)/shard_map/ppermute | solution.py:394

commit v10 on v9

--- a/solution.py
+++ b/solution.py
@@ -185,13 +185,13 @@
     out_ref[...] = sum(dot(part, cols) for part in parts(x))
 
 
-def halo_kernel(info_ref, across_ref, beside_ref, out_ref):
+def halo_kernel(info_ref, across_ref, beside_ref, first_out, second_out):
     from_beside, kept = masks(info_ref, 1)
-    for j in range(2):
+    for j, out_ref in enumerate((first_out, second_out)):
         for c in range(2):
             left, right = halo_of(across_ref, beside_ref, (j, c), from_beside, kept)
-            out_ref[j, c, :, :HALF] = left
-            out_ref[j, c, :, HALF:] = right
+            out_ref[c, :, :HALF] = left
+            out_ref[c, :, HALF:] = right
 
 
 def window_kernel(info_ref, own_ref, across_ref, beside_ref, out_ref):
@@ -206,6 +206,29 @@
             out_ref[j, c, HALO:, HALF:] = right
 
 
+def selector(info_ref, own_ref, core_ref, halo_refs):
+    place, odd, turned = here()
+    from_beside = masks(info_ref, 0)[0]
+    turned = jnp.where(jnp.concatenate([from_beside, from_beside], axis=1), 0, turned)
+
+    def window_of(s):
+        mine = jnp.where(place == s // 2, 1, 0)
+        out = []
+        for c in range(2):
+            halo = jnp.where(turned == mine, halo_refs[s % 2][c], own_ref[s % 2, c, :HALO])
+            core = jnp.where(mine == 1, own_ref[s % 2, c, HALO:], core_ref[s % 2, c])
+            out.append(jnp.concatenate([halo, core], axis=0))
+        return out
+
+    return window_of
+
+
+def first_kernel(info_ref, tables_ref, probe_ref, own_ref, core_ref, halo_ref, wave_out, window_out):
+    window = selector(info_ref, own_ref, core_ref, (halo_ref, None))(0)
+    window_out[0], window_out[1] = window
+    wave_out[0], wave_out[1] = propagate(times((probe_ref[0], probe_ref[1]), window), tables_ref)
+
+
 def position_kernel(
     info_ref,
     offsets_ref,
@@ -215,6 +238,9 @@
     own_ref,
     core_ref,
     halo_ref,
+    second_halo_ref,
+    first_wave_ref,
+    first_window_ref,
     keep_out,
     send_out,
     core_out,
@@ -227,31 +253,28 @@
     offsets,
     sems,
 ):
-    place, odd, turned = here()
+    place, odd, across_turned = here()
     load = pltpu.make_async_copy(offsets_ref, offsets, sems.at[0, 5])
     load.start()
-    from_beside = masks(info_ref, 0)[0]
-    across_turned = turned
-    turned = jnp.where(jnp.concatenate([from_beside, from_beside], axis=1), 0, turned)
-
-    def window_of(s):
-        mine = jnp.where(place == s // 2, 1, 0)
-        out = []
-        for c in range(2):
-            halo = jnp.where(turned == mine, halo_ref[s % 2, c], own_ref[s % 2, c, :HALO])
-            core = jnp.where(mine == 1, own_ref[s % 2, c, HALO:], core_ref[s % 2, c])
-            out.append(jnp.concatenate([halo, core], axis=0))
-        return out
-
-    wave = (probe_ref[0], probe_ref[1])
-    for s in range(4):
-        if s > 0:
-            waves[s - 1, 0], waves[s - 1, 1] = wave
+    window_of = selector(info_ref, own_ref, core_ref, (halo_ref, second_halo_ref))
+    wave = (first_wave_ref[0], first_wave_ref[1])
+    for s in range(1, 4):
+        if s > 1:
+            waves[s - 2, 0], waves[s - 2, 1] = wave
         window = window_of(s)
-        windows[s, 0], windows[s, 1] = window
+        windows[s - 1, 0], windows[s - 1, 1] = window
         prod = times(wave, window)
         if s < 3:
             wave = propagate(prod, tables_ref)
+
+    def before(s):
+        ref = (probe_ref, first_wave_ref, waves.at[0], waves.at[1])[s]
+        return ref[0], ref[1]
+
+    def window_at(s):
+        ref = first_window_ref if s == 0 else windows.at[s - 1]
+        return ref[0], ref[1]
+
     field = right_mult((fold(prod[0]), fold(prod[1])), tables_ref, FAR_RIGHT)
     field = left_mult(field, tables_ref, FAR_LEFT)
     model = jnp.sqrt(field[0] * field[0] + field[1] * field[1] + 1.0)
@@ -262,8 +285,7 @@
     grad = (fold(grad[0]), fold(grad[1]))
     copies = []
     for s in range(3, -1, -1):
-        wave = (waves[s - 1, 0], waves[s - 1, 1]) if s > 0 else (probe_ref[0], probe_ref[1])
-        object_grad = times(wave, grad)
+        object_grad = times(before(s), grad)
         slot = jnp.where(place == s // 2, s % 2, 2 + s % 2)
         for c in range(2):
             value = object_grad[c] if c == 0 else -object_grad[c]
@@ -283,7 +305,7 @@
                 copy.start()
 
         copies.append(copy)
-        grad = times((windows[s, 0], windows[s, 1]), grad)
+        grad = times(window_at(s), grad)
         if s > 0:
             grad = propagate(grad, tables_ref)
     meta = info_ref[...].astype(F32)
@@ -445,24 +467,32 @@
     beside, across = swap_tile(own, 1), swap_tile(own, 0)
     rolled = call(roll_probe_kernel, (2, WIDTH, WIDTH), where, (probe,), "roll")
     amp = call(amp_kernel, (WIDTH, WIDTH), where, (amplitudes,), "amp")
-    halo = swap_slab(call(halo_kernel, part, (), (info, across, beside), "halo"))
+    halo, second_halo = call(halo_kernel, (part[1:],) * 2, (), (info, across, beside), "halo")
+    halo, second_halo = swap_slab(halo), swap_slab(second_halo)
     windows = call(window_kernel, whole, (), (info, own, across, beside), "window")
 
+    wave, window = call(
+        first_kernel,
+        (probe.shape, probe.shape),
+        (),
+        (info, tables, rolled, windows, core, halo),
+        "first",
+    )
     tiles = (WIDTH // 8, 2, 8, HALF)
     keep, send, cores, beside, early, late = call(
         position_kernel,
         (tiles, tiles, (4, 2, HALO, WIDTH), (8 * HALO + 8, WIDTH), (4 * HALO + 8, WIDTH), (4 * HALO, WIDTH)),
         (),
-        (info, scan_offsets, tables, rolled, amp, windows, core, halo),
+        (info, scan_offsets, tables, rolled, amp, windows, core, halo, second_halo, wave, window),
         "position",
         scratch=[
+            pltpu.VMEM((2, 2, WIDTH, WIDTH), F32),
             pltpu.VMEM((3, 2, WIDTH, WIDTH), F32),
-            pltpu.VMEM((4, 2, WIDTH, WIDTH), F32),
             pltpu.VMEM((5, 2 * HALO, WIDTH), F32),
             pltpu.SMEM((2, 2), jnp.int32),
             pltpu.SemaphoreType.DMA((2, 6)),
         ],
-        ins=(VMEM, HBM) + (VMEM,) * 6,
+        ins=(VMEM, HBM) + (VMEM,) * 9,
         flops=3_300_000_000,
         nbytes=10_000_000,
         outs=(VMEM, VMEM, VMEM, HBM, HBM, HBM),

time: 82.7 us -> 82 us (level)
  waiting for transfers between devices: 21.5 us -> 20.6 us
    ppermute x4 -> x5, waiting for transfers between devices: 13 us -> 12.1 us  [swap_slab(): return lax.ppermute(x, 'slab', [(0, 1), (1, 0)])]
    pallas_call x13 -> x14, Pallas kernels: 13 us -> 13.2 us  [call(): pl.pallas_call(kernel, out_shape=tuple((jax.ShapeDtypeStruct(shape, F32)...]
    ppermute x4 -> x5, starting transfers between devices: 3.69 us -> 3.78 us  [swap_slab(): return lax.ppermute(x, 'slab', [(0, 1), (1, 0)])]
  transfers between devices with their start and end apart: 12 -> 13, of which waited for: 4 -> 5; matrix products, arithmetic and copies ran while one was open for 0% -> 0% of each run, Pallas kernels for 6% -> 7%
where the time goes in v10:
time: 82 us; the launch traced here: 81.8 us
  blocking collectives  24.7 us (30%)
  starting transfers between devices  22.2 us (27%)
  waiting for transfers between devices  20.6 us (25%)
  Pallas kernels  13.2 us (16%)
    all_to_all x2, blocking collectives, among_columns(): lax.all_to_all(x, ('slab', 'tile'), 0, 0, tiled=True, axis_index_groups=g...  24.7 us
    pallas_call x14, Pallas kernels, call(): pl.pallas_call(kernel, out_shape=tuple((jax.ShapeDtypeStruct(shape, F32)...  13.2 us
    ppermute x5, waiting for transfers between devices, swap_slab(): return lax.ppermute(x, 'slab', [(0, 1), (1, 0)])  12.1 us
    ppermute x5, starting transfers between devices, swap_tile(): return lax.ppermute(x, ('slab', 'tile'), pairs)  10.9 us
    ppermute x5, waiting for transfers between devices, swap_tile(): return lax.ppermute(x, ('slab', 'tile'), pairs)  7.34 us
    ppermute x2, starting transfers between devices, swap_core(): return lax.ppermute(x, 'tile', [(i, i ^ 1) for i in range(count)])  5.96 us
    ppermute x5, starting transfers between devices, swap_slab(): return lax.ppermute(x, 'slab', [(0, 1), (1, 0)])  3.78 us
  transfers between devices with their start and end apart: 13, of which 5 were waited for; matrix products, arithmetic and copies ran while one was open for 0% of the time, Pallas kernels for 7%

profile of v10, /device:TPU:1, one launch (start us, length us, event | category | flops | bytes accessed | tf_op | source)
XLA Modules:
  0.0 81.8 jit_solution(8712986216236683664)
XLA Ops:
  0.6 0.0 copy-start.4
  0.6 1.5 %collective-permute-start.1 = (f32[2,2,128,384]{3,2,1,0:T(8,128)}, f32[2,2,128,384]{3,2,1,0:T(8,128)S(1)}, u32[]{:S(2)}, u32[]{:S(2)}) collective-permute-start(f32[2,2,128,384]{3,2,1,0:T(8,128)} %own_ref.3), channel_id=1, source_target_pairs={{0,1},{1,0},{2,3},{3,2},{4,5},{5,4},{6,7},{7,6},{8,9},{9,8},{10,11... | collective-permute-start | bytes 2359304 | tf_op jit(solution)/shard_map/ppermute | solution.py:411
  2.1 1.4 %collective-permute-start = (f32[2,2,128,384]{3,2,1,0:T(8,128)}, f32[2,2,128,384]{3,2,1,0:T(8,128)S(1)}, u32[]{:S(2)}, u32[]{:S(2)}) collective-permute-start(f32[2,2,128,384]{3,2,1,0:T(8,128)} %own_ref.3), channel_id=1, source_target_pairs={{0,127},{1,2},{2,1},{3,4},{4,3},{5,6},{6,5},{7,8},{8,7},{9,10},{10... | collective-permute-start | bytes 2359304 | tf_op jit(solution)/shard_map/ppermute | solution.py:411
  3.5 1.3 %core.1 = f32[2,2,128,256]{3,2,1,0:T(8,128)S(1)} custom-call(s32[2,2]{1,0:T(2,128)} %offsets_ref.7, f32[2,2,128,384]{3,2,1,0:T(8,128)} %own_ref.3), custom_call_target="tpu_custom_call" | custom-call | bytes 2000000 | tf_op jit(solution)/shard_map/core/pallas_call | solution.py:390
  4.8 0.0 copy-start.2
  4.8 1.7 %collective-permute-start.2 = (f32[2,2,128,256]{3,2,1,0:T(8,128)S(1)}, f32[2,2,128,256]{3,2,1,0:T(8,128)S(1)}, u32[]{:S(2)}, u32[]{:S(2)}) collective-permute-start(f32[2,2,128,256]{3,2,1,0:T(8,128)S(1)} %core.1), channel_id=1, source_target_pairs={{0,64},{64,0},{1,65},{65,1},{2,66},{66,2},{3,67},{67,3},{4,68},{68... | collective-permute-start | bytes 1572872 | tf_op jit(solution)/shard_map/ppermute | solution.py:439
  6.5 0.0 copy-done.4
  6.6 0.1 reshape.19
  6.7 0.1 add_bitcast_fusion
  6.7 0.0 collective-permute-done.1.beside_ref
  6.7 7.3 %collective-permute-done.across_ref = f32[2,2,128,384]{3,2,1,0:T(8,128)S(1)} collective-permute-done((f32[2,2,128,384]{3,2,1,0:T(8,128)}, f32[2,2,128,384]{3,2,1,0:T(8,128)S(1)}, u32[]{:S(2)}, u32[]{:S(2)}) %collective-permute-start) | collective-permute-done | bytes 786464 | tf_op jit(solution)/shard_map/ppermute | solution.py:411
  14.1 0.1 broadcast_in_dim.8.info_ref
  14.1 0.0 copy-start.3
  14.1 0.1 halo.1
  14.2 0.0 copy-start.1
  14.2 1.8 %collective-permute-start.3 = (f32[2,128,256]{2,1,0:T(8,128)S(1)}, f32[2,128,256]{2,1,0:T(8,128)S(1)}, u32[]{:S(2)}, u32[]{:S(2)}) collective-permute-start(f32[2,128,256]{2,1,0:T(8,128)S(1)} %get-tuple-element.16), channel_id=1, source_target_pairs={{0,64},{64,0},{1,65},{65,1},{2,66},{66,2},{3,67},{67,3},{4,68},{68... | collective-permute-start | bytes 786440 | tf_op jit(solution)/shard_map/ppermute | solution.py:439
  16.0 0.1 collective-permute-start.4
  16.1 0.0 copy-done.2
  16.1 1.2 %amp.1.amp_ref = f32[256,256]{1,0:T(8,128)S(1)} custom-call(s32[1]{0:T(128)} %bitcast.1.place_ref, s32[2,2]{1,0:T(2,128)S(1)} %copy-done.4, f32[2,256,256]{2,1,0:T(8,128)S(1)} %copy-done.2), custom_call_target="tpu_custom_call" | custom-call | bytes 2000000 | tf_op jit(solution)/shard_map/amp/pallas_call | solution.py:390
  17.3 0.0 copy-done.3
  17.3 0.8 roll.1.probe_ref
  18.1 0.0 copy-done.1
  18.1 0.0 copy-start
  18.1 0.1 window.1.own_ref
  18.3 0.0 collective-permute-done.2.core_ref
  18.3 4.7 %collective-permute-done.3.halo_ref = f32[2,128,256]{2,1,0:T(8,128)S(1)} collective-permute-done((f32[2,128,256]{2,1,0:T(8,128)S(1)}, f32[2,128,256]{2,1,0:T(8,128)S(1)}, u32[]{:S(2)}, u32[]{:S(2)}) %collective-permute-start.3) | collective-permute-done | bytes 262176 | tf_op jit(solution)/shard_map/ppermute | solution.py:439
  23.0 0.0 copy-done
  23.0 0.8 %first.1 = (f32[2,256,256]{2,1,0:T(8,128)S(1)}, f32[2,256,256]{2,1,0:T(8,128)S(1)}) custom-call(s32[8,128]{1,0:T(8,128)S(1)} %broadcast_in_dim.8.info_ref, bf16[6,2,2,256,256]{4,3,2,1,0:T(8,128)(2,1)S(1)} %copy-done, f32[2,256,256]{2,1,0:T(8,128)S(1)} %roll.1.probe_ref, f32[2,2,256,256]{3,2,1,0:T(8,128)S(1)} %window.1.own_ref, ...), custom_call_target="tpu_custom_call" | custom-call | bytes 2000000 | tf_op jit(solution)/shard_map/first/pallas_call | solution.py:390
  23.8 4.8 %collective-permute-done.4.second_halo_ref = f32[2,128,256]{2,1,0:T(8,128)S(1)} collective-permute-done((f32[2,128,256]{2,1,0:T(8,128)S(1)}, f32[2,128,256]{2,1,0:T(8,128)S(1)}, u32[]{:S(2)}, u32[]{:S(2)}) %collective-permute-start.4) | collective-permute-done | bytes 262176 | tf_op jit(solution)/shard_map/ppermute | solution.py:439
  28.6 6.6 %position.1 = (f32[32,2,8,128]{3,2,1,0:T(8,128)S(1)}, f32[32,2,8,128]{3,2,1,0:T(8,128)S(1)}, f32[4,2,128,256]{3,2,1,0:T(8,128)S(1)}, f32[1032,256]{1,0:T(8,128)S...) custom-call(s32[8,128]{1,0:T(8,128)S(1)} %broadcast_in_dim.8.info_ref, s32[2,2]{1,0:T(2,128)S(1)} %copy-done.4, ...), custom_call_target="tpu_custom_call" | custom-call | flops 3300000000 | bytes 10000000 | tf_op jit(solution)/shard_map/position/pallas_call | solution.py:390
  35.2 4.3 %collective-permute-start.6 = (f32[1032,256]{1,0:T(8,128)S(1)}, f32[1032,256]{1,0:T(8,128)S(1)}, u32[]{:S(2)}, u32[]{:S(2)}) collective-permute-start(f32[1032,256]{1,0:T(8,128)S(1)} %get-tuple-element.22), channel_id=1, source_target_pairs={{0,1},{1,0},{2,3},{3,2},{4,5},{5,4},{6,7},{7,6},{8,9},{9,8},{10,11... | collective-permute-start | bytes 3170312 | tf_op jit(solution)/shard_map/ppermute | solution.py:411
  39.5 0.0 collective-permute-start.5
  39.5 4.5 %collective-permute-start.7 = (f32[32,2,8,128]{3,2,1,0:T(8,128)S(1)}, f32[32,2,8,128]{3,2,1,0:T(8,128)S(1)}, u32[]{:S(2)}, u32[]{:S(2)}) collective-permute-start(f32[32,2,8,128]{3,2,1,0:T(8,128)S(1)} %get-tuple-element.25), channel_id=1, source_target_pairs={{0,1},{1,0},{2,3},{3,2},{4,5},{5,4},{6,7},{7,6},{8,9},{9,8},{10,11... | collective-permute-start | bytes 786440 | tf_op jit(solution)/shard_map/ppermute | solution.py:416
  44.1 1.2 %collective-permute-done.7.got_ref = f32[32,2,8,128]{3,2,1,0:T(8,128)S(1)} collective-permute-done((f32[32,2,8,128]{3,2,1,0:T(8,128)S(1)}, f32[32,2,8,128]{3,2,1,0:T(8,128)S(1)}, u32[]{:S(2)}, u32[]{:S(2)}) %collective-permute-start.7) | collective-permute-done | bytes 262176 | tf_op jit(solution)/shard_map/ppermute | solution.py:416
  45.3 10.6 %all_to_all.10.parts_ref = f32[16,4,8,128]{3,2,1,0:T(8,128)S(1)} all-to-all(f32[16,4,8,128]{3,2,1,0:T(8,128)S(1)} %bitcast.7), channel_id=1, replica_groups={{0,2,4,6,8,10,12,14,16,18,20,22,24,26,28,30},{1,3,5,7,9,11,13,15,17,19,..., dimensions={0} | all-to-all | bytes 524288 | tf_op jit(solution)/shard_map/all_to_all | solution.py:424
  55.9 0.1 collective-permute-start.9
  56.0 2.6 %collective-permute-done.9.got_ref = f32[4,8,128]{2,1,0:T(8,128)S(1)} collective-permute-done((f32[4,8,128]{2,1,0:T(8,128)S(1)}, f32[4,8,128]{2,1,0:T(8,128)S(1)}, u32[]{:S(2)}, u32[]{:S(2)}) %collective-permute-start.9) | collective-permute-done | bytes 16416 | tf_op jit(solution)/shard_map/ppermute | solution.py:439
  58.6 0.0 collective-permute-done.5.early_ref
  58.6 0.0 collective-permute-done.6.beside_ref
  58.6 0.2 sum.1
  58.9 0.1 collective-permute-start.10
  58.9 1.6 %collective-permute-start.11 = (f32[4,8,128]{2,1,0:T(8,128)S(1)}, f32[4,8,128]{2,1,0:T(8,128)S(1)}, u32[]{:S(2)}, u32[]{:S(2)}) collective-permute-start(f32[4,8,128]{2,1,0:T(8,128)S(1)} %add_slabs.1.after_ref.first_ref), channel_id=1, source_target_pairs={{0,96},{1,97},{2,98},{3,99},{4,100},{5,101},{6,102},{7,103},{8,104... | collective-permute-start | bytes 49160 | tf_op jit(solution)/shard_map/ppermute | solution.py:435
  60.6 3.7 %collective-permute-start.8 = (f32[512,256]{1,0:T(8,128)S(1)}, f32[512,256]{1,0:T(8,128)S(1)}, u32[]{:S(2)}, u32[]{:S(2)}) collective-permute-start(f32[512,256]{1,0:T(8,128)S(1)} %get-tuple-element.26), channel_id=1, source_target_pairs={{0,127},{1,2},{2,1},{3,4},{4,3},{5,6},{6,5},{7,8},{8,7},{9,10},{10... | collective-permute-start | bytes 1572872 | tf_op jit(solution)/shard_map/ppermute | solution.py:411
  64.2 0.0 collective-permute-done.11.second_ref
  64.3 14.1 %all_to_all.11.after_ref = f32[16,4,8,128]{3,2,1,0:T(8,128)S(1)} all-to-all(f32[16,4,8,128]{3,2,1,0:T(8,128)S(1)} %total.1), channel_id=1, replica_groups={{0,2,4,6,8,10,12,14,16,18,20,22,24,26,28,30},{1,3,5,7,9,11,13,15,17,19,..., dimensions={0} | all-to-all | bytes 524288 | tf_op jit(solution)/shard_map/all_to_all | solution.py:424
  78.4 1.4 %collective-permute-start.12 = (f32[16,4,8,128]{3,2,1,0:T(8,128)S(1)}, f32[16,4,8,128]{3,2,1,0:T(8,128)S(1)}, u32[]{:S(2)}, u32[]{:S(2)}) collective-permute-start(f32[16,4,8,128]{3,2,1,0:T(8,128)S(1)} %all_to_all.11.after_ref), channel_id=1, source_target_pairs={{0,1},{1,0},{2,3},{3,2},{4,5},{5,4},{6,7},{7,6},{8,9},{9,8},{10,11... | collective-permute-start | bytes 786440 | tf_op jit(solution)/shard_map/ppermute | solution.py:416
  79.8 0.0 collective-permute-done.8.late_ref
  79.8 0.0 collective-permute-done.10.swapped_ref
  79.8 1.1 %object.1 = (f32[2,2,128,384]{3,2,1,0:T(8,128)}, f32[8,128]{1,0:T(8,128)S(1)}) custom-call(s32[8,128]{1,0:T(8,128)S(1)} %broadcast_in_dim.8.info_ref, f32[4,2,128,256]{3,2,1,0:T(8,128)S(1)} %get-tuple-element.20.core_ref, f32[520,256]{1,0:T(8,128)S(1)} %collective-permute-done.5.early_ref, f32[1032,256]{1,0:T(8,128)S(1)} %collective-permute-done.6.beside_ref, ...), custom_call_target="tpu_custom_call" | custom-call | bytes 2000000 | tf_op jit(solution)/shard_map/object/pallas_call | solution.py:390
  80.9 0.0 collective-permute-done.12
  80.9 0.9 %probe.1 = f32[2,256,256]{2,1,0:T(8,128)} custom-call(f32[8,128]{1,0:T(8,128)S(1)} %get-tuple-element.29.after_ref, f32[32,2,8,128]{3,2,1,0:T(8,128)S(1)} %bitcast.6, f32[32,2,8,128]{3,2,1,0:T(8,128)S(1)} %bitcast.8), custom_call_target="tpu_custom_call" | custom-call | bytes 2000000 | tf_op jit(solution)/shard_map/probe/pallas_call | solution.py:390
  (6 shorter events, 0.1 us)
Async XLA Ops:
  0.6 5.9 %copy-start.4 = (s32[2,2]{1,0:T(2,128)S(1)}, s32[2,2]{1,0:T(2,128)}, u32[]{:S(2)}) copy-start(s32[2,2]{1,0:T(2,128)} %offsets_ref.7) | copy-start | bytes 52
  0.6 6.1 %collective-permute-start.1 = (f32[2,2,128,384]{3,2,1,0:T(8,128)}, f32[2,2,128,384]{3,2,1,0:T(8,128)S(1)}, u32[]{:S(2)}, u32[]{:S(2)}) collective-permute-start(f32[2,2,128,384]{3,2,1,0:T(8,128)} %own_ref.3), channel_id=1, source_target_pairs={{0,1},{1,0},{2,3},{3,2},{4,5},{5,4},{6,7},{7,6},{8,9},{9,8},{10,11... | collective-permute-start | bytes 2359304 | tf_op jit(solution)/shard_map/ppermute | solution.py:411
  2.1 11.9 %collective-permute-start = (f32[2,2,128,384]{3,2,1,0:T(8,128)}, f32[2,2,128,384]{3,2,1,0:T(8,128)S(1)}, u32[]{:S(2)}, u32[]{:S(2)}) collective-permute-start(f32[2,2,128,384]{3,2,1,0:T(8,128)} %own_ref.3), channel_id=1, source_target_pairs={{0,127},{1,2},{2,1},{3,4},{4,3},{5,6},{6,5},{7,8},{8,7},{9,10},{10... | collective-permute-start | bytes 2359304 | tf_op jit(solution)/shard_map/ppermute | solution.py:411
  4.8 11.3 %copy-start.2 = (f32[2,256,256]{2,1,0:T(8,128)S(1)}, f32[2,256,256]{2,1,0:T(8,128)}, u32[]{:S(2)}) copy-start(f32[2,256,256]{2,1,0:T(8,128)} %amp_ref.1) | copy-start | bytes 1572868
  4.8 13.5 %collective-permute-start.2 = (f32[2,2,128,256]{3,2,1,0:T(8,128)S(1)}, f32[2,2,128,256]{3,2,1,0:T(8,128)S(1)}, u32[]{:S(2)}, u32[]{:S(2)}) collective-permute-start(f32[2,2,128,256]{3,2,1,0:T(8,128)S(1)} %core.1), channel_id=1, source_target_pairs={{0,64},{64,0},{1,65},{65,1},{2,66},{66,2},{3,67},{67,3},{4,68},{68... | collective-permute-start | bytes 1572872 | tf_op jit(solution)/shard_map/ppermute | solution.py:439
  14.1 3.2 %copy-start.3 = (f32[2,256,256]{2,1,0:T(8,128)S(1)}, f32[2,256,256]{2,1,0:T(8,128)}, u32[]{:S(2)}) copy-start(f32[2,256,256]{2,1,0:T(8,128)} %probe_ref.1) | copy-start | bytes 1572868
  14.2 3.9 %copy-start.1 = (f32[2,2,128,384]{3,2,1,0:T(8,128)S(1)}, f32[2,2,128,384]{3,2,1,0:T(8,128)}, u32[]{:S(2)}) copy-start(f32[2,2,128,384]{3,2,1,0:T(8,128)} %own_ref.3) | copy-start | bytes 2359300
  14.2 8.7 %collective-permute-start.3 = (f32[2,128,256]{2,1,0:T(8,128)S(1)}, f32[2,128,256]{2,1,0:T(8,128)S(1)}, u32[]{:S(2)}, u32[]{:S(2)}) collective-permute-start(f32[2,128,256]{2,1,0:T(8,128)S(1)} %get-tuple-element.16), channel_id=1, source_target_pairs={{0,64},{64,0},{1,65},{65,1},{2,66},{66,2},{3,67},{67,3},{4,68},{68... | collective-permute-start | bytes 786440 | tf_op jit(solution)/shard_map/ppermute | solution.py:439
  16.0 12.5 %collective-permute-start.4 = (f32[2,128,256]{2,1,0:T(8,128)S(1)}, f32[2,128,256]{2,1,0:T(8,128)S(1)}, u32[]{:S(2)}, u32[]{:S(2)}) collective-permute-start(f32[2,128,256]{2,1,0:T(8,128)S(1)} %get-tuple-element.17), channel_id=1, source_target_pairs={{0,64},{64,0},{1,65},{65,1},{2,66},{66,2},{3,67},{67,3},{4,68},{68... | collective-permute-start | bytes 786440 | tf_op jit(solution)/shard_map/ppermute | solution.py:439
  18.1 4.8 %copy-start = (bf16[6,2,2,256,256]{4,3,2,1,0:T(8,128)(2,1)S(1)}, bf16[6,2,2,256,256]{4,3,2,1,0:T(8,128)(2,1)}, u32[]{:S(2)}) copy-start(bf16[6,2,2,256,256]{4,3,2,1,0:T(8,128)(2,1)} %constant.10.clone.tables_ref) | copy-start | bytes 9437188
  35.2 23.4 %collective-permute-start.6 = (f32[1032,256]{1,0:T(8,128)S(1)}, f32[1032,256]{1,0:T(8,128)S(1)}, u32[]{:S(2)}, u32[]{:S(2)}) collective-permute-start(f32[1032,256]{1,0:T(8,128)S(1)} %get-tuple-element.22), channel_id=1, source_target_pairs={{0,1},{1,0},{2,3},{3,2},{4,5},{5,4},{6,7},{7,6},{8,9},{9,8},{10,11... | collective-permute-start | bytes 3170312 | tf_op jit(solution)/shard_map/ppermute | solution.py:411
  39.5 19.1 %collective-permute-start.5 = (f32[520,256]{1,0:T(8,128)S(1)}, f32[520,256]{1,0:T(8,128)S(1)}, u32[]{:S(2)}, u32[]{:S(2)}) collective-permute-start(f32[520,256]{1,0:T(8,128)S(1)} %get-tuple-element.21), channel_id=1, source_target_pairs={{0,127},{1,2},{2,1},{3,4},{4,3},{5,6},{6,5},{7,8},{8,7},{9,10},{10... | collective-permute-start | bytes 1597448 | tf_op jit(solution)/shard_map/ppermute | solution.py:411
  39.5 5.7 %collective-permute-start.7 = (f32[32,2,8,128]{3,2,1,0:T(8,128)S(1)}, f32[32,2,8,128]{3,2,1,0:T(8,128)S(1)}, u32[]{:S(2)}, u32[]{:S(2)}) collective-permute-start(f32[32,2,8,128]{3,2,1,0:T(8,128)S(1)} %get-tuple-element.25), channel_id=1, source_target_pairs={{0,1},{1,0},{2,3},{3,2},{4,5},{5,4},{6,7},{7,6},{8,9},{9,8},{10,11... | collective-permute-start | bytes 786440 | tf_op jit(solution)/shard_map/ppermute | solution.py:416
  55.9 2.7 %collective-permute-start.9 = (f32[4,8,128]{2,1,0:T(8,128)S(1)}, f32[4,8,128]{2,1,0:T(8,128)S(1)}, u32[]{:S(2)}, u32[]{:S(2)}) collective-permute-start(f32[4,8,128]{2,1,0:T(8,128)S(1)} %reduce.1.keep_ref), channel_id=1, source_target_pairs={{0,64},{64,0},{1,65},{65,1},{2,66},{66,2},{3,67},{67,3},{4,68},{68... | collective-permute-start | bytes 49160 | tf_op jit(solution)/shard_map/ppermute | solution.py:439
  58.9 20.9 %collective-permute-start.10 = (f32[2,2,128,384]{3,2,1,0:T(8,128)S(1)}, f32[2,2,128,384]{3,2,1,0:T(8,128)S(1)}, u32[]{:S(2)}, u32[]{:S(2)}) collective-permute-start(f32[2,2,128,384]{3,2,1,0:T(8,128)S(1)} %sum.1), channel_id=1, source_target_pairs={{0,64},{64,0},{1,65},{65,1},{2,66},{66,2},{3,67},{67,3},{4,68},{68... | collective-permute-start | bytes 2359304 | tf_op jit(solution)/shard_map/ppermute | solution.py:439
  58.9 5.3 %collective-permute-start.11 = (f32[4,8,128]{2,1,0:T(8,128)S(1)}, f32[4,8,128]{2,1,0:T(8,128)S(1)}, u32[]{:S(2)}, u32[]{:S(2)}) collective-permute-start(f32[4,8,128]{2,1,0:T(8,128)S(1)} %add_slabs.1.after_ref.first_ref), channel_id=1, source_target_pairs={{0,96},{1,97},{2,98},{3,99},{4,100},{5,101},{6,102},{7,103},{8,104... | collective-permute-start | bytes 49160 | tf_op jit(solution)/shard_map/ppermute | solution.py:435
  60.6 19.2 %collective-permute-start.8 = (f32[512,256]{1,0:T(8,128)S(1)}, f32[512,256]{1,0:T(8,128)S(1)}, u32[]{:S(2)}, u32[]{:S(2)}) collective-permute-start(f32[512,256]{1,0:T(8,128)S(1)} %get-tuple-element.26), channel_id=1, source_target_pairs={{0,127},{1,2},{2,1},{3,4},{4,3},{5,6},{6,5},{7,8},{8,7},{9,10},{10... | collective-permute-start | bytes 1572872 | tf_op jit(solution)/shard_map/ppermute | solution.py:411
  78.4 2.6 %collective-permute-start.12 = (f32[16,4,8,128]{3,2,1,0:T(8,128)S(1)}, f32[16,4,8,128]{3,2,1,0:T(8,128)S(1)}, u32[]{:S(2)}, u32[]{:S(2)}) collective-permute-start(f32[16,4,8,128]{3,2,1,0:T(8,128)S(1)} %all_to_all.11.after_ref), channel_id=1, source_target_pairs={{0,1},{1,0},{2,3},{3,2},{4,5},{5,4},{6,7},{7,6},{8,9},{9,8},{10,11... | collective-permute-start | bytes 786440 | tf_op jit(solution)/shard_map/ppermute | solution.py:416

commit v11 on v10

--- a/solution.py
+++ b/solution.py
@@ -72,6 +72,10 @@
 
 def fold(x):
     x = jnp.concatenate([x[:HALF] + x[HALF:], x[:HALF] - x[HALF:]], axis=0)
+    return jnp.concatenate([x[:, :HALF] + x[:, HALF:], x[:, :HALF] - x[:, HALF:]], axis=1)
+
+
+def fold_columns(x):
     return jnp.concatenate([x[:, :HALF] + x[:, HALF:], x[:, :HALF] - x[:, HALF:]], axis=1)
 
 
@@ -223,10 +227,16 @@
     return window_of
 
 
-def first_kernel(info_ref, tables_ref, probe_ref, own_ref, core_ref, halo_ref, wave_out, window_out):
+def first_kernel(info_ref, tables_ref, probe_ref, own_ref, core_ref, halo_ref, wave_out, window_out, lower_out):
     window = selector(info_ref, own_ref, core_ref, (halo_ref, None))(0)
     window_out[0], window_out[1] = window
-    wave_out[0], wave_out[1] = propagate(times((probe_ref[0], probe_ref[1]), window), tables_ref)
+    wave = propagate(times((probe_ref[0], probe_ref[1]), window), tables_ref)
+    wave_out[0], wave_out[1] = wave
+    mine = here()[0] == 0
+    core = [jnp.where(mine, own_ref[1, c, HALO:], core_ref[1, c]) for c in range(2)]
+    lower = times((wave[0][HALO:], wave[1][HALO:]), core)
+    lower = right_mult((fold_columns(lower[0]), fold_columns(lower[1])), tables_ref, PROP_RIGHT)
+    lower_out[0], lower_out[1] = lower
 
 
 def position_kernel(
@@ -241,6 +251,7 @@
     second_halo_ref,
     first_wave_ref,
     first_window_ref,
+    lower_ref,
     keep_out,
     send_out,
     core_out,
@@ -249,7 +260,6 @@
     late_out,
     waves,
     windows,
-    halos,
     offsets,
     sems,
 ):
@@ -263,6 +273,15 @@
             waves[s - 2, 0], waves[s - 2, 1] = wave
         window = window_of(s)
         windows[s - 1, 0], windows[s - 1, 1] = window
+        if s == 1:
+            upper = times((wave[0][:HALO], wave[1][:HALO]), (window[0][:HALO], window[1][:HALO]))
+            upper = right_mult((fold_columns(upper[0]), fold_columns(upper[1])), tables_ref, PROP_RIGHT)
+            rows = [
+                jnp.concatenate([upper[c] + lower_ref[c], upper[c] - lower_ref[c]], axis=0) for c in range(2)
+            ]
+            rows = left_mult(rows, tables_ref, PROP_LEFT)
+            wave = (fold(rows[0]), fold(rows[1]))
+            continue
         prod = times(wave, window)
         if s < 3:
             wave = propagate(prod, tables_ref)
@@ -287,18 +306,16 @@
     for s in range(3, -1, -1):
         object_grad = times(before(s), grad)
         slot = jnp.where(place == s // 2, s % 2, 2 + s % 2)
+        start = pl.multiple_of(slot * 2 * HALO, HALO)
         for c in range(2):
             value = object_grad[c] if c == 0 else -object_grad[c]
             core_out[slot, c] = value[HALO:]
-            halos[slot, pl.ds(c * HALO, HALO)] = value[:HALO]
-        start = pl.multiple_of(slot * 2 * HALO, HALO)
-        copy = pltpu.make_async_copy(halos.at[slot], beside_out.at[pl.ds(start, 2 * HALO)], sems.at[0, s])
-        copy.start()
-        copies.append(copy)
-        start = pl.multiple_of(s % 2 * 2 * HALO, HALO)
+            beside_out[pl.ds(start + c * HALO, HALO)] = value[:HALO]
+        source = beside_out.at[pl.ds(start, 2 * HALO)]
+        target = pl.multiple_of(s % 2 * 2 * HALO, HALO)
         early = jnp.where(slot // 2 == 1, 1, 0) != across_turned
         for which, ref in enumerate((late_out, early_out)):
-            copy = pltpu.make_async_copy(halos.at[slot], ref.at[pl.ds(start, 2 * HALO)], sems.at[1, s])
+            copy = pltpu.make_async_copy(source, ref.at[pl.ds(target, 2 * HALO)], sems.at[1, s])
 
             @pl.when(early == (which == 1))
             def _():
@@ -309,11 +326,10 @@
         if s > 0:
             grad = propagate(grad, tables_ref)
     meta = info_ref[...].astype(F32)
-    halos[4, :8] = jnp.concatenate([meta, meta], axis=1)
-    for i, (ref, start) in enumerate(((beside_out, 8 * HALO), (early_out, 4 * HALO))):
-        copy = pltpu.make_async_copy(halos.at[4, :8], ref.at[pl.ds(start, 8)], sems.at[i, 4])
-        copy.start()
-        copies.append(copy)
+    beside_out[8 * HALO :] = jnp.concatenate([meta, meta], axis=1)
+    copy = pltpu.make_async_copy(beside_out.at[pl.ds(8 * HALO, 8)], early_out.at[pl.ds(4 * HALO, 8)], sems.at[1, 4])
+    copy.start()
+    copies.append(copy)
     load.wait()
     row, col = offsets[place, 0], offsets[place, 1]
     value = [grad[0], -grad[1]]
@@ -471,9 +487,9 @@
     halo, second_halo = swap_slab(halo), swap_slab(second_halo)
     windows = call(window_kernel, whole, (), (info, own, across, beside), "window")
 
-    wave, window = call(
+    wave, window, lower = call(
         first_kernel,
-        (probe.shape, probe.shape),
+        (probe.shape, probe.shape, part[1:]),
         (),
         (info, tables, rolled, windows, core, halo),
         "first",
@@ -483,19 +499,18 @@
         position_kernel,
         (tiles, tiles, (4, 2, HALO, WIDTH), (8 * HALO + 8, WIDTH), (4 * HALO + 8, WIDTH), (4 * HALO, WIDTH)),
         (),
-        (info, scan_offsets, tables, rolled, amp, windows, core, halo, second_halo, wave, window),
+        (info, scan_offsets, tables, rolled, amp, windows, core, halo, second_halo, wave, window, lower),
         "position",
         scratch=[
             pltpu.VMEM((2, 2, WIDTH, WIDTH), F32),
             pltpu.VMEM((3, 2, WIDTH, WIDTH), F32),
-            pltpu.VMEM((5, 2 * HALO, WIDTH), F32),
             pltpu.SMEM((2, 2), jnp.int32),
             pltpu.SemaphoreType.DMA((2, 6)),
         ],
-        ins=(VMEM, HBM) + (VMEM,) * 9,
+        ins=(VMEM, HBM) + (VMEM,) * 10,
         flops=3_300_000_000,
         nbytes=10_000_000,
-        outs=(VMEM, VMEM, VMEM, HBM, HBM, HBM),
+        outs=(VMEM, VMEM, VMEM, VMEM, HBM, HBM),
     )
     sides = (info, cores, swap_tile(early, 0), swap_tile(beside, 1))
     parts = (WIDTH // 16, 4, 8, HALF)

time: 82 us -> 81.8 us (level)
  no operation moved by 1% of the time
where the time goes in v11:
time: 81.8 us; the launch traced here: 81.5 us
  blocking collectives  24.7 us (30%)
  starting transfers between devices  22.2 us (27%)
  waiting for transfers between devices  20.3 us (25%)
  Pallas kernels  13.2 us (16%)
    all_to_all x2, blocking collectives, among_columns(): lax.all_to_all(x, ('slab', 'tile'), 0, 0, tiled=True, axis_index_groups=g...  24.7 us
    pallas_call x14, Pallas kernels, call(): pl.pallas_call(kernel, out_shape=tuple((jax.ShapeDtypeStruct(shape, F32)...  13.2 us
    ppermute x5, waiting for transfers between devices, swap_slab(): return lax.ppermute(x, 'slab', [(0, 1), (1, 0)])  11.8 us
    ppermute x5, starting transfers between devices, swap_tile(): return lax.ppermute(x, ('slab', 'tile'), pairs)  10.9 us
    ppermute x5, waiting for transfers between devices, swap_tile(): return lax.ppermute(x, ('slab', 'tile'), pairs)  7.34 us
    ppermute x2, starting transfers between devices, swap_core(): return lax.ppermute(x, 'tile', [(i, i ^ 1) for i in range(count)])  5.96 us
    ppermute x5, starting transfers between devices, swap_slab(): return lax.ppermute(x, 'slab', [(0, 1), (1, 0)])  3.78 us
  transfers between devices with their start and end apart: 13, of which 5 were waited for; matrix products, arithmetic and copies ran while one was open for 0% of the time, Pallas kernels for 7%

profile of v11, /device:TPU:1, one launch (start us, length us, event | category | flops | bytes accessed | tf_op | source)
XLA Modules:
  0.0 81.5 jit_solution(17458776653040385477)
XLA Ops:
  0.6 0.0 copy-start.4
  0.6 1.5 %collective-permute-start.1 = (f32[2,2,128,384]{3,2,1,0:T(8,128)}, f32[2,2,128,384]{3,2,1,0:T(8,128)S(1)}, u32[]{:S(2)}, u32[]{:S(2)}) collective-permute-start(f32[2,2,128,384]{3,2,1,0:T(8,128)} %own_ref.3), channel_id=1, source_target_pairs={{0,1},{1,0},{2,3},{3,2},{4,5},{5,4},{6,7},{7,6},{8,9},{9,8},{10,11... | collective-permute-start | bytes 2359304 | tf_op jit(solution)/shard_map/ppermute | solution.py:427
  2.1 1.4 %collective-permute-start = (f32[2,2,128,384]{3,2,1,0:T(8,128)}, f32[2,2,128,384]{3,2,1,0:T(8,128)S(1)}, u32[]{:S(2)}, u32[]{:S(2)}) collective-permute-start(f32[2,2,128,384]{3,2,1,0:T(8,128)} %own_ref.3), channel_id=1, source_target_pairs={{0,127},{1,2},{2,1},{3,4},{4,3},{5,6},{6,5},{7,8},{8,7},{9,10},{10... | collective-permute-start | bytes 2359304 | tf_op jit(solution)/shard_map/ppermute | solution.py:427
  3.5 1.3 %core.1 = f32[2,2,128,256]{3,2,1,0:T(8,128)S(1)} custom-call(s32[2,2]{1,0:T(2,128)} %offsets_ref.7, f32[2,2,128,384]{3,2,1,0:T(8,128)} %own_ref.3), custom_call_target="tpu_custom_call" | custom-call | bytes 2000000 | tf_op jit(solution)/shard_map/core/pallas_call | solution.py:406
  4.8 0.0 copy-start.2
  4.8 1.7 %collective-permute-start.2 = (f32[2,2,128,256]{3,2,1,0:T(8,128)S(1)}, f32[2,2,128,256]{3,2,1,0:T(8,128)S(1)}, u32[]{:S(2)}, u32[]{:S(2)}) collective-permute-start(f32[2,2,128,256]{3,2,1,0:T(8,128)S(1)} %core.1), channel_id=1, source_target_pairs={{0,64},{64,0},{1,65},{65,1},{2,66},{66,2},{3,67},{67,3},{4,68},{68... | collective-permute-start | bytes 1572872 | tf_op jit(solution)/shard_map/ppermute | solution.py:455
  6.5 0.0 copy-done.4
  6.6 0.1 reshape.19
  6.7 0.1 add_bitcast_fusion
  6.7 0.0 collective-permute-done.1.beside_ref
  6.7 7.3 %collective-permute-done.across_ref = f32[2,2,128,384]{3,2,1,0:T(8,128)S(1)} collective-permute-done((f32[2,2,128,384]{3,2,1,0:T(8,128)}, f32[2,2,128,384]{3,2,1,0:T(8,128)S(1)}, u32[]{:S(2)}, u32[]{:S(2)}) %collective-permute-start) | collective-permute-done | bytes 786464 | tf_op jit(solution)/shard_map/ppermute | solution.py:427
  14.1 0.1 broadcast_in_dim.8.info_ref
  14.1 0.0 copy-start.3
  14.1 0.1 halo.1
  14.2 0.0 copy-start.1
  14.2 1.8 %collective-permute-start.3 = (f32[2,128,256]{2,1,0:T(8,128)S(1)}, f32[2,128,256]{2,1,0:T(8,128)S(1)}, u32[]{:S(2)}, u32[]{:S(2)}) collective-permute-start(f32[2,128,256]{2,1,0:T(8,128)S(1)} %get-tuple-element.17), channel_id=1, source_target_pairs={{0,64},{64,0},{1,65},{65,1},{2,66},{66,2},{3,67},{67,3},{4,68},{68... | collective-permute-start | bytes 786440 | tf_op jit(solution)/shard_map/ppermute | solution.py:455
  16.0 0.1 collective-permute-start.4
  16.1 0.0 copy-done.2
  16.1 1.2 %amp.1.amp_ref = f32[256,256]{1,0:T(8,128)S(1)} custom-call(s32[1]{0:T(128)} %bitcast.1.place_ref, s32[2,2]{1,0:T(2,128)S(1)} %copy-done.4, f32[2,256,256]{2,1,0:T(8,128)S(1)} %copy-done.2), custom_call_target="tpu_custom_call" | custom-call | bytes 2000000 | tf_op jit(solution)/shard_map/amp/pallas_call | solution.py:406
  17.3 0.0 copy-done.3
  17.3 0.8 roll.1.probe_ref
  18.1 0.0 copy-done.1
  18.1 0.0 copy-start
  18.1 0.1 window.1.own_ref
  18.3 0.0 collective-permute-done.2.core_ref
  18.3 4.7 %collective-permute-done.3.halo_ref = f32[2,128,256]{2,1,0:T(8,128)S(1)} collective-permute-done((f32[2,128,256]{2,1,0:T(8,128)S(1)}, f32[2,128,256]{2,1,0:T(8,128)S(1)}, u32[]{:S(2)}, u32[]{:S(2)}) %collective-permute-start.3) | collective-permute-done | bytes 262176 | tf_op jit(solution)/shard_map/ppermute | solution.py:455
  23.0 0.0 copy-done
  23.0 1.1 %first.1 = (f32[2,256,256]{2,1,0:T(8,128)S(1)}, f32[2,256,256]{2,1,0:T(8,128)S(1)}, f32[2,128,256]{2,1,0:T(8,128)S(1)}) custom-call(s32[8,128]{1,0:T(8,128)S(1)} %broadcast_in_dim.8.info_ref, bf16[6,2,2,256,256]{4,3,2,1,0:T(8,128)(2,1)S(1)} %copy-done, f32[2,256,256]{2,1,0:T(8,128)S(1)} %roll.1.probe_ref, f32[2,2,256,256]{3,2,1,0:T(8,128)S(1)} %window.1.own_ref, ...), custom_call_target="tpu_custom_call" | custom-call | bytes 2000000 | tf_op jit(solution)/shard_map/first/pallas_call | solution.py:406
  24.1 4.5 %collective-permute-done.4.second_halo_ref = f32[2,128,256]{2,1,0:T(8,128)S(1)} collective-permute-done((f32[2,128,256]{2,1,0:T(8,128)S(1)}, f32[2,128,256]{2,1,0:T(8,128)S(1)}, u32[]{:S(2)}, u32[]{:S(2)}) %collective-permute-start.4) | collective-permute-done | bytes 262176 | tf_op jit(solution)/shard_map/ppermute | solution.py:455
  28.6 6.3 %position.1 = (f32[32,2,8,128]{3,2,1,0:T(8,128)S(1)}, f32[32,2,8,128]{3,2,1,0:T(8,128)S(1)}, f32[4,2,128,256]{3,2,1,0:T(8,128)S(1)}, f32[1032,256]{1,0:T(8,128)S...) custom-call(s32[8,128]{1,0:T(8,128)S(1)} %broadcast_in_dim.8.info_ref, s32[2,2]{1,0:T(2,128)S(1)} %copy-done.4, ...), custom_call_target="tpu_custom_call" | custom-call | flops 3300000000 | bytes 10000000 | tf_op jit(solution)/shard_map/position/pallas_call | solution.py:406
  34.9 4.3 %collective-permute-start.6 = (f32[1032,256]{1,0:T(8,128)S(1)}, f32[1032,256]{1,0:T(8,128)S(1)}, u32[]{:S(2)}, u32[]{:S(2)}) collective-permute-start(f32[1032,256]{1,0:T(8,128)S(1)} %get-tuple-element.24), channel_id=1, source_target_pairs={{0,1},{1,0},{2,3},{3,2},{4,5},{5,4},{6,7},{7,6},{8,9},{9,8},{10,11... | collective-permute-start | bytes 3170312 | tf_op jit(solution)/shard_map/ppermute | solution.py:427
  39.3 0.0 collective-permute-start.5
  39.3 4.6 %collective-permute-start.7 = (f32[32,2,8,128]{3,2,1,0:T(8,128)S(1)}, f32[32,2,8,128]{3,2,1,0:T(8,128)S(1)}, u32[]{:S(2)}, u32[]{:S(2)}) collective-permute-start(f32[32,2,8,128]{3,2,1,0:T(8,128)S(1)} %get-tuple-element.27), channel_id=1, source_target_pairs={{0,1},{1,0},{2,3},{3,2},{4,5},{5,4},{6,7},{7,6},{8,9},{9,8},{10,11... | collective-permute-start | bytes 786440 | tf_op jit(solution)/shard_map/ppermute | solution.py:432
  43.8 1.2 %collective-permute-done.7.got_ref = f32[32,2,8,128]{3,2,1,0:T(8,128)S(1)} collective-permute-done((f32[32,2,8,128]{3,2,1,0:T(8,128)S(1)}, f32[32,2,8,128]{3,2,1,0:T(8,128)S(1)}, u32[]{:S(2)}, u32[]{:S(2)}) %collective-permute-start.7) | collective-permute-done | bytes 262176 | tf_op jit(solution)/shard_map/ppermute | solution.py:432
  45.0 10.6 %all_to_all.10.parts_ref = f32[16,4,8,128]{3,2,1,0:T(8,128)S(1)} all-to-all(f32[16,4,8,128]{3,2,1,0:T(8,128)S(1)} %bitcast.7), channel_id=1, replica_groups={{0,2,4,6,8,10,12,14,16,18,20,22,24,26,28,30},{1,3,5,7,9,11,13,15,17,19,..., dimensions={0} | all-to-all | bytes 524288 | tf_op jit(solution)/shard_map/all_to_all | solution.py:440
  55.7 0.1 collective-permute-start.9
  55.8 2.6 %collective-permute-done.9.got_ref = f32[4,8,128]{2,1,0:T(8,128)S(1)} collective-permute-done((f32[4,8,128]{2,1,0:T(8,128)S(1)}, f32[4,8,128]{2,1,0:T(8,128)S(1)}, u32[]{:S(2)}, u32[]{:S(2)}) %collective-permute-start.9) | collective-permute-done | bytes 16416 | tf_op jit(solution)/shard_map/ppermute | solution.py:455
  58.4 0.0 collective-permute-done.5.early_ref
  58.4 0.0 collective-permute-done.6.beside_ref
  58.4 0.2 sum.1
  58.6 0.1 collective-permute-start.10
  58.7 1.6 %collective-permute-start.11 = (f32[4,8,128]{2,1,0:T(8,128)S(1)}, f32[4,8,128]{2,1,0:T(8,128)S(1)}, u32[]{:S(2)}, u32[]{:S(2)}) collective-permute-start(f32[4,8,128]{2,1,0:T(8,128)S(1)} %add_slabs.1.after_ref.first_ref), channel_id=1, source_target_pairs={{0,96},{1,97},{2,98},{3,99},{4,100},{5,101},{6,102},{7,103},{8,104... | collective-permute-start | bytes 49160 | tf_op jit(solution)/shard_map/ppermute | solution.py:451
  60.3 3.7 %collective-permute-start.8 = (f32[512,256]{1,0:T(8,128)S(1)}, f32[512,256]{1,0:T(8,128)S(1)}, u32[]{:S(2)}, u32[]{:S(2)}) collective-permute-start(f32[512,256]{1,0:T(8,128)S(1)} %get-tuple-element.28), channel_id=1, source_target_pairs={{0,127},{1,2},{2,1},{3,4},{4,3},{5,6},{6,5},{7,8},{8,7},{9,10},{10... | collective-permute-start | bytes 1572872 | tf_op jit(solution)/shard_map/ppermute | solution.py:427
  64.0 0.0 collective-permute-done.11.second_ref
  64.0 14.1 %all_to_all.11.after_ref = f32[16,4,8,128]{3,2,1,0:T(8,128)S(1)} all-to-all(f32[16,4,8,128]{3,2,1,0:T(8,128)S(1)} %total.1), channel_id=1, replica_groups={{0,2,4,6,8,10,12,14,16,18,20,22,24,26,28,30},{1,3,5,7,9,11,13,15,17,19,..., dimensions={0} | all-to-all | bytes 524288 | tf_op jit(solution)/shard_map/all_to_all | solution.py:440
  78.1 1.4 %collective-permute-start.12 = (f32[16,4,8,128]{3,2,1,0:T(8,128)S(1)}, f32[16,4,8,128]{3,2,1,0:T(8,128)S(1)}, u32[]{:S(2)}, u32[]{:S(2)}) collective-permute-start(f32[16,4,8,128]{3,2,1,0:T(8,128)S(1)} %all_to_all.11.after_ref), channel_id=1, source_target_pairs={{0,1},{1,0},{2,3},{3,2},{4,5},{5,4},{6,7},{7,6},{8,9},{9,8},{10,11... | collective-permute-start | bytes 786440 | tf_op jit(solution)/shard_map/ppermute | solution.py:432
  79.5 0.0 collective-permute-done.8.late_ref
  79.5 0.0 collective-permute-done.10.swapped_ref
  79.5 1.1 %object.1 = (f32[2,2,128,384]{3,2,1,0:T(8,128)}, f32[8,128]{1,0:T(8,128)S(1)}) custom-call(s32[8,128]{1,0:T(8,128)S(1)} %broadcast_in_dim.8.info_ref, f32[4,2,128,256]{3,2,1,0:T(8,128)S(1)} %get-tuple-element.22.core_ref, f32[520,256]{1,0:T(8,128)S(1)} %collective-permute-done.5.early_ref, f32[1032,256]{1,0:T(8,128)S(1)} %collective-permute-done.6.beside_ref, ...), custom_call_target="tpu_custom_call" | custom-call | bytes 2000000 | tf_op jit(solution)/shard_map/object/pallas_call | solution.py:406
  80.7 0.0 collective-permute-done.12
  80.7 0.9 %probe.1 = f32[2,256,256]{2,1,0:T(8,128)} custom-call(f32[8,128]{1,0:T(8,128)S(1)} %get-tuple-element.31.after_ref, f32[32,2,8,128]{3,2,1,0:T(8,128)S(1)} %bitcast.6, f32[32,2,8,128]{3,2,1,0:T(8,128)S(1)} %bitcast.8), custom_call_target="tpu_custom_call" | custom-call | bytes 2000000 | tf_op jit(solution)/shard_map/probe/pallas_call | solution.py:406
  (6 shorter events, 0.1 us)
Async XLA Ops:
  0.6 5.9 %copy-start.4 = (s32[2,2]{1,0:T(2,128)S(1)}, s32[2,2]{1,0:T(2,128)}, u32[]{:S(2)}) copy-start(s32[2,2]{1,0:T(2,128)} %offsets_ref.7) | copy-start | bytes 52
  0.6 6.1 %collective-permute-start.1 = (f32[2,2,128,384]{3,2,1,0:T(8,128)}, f32[2,2,128,384]{3,2,1,0:T(8,128)S(1)}, u32[]{:S(2)}, u32[]{:S(2)}) collective-permute-start(f32[2,2,128,384]{3,2,1,0:T(8,128)} %own_ref.3), channel_id=1, source_target_pairs={{0,1},{1,0},{2,3},{3,2},{4,5},{5,4},{6,7},{7,6},{8,9},{9,8},{10,11... | collective-permute-start | bytes 2359304 | tf_op jit(solution)/shard_map/ppermute | solution.py:427
  2.1 11.9 %collective-permute-start = (f32[2,2,128,384]{3,2,1,0:T(8,128)}, f32[2,2,128,384]{3,2,1,0:T(8,128)S(1)}, u32[]{:S(2)}, u32[]{:S(2)}) collective-permute-start(f32[2,2,128,384]{3,2,1,0:T(8,128)} %own_ref.3), channel_id=1, source_target_pairs={{0,127},{1,2},{2,1},{3,4},{4,3},{5,6},{6,5},{7,8},{8,7},{9,10},{10... | collective-permute-start | bytes 2359304 | tf_op jit(solution)/shard_map/ppermute | solution.py:427
  4.8 11.3 %copy-start.2 = (f32[2,256,256]{2,1,0:T(8,128)S(1)}, f32[2,256,256]{2,1,0:T(8,128)}, u32[]{:S(2)}) copy-start(f32[2,256,256]{2,1,0:T(8,128)} %amp_ref.1) | copy-start | bytes 1572868
  4.8 13.5 %collective-permute-start.2 = (f32[2,2,128,256]{3,2,1,0:T(8,128)S(1)}, f32[2,2,128,256]{3,2,1,0:T(8,128)S(1)}, u32[]{:S(2)}, u32[]{:S(2)}) collective-permute-start(f32[2,2,128,256]{3,2,1,0:T(8,128)S(1)} %core.1), channel_id=1, source_target_pairs={{0,64},{64,0},{1,65},{65,1},{2,66},{66,2},{3,67},{67,3},{4,68},{68... | collective-permute-start | bytes 1572872 | tf_op jit(solution)/shard_map/ppermute | solution.py:455
  14.1 3.2 %copy-start.3 = (f32[2,256,256]{2,1,0:T(8,128)S(1)}, f32[2,256,256]{2,1,0:T(8,128)}, u32[]{:S(2)}) copy-start(f32[2,256,256]{2,1,0:T(8,128)} %probe_ref.1) | copy-start | bytes 1572868
  14.2 3.9 %copy-start.1 = (f32[2,2,128,384]{3,2,1,0:T(8,128)S(1)}, f32[2,2,128,384]{3,2,1,0:T(8,128)}, u32[]{:S(2)}) copy-start(f32[2,2,128,384]{3,2,1,0:T(8,128)} %own_ref.3) | copy-start | bytes 2359300
  14.2 8.7 %collective-permute-start.3 = (f32[2,128,256]{2,1,0:T(8,128)S(1)}, f32[2,128,256]{2,1,0:T(8,128)S(1)}, u32[]{:S(2)}, u32[]{:S(2)}) collective-permute-start(f32[2,128,256]{2,1,0:T(8,128)S(1)} %get-tuple-element.17), channel_id=1, source_target_pairs={{0,64},{64,0},{1,65},{65,1},{2,66},{66,2},{3,67},{67,3},{4,68},{68... | collective-permute-start | bytes 786440 | tf_op jit(solution)/shard_map/ppermute | solution.py:455
  16.0 12.5 %collective-permute-start.4 = (f32[2,128,256]{2,1,0:T(8,128)S(1)}, f32[2,128,256]{2,1,0:T(8,128)S(1)}, u32[]{:S(2)}, u32[]{:S(2)}) collective-permute-start(f32[2,128,256]{2,1,0:T(8,128)S(1)} %get-tuple-element.18), channel_id=1, source_target_pairs={{0,64},{64,0},{1,65},{65,1},{2,66},{66,2},{3,67},{67,3},{4,68},{68... | collective-permute-start | bytes 786440 | tf_op jit(solution)/shard_map/ppermute | solution.py:455
  18.1 4.8 %copy-start = (bf16[6,2,2,256,256]{4,3,2,1,0:T(8,128)(2,1)S(1)}, bf16[6,2,2,256,256]{4,3,2,1,0:T(8,128)(2,1)}, u32[]{:S(2)}) copy-start(bf16[6,2,2,256,256]{4,3,2,1,0:T(8,128)(2,1)} %constant.10.clone.tables_ref) | copy-start | bytes 9437188
  34.9 23.4 %collective-permute-start.6 = (f32[1032,256]{1,0:T(8,128)S(1)}, f32[1032,256]{1,0:T(8,128)S(1)}, u32[]{:S(2)}, u32[]{:S(2)}) collective-permute-start(f32[1032,256]{1,0:T(8,128)S(1)} %get-tuple-element.24), channel_id=1, source_target_pairs={{0,1},{1,0},{2,3},{3,2},{4,5},{5,4},{6,7},{7,6},{8,9},{9,8},{10,11... | collective-permute-start | bytes 3170312 | tf_op jit(solution)/shard_map/ppermute | solution.py:427
  39.3 19.1 %collective-permute-start.5 = (f32[520,256]{1,0:T(8,128)S(1)}, f32[520,256]{1,0:T(8,128)S(1)}, u32[]{:S(2)}, u32[]{:S(2)}) collective-permute-start(f32[520,256]{1,0:T(8,128)S(1)} %get-tuple-element.23), channel_id=1, source_target_pairs={{0,127},{1,2},{2,1},{3,4},{4,3},{5,6},{6,5},{7,8},{8,7},{9,10},{10... | collective-permute-start | bytes 1597448 | tf_op jit(solution)/shard_map/ppermute | solution.py:427
  39.3 5.7 %collective-permute-start.7 = (f32[32,2,8,128]{3,2,1,0:T(8,128)S(1)}, f32[32,2,8,128]{3,2,1,0:T(8,128)S(1)}, u32[]{:S(2)}, u32[]{:S(2)}) collective-permute-start(f32[32,2,8,128]{3,2,1,0:T(8,128)S(1)} %get-tuple-element.27), channel_id=1, source_target_pairs={{0,1},{1,0},{2,3},{3,2},{4,5},{5,4},{6,7},{7,6},{8,9},{9,8},{10,11... | collective-permute-start | bytes 786440 | tf_op jit(solution)/shard_map/ppermute | solution.py:432
  55.7 2.7 %collective-permute-start.9 = (f32[4,8,128]{2,1,0:T(8,128)S(1)}, f32[4,8,128]{2,1,0:T(8,128)S(1)}, u32[]{:S(2)}, u32[]{:S(2)}) collective-permute-start(f32[4,8,128]{2,1,0:T(8,128)S(1)} %reduce.1.keep_ref), channel_id=1, source_target_pairs={{0,64},{64,0},{1,65},{65,1},{2,66},{66,2},{3,67},{67,3},{4,68},{68... | collective-permute-start | bytes 49160 | tf_op jit(solution)/shard_map/ppermute | solution.py:455
  58.6 20.9 %collective-permute-start.10 = (f32[2,2,128,384]{3,2,1,0:T(8,128)S(1)}, f32[2,2,128,384]{3,2,1,0:T(8,128)S(1)}, u32[]{:S(2)}, u32[]{:S(2)}) collective-permute-start(f32[2,2,128,384]{3,2,1,0:T(8,128)S(1)} %sum.1), channel_id=1, source_target_pairs={{0,64},{64,0},{1,65},{65,1},{2,66},{66,2},{3,67},{67,3},{4,68},{68... | collective-permute-start | bytes 2359304 | tf_op jit(solution)/shard_map/ppermute | solution.py:455
  58.7 5.3 %collective-permute-start.11 = (f32[4,8,128]{2,1,0:T(8,128)S(1)}, f32[4,8,128]{2,1,0:T(8,128)S(1)}, u32[]{:S(2)}, u32[]{:S(2)}) collective-permute-start(f32[4,8,128]{2,1,0:T(8,128)S(1)} %add_slabs.1.after_ref.first_ref), channel_id=1, source_target_pairs={{0,96},{1,97},{2,98},{3,99},{4,100},{5,101},{6,102},{7,103},{8,104... | collective-permute-start | bytes 49160 | tf_op jit(solution)/shard_map/ppermute | solution.py:451
  60.3 19.2 %collective-permute-start.8 = (f32[512,256]{1,0:T(8,128)S(1)}, f32[512,256]{1,0:T(8,128)S(1)}, u32[]{:S(2)}, u32[]{:S(2)}) collective-permute-start(f32[512,256]{1,0:T(8,128)S(1)} %get-tuple-element.28), channel_id=1, source_target_pairs={{0,127},{1,2},{2,1},{3,4},{4,3},{5,6},{6,5},{7,8},{8,7},{9,10},{10... | collective-permute-start | bytes 1572872 | tf_op jit(solution)/shard_map/ppermute | solution.py:427
  78.1 2.6 %collective-permute-start.12 = (f32[16,4,8,128]{3,2,1,0:T(8,128)S(1)}, f32[16,4,8,128]{3,2,1,0:T(8,128)S(1)}, u32[]{:S(2)}, u32[]{:S(2)}) collective-permute-start(f32[16,4,8,128]{3,2,1,0:T(8,128)S(1)} %all_to_all.11.after_ref), channel_id=1, source_target_pairs={{0,1},{1,0},{2,3},{3,2},{4,5},{5,4},{6,7},{7,6},{8,9},{9,8},{10,11... | collective-permute-start | bytes 786440 | tf_op jit(solution)/shard_map/ppermute | solution.py:432

commit v12 on v11

--- a/solution.py
+++ b/solution.py
@@ -375,7 +375,7 @@
     out_ref[...] = keep_ref[...] + got_ref[...]
 
 
-def reduce_kernel(parts_ref, out_ref):
+def reduce_kernel(parts_ref, after_ref, out_ref):
     out_ref[...] = jnp.sum(parts_ref[...], axis=0)
 
 
@@ -512,11 +512,12 @@
         nbytes=10_000_000,
         outs=(VMEM, VMEM, VMEM, VMEM, HBM, HBM),
     )
-    sides = (info, cores, swap_tile(early, 0), swap_tile(beside, 1))
+    early = swap_tile(early, 0)
     parts = (WIDTH // 16, 4, 8, HALF)
     kept = call(add_kernel, tiles, (), (keep, swap_core(send)), "add").reshape(parts)
-    kept = call(reduce_kernel, parts[1:], (), (among_columns(kept),), "reduce")
-    late, kept = lax.optimization_barrier((late, kept))
+    kept = call(reduce_kernel, parts[1:], (), (among_columns(kept), early), "reduce")
+    beside, late, kept = lax.optimization_barrier((beside, late, kept))
+    sides = (info, cores, early, swap_tile(beside, 1))
     late = swap_tile(late, 0)
     kept = call(add_kernel, parts[1:], (), (kept, swap_slab(kept)), "add_slabs")
     got = swap_slab(call(sum_kernel, band, (), sides + (kept,), "sum"))

time: 81.8 us -> 81.8 us (level)
    ppermute x5, starting transfers between devices: 10.9 us -> 8.78 us  [swap_tile(): return lax.ppermute(x, ('slab', 'tile'), pairs)]
    ppermute x2, starting transfers between devices: 5.96 us -> 7.83 us  [swap_core(): return lax.ppermute(x, 'tile', [(i, i ^ 1) for i in range(count)])]
  transfers between devices with their start and end apart: 13 -> 13, of which waited for: 5 -> 6; matrix products, arithmetic and copies ran while one was open for 0% -> 0% of each run, Pallas kernels for 7% -> 7%
where the time goes in v12:
time: 81.8 us; the launch traced here: 81.5 us
  blocking collectives  24.6 us (30%)
  starting transfers between devices  21.7 us (27%)
  waiting for transfers between devices  21.1 us (26%)
  Pallas kernels  13.2 us (16%)
    all_to_all x2, blocking collectives, among_columns(): lax.all_to_all(x, ('slab', 'tile'), 0, 0, tiled=True, axis_index_groups=g...  24.6 us
    pallas_call x14, Pallas kernels, call(): pl.pallas_call(kernel, out_shape=tuple((jax.ShapeDtypeStruct(shape, F32)...  13.2 us
    ppermute x5, waiting for transfers between devices, swap_slab(): return lax.ppermute(x, 'slab', [(0, 1), (1, 0)])  11.8 us
    ppermute x5, starting transfers between devices, swap_tile(): return lax.ppermute(x, ('slab', 'tile'), pairs)  8.78 us
    ppermute x2, starting transfers between devices, swap_core(): return lax.ppermute(x, 'tile', [(i, i ^ 1) for i in range(count)])  7.83 us
    ppermute x5, waiting for transfers between devices, swap_tile(): return lax.ppermute(x, ('slab', 'tile'), pairs)  7.34 us
    ppermute x5, starting transfers between devices, swap_slab(): return lax.ppermute(x, 'slab', [(0, 1), (1, 0)])  3.7 us
  transfers between devices with their start and end apart: 13, of which 6 were waited for; matrix products, arithmetic and copies ran while one was open for 0% of the time, Pallas kernels for 7%

profile of v12, /device:TPU:1, one launch (start us, length us, event | category | flops | bytes accessed | tf_op | source)
XLA Modules:
  0.0 81.5 jit_solution(2480903457756910333)
XLA Ops:
  0.6 0.0 copy-start.4
  0.6 1.5 %collective-permute-start.1 = (f32[2,2,128,384]{3,2,1,0:T(8,128)}, f32[2,2,128,384]{3,2,1,0:T(8,128)S(1)}, u32[]{:S(2)}, u32[]{:S(2)}) collective-permute-start(f32[2,2,128,384]{3,2,1,0:T(8,128)} %own_ref.3), channel_id=1, source_target_pairs={{0,1},{1,0},{2,3},{3,2},{4,5},{5,4},{6,7},{7,6},{8,9},{9,8},{10,11... | collective-permute-start | bytes 2359304 | tf_op jit(solution)/shard_map/ppermute | solution.py:427
  2.1 1.4 %collective-permute-start = (f32[2,2,128,384]{3,2,1,0:T(8,128)}, f32[2,2,128,384]{3,2,1,0:T(8,128)S(1)}, u32[]{:S(2)}, u32[]{:S(2)}) collective-permute-start(f32[2,2,128,384]{3,2,1,0:T(8,128)} %own_ref.3), channel_id=1, source_target_pairs={{0,127},{1,2},{2,1},{3,4},{4,3},{5,6},{6,5},{7,8},{8,7},{9,10},{10... | collective-permute-start | bytes 2359304 | tf_op jit(solution)/shard_map/ppermute | solution.py:427
  3.5 1.3 %core.1 = f32[2,2,128,256]{3,2,1,0:T(8,128)S(1)} custom-call(s32[2,2]{1,0:T(2,128)} %offsets_ref.7, f32[2,2,128,384]{3,2,1,0:T(8,128)} %own_ref.3), custom_call_target="tpu_custom_call" | custom-call | bytes 2000000 | tf_op jit(solution)/shard_map/core/pallas_call | solution.py:406
  4.8 0.0 copy-start.2
  4.8 1.7 %collective-permute-start.2 = (f32[2,2,128,256]{3,2,1,0:T(8,128)S(1)}, f32[2,2,128,256]{3,2,1,0:T(8,128)S(1)}, u32[]{:S(2)}, u32[]{:S(2)}) collective-permute-start(f32[2,2,128,256]{3,2,1,0:T(8,128)S(1)} %core.1), channel_id=1, source_target_pairs={{0,64},{64,0},{1,65},{65,1},{2,66},{66,2},{3,67},{67,3},{4,68},{68... | collective-permute-start | bytes 1572872 | tf_op jit(solution)/shard_map/ppermute | solution.py:455
  6.5 0.0 copy-done.4
  6.6 0.1 reshape.19
  6.7 0.1 add_bitcast_fusion
  6.7 0.0 collective-permute-done.1.beside_ref
  6.7 7.3 %collective-permute-done.across_ref = f32[2,2,128,384]{3,2,1,0:T(8,128)S(1)} collective-permute-done((f32[2,2,128,384]{3,2,1,0:T(8,128)}, f32[2,2,128,384]{3,2,1,0:T(8,128)S(1)}, u32[]{:S(2)}, u32[]{:S(2)}) %collective-permute-start) | collective-permute-done | bytes 786464 | tf_op jit(solution)/shard_map/ppermute | solution.py:427
  14.1 0.1 broadcast_in_dim.8.info_ref
  14.1 0.0 copy-start.3
  14.1 0.1 halo.1
  14.2 0.0 copy-start.1
  14.2 1.8 %collective-permute-start.3 = (f32[2,128,256]{2,1,0:T(8,128)S(1)}, f32[2,128,256]{2,1,0:T(8,128)S(1)}, u32[]{:S(2)}, u32[]{:S(2)}) collective-permute-start(f32[2,128,256]{2,1,0:T(8,128)S(1)} %get-tuple-element.18), channel_id=1, source_target_pairs={{0,64},{64,0},{1,65},{65,1},{2,66},{66,2},{3,67},{67,3},{4,68},{68... | collective-permute-start | bytes 786440 | tf_op jit(solution)/shard_map/ppermute | solution.py:455
  16.0 0.1 collective-permute-start.4
  16.1 0.0 copy-done.2
  16.1 1.2 %amp.1.amp_ref = f32[256,256]{1,0:T(8,128)S(1)} custom-call(s32[1]{0:T(128)} %bitcast.1.place_ref, s32[2,2]{1,0:T(2,128)S(1)} %copy-done.4, f32[2,256,256]{2,1,0:T(8,128)S(1)} %copy-done.2), custom_call_target="tpu_custom_call" | custom-call | bytes 2000000 | tf_op jit(solution)/shard_map/amp/pallas_call | solution.py:406
  17.3 0.0 copy-done.3
  17.3 0.8 roll.1.probe_ref
  18.1 0.0 copy-done.1
  18.1 0.0 copy-start
  18.1 0.1 window.1.own_ref
  18.3 0.0 collective-permute-done.2.core_ref
  18.3 4.7 %collective-permute-done.3.halo_ref = f32[2,128,256]{2,1,0:T(8,128)S(1)} collective-permute-done((f32[2,128,256]{2,1,0:T(8,128)S(1)}, f32[2,128,256]{2,1,0:T(8,128)S(1)}, u32[]{:S(2)}, u32[]{:S(2)}) %collective-permute-start.3) | collective-permute-done | bytes 262176 | tf_op jit(solution)/shard_map/ppermute | solution.py:455
  23.0 0.0 copy-done
  23.0 1.1 %first.1 = (f32[2,256,256]{2,1,0:T(8,128)S(1)}, f32[2,256,256]{2,1,0:T(8,128)S(1)}, f32[2,128,256]{2,1,0:T(8,128)S(1)}) custom-call(s32[8,128]{1,0:T(8,128)S(1)} %broadcast_in_dim.8.info_ref, bf16[6,2,2,256,256]{4,3,2,1,0:T(8,128)(2,1)S(1)} %copy-done, f32[2,256,256]{2,1,0:T(8,128)S(1)} %roll.1.probe_ref, f32[2,2,256,256]{3,2,1,0:T(8,128)S(1)} %window.1.own_ref, ...), custom_call_target="tpu_custom_call" | custom-call | bytes 2000000 | tf_op jit(solution)/shard_map/first/pallas_call | solution.py:406
  24.1 4.5 %collective-permute-done.4.second_halo_ref = f32[2,128,256]{2,1,0:T(8,128)S(1)} collective-permute-done((f32[2,128,256]{2,1,0:T(8,128)S(1)}, f32[2,128,256]{2,1,0:T(8,128)S(1)}, u32[]{:S(2)}, u32[]{:S(2)}) %collective-permute-start.4) | collective-permute-done | bytes 262176 | tf_op jit(solution)/shard_map/ppermute | solution.py:455
  28.6 6.4 %position.1 = (f32[32,2,8,128]{3,2,1,0:T(8,128)S(1)}, f32[32,2,8,128]{3,2,1,0:T(8,128)S(1)}, f32[4,2,128,256]{3,2,1,0:T(8,128)S(1)}, f32[1032,256]{1,0:T(8,128)S...) custom-call(s32[8,128]{1,0:T(8,128)S(1)} %broadcast_in_dim.8.info_ref, s32[2,2]{1,0:T(2,128)S(1)} %copy-done.4, ...), custom_call_target="tpu_custom_call" | custom-call | flops 3300000000 | bytes 10000000 | tf_op jit(solution)/shard_map/position/pallas_call | solution.py:406
  35.0 2.4 %collective-permute-start.5 = (f32[520,256]{1,0:T(8,128)S(1)}, f32[520,256]{1,0:T(8,128)S(1)}, u32[]{:S(2)}, u32[]{:S(2)}) collective-permute-start(f32[520,256]{1,0:T(8,128)S(1)} %get-tuple-element.24), channel_id=1, source_target_pairs={{0,127},{1,2},{2,1},{3,4},{4,3},{5,6},{6,5},{7,8},{8,7},{9,10},{10... | collective-permute-start | bytes 1597448 | tf_op jit(solution)/shard_map/ppermute | solution.py:427
  37.3 6.4 %collective-permute-start.6 = (f32[32,2,8,128]{3,2,1,0:T(8,128)S(1)}, f32[32,2,8,128]{3,2,1,0:T(8,128)S(1)}, u32[]{:S(2)}, u32[]{:S(2)}) collective-permute-start(f32[32,2,8,128]{3,2,1,0:T(8,128)S(1)} %get-tuple-element.28), channel_id=1, source_target_pairs={{0,1},{1,0},{2,3},{3,2},{4,5},{5,4},{6,7},{7,6},{8,9},{9,8},{10,11... | collective-permute-start | bytes 786440 | tf_op jit(solution)/shard_map/ppermute | solution.py:432
  43.8 1.2 %collective-permute-done.6.got_ref = f32[32,2,8,128]{3,2,1,0:T(8,128)S(1)} collective-permute-done((f32[32,2,8,128]{3,2,1,0:T(8,128)S(1)}, f32[32,2,8,128]{3,2,1,0:T(8,128)S(1)}, u32[]{:S(2)}, u32[]{:S(2)}) %collective-permute-start.6) | collective-permute-done | bytes 262176 | tf_op jit(solution)/shard_map/ppermute | solution.py:432
  45.0 10.6 %all_to_all.10.parts_ref = f32[16,4,8,128]{3,2,1,0:T(8,128)S(1)} all-to-all(f32[16,4,8,128]{3,2,1,0:T(8,128)S(1)} %bitcast.7), channel_id=1, replica_groups={{0,2,4,6,8,10,12,14,16,18,20,22,24,26,28,30},{1,3,5,7,9,11,13,15,17,19,..., dimensions={0} | all-to-all | bytes 524288 | tf_op jit(solution)/shard_map/all_to_all | solution.py:440
  55.6 0.0 collective-permute-done.5.after_ref.early_ref
  55.6 1.8 %collective-permute-start.7 = (f32[1032,256]{1,0:T(8,128)S(1)}, f32[1032,256]{1,0:T(8,128)S(1)}, u32[]{:S(2)}, u32[]{:S(2)}) collective-permute-start(f32[1032,256]{1,0:T(8,128)S(1)} %get-tuple-element.29), channel_id=1, source_target_pairs={{0,1},{1,0},{2,3},{3,2},{4,5},{5,4},{6,7},{7,6},{8,9},{9,8},{10,11... | collective-permute-start | bytes 3170312 | tf_op jit(solution)/shard_map/ppermute | solution.py:427
  57.4 0.0 collective-permute-start.9
  57.4 2.6 %collective-permute-done.9.got_ref = f32[4,8,128]{2,1,0:T(8,128)S(1)} collective-permute-done((f32[4,8,128]{2,1,0:T(8,128)S(1)}, f32[4,8,128]{2,1,0:T(8,128)S(1)}, u32[]{:S(2)}, u32[]{:S(2)}) %collective-permute-start.9) | collective-permute-done | bytes 16416 | tf_op jit(solution)/shard_map/ppermute | solution.py:455
  60.0 0.0 collective-permute-done.7.beside_ref
  60.0 0.2 sum.1
  60.2 0.1 collective-permute-start.10
  60.3 1.4 %collective-permute-start.11 = (f32[4,8,128]{2,1,0:T(8,128)S(1)}, f32[4,8,128]{2,1,0:T(8,128)S(1)}, u32[]{:S(2)}, u32[]{:S(2)}) collective-permute-start(f32[4,8,128]{2,1,0:T(8,128)S(1)} %add_slabs.1.after_ref.first_ref), channel_id=1, source_target_pairs={{0,96},{1,97},{2,98},{3,99},{4,100},{5,101},{6,102},{7,103},{8,104... | collective-permute-start | bytes 49160 | tf_op jit(solution)/shard_map/ppermute | solution.py:451
  61.7 1.8 %collective-permute-start.8 = (f32[512,256]{1,0:T(8,128)S(1)}, f32[512,256]{1,0:T(8,128)S(1)}, u32[]{:S(2)}, u32[]{:S(2)}) collective-permute-start(f32[512,256]{1,0:T(8,128)S(1)} %get-tuple-element.30), channel_id=1, source_target_pairs={{0,127},{1,2},{2,1},{3,4},{4,3},{5,6},{6,5},{7,8},{8,7},{9,10},{10... | collective-permute-start | bytes 1572872 | tf_op jit(solution)/shard_map/ppermute | solution.py:427
  63.5 0.7 collective-permute-done.11.second_ref
  64.2 13.9 %all_to_all.11.after_ref = f32[16,4,8,128]{3,2,1,0:T(8,128)S(1)} all-to-all(f32[16,4,8,128]{3,2,1,0:T(8,128)S(1)} %total.1), channel_id=1, replica_groups={{0,2,4,6,8,10,12,14,16,18,20,22,24,26,28,30},{1,3,5,7,9,11,13,15,17,19,..., dimensions={0} | all-to-all | bytes 524288 | tf_op jit(solution)/shard_map/all_to_all | solution.py:440
  78.1 1.4 %collective-permute-start.12 = (f32[16,4,8,128]{3,2,1,0:T(8,128)S(1)}, f32[16,4,8,128]{3,2,1,0:T(8,128)S(1)}, u32[]{:S(2)}, u32[]{:S(2)}) collective-permute-start(f32[16,4,8,128]{3,2,1,0:T(8,128)S(1)} %all_to_all.11.after_ref), channel_id=1, source_target_pairs={{0,1},{1,0},{2,3},{3,2},{4,5},{5,4},{6,7},{7,6},{8,9},{9,8},{10,11... | collective-permute-start | bytes 786440 | tf_op jit(solution)/shard_map/ppermute | solution.py:432
  79.5 0.0 collective-permute-done.8.late_ref
  79.5 0.0 collective-permute-done.10.swapped_ref
  79.5 1.1 %object.1 = (f32[2,2,128,384]{3,2,1,0:T(8,128)}, f32[8,128]{1,0:T(8,128)S(1)}) custom-call(s32[8,128]{1,0:T(8,128)S(1)} %broadcast_in_dim.8.info_ref, f32[4,2,128,256]{3,2,1,0:T(8,128)S(1)} %get-tuple-element.23.core_ref, f32[520,256]{1,0:T(8,128)S(1)} %collective-permute-done.5.after_ref.early_ref, f32[1032,256]{1,0:T(8,128)S(1)} %collective-permute-done.7.beside_ref, ...), custom_call_target="tpu_custom_call" | custom-call | bytes 2000000 | tf_op jit(solution)/shard_map/object/pallas_call | solution.py:406
  80.7 0.0 collective-permute-done.12
  80.7 0.8 %probe.1 = f32[2,256,256]{2,1,0:T(8,128)} custom-call(f32[8,128]{1,0:T(8,128)S(1)} %get-tuple-element.33.after_ref, f32[32,2,8,128]{3,2,1,0:T(8,128)S(1)} %bitcast.6, f32[32,2,8,128]{3,2,1,0:T(8,128)S(1)} %bitcast.8), custom_call_target="tpu_custom_call" | custom-call | bytes 2000000 | tf_op jit(solution)/shard_map/probe/pallas_call | solution.py:406
  (6 shorter events, 0.1 us)
Async XLA Ops:
  0.6 5.9 %copy-start.4 = (s32[2,2]{1,0:T(2,128)S(1)}, s32[2,2]{1,0:T(2,128)}, u32[]{:S(2)}) copy-start(s32[2,2]{1,0:T(2,128)} %offsets_ref.7) | copy-start | bytes 52
  0.6 6.1 %collective-permute-start.1 = (f32[2,2,128,384]{3,2,1,0:T(8,128)}, f32[2,2,128,384]{3,2,1,0:T(8,128)S(1)}, u32[]{:S(2)}, u32[]{:S(2)}) collective-permute-start(f32[2,2,128,384]{3,2,1,0:T(8,128)} %own_ref.3), channel_id=1, source_target_pairs={{0,1},{1,0},{2,3},{3,2},{4,5},{5,4},{6,7},{7,6},{8,9},{9,8},{10,11... | collective-permute-start | bytes 2359304 | tf_op jit(solution)/shard_map/ppermute | solution.py:427
  2.1 11.9 %collective-permute-start = (f32[2,2,128,384]{3,2,1,0:T(8,128)}, f32[2,2,128,384]{3,2,1,0:T(8,128)S(1)}, u32[]{:S(2)}, u32[]{:S(2)}) collective-permute-start(f32[2,2,128,384]{3,2,1,0:T(8,128)} %own_ref.3), channel_id=1, source_target_pairs={{0,127},{1,2},{2,1},{3,4},{4,3},{5,6},{6,5},{7,8},{8,7},{9,10},{10... | collective-permute-start | bytes 2359304 | tf_op jit(solution)/shard_map/ppermute | solution.py:427
  4.8 11.3 %copy-start.2 = (f32[2,256,256]{2,1,0:T(8,128)S(1)}, f32[2,256,256]{2,1,0:T(8,128)}, u32[]{:S(2)}) copy-start(f32[2,256,256]{2,1,0:T(8,128)} %amp_ref.1) | copy-start | bytes 1572868
  4.8 13.5 %collective-permute-start.2 = (f32[2,2,128,256]{3,2,1,0:T(8,128)S(1)}, f32[2,2,128,256]{3,2,1,0:T(8,128)S(1)}, u32[]{:S(2)}, u32[]{:S(2)}) collective-permute-start(f32[2,2,128,256]{3,2,1,0:T(8,128)S(1)} %core.1), channel_id=1, source_target_pairs={{0,64},{64,0},{1,65},{65,1},{2,66},{66,2},{3,67},{67,3},{4,68},{68... | collective-permute-start | bytes 1572872 | tf_op jit(solution)/shard_map/ppermute | solution.py:455
  14.1 3.2 %copy-start.3 = (f32[2,256,256]{2,1,0:T(8,128)S(1)}, f32[2,256,256]{2,1,0:T(8,128)}, u32[]{:S(2)}) copy-start(f32[2,256,256]{2,1,0:T(8,128)} %probe_ref.1) | copy-start | bytes 1572868
  14.2 3.9 %copy-start.1 = (f32[2,2,128,384]{3,2,1,0:T(8,128)S(1)}, f32[2,2,128,384]{3,2,1,0:T(8,128)}, u32[]{:S(2)}) copy-start(f32[2,2,128,384]{3,2,1,0:T(8,128)} %own_ref.3) | copy-start | bytes 2359300
  14.2 8.7 %collective-permute-start.3 = (f32[2,128,256]{2,1,0:T(8,128)S(1)}, f32[2,128,256]{2,1,0:T(8,128)S(1)}, u32[]{:S(2)}, u32[]{:S(2)}) collective-permute-start(f32[2,128,256]{2,1,0:T(8,128)S(1)} %get-tuple-element.18), channel_id=1, source_target_pairs={{0,64},{64,0},{1,65},{65,1},{2,66},{66,2},{3,67},{67,3},{4,68},{68... | collective-permute-start | bytes 786440 | tf_op jit(solution)/shard_map/ppermute | solution.py:455
  16.0 12.5 %collective-permute-start.4 = (f32[2,128,256]{2,1,0:T(8,128)S(1)}, f32[2,128,256]{2,1,0:T(8,128)S(1)}, u32[]{:S(2)}, u32[]{:S(2)}) collective-permute-start(f32[2,128,256]{2,1,0:T(8,128)S(1)} %get-tuple-element.19), channel_id=1, source_target_pairs={{0,64},{64,0},{1,65},{65,1},{2,66},{66,2},{3,67},{67,3},{4,68},{68... | collective-permute-start | bytes 786440 | tf_op jit(solution)/shard_map/ppermute | solution.py:455
  18.1 4.8 %copy-start = (bf16[6,2,2,256,256]{4,3,2,1,0:T(8,128)(2,1)S(1)}, bf16[6,2,2,256,256]{4,3,2,1,0:T(8,128)(2,1)}, u32[]{:S(2)}) copy-start(bf16[6,2,2,256,256]{4,3,2,1,0:T(8,128)(2,1)} %constant.10.clone.tables_ref) | copy-start | bytes 9437188
  35.0 20.7 %collective-permute-start.5 = (f32[520,256]{1,0:T(8,128)S(1)}, f32[520,256]{1,0:T(8,128)S(1)}, u32[]{:S(2)}, u32[]{:S(2)}) collective-permute-start(f32[520,256]{1,0:T(8,128)S(1)} %get-tuple-element.24), channel_id=1, source_target_pairs={{0,127},{1,2},{2,1},{3,4},{4,3},{5,6},{6,5},{7,8},{8,7},{9,10},{10... | collective-permute-start | bytes 1597448 | tf_op jit(solution)/shard_map/ppermute | solution.py:427
  37.3 7.6 %collective-permute-start.6 = (f32[32,2,8,128]{3,2,1,0:T(8,128)S(1)}, f32[32,2,8,128]{3,2,1,0:T(8,128)S(1)}, u32[]{:S(2)}, u32[]{:S(2)}) collective-permute-start(f32[32,2,8,128]{3,2,1,0:T(8,128)S(1)} %get-tuple-element.28), channel_id=1, source_target_pairs={{0,1},{1,0},{2,3},{3,2},{4,5},{5,4},{6,7},{7,6},{8,9},{9,8},{10,11... | collective-permute-start | bytes 786440 | tf_op jit(solution)/shard_map/ppermute | solution.py:432
  55.6 4.4 %collective-permute-start.7 = (f32[1032,256]{1,0:T(8,128)S(1)}, f32[1032,256]{1,0:T(8,128)S(1)}, u32[]{:S(2)}, u32[]{:S(2)}) collective-permute-start(f32[1032,256]{1,0:T(8,128)S(1)} %get-tuple-element.29), channel_id=1, source_target_pairs={{0,1},{1,0},{2,3},{3,2},{4,5},{5,4},{6,7},{7,6},{8,9},{9,8},{10,11... | collective-permute-start | bytes 3170312 | tf_op jit(solution)/shard_map/ppermute | solution.py:427
  57.4 2.6 %collective-permute-start.9 = (f32[4,8,128]{2,1,0:T(8,128)S(1)}, f32[4,8,128]{2,1,0:T(8,128)S(1)}, u32[]{:S(2)}, u32[]{:S(2)}) collective-permute-start(f32[4,8,128]{2,1,0:T(8,128)S(1)} %reduce.1.keep_ref), channel_id=1, source_target_pairs={{0,64},{64,0},{1,65},{65,1},{2,66},{66,2},{3,67},{67,3},{4,68},{68... | collective-permute-start | bytes 49160 | tf_op jit(solution)/shard_map/ppermute | solution.py:455
  60.2 19.3 %collective-permute-start.10 = (f32[2,2,128,384]{3,2,1,0:T(8,128)S(1)}, f32[2,2,128,384]{3,2,1,0:T(8,128)S(1)}, u32[]{:S(2)}, u32[]{:S(2)}) collective-permute-start(f32[2,2,128,384]{3,2,1,0:T(8,128)S(1)} %sum.1), channel_id=1, source_target_pairs={{0,64},{64,0},{1,65},{65,1},{2,66},{66,2},{3,67},{67,3},{4,68},{68... | collective-permute-start | bytes 2359304 | tf_op jit(solution)/shard_map/ppermute | solution.py:455
  60.3 3.9 %collective-permute-start.11 = (f32[4,8,128]{2,1,0:T(8,128)S(1)}, f32[4,8,128]{2,1,0:T(8,128)S(1)}, u32[]{:S(2)}, u32[]{:S(2)}) collective-permute-start(f32[4,8,128]{2,1,0:T(8,128)S(1)} %add_slabs.1.after_ref.first_ref), channel_id=1, source_target_pairs={{0,96},{1,97},{2,98},{3,99},{4,100},{5,101},{6,102},{7,103},{8,104... | collective-permute-start | bytes 49160 | tf_op jit(solution)/shard_map/ppermute | solution.py:451
  61.7 17.9 %collective-permute-start.8 = (f32[512,256]{1,0:T(8,128)S(1)}, f32[512,256]{1,0:T(8,128)S(1)}, u32[]{:S(2)}, u32[]{:S(2)}) collective-permute-start(f32[512,256]{1,0:T(8,128)S(1)} %get-tuple-element.30), channel_id=1, source_target_pairs={{0,127},{1,2},{2,1},{3,4},{4,3},{5,6},{6,5},{7,8},{8,7},{9,10},{10... | collective-permute-start | bytes 1572872 | tf_op jit(solution)/shard_map/ppermute | solution.py:427
  78.1 2.6 %collective-permute-start.12 = (f32[16,4,8,128]{3,2,1,0:T(8,128)S(1)}, f32[16,4,8,128]{3,2,1,0:T(8,128)S(1)}, u32[]{:S(2)}, u32[]{:S(2)}) collective-permute-start(f32[16,4,8,128]{3,2,1,0:T(8,128)S(1)} %all_to_all.11.after_ref), channel_id=1, source_target_pairs={{0,1},{1,0},{2,3},{3,2},{4,5},{5,4},{6,7},{7,6},{8,9},{9,8},{10,11... | collective-permute-start | bytes 786440 | tf_op jit(solution)/shard_map/ppermute | solution.py:432

commit v13 on v12

--- a/solution.py
+++ b/solution.py
@@ -227,8 +227,10 @@
     return window_of
 
 
-def first_kernel(info_ref, tables_ref, probe_ref, own_ref, core_ref, halo_ref, wave_out, window_out, lower_out):
-    window = selector(info_ref, own_ref, core_ref, (halo_ref, None))(0)
+def first_kernel(info_ref, tables_ref, probe_ref, own_ref, core_ref, halo_ref, wave_out, window_out, third_out, lower_out):
+    window_of = selector(info_ref, own_ref, core_ref, (halo_ref, None))
+    window = window_of(0)
+    third_out[0], third_out[1] = window_of(2)
     window_out[0], window_out[1] = window
     wave = propagate(times((probe_ref[0], probe_ref[1]), window), tables_ref)
     wave_out[0], wave_out[1] = wave
@@ -251,6 +253,7 @@
     second_halo_ref,
     first_wave_ref,
     first_window_ref,
+    third_window_ref,
     lower_ref,
     keep_out,
     send_out,
@@ -271,8 +274,11 @@
     for s in range(1, 4):
         if s > 1:
             waves[s - 2, 0], waves[s - 2, 1] = wave
-        window = window_of(s)
-        windows[s - 1, 0], windows[s - 1, 1] = window
+        if s == 2:
+            window = (third_window_ref[0], third_window_ref[1])
+        else:
+            window = window_of(s)
+            windows[s // 2, 0], windows[s // 2, 1] = window
         if s == 1:
             upper = times((wave[0][:HALO], wave[1][:HALO]), (window[0][:HALO], window[1][:HALO]))
             upper = right_mult((fold_columns(upper[0]), fold_columns(upper[1])), tables_ref, PROP_RIGHT)
@@ -291,7 +297,7 @@
         return ref[0], ref[1]
 
     def window_at(s):
-        ref = first_window_ref if s == 0 else windows.at[s - 1]
+        ref = (first_window_ref, windows.at[0], third_window_ref, windows.at[1])[s]
         return ref[0], ref[1]
 
     field = right_mult((fold(prod[0]), fold(prod[1])), tables_ref, FAR_RIGHT)
@@ -487,9 +493,9 @@
     halo, second_halo = swap_slab(halo), swap_slab(second_halo)
     windows = call(window_kernel, whole, (), (info, own, across, beside), "window")
 
-    wave, window, lower = call(
+    wave, window, third, lower = call(
         first_kernel,
-        (probe.shape, probe.shape, part[1:]),
+        (probe.shape, probe.shape, probe.shape, part[1:]),
         (),
         (info, tables, rolled, windows, core, halo),
         "first",
@@ -499,15 +505,15 @@
         position_kernel,
         (tiles, tiles, (4, 2, HALO, WIDTH), (8 * HALO + 8, WIDTH), (4 * HALO + 8, WIDTH), (4 * HALO, WIDTH)),
         (),
-        (info, scan_offsets, tables, rolled, amp, windows, core, halo, second_halo, wave, window, lower),
+        (info, scan_offsets, tables, rolled, amp, windows, core, halo, second_halo, wave, window, third, lower),
         "position",
         scratch=[
             pltpu.VMEM((2, 2, WIDTH, WIDTH), F32),
-            pltpu.VMEM((3, 2, WIDTH, WIDTH), F32),
+            pltpu.VMEM((2, 2, WIDTH, WIDTH), F32),
             pltpu.SMEM((2, 2), jnp.int32),
             pltpu.SemaphoreType.DMA((2, 6)),
         ],
-        ins=(VMEM, HBM) + (VMEM,) * 10,
+        ins=(VMEM, HBM) + (VMEM,) * 11,
         flops=3_300_000_000,
         nbytes=10_000_000,
         outs=(VMEM, VMEM, VMEM, VMEM, HBM, HBM),

time: 81.8 us -> 81.7 us (level)
  no operation moved by 1% of the time
where the time goes in v13:
time: 81.7 us; the launch traced here: 81.5 us
  blocking collectives  24.6 us (30%)
  starting transfers between devices  21.7 us (27%)
  waiting for transfers between devices  21 us (26%)
  Pallas kernels  13.1 us (16%)
    all_to_all x2, blocking collectives, among_columns(): lax.all_to_all(x, ('slab', 'tile'), 0, 0, tiled=True, axis_index_groups=g...  24.6 us
    pallas_call x14, Pallas kernels, call(): pl.pallas_call(kernel, out_shape=tuple((jax.ShapeDtypeStruct(shape, F32)...  13.1 us
    ppermute x5, waiting for transfers between devices, swap_slab(): return lax.ppermute(x, 'slab', [(0, 1), (1, 0)])  11.8 us
    ppermute x5, starting transfers between devices, swap_tile(): return lax.ppermute(x, ('slab', 'tile'), pairs)  8.78 us
    ppermute x2, starting transfers between devices, swap_core(): return lax.ppermute(x, 'tile', [(i, i ^ 1) for i in range(count)])  7.83 us
    ppermute x5, waiting for transfers between devices, swap_tile(): return lax.ppermute(x, ('slab', 'tile'), pairs)  7.34 us
    ppermute x5, starting transfers between devices, swap_slab(): return lax.ppermute(x, 'slab', [(0, 1), (1, 0)])  3.7 us
  transfers between devices with their start and end apart: 13, of which 6 were waited for; matrix products, arithmetic and copies ran while one was open for 0% of the time, Pallas kernels for 7%

profile of v13, /device:TPU:1, one launch (start us, length us, event | category | flops | bytes accessed | tf_op | source)
XLA Modules:
  0.0 81.5 jit_solution(9509144363345731648)
XLA Ops:
  0.6 0.0 copy-start.4
  0.6 1.5 %collective-permute-start.1 = (f32[2,2,128,384]{3,2,1,0:T(8,128)}, f32[2,2,128,384]{3,2,1,0:T(8,128)S(1)}, u32[]{:S(2)}, u32[]{:S(2)}) collective-permute-start(f32[2,2,128,384]{3,2,1,0:T(8,128)} %own_ref.3), channel_id=1, source_target_pairs={{0,1},{1,0},{2,3},{3,2},{4,5},{5,4},{6,7},{7,6},{8,9},{9,8},{10,11... | collective-permute-start | bytes 2359304 | tf_op jit(solution)/shard_map/ppermute | solution.py:433
  2.1 1.4 %collective-permute-start = (f32[2,2,128,384]{3,2,1,0:T(8,128)}, f32[2,2,128,384]{3,2,1,0:T(8,128)S(1)}, u32[]{:S(2)}, u32[]{:S(2)}) collective-permute-start(f32[2,2,128,384]{3,2,1,0:T(8,128)} %own_ref.3), channel_id=1, source_target_pairs={{0,127},{1,2},{2,1},{3,4},{4,3},{5,6},{6,5},{7,8},{8,7},{9,10},{10... | collective-permute-start | bytes 2359304 | tf_op jit(solution)/shard_map/ppermute | solution.py:433
  3.5 1.3 %core.1 = f32[2,2,128,256]{3,2,1,0:T(8,128)S(1)} custom-call(s32[2,2]{1,0:T(2,128)} %offsets_ref.7, f32[2,2,128,384]{3,2,1,0:T(8,128)} %own_ref.3), custom_call_target="tpu_custom_call" | custom-call | bytes 2000000 | tf_op jit(solution)/shard_map/core/pallas_call | solution.py:412
  4.8 0.0 copy-start.2
  4.8 1.7 %collective-permute-start.2 = (f32[2,2,128,256]{3,2,1,0:T(8,128)S(1)}, f32[2,2,128,256]{3,2,1,0:T(8,128)S(1)}, u32[]{:S(2)}, u32[]{:S(2)}) collective-permute-start(f32[2,2,128,256]{3,2,1,0:T(8,128)S(1)} %core.1), channel_id=1, source_target_pairs={{0,64},{64,0},{1,65},{65,1},{2,66},{66,2},{3,67},{67,3},{4,68},{68... | collective-permute-start | bytes 1572872 | tf_op jit(solution)/shard_map/ppermute | solution.py:461
  6.5 0.0 copy-done.4
  6.6 0.1 reshape.19
  6.7 0.1 add_bitcast_fusion
  6.7 0.0 collective-permute-done.1.beside_ref
  6.7 7.3 %collective-permute-done.across_ref = f32[2,2,128,384]{3,2,1,0:T(8,128)S(1)} collective-permute-done((f32[2,2,128,384]{3,2,1,0:T(8,128)}, f32[2,2,128,384]{3,2,1,0:T(8,128)S(1)}, u32[]{:S(2)}, u32[]{:S(2)}) %collective-permute-start) | collective-permute-done | bytes 786464 | tf_op jit(solution)/shard_map/ppermute | solution.py:433
  14.1 0.1 broadcast_in_dim.8.info_ref
  14.1 0.0 copy-start.3
  14.1 0.1 halo.1
  14.2 0.0 copy-start.1
  14.2 1.8 %collective-permute-start.3 = (f32[2,128,256]{2,1,0:T(8,128)S(1)}, f32[2,128,256]{2,1,0:T(8,128)S(1)}, u32[]{:S(2)}, u32[]{:S(2)}) collective-permute-start(f32[2,128,256]{2,1,0:T(8,128)S(1)} %get-tuple-element.19), channel_id=1, source_target_pairs={{0,64},{64,0},{1,65},{65,1},{2,66},{66,2},{3,67},{67,3},{4,68},{68... | collective-permute-start | bytes 786440 | tf_op jit(solution)/shard_map/ppermute | solution.py:461
  16.0 0.1 collective-permute-start.4
  16.1 0.0 copy-done.2
  16.1 1.2 %amp.1.amp_ref = f32[256,256]{1,0:T(8,128)S(1)} custom-call(s32[1]{0:T(128)} %bitcast.1.place_ref, s32[2,2]{1,0:T(2,128)S(1)} %copy-done.4, f32[2,256,256]{2,1,0:T(8,128)S(1)} %copy-done.2), custom_call_target="tpu_custom_call" | custom-call | bytes 2000000 | tf_op jit(solution)/shard_map/amp/pallas_call | solution.py:412
  17.3 0.0 copy-done.3
  17.3 0.8 roll.1.probe_ref
  18.1 0.0 copy-done.1
  18.1 0.0 copy-start
  18.1 0.1 window.1.own_ref
  18.3 0.0 collective-permute-done.2.core_ref
  18.3 4.7 %collective-permute-done.3.halo_ref = f32[2,128,256]{2,1,0:T(8,128)S(1)} collective-permute-done((f32[2,128,256]{2,1,0:T(8,128)S(1)}, f32[2,128,256]{2,1,0:T(8,128)S(1)}, u32[]{:S(2)}, u32[]{:S(2)}) %collective-permute-start.3) | collective-permute-done | bytes 262176 | tf_op jit(solution)/shard_map/ppermute | solution.py:461
  23.0 0.0 copy-done
  23.0 1.1 %first.1 = (f32[2,256,256]{2,1,0:T(8,128)S(1)}, f32[2,256,256]{2,1,0:T(8,128)S(1)}, f32[2,256,256]{2,1,0:T(8,128)S(1)}, f32[2,128,256]{2,1,0:T(8,128)S(1)}) custom-call(s32[8,128]{1,0:T(8,128)S(1)} %broadcast_in_dim.8.info_ref, bf16[6,2,2,256,256]{4,3,2,1,0:T(8,128)(2,1)S(1)} %copy-done, f32[2,256,256]{2,1,0:T(8,128)S(1)} %roll.1.probe_ref, ...), custom_call_target="tpu_custom_call" | custom-call | bytes 2000000 | tf_op jit(solution)/shard_map/first/pallas_call | solution.py:412
  24.1 4.5 %collective-permute-done.4.second_halo_ref = f32[2,128,256]{2,1,0:T(8,128)S(1)} collective-permute-done((f32[2,128,256]{2,1,0:T(8,128)S(1)}, f32[2,128,256]{2,1,0:T(8,128)S(1)}, u32[]{:S(2)}, u32[]{:S(2)}) %collective-permute-start.4) | collective-permute-done | bytes 262176 | tf_op jit(solution)/shard_map/ppermute | solution.py:461
  28.6 6.3 %position.1 = (f32[32,2,8,128]{3,2,1,0:T(8,128)S(1)}, f32[32,2,8,128]{3,2,1,0:T(8,128)S(1)}, f32[4,2,128,256]{3,2,1,0:T(8,128)S(1)}, f32[1032,256]{1,0:T(8,128)S...) custom-call(s32[8,128]{1,0:T(8,128)S(1)} %broadcast_in_dim.8.info_ref, s32[2,2]{1,0:T(2,128)S(1)} %copy-done.4, ...), custom_call_target="tpu_custom_call" | custom-call | flops 3300000000 | bytes 10000000 | tf_op jit(solution)/shard_map/position/pallas_call | solution.py:412
  34.9 2.4 %collective-permute-start.5 = (f32[520,256]{1,0:T(8,128)S(1)}, f32[520,256]{1,0:T(8,128)S(1)}, u32[]{:S(2)}, u32[]{:S(2)}) collective-permute-start(f32[520,256]{1,0:T(8,128)S(1)} %get-tuple-element.26), channel_id=1, source_target_pairs={{0,127},{1,2},{2,1},{3,4},{4,3},{5,6},{6,5},{7,8},{8,7},{9,10},{10... | collective-permute-start | bytes 1597448 | tf_op jit(solution)/shard_map/ppermute | solution.py:433
  37.2 6.4 %collective-permute-start.6 = (f32[32,2,8,128]{3,2,1,0:T(8,128)S(1)}, f32[32,2,8,128]{3,2,1,0:T(8,128)S(1)}, u32[]{:S(2)}, u32[]{:S(2)}) collective-permute-start(f32[32,2,8,128]{3,2,1,0:T(8,128)S(1)} %get-tuple-element.30), channel_id=1, source_target_pairs={{0,1},{1,0},{2,3},{3,2},{4,5},{5,4},{6,7},{7,6},{8,9},{9,8},{10,11... | collective-permute-start | bytes 786440 | tf_op jit(solution)/shard_map/ppermute | solution.py:438
  43.7 1.2 %collective-permute-done.6.got_ref = f32[32,2,8,128]{3,2,1,0:T(8,128)S(1)} collective-permute-done((f32[32,2,8,128]{3,2,1,0:T(8,128)S(1)}, f32[32,2,8,128]{3,2,1,0:T(8,128)S(1)}, u32[]{:S(2)}, u32[]{:S(2)}) %collective-permute-start.6) | collective-permute-done | bytes 262176 | tf_op jit(solution)/shard_map/ppermute | solution.py:438
  44.9 10.6 %all_to_all.10.parts_ref = f32[16,4,8,128]{3,2,1,0:T(8,128)S(1)} all-to-all(f32[16,4,8,128]{3,2,1,0:T(8,128)S(1)} %bitcast.7), channel_id=1, replica_groups={{0,2,4,6,8,10,12,14,16,18,20,22,24,26,28,30},{1,3,5,7,9,11,13,15,17,19,..., dimensions={0} | all-to-all | bytes 524288 | tf_op jit(solution)/shard_map/all_to_all | solution.py:446
  55.5 0.0 collective-permute-done.5.after_ref.early_ref
  55.6 1.8 %collective-permute-start.7 = (f32[1032,256]{1,0:T(8,128)S(1)}, f32[1032,256]{1,0:T(8,128)S(1)}, u32[]{:S(2)}, u32[]{:S(2)}) collective-permute-start(f32[1032,256]{1,0:T(8,128)S(1)} %get-tuple-element.31), channel_id=1, source_target_pairs={{0,1},{1,0},{2,3},{3,2},{4,5},{5,4},{6,7},{7,6},{8,9},{9,8},{10,11... | collective-permute-start | bytes 3170312 | tf_op jit(solution)/shard_map/ppermute | solution.py:433
  57.3 0.0 collective-permute-start.9
  57.3 2.6 %collective-permute-done.9.got_ref = f32[4,8,128]{2,1,0:T(8,128)S(1)} collective-permute-done((f32[4,8,128]{2,1,0:T(8,128)S(1)}, f32[4,8,128]{2,1,0:T(8,128)S(1)}, u32[]{:S(2)}, u32[]{:S(2)}) %collective-permute-start.9) | collective-permute-done | bytes 16416 | tf_op jit(solution)/shard_map/ppermute | solution.py:461
  59.9 0.0 collective-permute-done.7.beside_ref
  59.9 0.2 sum.1
  60.1 0.1 collective-permute-start.10
  60.2 1.4 %collective-permute-start.11 = (f32[4,8,128]{2,1,0:T(8,128)S(1)}, f32[4,8,128]{2,1,0:T(8,128)S(1)}, u32[]{:S(2)}, u32[]{:S(2)}) collective-permute-start(f32[4,8,128]{2,1,0:T(8,128)S(1)} %add_slabs.1.after_ref.first_ref), channel_id=1, source_target_pairs={{0,96},{1,97},{2,98},{3,99},{4,100},{5,101},{6,102},{7,103},{8,104... | collective-permute-start | bytes 49160 | tf_op jit(solution)/shard_map/ppermute | solution.py:457
  61.6 1.8 %collective-permute-start.8 = (f32[512,256]{1,0:T(8,128)S(1)}, f32[512,256]{1,0:T(8,128)S(1)}, u32[]{:S(2)}, u32[]{:S(2)}) collective-permute-start(f32[512,256]{1,0:T(8,128)S(1)} %get-tuple-element.32), channel_id=1, source_target_pairs={{0,127},{1,2},{2,1},{3,4},{4,3},{5,6},{6,5},{7,8},{8,7},{9,10},{10... | collective-permute-start | bytes 1572872 | tf_op jit(solution)/shard_map/ppermute | solution.py:433
  63.4 0.7 collective-permute-done.11.second_ref
  64.1 13.9 %all_to_all.11.after_ref = f32[16,4,8,128]{3,2,1,0:T(8,128)S(1)} all-to-all(f32[16,4,8,128]{3,2,1,0:T(8,128)S(1)} %total.1), channel_id=1, replica_groups={{0,2,4,6,8,10,12,14,16,18,20,22,24,26,28,30},{1,3,5,7,9,11,13,15,17,19,..., dimensions={0} | all-to-all | bytes 524288 | tf_op jit(solution)/shard_map/all_to_all | solution.py:446
  78.1 1.4 %collective-permute-start.12 = (f32[16,4,8,128]{3,2,1,0:T(8,128)S(1)}, f32[16,4,8,128]{3,2,1,0:T(8,128)S(1)}, u32[]{:S(2)}, u32[]{:S(2)}) collective-permute-start(f32[16,4,8,128]{3,2,1,0:T(8,128)S(1)} %all_to_all.11.after_ref), channel_id=1, source_target_pairs={{0,1},{1,0},{2,3},{3,2},{4,5},{5,4},{6,7},{7,6},{8,9},{9,8},{10,11... | collective-permute-start | bytes 786440 | tf_op jit(solution)/shard_map/ppermute | solution.py:438
  79.5 0.0 collective-permute-done.8.late_ref
  79.5 0.0 collective-permute-done.10.swapped_ref
  79.5 1.1 %object.1 = (f32[2,2,128,384]{3,2,1,0:T(8,128)}, f32[8,128]{1,0:T(8,128)S(1)}) custom-call(s32[8,128]{1,0:T(8,128)S(1)} %broadcast_in_dim.8.info_ref, f32[4,2,128,256]{3,2,1,0:T(8,128)S(1)} %get-tuple-element.25.core_ref, f32[520,256]{1,0:T(8,128)S(1)} %collective-permute-done.5.after_ref.early_ref, f32[1032,256]{1,0:T(8,128)S(1)} %collective-permute-done.7.beside_ref, ...), custom_call_target="tpu_custom_call" | custom-call | bytes 2000000 | tf_op jit(solution)/shard_map/object/pallas_call | solution.py:412
  80.6 0.0 collective-permute-done.12
  80.6 0.9 %probe.1 = f32[2,256,256]{2,1,0:T(8,128)} custom-call(f32[8,128]{1,0:T(8,128)S(1)} %get-tuple-element.35.after_ref, f32[32,2,8,128]{3,2,1,0:T(8,128)S(1)} %bitcast.6, f32[32,2,8,128]{3,2,1,0:T(8,128)S(1)} %bitcast.8), custom_call_target="tpu_custom_call" | custom-call | bytes 2000000 | tf_op jit(solution)/shard_map/probe/pallas_call | solution.py:412
  (6 shorter events, 0.1 us)
Async XLA Ops:
  0.6 5.9 %copy-start.4 = (s32[2,2]{1,0:T(2,128)S(1)}, s32[2,2]{1,0:T(2,128)}, u32[]{:S(2)}) copy-start(s32[2,2]{1,0:T(2,128)} %offsets_ref.7) | copy-start | bytes 52
  0.6 6.1 %collective-permute-start.1 = (f32[2,2,128,384]{3,2,1,0:T(8,128)}, f32[2,2,128,384]{3,2,1,0:T(8,128)S(1)}, u32[]{:S(2)}, u32[]{:S(2)}) collective-permute-start(f32[2,2,128,384]{3,2,1,0:T(8,128)} %own_ref.3), channel_id=1, source_target_pairs={{0,1},{1,0},{2,3},{3,2},{4,5},{5,4},{6,7},{7,6},{8,9},{9,8},{10,11... | collective-permute-start | bytes 2359304 | tf_op jit(solution)/shard_map/ppermute | solution.py:433
  2.1 11.9 %collective-permute-start = (f32[2,2,128,384]{3,2,1,0:T(8,128)}, f32[2,2,128,384]{3,2,1,0:T(8,128)S(1)}, u32[]{:S(2)}, u32[]{:S(2)}) collective-permute-start(f32[2,2,128,384]{3,2,1,0:T(8,128)} %own_ref.3), channel_id=1, source_target_pairs={{0,127},{1,2},{2,1},{3,4},{4,3},{5,6},{6,5},{7,8},{8,7},{9,10},{10... | collective-permute-start | bytes 2359304 | tf_op jit(solution)/shard_map/ppermute | solution.py:433
  4.8 11.3 %copy-start.2 = (f32[2,256,256]{2,1,0:T(8,128)S(1)}, f32[2,256,256]{2,1,0:T(8,128)}, u32[]{:S(2)}) copy-start(f32[2,256,256]{2,1,0:T(8,128)} %amp_ref.1) | copy-start | bytes 1572868
  4.8 13.5 %collective-permute-start.2 = (f32[2,2,128,256]{3,2,1,0:T(8,128)S(1)}, f32[2,2,128,256]{3,2,1,0:T(8,128)S(1)}, u32[]{:S(2)}, u32[]{:S(2)}) collective-permute-start(f32[2,2,128,256]{3,2,1,0:T(8,128)S(1)} %core.1), channel_id=1, source_target_pairs={{0,64},{64,0},{1,65},{65,1},{2,66},{66,2},{3,67},{67,3},{4,68},{68... | collective-permute-start | bytes 1572872 | tf_op jit(solution)/shard_map/ppermute | solution.py:461
  14.1 3.2 %copy-start.3 = (f32[2,256,256]{2,1,0:T(8,128)S(1)}, f32[2,256,256]{2,1,0:T(8,128)}, u32[]{:S(2)}) copy-start(f32[2,256,256]{2,1,0:T(8,128)} %probe_ref.1) | copy-start | bytes 1572868
  14.2 3.9 %copy-start.1 = (f32[2,2,128,384]{3,2,1,0:T(8,128)S(1)}, f32[2,2,128,384]{3,2,1,0:T(8,128)}, u32[]{:S(2)}) copy-start(f32[2,2,128,384]{3,2,1,0:T(8,128)} %own_ref.3) | copy-start | bytes 2359300
  14.2 8.7 %collective-permute-start.3 = (f32[2,128,256]{2,1,0:T(8,128)S(1)}, f32[2,128,256]{2,1,0:T(8,128)S(1)}, u32[]{:S(2)}, u32[]{:S(2)}) collective-permute-start(f32[2,128,256]{2,1,0:T(8,128)S(1)} %get-tuple-element.19), channel_id=1, source_target_pairs={{0,64},{64,0},{1,65},{65,1},{2,66},{66,2},{3,67},{67,3},{4,68},{68... | collective-permute-start | bytes 786440 | tf_op jit(solution)/shard_map/ppermute | solution.py:461
  16.0 12.5 %collective-permute-start.4 = (f32[2,128,256]{2,1,0:T(8,128)S(1)}, f32[2,128,256]{2,1,0:T(8,128)S(1)}, u32[]{:S(2)}, u32[]{:S(2)}) collective-permute-start(f32[2,128,256]{2,1,0:T(8,128)S(1)} %get-tuple-element.20), channel_id=1, source_target_pairs={{0,64},{64,0},{1,65},{65,1},{2,66},{66,2},{3,67},{67,3},{4,68},{68... | collective-permute-start | bytes 786440 | tf_op jit(solution)/shard_map/ppermute | solution.py:461
  18.1 4.8 %copy-start = (bf16[6,2,2,256,256]{4,3,2,1,0:T(8,128)(2,1)S(1)}, bf16[6,2,2,256,256]{4,3,2,1,0:T(8,128)(2,1)}, u32[]{:S(2)}) copy-start(bf16[6,2,2,256,256]{4,3,2,1,0:T(8,128)(2,1)} %constant.10.clone.tables_ref) | copy-start | bytes 9437188
  34.9 20.7 %collective-permute-start.5 = (f32[520,256]{1,0:T(8,128)S(1)}, f32[520,256]{1,0:T(8,128)S(1)}, u32[]{:S(2)}, u32[]{:S(2)}) collective-permute-start(f32[520,256]{1,0:T(8,128)S(1)} %get-tuple-element.26), channel_id=1, source_target_pairs={{0,127},{1,2},{2,1},{3,4},{4,3},{5,6},{6,5},{7,8},{8,7},{9,10},{10... | collective-permute-start | bytes 1597448 | tf_op jit(solution)/shard_map/ppermute | solution.py:433
  37.2 7.6 %collective-permute-start.6 = (f32[32,2,8,128]{3,2,1,0:T(8,128)S(1)}, f32[32,2,8,128]{3,2,1,0:T(8,128)S(1)}, u32[]{:S(2)}, u32[]{:S(2)}) collective-permute-start(f32[32,2,8,128]{3,2,1,0:T(8,128)S(1)} %get-tuple-element.30), channel_id=1, source_target_pairs={{0,1},{1,0},{2,3},{3,2},{4,5},{5,4},{6,7},{7,6},{8,9},{9,8},{10,11... | collective-permute-start | bytes 786440 | tf_op jit(solution)/shard_map/ppermute | solution.py:438
  55.6 4.4 %collective-permute-start.7 = (f32[1032,256]{1,0:T(8,128)S(1)}, f32[1032,256]{1,0:T(8,128)S(1)}, u32[]{:S(2)}, u32[]{:S(2)}) collective-permute-start(f32[1032,256]{1,0:T(8,128)S(1)} %get-tuple-element.31), channel_id=1, source_target_pairs={{0,1},{1,0},{2,3},{3,2},{4,5},{5,4},{6,7},{7,6},{8,9},{9,8},{10,11... | collective-permute-start | bytes 3170312 | tf_op jit(solution)/shard_map/ppermute | solution.py:433
  57.3 2.6 %collective-permute-start.9 = (f32[4,8,128]{2,1,0:T(8,128)S(1)}, f32[4,8,128]{2,1,0:T(8,128)S(1)}, u32[]{:S(2)}, u32[]{:S(2)}) collective-permute-start(f32[4,8,128]{2,1,0:T(8,128)S(1)} %reduce.1.keep_ref), channel_id=1, source_target_pairs={{0,64},{64,0},{1,65},{65,1},{2,66},{66,2},{3,67},{67,3},{4,68},{68... | collective-permute-start | bytes 49160 | tf_op jit(solution)/shard_map/ppermute | solution.py:461
  60.1 19.3 %collective-permute-start.10 = (f32[2,2,128,384]{3,2,1,0:T(8,128)S(1)}, f32[2,2,128,384]{3,2,1,0:T(8,128)S(1)}, u32[]{:S(2)}, u32[]{:S(2)}) collective-permute-start(f32[2,2,128,384]{3,2,1,0:T(8,128)S(1)} %sum.1), channel_id=1, source_target_pairs={{0,64},{64,0},{1,65},{65,1},{2,66},{66,2},{3,67},{67,3},{4,68},{68... | collective-permute-start | bytes 2359304 | tf_op jit(solution)/shard_map/ppermute | solution.py:461
  60.2 3.9 %collective-permute-start.11 = (f32[4,8,128]{2,1,0:T(8,128)S(1)}, f32[4,8,128]{2,1,0:T(8,128)S(1)}, u32[]{:S(2)}, u32[]{:S(2)}) collective-permute-start(f32[4,8,128]{2,1,0:T(8,128)S(1)} %add_slabs.1.after_ref.first_ref), channel_id=1, source_target_pairs={{0,96},{1,97},{2,98},{3,99},{4,100},{5,101},{6,102},{7,103},{8,104... | collective-permute-start | bytes 49160 | tf_op jit(solution)/shard_map/ppermute | solution.py:457
  61.6 17.9 %collective-permute-start.8 = (f32[512,256]{1,0:T(8,128)S(1)}, f32[512,256]{1,0:T(8,128)S(1)}, u32[]{:S(2)}, u32[]{:S(2)}) collective-permute-start(f32[512,256]{1,0:T(8,128)S(1)} %get-tuple-element.32), channel_id=1, source_target_pairs={{0,127},{1,2},{2,1},{3,4},{4,3},{5,6},{6,5},{7,8},{8,7},{9,10},{10... | collective-permute-start | bytes 1572872 | tf_op jit(solution)/shard_map/ppermute | solution.py:433
  78.1 2.6 %collective-permute-start.12 = (f32[16,4,8,128]{3,2,1,0:T(8,128)S(1)}, f32[16,4,8,128]{3,2,1,0:T(8,128)S(1)}, u32[]{:S(2)}, u32[]{:S(2)}) collective-permute-start(f32[16,4,8,128]{3,2,1,0:T(8,128)S(1)} %all_to_all.11.after_ref), channel_id=1, source_target_pairs={{0,1},{1,0},{2,3},{3,2},{4,5},{5,4},{6,7},{7,6},{8,9},{9,8},{10,11... | collective-permute-start | bytes 786440 | tf_op jit(solution)/shard_map/ppermute | solution.py:438
